TPU v7x, 32 devices: a whole 2x2x4 slice. The times are simulated.
32 devices in a mesh: groups: 2 (over y), rows: 4 (over z), segment: 2 (over x), sub: 2 (over core).
Axes of the slice: x: 2, y: 2, z: 4, core: 2. Of those that a mesh axis runs over, the one named last changes fastest.
Arguments:
- activations: bfloat16 [2, 8, 32, 256, 128], P('segment', 'groups', 'rows', 'sub'), parts along dimension 1, may hold values from -16 to 16
- latent: bfloat16 [8, 4, 32, 256], P('groups', None, 'rows', 'sub'), parts along dimension 0, may hold values from -6 to 6
- recon: bfloat16 [8, 3, 32, 256], P('groups', None, 'rows', 'sub'), parts along dimension 0, may hold values from -8 to 8, as said below
- target: bfloat16 [8, 3, 32, 256], P('groups', None, 'rows', 'sub'), parts along dimension 0, may hold values from -6 to 6
- boxes: int32 [8, 4, 4], P('groups'), parts along dimension 0, may hold values from 0 to 8, as said below
- kernel: bfloat16 [2, 1152, 128], P('segment'), may hold values from -0.1875 to 0.1875
- mod_weight: bfloat16 [2, 4, 256], P('segment'), may hold values from -3 to 3
- scale_bias: bfloat16 [2, 128], P('segment'), may hold values from 0.5 to 1.5
- shift_bias: bfloat16 [2, 128], P('segment'), may hold values from -3 to 3
- out_weight: bfloat16 [3, 128], replicated, may hold values from -3.5 to 3.5
Outputs:
- grad_acts: bfloat16 [2, 8, 32, 256, 128], P('segment', 'groups', 'rows', 'sub'), parts along dimension 1
- grad_kernel: float32 [2, 2304, 128], P('segment', 'groups'), parts along dimension 1
- grad_mod_weight: float32 [2, 8, 256], P('segment', 'groups'), parts along dimension 1
- grad_bias: float32 [2, 512], P('segment', 'groups'), parts along dimension 1
There are 2 independent parts, one for each index of `groups`. A program takes and returns all parts, laid end to end along the dimension named above; an argument that names none is the same for every part. Nothing has to cross between parts.
Inputs may be any that keep to these rules, and one draw needn't show every extreme that they name: `recon`: saved reconstruction. `boxes`: every box lies inside the image; its height is at least 0 tiles and its width at least 2 tiles, and box 0 of micro-batch 0 covers the whole image.
All inputs are finite; a program needn't handle non-finite values.
Results may differ from a plain program's by a relative error of at most 0.019.
Values may be sent and summed in bfloat16 or wider, within the bound.
No kernel may reach another device: no remote copies, remote signals or barrier semaphores. Data moves between devices by JAX's collectives and lax.ppermute only.
A program may use at most 64 MiB of HBM per device.

v0:
```python
import jax
import jax.numpy as jnp
from jax import lax
from jax.sharding import PartitionSpec as P

GROUPS = 32
TILE = 32


EPS = 1e-06


def extended(block, sides, width):
    for axis, dim in sides:
        count = lax.axis_size(axis)
        forward = [(i, i + 1) for i in range(count - 1)]
        backward = [(target, source) for source, target in forward]
        low = lax.ppermute(
            lax.slice_in_dim(block, block.shape[dim] - width, None, axis=dim), axis, forward
        )
        high = lax.ppermute(lax.slice_in_dim(block, 0, width, axis=dim), axis, backward)
        block = jnp.concatenate([low, block, high], axis=dim)
    return block


def from_behind(value, axis, steps):
    count = lax.axis_size(axis)
    initial, last = (max(0, -steps), min(count, count - steps))
    return lax.ppermute(value, axis, [(source, source + steps) for source in range(initial, last)])


def crop_weights(boxes, row_start, col_start, row_count, col_count, total_rows, total_cols):
    row_tile = (row_start + jnp.arange(row_count, dtype=jnp.int32)) // TILE
    col_tile = (col_start + jnp.arange(col_count, dtype=jnp.int32)) // TILE
    first_row = boxes[:, :, 0:1]
    first_col = boxes[:, :, 1:2]
    box_height = boxes[:, :, 2:3]
    box_width = boxes[:, :, 3:4]
    in_rows = ((row_tile >= first_row) & (row_tile < first_row + box_height)).astype(jnp.float32)
    in_cols = ((col_tile >= first_col) & (col_tile < first_col + box_width)).astype(jnp.float32)
    tiles = total_rows // TILE * (total_cols // TILE)
    share = tiles / (boxes.shape[1] * (box_height * box_width).astype(jnp.float32))
    return jnp.einsum("mkr,mkc->mrc", in_rows * share, in_cols)


def top_gradient(recon, target, cropped, out_weight):
    diff = 2.0 * (recon.astype(jnp.float32) - target.astype(jnp.float32)) * cropped[:, None]
    return jnp.einsum("mkhw,kc->mhwc", diff, out_weight.astype(jnp.float32)).astype(jnp.bfloat16)


def loss_gradient(
    boxes,
    recon,
    target,
    out_weight,
    row_start,
    col_start,
    row_count,
    col_count,
    total_rows,
    total_cols,
):
    cropped = crop_weights(
        boxes, row_start, col_start, row_count, col_count, total_rows, total_cols
    )
    return top_gradient(recon, target, cropped, out_weight)


def grouped_layout(value_array):
    return value_array.reshape(value_array.shape[:-1] + (GROUPS, value_array.shape[-1] // GROUPS))


def group_sums(value_array):
    shaped = grouped_layout(value_array)
    return (jnp.sum(shaped, axis=(-4, -3, -1)), jnp.sum(shaped * shaped, axis=(-4, -3, -1)))


def expand(stat):
    return stat[..., None, None, :, None]


def normalized_values(value_array, mean_val, rstd_val):
    shaped = grouped_layout(value_array)
    return ((shaped - expand(mean_val)) * expand(rstd_val)).reshape(value_array.shape)


def modulation(latent_batch, mix_weight, scale_row, shift_row):
    channel_count = scale_row.shape[-1]
    coefficients = jnp.einsum(
        "bzhw,zc->bhwc", latent_batch.astype(jnp.float32), mix_weight.astype(jnp.float32)
    )
    return (
        coefficients[..., :channel_count] + scale_row.astype(jnp.float32),
        coefficients[..., channel_count:] + shift_row.astype(jnp.float32),
    )


def transposed(weights):
    channel_count = weights.shape[-1]
    return (
        weights.reshape(9, channel_count, channel_count)
        .transpose(0, 2, 1)
        .reshape(9 * channel_count, channel_count)
    )


def taps(padded, row_count, col_count, flipped):
    pieces = []
    for tap_row in range(3):
        for tap_col in range(3):
            if flipped:
                row_offset, col_offset = (2 - tap_row, 2 - tap_col)
            else:
                row_offset, col_offset = (tap_row, tap_col)
            pieces.append(
                padded[:, row_offset : row_offset + row_count, col_offset : col_offset + col_count]
            )
    return jnp.concatenate(pieces, axis=-1).reshape(-1, 9 * padded.shape[-1])


def pick(value_array, index):
    return lax.dynamic_slice_in_dim(value_array, index, 1, 0)


def section_backward(
    value_array, latent_batch, incoming, spatial_scale, spatial_shift, weights_t, count
):
    batch, row_count, col_count, channel_count = value_array.shape
    sum_one, sum_two = group_sums(value_array)
    sum_one, sum_two = lax.psum((sum_one, sum_two), ("rows", "sub"))
    group_mean = sum_one / count
    inverse_deviation = lax.rsqrt(sum_two / count - group_mean * group_mean + EPS)
    centered_scaled = normalized_values(value_array, group_mean, inverse_deviation)
    pre_activation = centered_scaled * spatial_scale + spatial_shift
    hidden = jax.nn.silu(pre_activation).astype(jnp.bfloat16)
    padded_h = extended(hidden, (("rows", 1), ("sub", 2)), 1)
    padded_g = extended(incoming, (("rows", 1), ("sub", 2)), 1)
    patches = taps(padded_h, row_count, col_count, False)
    kernel_term = lax.dot_general(
        patches,
        incoming.reshape(-1, channel_count),
        (((0,), (0,)), ((), ())),
        preferred_element_type=jnp.float32,
    )
    hidden_grad = jnp.dot(
        taps(padded_g, row_count, col_count, True), weights_t, preferred_element_type=jnp.float32
    ).reshape(value_array.shape)
    sig = jax.nn.sigmoid(pre_activation)
    pre_activation_gradient = hidden_grad * (sig * (1.0 + pre_activation * (1.0 - sig)))
    paired_parts = jnp.concatenate(
        [pre_activation_gradient * centered_scaled, pre_activation_gradient], axis=-1
    )
    mod_term = jnp.einsum("bzhw,bhwc->zc", latent_batch.astype(jnp.float32), paired_parts)
    bias_term = jnp.sum(paired_parts, axis=(0, 1, 2))
    shaped_grad = grouped_layout(pre_activation_gradient * spatial_scale)
    reshaped_normalized = grouped_layout(centered_scaled)
    part_one = jnp.sum(shaped_grad, axis=(1, 2, 4))
    part_two = jnp.sum(shaped_grad * reshaped_normalized, axis=(1, 2, 4))
    part_one, part_two = lax.psum((part_one, part_two), ("rows", "sub"))
    mean_grad = part_one / count
    mean_cross = part_two / count
    adjust = expand(inverse_deviation) * (
        shaped_grad - expand(mean_grad) - reshaped_normalized * expand(mean_cross)
    )
    result = (incoming.astype(jnp.float32) + adjust.reshape(value_array.shape)).astype(jnp.bfloat16)
    return (result, kernel_term, mod_term, bias_term)


def body(
    activations,
    latent,
    recon,
    target,
    boxes,
    kernel,
    mod_weight,
    scale_bias,
    shift_bias,
    out_weight,
):
    segments = lax.axis_size("segment")
    segment_index = lax.axis_index("segment")
    micro, row_count, col_count, channel_count = activations.shape[1:]
    total_rows = row_count * lax.axis_size("rows")
    total_cols = col_count * lax.axis_size("sub")
    count = total_rows * total_cols * (channel_count // GROUPS)
    row_start = lax.axis_index("rows") * row_count
    col_start = lax.axis_index("sub") * col_count
    acts = activations[0]
    weights_t = transposed(kernel[0])
    mix_weight = mod_weight[0]
    scale_row = scale_bias[0]
    shift_row = shift_bias[0]
    top = loss_gradient(
        boxes,
        recon,
        target,
        out_weight,
        row_start,
        col_start,
        row_count,
        col_count,
        total_rows,
        total_cols,
    )

    def tick(step, carry):
        passing, grads_out, kernel_grad, mod_grad, bias_grad = carry
        offset = step - (segments - 1 - segment_index)
        valid = (offset >= 0) & (offset < micro)
        index = jnp.clip(offset, 0, micro - 1)
        received = from_behind(passing, "segment", -1)
        incoming = jnp.where(segment_index == segments - 1, pick(top, index), received)
        value_array = pick(acts, index).astype(jnp.float32)
        latent_m = pick(latent, index)
        spatial_scale, spatial_shift = modulation(latent_m, mix_weight, scale_row, shift_row)
        result, kernel_term, mod_term, bias_term = section_backward(
            value_array, latent_m, incoming, spatial_scale, spatial_shift, weights_t, count
        )
        weight = valid.astype(jnp.float32)
        current = pick(grads_out, index)
        grads_out = lax.dynamic_update_slice_in_dim(
            grads_out, jnp.where(valid, result, current), index, 0
        )
        return (
            result,
            grads_out,
            kernel_grad + weight * kernel_term,
            mod_grad + weight * mod_term,
            bias_grad + weight * bias_term,
        )

    initial = (
        jnp.zeros((1, row_count, col_count, channel_count), jnp.bfloat16),
        jnp.zeros_like(acts),
        jnp.zeros((9 * channel_count, channel_count), jnp.float32),
        jnp.zeros((mix_weight.shape[0], 2 * channel_count), jnp.float32),
        jnp.zeros((2 * channel_count,), jnp.float32),
    )
    final = lax.fori_loop(0, micro + segments - 1, tick, initial)
    grads_out = final[1][None]
    kernel_grad = final[2][None]
    mod_grad = final[3][None]
    bias_grad = final[4][None]
    kernel_grad, mod_grad, bias_grad = lax.psum((kernel_grad, mod_grad, bias_grad), ("rows", "sub"))
    return (grads_out, kernel_grad, mod_grad, bias_grad)


def solution(mesh):
    placed = (
        P("segment", "groups", "rows", "sub", None),
        P("groups", None, "rows", "sub"),
        P("groups", None, "rows", "sub"),
        P("groups", None, "rows", "sub"),
        P("groups", None, None),
        P("segment", None, None),
        P("segment", None, None),
        P("segment", None),
        P("segment", None),
        P(),
    )
    return jax.shard_map(
        body,
        mesh=mesh,
        in_specs=placed,
        out_specs=(
            P("segment", "groups", "rows", "sub", None),
            P("segment", "groups", None),
            P("segment", "groups", None),
            P("segment", "groups"),
        ),
        check_vma=False,
    )
```

profile of v0, /device:TPU:0, one launch (start us, length us, event | category | flops | bytes accessed | tf_op | source)
XLA Modules:
  0.0 399.3 jit_solution(1362469412913186722)
XLA Ops:
  9.5 1.9 copy.20
  14.2 319.4 %while.24 = (s32[]{:T(128)}, bf16[1,8,128,128]{3,2,1,0:T(8,128)(2,1)S(1)}, bf16[4,8,128,128]{3,2,1,0:T(8,128)(2,1)}, f32[1152,128]{1,0:T(8,128)S(1)}, f32[4,256]...) while((s32[]{:T(128)}, ...), condition=%wide.region_14.15_spmd.clone, body=%wide.region_0.14_spmd.clone.sunk | while | flops 622716928 | bytes 39912900 | solution.py:240
  14.2 1.3 collective-permute-start
  17.1 18.1 %all-reduce.5 = (f32[1,32]{1,0:T(1,128)S(1)}, f32[1,32]{1,0:T(1,128)S(1)}) all-reduce(f32[1,32]{1,0:T(1,128)S(1)} %bitcast.121, f32[1,32]{1,0:T(1,128)S(1)} %bitcast.123), channel_id=1, replica_groups=mesh['groups'=2,'rows'=4,'segment'=2,'sub'=2] {'rows','sub'}, use_global_device_ids=true, to_apply=%region_3.3 | all-reduce | flops 64 | bytes 512 | tf_op jit(solution)/shard_map/while/body/eval_jaxpr/psum | solution.py:130
  35.2 1.3 collective-permute-start.1
  36.5 4.5 %collective-permute-start.2 = (bf16[1,1,128,128]{3,2,1,0:T(8,128)(2,1)S(1)}, bf16[1,1,128,128]{3,2,1,0:T(8,128)(2,1)S(1)}, u32[]{:S(2)}, u32[]{:S(2)}) collective-permute-start(bf16[1,1,128,128]{3,2,1,0:T(8,128)(2,1)S(1)} %get-tuple-element.605), channel_id=1, source_target_pairs={{0,4},{4,8},{8,12},{1,5},{5,9},{9,13},{2,6},{6,10},{10,14},{3,7},{... | collective-permute-start | bytes 98312 | tf_op jit(solution)/shard_map/while/body/eval_jaxpr/ppermute | solution.py:18
  44.0 1.3 collective-permute-start.4
  48.2 2.8 fusion.81
  50.9 1.3 collective-permute-start.5
  52.2 4.9 %collective-permute-start.6 = (bf16[1,1,128,128]{3,2,1,0:T(8,128)(2,1)S(1)}, bf16[1,1,128,128]{3,2,1,0:T(8,128)(2,1)S(1)}, u32[]{:S(2)}, u32[]{:S(2)}) collective-permute-start(bf16[1,1,128,128]{3,2,1,0:T(8,128)(2,1)S(1)} %get-tuple-element.621), channel_id=1, source_target_pairs={{0,4},{4,8},{8,12},{1,5},{5,9},{9,13},{2,6},{6,10},{10,14},{3,7},{... | collective-permute-start | bytes 98312 | tf_op jit(solution)/shard_map/while/body/eval_jaxpr/ppermute | solution.py:18
  57.6 13.6 %all-reduce.6 = (f32[1,32]{1,0:T(1,128)S(1)}, f32[1,32]{1,0:T(1,128)S(1)}) all-reduce(f32[1,32]{1,0:T(1,128)S(1)} %bitcast.120, f32[1,32]{1,0:T(1,128)S(1)} %bitcast.122), channel_id=1, replica_groups=mesh['groups'=2,'rows'=4,'segment'=2,'sub'=2] {'rows','sub'}, use_global_device_ids=true, to_apply=%region_12.12 | all-reduce | flops 64 | bytes 512 | tf_op jit(solution)/shard_map/while/body/eval_jaxpr/psum | solution.py:159
  71.5 2.1 select_dynamic-update-slice_fusion.2
  74.1 1.3 collective-permute-start.7
  75.4 3.0 collective-permute-start.8
  81.4 1.3 collective-permute-start
  84.3 13.9 %all-reduce.5 = (f32[1,32]{1,0:T(1,128)S(1)}, f32[1,32]{1,0:T(1,128)S(1)}) all-reduce(f32[1,32]{1,0:T(1,128)S(1)} %bitcast.121, f32[1,32]{1,0:T(1,128)S(1)} %bitcast.123), channel_id=1, replica_groups=mesh['groups'=2,'rows'=4,'segment'=2,'sub'=2] {'rows','sub'}, use_global_device_ids=true, to_apply=%region_3.3 | all-reduce | flops 64 | bytes 512 | tf_op jit(solution)/shard_map/while/body/eval_jaxpr/psum | solution.py:130
  98.3 1.3 collective-permute-start.1
  99.6 4.5 %collective-permute-start.2 = (bf16[1,1,128,128]{3,2,1,0:T(8,128)(2,1)S(1)}, bf16[1,1,128,128]{3,2,1,0:T(8,128)(2,1)S(1)}, u32[]{:S(2)}, u32[]{:S(2)}) collective-permute-start(bf16[1,1,128,128]{3,2,1,0:T(8,128)(2,1)S(1)} %get-tuple-element.605), channel_id=1, source_target_pairs={{0,4},{4,8},{8,12},{1,5},{5,9},{9,13},{2,6},{6,10},{10,14},{3,7},{... | collective-permute-start | bytes 98312 | tf_op jit(solution)/shard_map/while/body/eval_jaxpr/ppermute | solution.py:18
  107.0 1.3 collective-permute-start.4
  111.2 2.8 fusion.81
  114.0 1.3 collective-permute-start.5
  115.3 4.9 %collective-permute-start.6 = (bf16[1,1,128,128]{3,2,1,0:T(8,128)(2,1)S(1)}, bf16[1,1,128,128]{3,2,1,0:T(8,128)(2,1)S(1)}, u32[]{:S(2)}, u32[]{:S(2)}) collective-permute-start(bf16[1,1,128,128]{3,2,1,0:T(8,128)(2,1)S(1)} %get-tuple-element.621), channel_id=1, source_target_pairs={{0,4},{4,8},{8,12},{1,5},{5,9},{9,13},{2,6},{6,10},{10,14},{3,7},{... | collective-permute-start | bytes 98312 | tf_op jit(solution)/shard_map/while/body/eval_jaxpr/ppermute | solution.py:18
  120.6 13.6 %all-reduce.6 = (f32[1,32]{1,0:T(1,128)S(1)}, f32[1,32]{1,0:T(1,128)S(1)}) all-reduce(f32[1,32]{1,0:T(1,128)S(1)} %bitcast.120, f32[1,32]{1,0:T(1,128)S(1)} %bitcast.122), channel_id=1, replica_groups=mesh['groups'=2,'rows'=4,'segment'=2,'sub'=2] {'rows','sub'}, use_global_device_ids=true, to_apply=%region_12.12 | all-reduce | flops 64 | bytes 512 | tf_op jit(solution)/shard_map/while/body/eval_jaxpr/psum | solution.py:159
  134.6 2.1 select_dynamic-update-slice_fusion.2
  137.1 1.3 collective-permute-start.7
  138.4 3.0 collective-permute-start.8
  144.5 1.3 collective-permute-start
  147.3 13.9 %all-reduce.5 = (f32[1,32]{1,0:T(1,128)S(1)}, f32[1,32]{1,0:T(1,128)S(1)}) all-reduce(f32[1,32]{1,0:T(1,128)S(1)} %bitcast.121, f32[1,32]{1,0:T(1,128)S(1)} %bitcast.123), channel_id=1, replica_groups=mesh['groups'=2,'rows'=4,'segment'=2,'sub'=2] {'rows','sub'}, use_global_device_ids=true, to_apply=%region_3.3 | all-reduce | flops 64 | bytes 512 | tf_op jit(solution)/shard_map/while/body/eval_jaxpr/psum | solution.py:130
  161.3 1.3 collective-permute-start.1
  162.6 4.5 %collective-permute-start.2 = (bf16[1,1,128,128]{3,2,1,0:T(8,128)(2,1)S(1)}, bf16[1,1,128,128]{3,2,1,0:T(8,128)(2,1)S(1)}, u32[]{:S(2)}, u32[]{:S(2)}) collective-permute-start(bf16[1,1,128,128]{3,2,1,0:T(8,128)(2,1)S(1)} %get-tuple-element.605), channel_id=1, source_target_pairs={{0,4},{4,8},{8,12},{1,5},{5,9},{9,13},{2,6},{6,10},{10,14},{3,7},{... | collective-permute-start | bytes 98312 | tf_op jit(solution)/shard_map/while/body/eval_jaxpr/ppermute | solution.py:18
  170.1 1.3 collective-permute-start.4
  174.2 2.8 fusion.81
  177.0 1.3 collective-permute-start.5
  178.3 4.9 %collective-permute-start.6 = (bf16[1,1,128,128]{3,2,1,0:T(8,128)(2,1)S(1)}, bf16[1,1,128,128]{3,2,1,0:T(8,128)(2,1)S(1)}, u32[]{:S(2)}, u32[]{:S(2)}) collective-permute-start(bf16[1,1,128,128]{3,2,1,0:T(8,128)(2,1)S(1)} %get-tuple-element.621), channel_id=1, source_target_pairs={{0,4},{4,8},{8,12},{1,5},{5,9},{9,13},{2,6},{6,10},{10,14},{3,7},{... | collective-permute-start | bytes 98312 | tf_op jit(solution)/shard_map/while/body/eval_jaxpr/ppermute | solution.py:18
  183.6 13.6 %all-reduce.6 = (f32[1,32]{1,0:T(1,128)S(1)}, f32[1,32]{1,0:T(1,128)S(1)}) all-reduce(f32[1,32]{1,0:T(1,128)S(1)} %bitcast.120, f32[1,32]{1,0:T(1,128)S(1)} %bitcast.122), channel_id=1, replica_groups=mesh['groups'=2,'rows'=4,'segment'=2,'sub'=2] {'rows','sub'}, use_global_device_ids=true, to_apply=%region_12.12 | all-reduce | flops 64 | bytes 512 | tf_op jit(solution)/shard_map/while/body/eval_jaxpr/psum | solution.py:159
  197.6 2.1 select_dynamic-update-slice_fusion.2
  200.1 1.3 collective-permute-start.7
  201.4 3.0 collective-permute-start.8
  207.5 1.3 collective-permute-start
  210.4 13.9 %all-reduce.5 = (f32[1,32]{1,0:T(1,128)S(1)}, f32[1,32]{1,0:T(1,128)S(1)}) all-reduce(f32[1,32]{1,0:T(1,128)S(1)} %bitcast.121, f32[1,32]{1,0:T(1,128)S(1)} %bitcast.123), channel_id=1, replica_groups=mesh['groups'=2,'rows'=4,'segment'=2,'sub'=2] {'rows','sub'}, use_global_device_ids=true, to_apply=%region_3.3 | all-reduce | flops 64 | bytes 512 | tf_op jit(solution)/shard_map/while/body/eval_jaxpr/psum | solution.py:130
  224.4 1.3 collective-permute-start.1
  225.7 4.5 %collective-permute-start.2 = (bf16[1,1,128,128]{3,2,1,0:T(8,128)(2,1)S(1)}, bf16[1,1,128,128]{3,2,1,0:T(8,128)(2,1)S(1)}, u32[]{:S(2)}, u32[]{:S(2)}) collective-permute-start(bf16[1,1,128,128]{3,2,1,0:T(8,128)(2,1)S(1)} %get-tuple-element.605), channel_id=1, source_target_pairs={{0,4},{4,8},{8,12},{1,5},{5,9},{9,13},{2,6},{6,10},{10,14},{3,7},{... | collective-permute-start | bytes 98312 | tf_op jit(solution)/shard_map/while/body/eval_jaxpr/ppermute | solution.py:18
  233.1 1.3 collective-permute-start.4
  237.3 2.8 fusion.81
  240.1 1.3 collective-permute-start.5
  241.4 4.9 %collective-permute-start.6 = (bf16[1,1,128,128]{3,2,1,0:T(8,128)(2,1)S(1)}, bf16[1,1,128,128]{3,2,1,0:T(8,128)(2,1)S(1)}, u32[]{:S(2)}, u32[]{:S(2)}) collective-permute-start(bf16[1,1,128,128]{3,2,1,0:T(8,128)(2,1)S(1)} %get-tuple-element.621), channel_id=1, source_target_pairs={{0,4},{4,8},{8,12},{1,5},{5,9},{9,13},{2,6},{6,10},{10,14},{3,7},{... | collective-permute-start | bytes 98312 | tf_op jit(solution)/shard_map/while/body/eval_jaxpr/ppermute | solution.py:18
  246.7 13.6 %all-reduce.6 = (f32[1,32]{1,0:T(1,128)S(1)}, f32[1,32]{1,0:T(1,128)S(1)}) all-reduce(f32[1,32]{1,0:T(1,128)S(1)} %bitcast.120, f32[1,32]{1,0:T(1,128)S(1)} %bitcast.122), channel_id=1, replica_groups=mesh['groups'=2,'rows'=4,'segment'=2,'sub'=2] {'rows','sub'}, use_global_device_ids=true, to_apply=%region_12.12 | all-reduce | flops 64 | bytes 512 | tf_op jit(solution)/shard_map/while/body/eval_jaxpr/psum | solution.py:159
  260.7 2.1 select_dynamic-update-slice_fusion.2
  263.2 1.3 collective-permute-start.7
  264.5 3.0 collective-permute-start.8
  270.5 1.3 collective-permute-start
  273.4 13.9 %all-reduce.5 = (f32[1,32]{1,0:T(1,128)S(1)}, f32[1,32]{1,0:T(1,128)S(1)}) all-reduce(f32[1,32]{1,0:T(1,128)S(1)} %bitcast.121, f32[1,32]{1,0:T(1,128)S(1)} %bitcast.123), channel_id=1, replica_groups=mesh['groups'=2,'rows'=4,'segment'=2,'sub'=2] {'rows','sub'}, use_global_device_ids=true, to_apply=%region_3.3 | all-reduce | flops 64 | bytes 512 | tf_op jit(solution)/shard_map/while/body/eval_jaxpr/psum | solution.py:130
  287.4 1.3 collective-permute-start.1
  288.7 4.5 %collective-permute-start.2 = (bf16[1,1,128,128]{3,2,1,0:T(8,128)(2,1)S(1)}, bf16[1,1,128,128]{3,2,1,0:T(8,128)(2,1)S(1)}, u32[]{:S(2)}, u32[]{:S(2)}) collective-permute-start(bf16[1,1,128,128]{3,2,1,0:T(8,128)(2,1)S(1)} %get-tuple-element.605), channel_id=1, source_target_pairs={{0,4},{4,8},{8,12},{1,5},{5,9},{9,13},{2,6},{6,10},{10,14},{3,7},{... | collective-permute-start | bytes 98312 | tf_op jit(solution)/shard_map/while/body/eval_jaxpr/ppermute | solution.py:18
  296.2 1.3 collective-permute-start.4
  300.3 2.8 fusion.81
  303.1 1.3 collective-permute-start.5
  304.4 4.9 %collective-permute-start.6 = (bf16[1,1,128,128]{3,2,1,0:T(8,128)(2,1)S(1)}, bf16[1,1,128,128]{3,2,1,0:T(8,128)(2,1)S(1)}, u32[]{:S(2)}, u32[]{:S(2)}) collective-permute-start(bf16[1,1,128,128]{3,2,1,0:T(8,128)(2,1)S(1)} %get-tuple-element.621), channel_id=1, source_target_pairs={{0,4},{4,8},{8,12},{1,5},{5,9},{9,13},{2,6},{6,10},{10,14},{3,7},{... | collective-permute-start | bytes 98312 | tf_op jit(solution)/shard_map/while/body/eval_jaxpr/ppermute | solution.py:18
  309.7 13.6 %all-reduce.6 = (f32[1,32]{1,0:T(1,128)S(1)}, f32[1,32]{1,0:T(1,128)S(1)}) all-reduce(f32[1,32]{1,0:T(1,128)S(1)} %bitcast.120, f32[1,32]{1,0:T(1,128)S(1)} %bitcast.122), channel_id=1, replica_groups=mesh['groups'=2,'rows'=4,'segment'=2,'sub'=2] {'rows','sub'}, use_global_device_ids=true, to_apply=%region_12.12 | all-reduce | flops 64 | bytes 512 | tf_op jit(solution)/shard_map/while/body/eval_jaxpr/psum | solution.py:159
  323.7 2.1 select_dynamic-update-slice_fusion.2
  327.5 3.0 collective-permute-start.8
  334.4 15.1 %all-reduce.2 = (f32[1,4,256]{2,1,0:T(4,128)}, f32[1,256]{1,0:T(1,128)}) all-reduce(f32[1,4,256]{2,1,0:T(4,128)S(1)} %bitcast.116, f32[1,256]{1,0:T(1,128)} %bitcast.119), channel_id=1, replica_groups=mesh['groups'=2,'rows'=4,'segment'=2,'sub'=2] {'rows','sub'}, use_global_device_ids=true, to_apply=%region_16.17 | all-reduce | flops 1280 | bytes 10240 | tf_op jit(solution)/shard_map/psum | solution.py:245
  349.5 41.0 %all-reduce.9.cloned.1.call-done = f32[1,1152,128]{2,1,0:T(8,128)} async-done(((f32[1,1152,128]{2,1,0:T(8,128)}), f32[1,1152,128]{2,1,0:T(8,128)}) %all-reduce.9.cloned.1.call-update) | async-done | bytes 589840 | tf_op jit(solution)/shard_map/psum | solution.py:245
  390.5 1.9 copy.70
  (440 shorter events, 63.1 us)
Async XLA Ops:
  7.2 5.3 %copy-start = (bf16[3,128]{1,0:T(4,128)(2,1)S(1)}, bf16[3,128]{1,0:T(4,128)(2,1)}, u32[]{:S(2)}) copy-start(bf16[3,128]{1,0:T(4,128)(2,1)} %param.21) | copy-start | bytes 2308
  7.2 7.0 %copy-start.5 = (bf16[1,4,256]{2,1,0:T(4,128)(2,1)S(1)}, bf16[1,4,256]{2,1,0:T(4,128)(2,1)}, u32[]{:S(2)}) copy-start(bf16[1,4,256]{2,1,0:T(4,128)(2,1)} %param.18) | copy-start | bytes 6148
  7.2 7.0 %copy-start.11 = (bf16[1,128]{1,0:T(2,128)(2,1)S(1)}, bf16[1,128]{1,0:T(2,128)(2,1)}, u32[]{:S(2)}) copy-start(bf16[1,128]{1,0:T(2,128)(2,1)} %param.19) | copy-start | bytes 772
  7.2 7.0 %copy-start.13 = (bf16[1,128]{1,0:T(2,128)(2,1)S(1)}, bf16[1,128]{1,0:T(2,128)(2,1)}, u32[]{:S(2)}) copy-start(bf16[1,128]{1,0:T(2,128)(2,1)} %param.20) | copy-start | bytes 772
  7.2 383.3 %all-reduce.9.cloned.1.call-start = ((), (), s32[]{:S(2)}) async-start(), calls=%async_computation | async-start | bytes 1179648 | tf_op jit(solution)/shard_map/psum | solution.py:245
  14.2 31.9 %copy-start.2 = (bf16[4,8,128,128]{3,2,1,0:T(8,128)(2,1)}, bf16[4,8,128,128]{3,2,1,0:T(8,128)(2,1)S(1)}, u32[]{:S(2)}) copy-start(bf16[4,8,128,128]{3,2,1,0:T(8,128)(2,1)S(1)} %get-tuple-element.676) | copy-start | bytes 3145732 | tf_op jit(solution)/shard_map/while
  14.2 20.9 %collective-permute-start = (bf16[1,8,128,128]{3,2,1,0:T(8,128)(2,1)S(1)}, bf16[1,8,128,128]{3,2,1,0:T(8,128)(2,1)S(1)}, u32[]{:S(2)}, u32[]{:S(2)}) collective-permute-start(bf16[1,8,128,128]{3,2,1,0:T(8,128)(2,1)S(1)} %broadcast_select_fusion.2), channel_id=1, source_target_pairs={{2,0},{3,1},{6,4},{7,5},{10,8},{11,9},{14,12},{15,13},{18,16},{19,... | collective-permute-start | bytes 786440 | tf_op jit(solution)/shard_map/while/body/eval_jaxpr/ppermute | solution.py:29
  35.2 6.6 %collective-permute-start.1 = (bf16[1,1,128,128]{3,2,1,0:T(8,128)(2,1)S(1)}, bf16[1,1,128,128]{3,2,1,0:T(8,128)(2,1)S(1)}, u32[]{:S(2)}, u32[]{:S(2)}) collective-permute-start(bf16[1,1,128,128]{3,2,1,0:T(8,128)(2,1)S(1)} %get-tuple-element.604), channel_id=1, source_target_pairs={{4,0},{8,4},{12,8},{5,1},{9,5},{13,9},{6,2},{10,6},{14,10},{7,3},{... | collective-permute-start | bytes 98312 | tf_op jit(solution)/shard_map/while/body/eval_jaxpr/ppermute | solution.py:21
  36.5 6.1 %collective-permute-start.2 = (bf16[1,1,128,128]{3,2,1,0:T(8,128)(2,1)S(1)}, bf16[1,1,128,128]{3,2,1,0:T(8,128)(2,1)S(1)}, u32[]{:S(2)}, u32[]{:S(2)}) collective-permute-start(bf16[1,1,128,128]{3,2,1,0:T(8,128)(2,1)S(1)} %get-tuple-element.605), channel_id=1, source_target_pairs={{0,4},{4,8},{8,12},{1,5},{5,9},{9,13},{2,6},{6,10},{10,14},{3,7},{... | collective-permute-start | bytes 98312 | tf_op jit(solution)/shard_map/while/body/eval_jaxpr/ppermute | solution.py:18
  42.7 3.4 collective-permute-start.3
  44.0 3.1 collective-permute-start.4
  45.8 2.2 copy-start.7
  50.9 27.5 %copy-start.9 = (f32[256]{0:T(256)S(1)}, f32[256]{0:T(256)}, u32[]{:S(2)}) copy-start(f32[256]{0:T(256)} %get-tuple-element.653) | copy-start | bytes 3076 | tf_op jit(solution)/shard_map/while
  50.9 23.1 %collective-permute-start.5 = (bf16[1,1,128,128]{3,2,1,0:T(8,128)(2,1)S(1)}, bf16[1,1,128,128]{3,2,1,0:T(8,128)(2,1)S(1)}, u32[]{:S(2)}, u32[]{:S(2)}) collective-permute-start(bf16[1,1,128,128]{3,2,1,0:T(8,128)(2,1)S(1)} %get-tuple-element.620), channel_id=1, source_target_pairs={{4,0},{8,4},{12,8},{5,1},{9,5},{13,9},{6,2},{10,6},{14,10},{7,3},{... | collective-permute-start | bytes 98312 | tf_op jit(solution)/shard_map/while/body/eval_jaxpr/ppermute | solution.py:21
  52.2 21.8 %collective-permute-start.6 = (bf16[1,1,128,128]{3,2,1,0:T(8,128)(2,1)S(1)}, bf16[1,1,128,128]{3,2,1,0:T(8,128)(2,1)S(1)}, u32[]{:S(2)}, u32[]{:S(2)}) collective-permute-start(bf16[1,1,128,128]{3,2,1,0:T(8,128)(2,1)S(1)} %get-tuple-element.621), channel_id=1, source_target_pairs={{0,4},{4,8},{8,12},{1,5},{5,9},{9,13},{2,6},{6,10},{10,14},{3,7},{... | collective-permute-start | bytes 98312 | tf_op jit(solution)/shard_map/while/body/eval_jaxpr/ppermute | solution.py:18
  74.1 4.4 %collective-permute-start.7 = (bf16[1,10,1,128]{3,2,1,0:T(2,128)(2,1)S(1)}, bf16[1,10,1,128]{3,2,1,0:T(2,128)(2,1)S(1)}, u32[]{:S(2)}, u32[]{:S(2)}) collective-permute-start(bf16[1,10,1,128]{3,2,1,0:T(2,128)(2,1)S(1)} %get-tuple-element.622), channel_id=1, source_target_pairs={{1,0},{3,2},{5,4},{7,6},{9,8},{11,10},{13,12},{15,14},{17,16},{19,... | collective-permute-start | bytes 7688 | tf_op jit(solution)/shard_map/while/body/eval_jaxpr/ppermute | solution.py:21
  75.4 3.8 collective-permute-start.8
  81.4 27.7 %copy-start.2 = (bf16[4,8,128,128]{3,2,1,0:T(8,128)(2,1)}, bf16[4,8,128,128]{3,2,1,0:T(8,128)(2,1)S(1)}, u32[]{:S(2)}) copy-start(bf16[4,8,128,128]{3,2,1,0:T(8,128)(2,1)S(1)} %get-tuple-element.676) | copy-start | bytes 3145732 | tf_op jit(solution)/shard_map/while
  81.4 16.8 %collective-permute-start = (bf16[1,8,128,128]{3,2,1,0:T(8,128)(2,1)S(1)}, bf16[1,8,128,128]{3,2,1,0:T(8,128)(2,1)S(1)}, u32[]{:S(2)}, u32[]{:S(2)}) collective-permute-start(bf16[1,8,128,128]{3,2,1,0:T(8,128)(2,1)S(1)} %broadcast_select_fusion.2), channel_id=1, source_target_pairs={{2,0},{3,1},{6,4},{7,5},{10,8},{11,9},{14,12},{15,13},{18,16},{19,... | collective-permute-start | bytes 786440 | tf_op jit(solution)/shard_map/while/body/eval_jaxpr/ppermute | solution.py:29
  98.3 6.6 %collective-permute-start.1 = (bf16[1,1,128,128]{3,2,1,0:T(8,128)(2,1)S(1)}, bf16[1,1,128,128]{3,2,1,0:T(8,128)(2,1)S(1)}, u32[]{:S(2)}, u32[]{:S(2)}) collective-permute-start(bf16[1,1,128,128]{3,2,1,0:T(8,128)(2,1)S(1)} %get-tuple-element.604), channel_id=1, source_target_pairs={{4,0},{8,4},{12,8},{5,1},{9,5},{13,9},{6,2},{10,6},{14,10},{7,3},{... | collective-permute-start | bytes 98312 | tf_op jit(solution)/shard_map/while/body/eval_jaxpr/ppermute | solution.py:21
  99.6 6.1 %collective-permute-start.2 = (bf16[1,1,128,128]{3,2,1,0:T(8,128)(2,1)S(1)}, bf16[1,1,128,128]{3,2,1,0:T(8,128)(2,1)S(1)}, u32[]{:S(2)}, u32[]{:S(2)}) collective-permute-start(bf16[1,1,128,128]{3,2,1,0:T(8,128)(2,1)S(1)} %get-tuple-element.605), channel_id=1, source_target_pairs={{0,4},{4,8},{8,12},{1,5},{5,9},{9,13},{2,6},{6,10},{10,14},{3,7},{... | collective-permute-start | bytes 98312 | tf_op jit(solution)/shard_map/while/body/eval_jaxpr/ppermute | solution.py:18
  105.7 3.4 collective-permute-start.3
  107.0 3.1 collective-permute-start.4
  114.0 27.5 %copy-start.9 = (f32[256]{0:T(256)S(1)}, f32[256]{0:T(256)}, u32[]{:S(2)}) copy-start(f32[256]{0:T(256)} %get-tuple-element.653) | copy-start | bytes 3076 | tf_op jit(solution)/shard_map/while
  114.0 23.1 %collective-permute-start.5 = (bf16[1,1,128,128]{3,2,1,0:T(8,128)(2,1)S(1)}, bf16[1,1,128,128]{3,2,1,0:T(8,128)(2,1)S(1)}, u32[]{:S(2)}, u32[]{:S(2)}) collective-permute-start(bf16[1,1,128,128]{3,2,1,0:T(8,128)(2,1)S(1)} %get-tuple-element.620), channel_id=1, source_target_pairs={{4,0},{8,4},{12,8},{5,1},{9,5},{13,9},{6,2},{10,6},{14,10},{7,3},{... | collective-permute-start | bytes 98312 | tf_op jit(solution)/shard_map/while/body/eval_jaxpr/ppermute | solution.py:21
  115.3 21.8 %collective-permute-start.6 = (bf16[1,1,128,128]{3,2,1,0:T(8,128)(2,1)S(1)}, bf16[1,1,128,128]{3,2,1,0:T(8,128)(2,1)S(1)}, u32[]{:S(2)}, u32[]{:S(2)}) collective-permute-start(bf16[1,1,128,128]{3,2,1,0:T(8,128)(2,1)S(1)} %get-tuple-element.621), channel_id=1, source_target_pairs={{0,4},{4,8},{8,12},{1,5},{5,9},{9,13},{2,6},{6,10},{10,14},{3,7},{... | collective-permute-start | bytes 98312 | tf_op jit(solution)/shard_map/while/body/eval_jaxpr/ppermute | solution.py:18
  137.1 4.4 %collective-permute-start.7 = (bf16[1,10,1,128]{3,2,1,0:T(2,128)(2,1)S(1)}, bf16[1,10,1,128]{3,2,1,0:T(2,128)(2,1)S(1)}, u32[]{:S(2)}, u32[]{:S(2)}) collective-permute-start(bf16[1,10,1,128]{3,2,1,0:T(2,128)(2,1)S(1)} %get-tuple-element.622), channel_id=1, source_target_pairs={{1,0},{3,2},{5,4},{7,6},{9,8},{11,10},{13,12},{15,14},{17,16},{19,... | collective-permute-start | bytes 7688 | tf_op jit(solution)/shard_map/while/body/eval_jaxpr/ppermute | solution.py:21
  138.4 3.8 collective-permute-start.8
  144.4 27.7 %copy-start.2 = (bf16[4,8,128,128]{3,2,1,0:T(8,128)(2,1)}, bf16[4,8,128,128]{3,2,1,0:T(8,128)(2,1)S(1)}, u32[]{:S(2)}) copy-start(bf16[4,8,128,128]{3,2,1,0:T(8,128)(2,1)S(1)} %get-tuple-element.676) | copy-start | bytes 3145732 | tf_op jit(solution)/shard_map/while
  144.5 16.8 %collective-permute-start = (bf16[1,8,128,128]{3,2,1,0:T(8,128)(2,1)S(1)}, bf16[1,8,128,128]{3,2,1,0:T(8,128)(2,1)S(1)}, u32[]{:S(2)}, u32[]{:S(2)}) collective-permute-start(bf16[1,8,128,128]{3,2,1,0:T(8,128)(2,1)S(1)} %broadcast_select_fusion.2), channel_id=1, source_target_pairs={{2,0},{3,1},{6,4},{7,5},{10,8},{11,9},{14,12},{15,13},{18,16},{19,... | collective-permute-start | bytes 786440 | tf_op jit(solution)/shard_map/while/body/eval_jaxpr/ppermute | solution.py:29
  161.3 6.6 %collective-permute-start.1 = (bf16[1,1,128,128]{3,2,1,0:T(8,128)(2,1)S(1)}, bf16[1,1,128,128]{3,2,1,0:T(8,128)(2,1)S(1)}, u32[]{:S(2)}, u32[]{:S(2)}) collective-permute-start(bf16[1,1,128,128]{3,2,1,0:T(8,128)(2,1)S(1)} %get-tuple-element.604), channel_id=1, source_target_pairs={{4,0},{8,4},{12,8},{5,1},{9,5},{13,9},{6,2},{10,6},{14,10},{7,3},{... | collective-permute-start | bytes 98312 | tf_op jit(solution)/shard_map/while/body/eval_jaxpr/ppermute | solution.py:21
  162.6 6.1 %collective-permute-start.2 = (bf16[1,1,128,128]{3,2,1,0:T(8,128)(2,1)S(1)}, bf16[1,1,128,128]{3,2,1,0:T(8,128)(2,1)S(1)}, u32[]{:S(2)}, u32[]{:S(2)}) collective-permute-start(bf16[1,1,128,128]{3,2,1,0:T(8,128)(2,1)S(1)} %get-tuple-element.605), channel_id=1, source_target_pairs={{0,4},{4,8},{8,12},{1,5},{5,9},{9,13},{2,6},{6,10},{10,14},{3,7},{... | collective-permute-start | bytes 98312 | tf_op jit(solution)/shard_map/while/body/eval_jaxpr/ppermute | solution.py:18
  168.8 3.4 collective-permute-start.3
  170.1 3.1 collective-permute-start.4
  171.9 2.2 copy-start.7
  177.0 27.5 %copy-start.9 = (f32[256]{0:T(256)S(1)}, f32[256]{0:T(256)}, u32[]{:S(2)}) copy-start(f32[256]{0:T(256)} %get-tuple-element.653) | copy-start | bytes 3076 | tf_op jit(solution)/shard_map/while
  177.0 23.1 %collective-permute-start.5 = (bf16[1,1,128,128]{3,2,1,0:T(8,128)(2,1)S(1)}, bf16[1,1,128,128]{3,2,1,0:T(8,128)(2,1)S(1)}, u32[]{:S(2)}, u32[]{:S(2)}) collective-permute-start(bf16[1,1,128,128]{3,2,1,0:T(8,128)(2,1)S(1)} %get-tuple-element.620), channel_id=1, source_target_pairs={{4,0},{8,4},{12,8},{5,1},{9,5},{13,9},{6,2},{10,6},{14,10},{7,3},{... | collective-permute-start | bytes 98312 | tf_op jit(solution)/shard_map/while/body/eval_jaxpr/ppermute | solution.py:21
  178.3 21.8 %collective-permute-start.6 = (bf16[1,1,128,128]{3,2,1,0:T(8,128)(2,1)S(1)}, bf16[1,1,128,128]{3,2,1,0:T(8,128)(2,1)S(1)}, u32[]{:S(2)}, u32[]{:S(2)}) collective-permute-start(bf16[1,1,128,128]{3,2,1,0:T(8,128)(2,1)S(1)} %get-tuple-element.621), channel_id=1, source_target_pairs={{0,4},{4,8},{8,12},{1,5},{5,9},{9,13},{2,6},{6,10},{10,14},{3,7},{... | collective-permute-start | bytes 98312 | tf_op jit(solution)/shard_map/while/body/eval_jaxpr/ppermute | solution.py:18
  200.1 4.4 %collective-permute-start.7 = (bf16[1,10,1,128]{3,2,1,0:T(2,128)(2,1)S(1)}, bf16[1,10,1,128]{3,2,1,0:T(2,128)(2,1)S(1)}, u32[]{:S(2)}, u32[]{:S(2)}) collective-permute-start(bf16[1,10,1,128]{3,2,1,0:T(2,128)(2,1)S(1)} %get-tuple-element.622), channel_id=1, source_target_pairs={{1,0},{3,2},{5,4},{7,6},{9,8},{11,10},{13,12},{15,14},{17,16},{19,... | collective-permute-start | bytes 7688 | tf_op jit(solution)/shard_map/while/body/eval_jaxpr/ppermute | solution.py:21
  201.4 3.8 collective-permute-start.8
  207.5 27.7 %copy-start.2 = (bf16[4,8,128,128]{3,2,1,0:T(8,128)(2,1)}, bf16[4,8,128,128]{3,2,1,0:T(8,128)(2,1)S(1)}, u32[]{:S(2)}) copy-start(bf16[4,8,128,128]{3,2,1,0:T(8,128)(2,1)S(1)} %get-tuple-element.676) | copy-start | bytes 3145732 | tf_op jit(solution)/shard_map/while
  207.5 16.8 %collective-permute-start = (bf16[1,8,128,128]{3,2,1,0:T(8,128)(2,1)S(1)}, bf16[1,8,128,128]{3,2,1,0:T(8,128)(2,1)S(1)}, u32[]{:S(2)}, u32[]{:S(2)}) collective-permute-start(bf16[1,8,128,128]{3,2,1,0:T(8,128)(2,1)S(1)} %broadcast_select_fusion.2), channel_id=1, source_target_pairs={{2,0},{3,1},{6,4},{7,5},{10,8},{11,9},{14,12},{15,13},{18,16},{19,... | collective-permute-start | bytes 786440 | tf_op jit(solution)/shard_map/while/body/eval_jaxpr/ppermute | solution.py:29
  224.4 6.6 %collective-permute-start.1 = (bf16[1,1,128,128]{3,2,1,0:T(8,128)(2,1)S(1)}, bf16[1,1,128,128]{3,2,1,0:T(8,128)(2,1)S(1)}, u32[]{:S(2)}, u32[]{:S(2)}) collective-permute-start(bf16[1,1,128,128]{3,2,1,0:T(8,128)(2,1)S(1)} %get-tuple-element.604), channel_id=1, source_target_pairs={{4,0},{8,4},{12,8},{5,1},{9,5},{13,9},{6,2},{10,6},{14,10},{7,3},{... | collective-permute-start | bytes 98312 | tf_op jit(solution)/shard_map/while/body/eval_jaxpr/ppermute | solution.py:21
  225.7 6.1 %collective-permute-start.2 = (bf16[1,1,128,128]{3,2,1,0:T(8,128)(2,1)S(1)}, bf16[1,1,128,128]{3,2,1,0:T(8,128)(2,1)S(1)}, u32[]{:S(2)}, u32[]{:S(2)}) collective-permute-start(bf16[1,1,128,128]{3,2,1,0:T(8,128)(2,1)S(1)} %get-tuple-element.605), channel_id=1, source_target_pairs={{0,4},{4,8},{8,12},{1,5},{5,9},{9,13},{2,6},{6,10},{10,14},{3,7},{... | collective-permute-start | bytes 98312 | tf_op jit(solution)/shard_map/while/body/eval_jaxpr/ppermute | solution.py:18
  231.8 3.4 collective-permute-start.3
  233.1 3.1 collective-permute-start.4
  234.9 2.2 copy-start.7
  240.1 27.5 %copy-start.9 = (f32[256]{0:T(256)S(1)}, f32[256]{0:T(256)}, u32[]{:S(2)}) copy-start(f32[256]{0:T(256)} %get-tuple-element.653) | copy-start | bytes 3076 | tf_op jit(solution)/shard_map/while
  240.1 23.1 %collective-permute-start.5 = (bf16[1,1,128,128]{3,2,1,0:T(8,128)(2,1)S(1)}, bf16[1,1,128,128]{3,2,1,0:T(8,128)(2,1)S(1)}, u32[]{:S(2)}, u32[]{:S(2)}) collective-permute-start(bf16[1,1,128,128]{3,2,1,0:T(8,128)(2,1)S(1)} %get-tuple-element.620), channel_id=1, source_target_pairs={{4,0},{8,4},{12,8},{5,1},{9,5},{13,9},{6,2},{10,6},{14,10},{7,3},{... | collective-permute-start | bytes 98312 | tf_op jit(solution)/shard_map/while/body/eval_jaxpr/ppermute | solution.py:21
  241.4 21.8 %collective-permute-start.6 = (bf16[1,1,128,128]{3,2,1,0:T(8,128)(2,1)S(1)}, bf16[1,1,128,128]{3,2,1,0:T(8,128)(2,1)S(1)}, u32[]{:S(2)}, u32[]{:S(2)}) collective-permute-start(bf16[1,1,128,128]{3,2,1,0:T(8,128)(2,1)S(1)} %get-tuple-element.621), channel_id=1, source_target_pairs={{0,4},{4,8},{8,12},{1,5},{5,9},{9,13},{2,6},{6,10},{10,14},{3,7},{... | collective-permute-start | bytes 98312 | tf_op jit(solution)/shard_map/while/body/eval_jaxpr/ppermute | solution.py:18
  263.2 4.4 %collective-permute-start.7 = (bf16[1,10,1,128]{3,2,1,0:T(2,128)(2,1)S(1)}, bf16[1,10,1,128]{3,2,1,0:T(2,128)(2,1)S(1)}, u32[]{:S(2)}, u32[]{:S(2)}) collective-permute-start(bf16[1,10,1,128]{3,2,1,0:T(2,128)(2,1)S(1)} %get-tuple-element.622), channel_id=1, source_target_pairs={{1,0},{3,2},{5,4},{7,6},{9,8},{11,10},{13,12},{15,14},{17,16},{19,... | collective-permute-start | bytes 7688 | tf_op jit(solution)/shard_map/while/body/eval_jaxpr/ppermute | solution.py:21
  264.5 3.8 collective-permute-start.8
  270.5 27.7 %copy-start.2 = (bf16[4,8,128,128]{3,2,1,0:T(8,128)(2,1)}, bf16[4,8,128,128]{3,2,1,0:T(8,128)(2,1)S(1)}, u32[]{:S(2)}) copy-start(bf16[4,8,128,128]{3,2,1,0:T(8,128)(2,1)S(1)} %get-tuple-element.676) | copy-start | bytes 3145732 | tf_op jit(solution)/shard_map/while
  270.5 16.8 %collective-permute-start = (bf16[1,8,128,128]{3,2,1,0:T(8,128)(2,1)S(1)}, bf16[1,8,128,128]{3,2,1,0:T(8,128)(2,1)S(1)}, u32[]{:S(2)}, u32[]{:S(2)}) collective-permute-start(bf16[1,8,128,128]{3,2,1,0:T(8,128)(2,1)S(1)} %broadcast_select_fusion.2), channel_id=1, source_target_pairs={{2,0},{3,1},{6,4},{7,5},{10,8},{11,9},{14,12},{15,13},{18,16},{19,... | collective-permute-start | bytes 786440 | tf_op jit(solution)/shard_map/while/body/eval_jaxpr/ppermute | solution.py:29
  287.4 6.6 %collective-permute-start.1 = (bf16[1,1,128,128]{3,2,1,0:T(8,128)(2,1)S(1)}, bf16[1,1,128,128]{3,2,1,0:T(8,128)(2,1)S(1)}, u32[]{:S(2)}, u32[]{:S(2)}) collective-permute-start(bf16[1,1,128,128]{3,2,1,0:T(8,128)(2,1)S(1)} %get-tuple-element.604), channel_id=1, source_target_pairs={{4,0},{8,4},{12,8},{5,1},{9,5},{13,9},{6,2},{10,6},{14,10},{7,3},{... | collective-permute-start | bytes 98312 | tf_op jit(solution)/shard_map/while/body/eval_jaxpr/ppermute | solution.py:21
  288.7 6.1 %collective-permute-start.2 = (bf16[1,1,128,128]{3,2,1,0:T(8,128)(2,1)S(1)}, bf16[1,1,128,128]{3,2,1,0:T(8,128)(2,1)S(1)}, u32[]{:S(2)}, u32[]{:S(2)}) collective-permute-start(bf16[1,1,128,128]{3,2,1,0:T(8,128)(2,1)S(1)} %get-tuple-element.605), channel_id=1, source_target_pairs={{0,4},{4,8},{8,12},{1,5},{5,9},{9,13},{2,6},{6,10},{10,14},{3,7},{... | collective-permute-start | bytes 98312 | tf_op jit(solution)/shard_map/while/body/eval_jaxpr/ppermute | solution.py:18
  294.9 3.4 collective-permute-start.3
  296.2 3.1 collective-permute-start.4
  298.0 2.2 copy-start.7
  303.1 27.5 %copy-start.9 = (f32[256]{0:T(256)S(1)}, f32[256]{0:T(256)}, u32[]{:S(2)}) copy-start(f32[256]{0:T(256)} %get-tuple-element.653) | copy-start | bytes 3076 | tf_op jit(solution)/shard_map/while
  303.1 23.1 %collective-permute-start.5 = (bf16[1,1,128,128]{3,2,1,0:T(8,128)(2,1)S(1)}, bf16[1,1,128,128]{3,2,1,0:T(8,128)(2,1)S(1)}, u32[]{:S(2)}, u32[]{:S(2)}) collective-permute-start(bf16[1,1,128,128]{3,2,1,0:T(8,128)(2,1)S(1)} %get-tuple-element.620), channel_id=1, source_target_pairs={{4,0},{8,4},{12,8},{5,1},{9,5},{13,9},{6,2},{10,6},{14,10},{7,3},{... | collective-permute-start | bytes 98312 | tf_op jit(solution)/shard_map/while/body/eval_jaxpr/ppermute | solution.py:21
  304.4 21.8 %collective-permute-start.6 = (bf16[1,1,128,128]{3,2,1,0:T(8,128)(2,1)S(1)}, bf16[1,1,128,128]{3,2,1,0:T(8,128)(2,1)S(1)}, u32[]{:S(2)}, u32[]{:S(2)}) collective-permute-start(bf16[1,1,128,128]{3,2,1,0:T(8,128)(2,1)S(1)} %get-tuple-element.621), channel_id=1, source_target_pairs={{0,4},{4,8},{8,12},{1,5},{5,9},{9,13},{2,6},{6,10},{10,14},{3,7},{... | collective-permute-start | bytes 98312 | tf_op jit(solution)/shard_map/while/body/eval_jaxpr/ppermute | solution.py:18
  326.2 4.4 %collective-permute-start.7 = (bf16[1,10,1,128]{3,2,1,0:T(2,128)(2,1)S(1)}, bf16[1,10,1,128]{3,2,1,0:T(2,128)(2,1)S(1)}, u32[]{:S(2)}, u32[]{:S(2)}) collective-permute-start(bf16[1,10,1,128]{3,2,1,0:T(2,128)(2,1)S(1)} %get-tuple-element.622), channel_id=1, source_target_pairs={{1,0},{3,2},{5,4},{7,6},{9,8},{11,10},{13,12},{15,14},{17,16},{19,... | collective-permute-start | bytes 7688 | tf_op jit(solution)/shard_map/while/body/eval_jaxpr/ppermute | solution.py:21
  327.5 3.8 collective-permute-start.8
  (37 other events, 49.6 us)
Sparse Core Ops, SparseCore 0:
  334.5 55.9 all-reduce.8
where the time goes:
time: 402 us; the launch traced here: 399 us
  blocking collectives  157 us (39%)
  starting transfers between devices  101 us (25%)
  waiting for transfers between devices  54.1 us (13%)
  other arithmetic  25.6 us (6%)
  matrix products  22.8 us (6%)
  local copies, waits for them, and re-layouts  22.2 us (6%)
  between operations  14.1 us (4%)
    psum x5, blocking collectives, section_backward(): sum_one, sum_two = lax.psum((sum_one, sum_two), ('rows', 'sub'))  73.8 us
    ppermute x20, starting transfers between devices, extended(): lax.ppermute(lax.slice_in_dim(block, block.shape[dim] - width, None, axis...  68.6 us
    psum x5, blocking collectives, section_backward(): part_one, part_two = lax.psum((part_one, part_two), ('rows', 'sub'))  68 us
    psum x1, waiting for transfers between devices, body(): lax.psum((kernel_grad, mod_grad, bias_grad), ('rows', 'sub'))  41 us
    ppermute x20, starting transfers between devices, extended(): lax.ppermute(lax.slice_in_dim(block, 0, width, axis=dim), axis, backward)  25.8 us
    psum x1, blocking collectives, body(): lax.psum((kernel_grad, mod_grad, bias_grad), ('rows', 'sub'))  15.1 us
    dot_general x5, matrix products, section_backward(): jnp.dot(taps(padded_g, row_count, col_count, True), weights_t, preferred_...  13.9 us
    dynamic_update_slice x5, other arithmetic, tick(): lax.dynamic_update_slice_in_dim(grads_out, jnp.where(valid, result, curre...  10.7 us
  transfers between devices with their start and end apart: 46, of which 16 were waited for; matrix products, arithmetic and copies ran while one was open for 8% of the time, Pallas kernels for 0%

commit v1 on v0

--- a/solution.py
+++ b/solution.py
@@ -1,6 +1,10 @@
+import functools
+
 import jax
 import jax.numpy as jnp
 from jax import lax
+from jax.experimental import pallas as pl
+from jax.experimental.pallas import tpu as pltpu
 from jax.sharding import PartitionSpec as P
 
 GROUPS = 32
@@ -166,7 +170,7 @@
     return (result, kernel_term, mod_term, bias_term)
 
 
-def body(
+def general_body(
     activations,
     latent,
     recon,
@@ -246,7 +250,583 @@
     return (grads_out, kernel_grad, mod_grad, bias_grad)
 
 
+HALO = 32
+EXACT = lax.Precision.HIGHEST
+TN = (((0,), (0,)), ((), ()))
+NT = (((1,), (1,)), ((), ()))
+F32 = jnp.float32
+BF16 = jnp.bfloat16
+
+
+def swap(value, axis):
+    return lax.ppermute(value, axis, [(0, 1), (1, 0)])
+
+
+def shift(value, axis, steps):
+    count = lax.axis_size(axis)
+    return lax.ppermute(value, axis, [(i, (i + steps) % count) for i in range(count)])
+
+
+def pixel_total(value):
+    value = value + swap(value, "sub")
+    one, two, three = [shift(value, "rows", steps) for steps in (1, 2, 3)]
+    return (value + two) + (one + three)
+
+
+def same_group(channels):
+    per = channels // GROUPS
+    left = lax.broadcasted_iota(jnp.int32, (channels, channels), 0) // per
+    right = lax.broadcasted_iota(jnp.int32, (channels, channels), 1) // per
+    return (left == right).astype(F32)
+
+
+def statistics(sums_ref, micro, micros, member, count):
+    both = jnp.concatenate([sums_ref[pl.ds(micro, 1), :], sums_ref[pl.ds(micros + micro, 1), :]], axis=0)
+    both = jnp.dot(both, member, precision=EXACT, preferred_element_type=F32) / count
+    mean = both[0:1]
+    return mean, lax.rsqrt(both[1:2] - mean * mean + EPS)
+
+
+def gradient_means(total, mix_ref, member, count):
+    mix = mix_ref[...].astype(F32)
+    channels = mix.shape[-1] // 2
+    mean_grad = jnp.sum(mix[:, :channels] * total[:, channels:], axis=0, keepdims=True)
+    mean_cross = jnp.sum(mix[:, :channels] * total[:, :channels], axis=0, keepdims=True)
+    both = jnp.concatenate([mean_grad, mean_cross], axis=0)
+    both = jnp.dot(both, member, precision=EXACT, preferred_element_type=F32) / count
+    return both[0:1], both[1:2]
+
+
+def sums_kernel(acts_ref, out_ref):
+    micro, micros = pl.program_id(0), pl.num_programs(0)
+    value = acts_ref[0].astype(F32)
+    out_ref[pl.ds(micro, 1), :] = jnp.sum(value, axis=0, keepdims=True)
+    out_ref[pl.ds(micros + micro, 1), :] = jnp.sum(value * value, axis=0, keepdims=True)
+
+
+def top_kernel(pixels, diff_ref, out_weight_ref, main_ref, halo_ref):
+    diff = diff_ref[0]
+    high = diff.astype(BF16)
+    rest = diff - high.astype(F32)
+    middle = rest.astype(BF16)
+    low = (rest - middle.astype(F32)).astype(BF16)
+    weight = out_weight_ref[...]
+    total = lax.dot_general(low, weight, TN, preferred_element_type=F32)
+    total = total + lax.dot_general(middle, weight, TN, preferred_element_type=F32)
+    total = total + lax.dot_general(high, weight, TN, preferred_element_type=F32)
+    total = total.astype(BF16)
+    main_ref[0] = total[:pixels]
+    halo_ref[0] = total[pixels : pixels + halo_ref.shape[1]]
+
+
+def spread(rows, cols, grad_ref, halo_ref, shifted):
+    channels = grad_ref.shape[-1]
+    sides = halo_ref[0, 2 * cols : 2 * cols + HALO, :].astype(F32)
+    place = lax.broadcasted_iota(jnp.int32, (cols, channels), 0)
+    for r in range(rows + 2):
+        if r == 0:
+            here = halo_ref[0, 0:cols, :]
+        elif r == rows + 1:
+            here = halo_ref[0, cols : 2 * cols, :]
+        else:
+            here = grad_ref[0, (r - 1) * cols : r * cols, :]
+        value = here.astype(F32)
+        left = jnp.where(place == 0, sides[r : r + 1], pltpu.roll(value, 1, 0))
+        right = jnp.where(place == cols - 1, sides[HALO // 2 + r : HALO // 2 + r + 1], pltpu.roll(value, cols - 1, 0))
+        at = slice(r * cols, (r + 1) * cols)
+        shifted[at, 0:channels] = left.astype(BF16)
+        shifted[at, channels : 2 * channels] = here
+        shifted[at, 2 * channels :] = right.astype(BF16)
+
+
+def tap_of(row, col):
+    return 3 * (2 - row) + (2 - col)
+
+
+def arrange_weights(kernel_ref, weights):
+    channels = kernel_ref.shape[-1]
+    for row in range(3):
+        for col in range(3):
+            tap = tap_of(row, col)
+            weights[row, :, col * channels : (col + 1) * channels] = kernel_ref[tap * channels : (tap + 1) * channels, :]
+
+
+def hidden_gradient(rows, cols, shifted, weights, hidden_grad):
+    pixels = rows * cols
+    total = lax.dot_general(shifted[0:pixels, :], weights[0], NT, preferred_element_type=F32)
+    total = total + lax.dot_general(shifted[cols : cols + pixels, :], weights[1], NT, preferred_element_type=F32)
+    hidden_grad[...] = total + lax.dot_general(
+        shifted[2 * cols : 2 * cols + pixels, :], weights[2], NT, preferred_element_type=F32
+    )
+
+
+def pixel_values(at, acts_ref, latent_ref, mix_ref, mean, rstd):
+    channels = mean.shape[-1]
+    xhat = (acts_ref[0, at, :].astype(F32) - mean) * rstd
+    mixed = lax.dot_general(latent_ref[0, :, at], mix_ref[...], TN, preferred_element_type=F32)
+    scale = mixed[:, :channels]
+    pre = xhat * scale + mixed[:, channels:]
+    sig = 0.5 * jnp.tanh(0.5 * pre) + 0.5
+    hidden = pre * sig
+    return xhat, scale, hidden, sig + hidden * (1.0 - sig)
+
+
+def block_kernel(
+    segment,
+    first,
+    micros,
+    rows,
+    cols,
+    count,
+    segment_ref,
+    sums_ref,
+    acts_ref,
+    latent_ref,
+    grad_ref,
+    halo_ref,
+    kernel_ref,
+    mix_ref,
+    before_ref,
+    norm_ref,
+    reduced_ref,
+    kernel_grad_ref,
+    shifted,
+    weights,
+    hidden_grad,
+    hidden_keep,
+    pairs,
+    total_kernel,
+):
+    step = pl.program_id(0)
+    channels = acts_ref.shape[-1]
+    pixels = rows * cols
+    active = segment_ref[0] == segment
+
+    @pl.when(active)
+    def _():
+        @pl.when(step == 0)
+        def _():
+            arrange_weights(kernel_ref, weights)
+            total_kernel[...] = jnp.zeros_like(total_kernel)
+
+        member = same_group(channels)
+        mean, rstd = statistics(sums_ref, first + step, micros, member, count)
+        spread(rows, cols, grad_ref, halo_ref, shifted)
+        hidden_gradient(rows, cols, shifted, weights, hidden_grad)
+
+        def one_row(r, carry):
+            at = pl.ds(pl.multiple_of(r * cols, cols), cols)
+            xhat, scale, hidden, slope = pixel_values(at, acts_ref, latent_ref, mix_ref, mean, rstd)
+            hidden_keep[at, :] = hidden.astype(BF16)
+            pre_grad = hidden_grad[at, :] * slope
+            norm_ref[0, at, :] = pre_grad * scale
+            pairs[at, 0:channels] = (pre_grad * xhat).astype(BF16)
+            pairs[at, channels:] = pre_grad.astype(BF16)
+            return carry
+
+        lax.fori_loop(0, rows, one_row, 0)
+        reduced_ref[0] = jnp.dot(latent_ref[0], pairs[...], preferred_element_type=F32)
+        for row in range(3):
+            total_kernel[row] += lax.dot_general(
+                hidden_keep[...], shifted[row * cols : row * cols + pixels, :], TN, preferred_element_type=F32
+            )
+
+    @pl.when(jnp.logical_not(active))
+    def _():
+        reduced_ref[...] = jnp.zeros_like(reduced_ref)
+
+    @pl.when(step == pl.num_programs(0) - 1)
+    def _():
+        @pl.when(active)
+        def _():
+            for row in range(3):
+                for col in range(3):
+                    tap = tap_of(row, col)
+                    at = slice(tap * channels, (tap + 1) * channels)
+                    kernel_grad_ref[at, :] = before_ref[at, :] + total_kernel[row, :, col * channels : (col + 1) * channels]
+
+        @pl.when(jnp.logical_not(active))
+        def _():
+            kernel_grad_ref[...] = before_ref[...]
+
+
+def redo_kernel(
+    first,
+    micros,
+    rows,
+    cols,
+    count,
+    segment_ref,
+    sums_ref,
+    total_ref,
+    acts_ref,
+    norm_ref,
+    passed_ref,
+    latent_ref,
+    grad_ref,
+    halo_ref,
+    kernel_ref,
+    mix_ref,
+    result_ref,
+    shifted,
+    weights,
+    hidden_grad,
+):
+    step = pl.program_id(0)
+    channels = acts_ref.shape[-1]
+    upper = segment_ref[0] == 1
+    member = same_group(channels)
+    mean, rstd = statistics(sums_ref, first + step, micros, member, count)
+    mean_grad, mean_cross = gradient_means(total_ref[0], mix_ref, member, count)
+
+    def finish(at, norm_grad, xhat):
+        change = rstd * (norm_grad - mean_grad - xhat * mean_cross)
+        result_ref[0, at, :] = (grad_ref[0, at, :].astype(F32) + change).astype(BF16)
+
+    @pl.when(upper)
+    def _():
+        def one_row(r, carry):
+            at = pl.ds(pl.multiple_of(r * cols, cols), cols)
+            xhat = (acts_ref[0, at, :].astype(F32) - mean) * rstd
+            finish(at, norm_ref[0, at, :], xhat)
+            return carry
+
+        lax.fori_loop(0, rows, one_row, 0)
+
+    @pl.when(jnp.logical_not(upper))
+    def _():
+        @pl.when(step == 0)
+        def _():
+            arrange_weights(kernel_ref, weights)
+
+        spread(rows, cols, grad_ref, halo_ref, shifted)
+        hidden_gradient(rows, cols, shifted, weights, hidden_grad)
+
+        def one_row(r, carry):
+            at = pl.ds(pl.multiple_of(r * cols, cols), cols)
+            xhat, scale, _, slope = pixel_values(at, passed_ref, latent_ref, mix_ref, mean, rstd)
+            finish(at, hidden_grad[at, :] * slope * scale, xhat)
+            return carry
+
+        lax.fori_loop(0, rows, one_row, 0)
+
+
+def last_kernel(
+    first, micros, rows, cols, count, segment_ref, sums_ref, total_ref, acts_ref, norm_ref, grad_ref, mix_ref, result_ref
+):
+    step = pl.program_id(0)
+    lower = segment_ref[0] == 0
+
+    @pl.when(lower)
+    def _():
+        member = same_group(acts_ref.shape[-1])
+        mean, rstd = statistics(sums_ref, first + step, micros, member, count)
+        mean_grad, mean_cross = gradient_means(total_ref[0], mix_ref, member, count)
+
+        def one_row(r, carry):
+            at = pl.ds(pl.multiple_of(r * cols, cols), cols)
+            xhat = (acts_ref[0, at, :].astype(F32) - mean) * rstd
+            change = rstd * (norm_ref[0, at, :] - mean_grad - xhat * mean_cross)
+            result_ref[0, at, :] = (grad_ref[0, at, :].astype(F32) + change).astype(BF16)
+            return carry
+
+        lax.fori_loop(0, rows, one_row, 0)
+
+    @pl.when(jnp.logical_not(lower))
+    def _():
+        result_ref[...] = grad_ref[...]
+
+
+def by_micro(shape, first=0):
+    rest = (0,) * (len(shape) - 1)
+    return pl.BlockSpec((1,) + tuple(shape[1:]), lambda m: (m + first,) + rest)
+
+
+def whole(shape):
+    return pl.BlockSpec(tuple(shape), lambda m: (0,) * len(shape))
+
+
+SCALAR = pl.BlockSpec(memory_space=pltpu.SMEM)
+PARAMS = pltpu.CompilerParams(vmem_limit_bytes=40 * 1024 * 1024)
+
+
+def run_block(segment, first, size, micros, rows, cols, count, me, sums, acts, latent, grad, halo, kernel, mix, before):
+    channels = acts.shape[-1]
+    pixels = rows * cols
+    return pl.pallas_call(
+        functools.partial(block_kernel, segment, first, micros, rows, cols, count),
+        grid=(size,),
+        in_specs=[
+            SCALAR,
+            whole(sums.shape),
+            by_micro(acts.shape, first),
+            by_micro(latent.shape, first),
+            by_micro(grad.shape),
+            by_micro(halo.shape),
+            whole(kernel.shape),
+            whole(mix.shape),
+            whole(before.shape),
+        ],
+        out_specs=[
+            by_micro((size, pixels, channels)),
+            by_micro((size, 8, 2 * channels)),
+            whole(before.shape),
+        ],
+        out_shape=[
+            jax.ShapeDtypeStruct((size, pixels, channels), F32),
+            jax.ShapeDtypeStruct((size, 8, 2 * channels), F32),
+            jax.ShapeDtypeStruct(before.shape, F32),
+        ],
+        scratch_shapes=[
+            pltpu.VMEM(((rows + 2) * cols, 3 * channels), BF16),
+            pltpu.VMEM((3, channels, 3 * channels), BF16),
+            pltpu.VMEM((pixels, channels), F32),
+            pltpu.VMEM((pixels, channels), BF16),
+            pltpu.VMEM((pixels, 2 * channels), BF16),
+            pltpu.VMEM((3, channels, 3 * channels), F32),
+        ],
+        compiler_params=PARAMS,
+        name="block_backward",
+    )(me, sums, acts, latent, grad, halo, kernel, mix, before)
+
+
+def run_redo(first, size, micros, rows, cols, count, me, sums, totals, acts, norm, passed, latent, grad, halo, kernel, mix):
+    channels = acts.shape[-1]
+    pixels = rows * cols
+    return pl.pallas_call(
+        functools.partial(redo_kernel, first, micros, rows, cols, count),
+        grid=(size,),
+        in_specs=[
+            SCALAR,
+            whole(sums.shape),
+            by_micro(totals.shape, first),
+            by_micro(acts.shape, first),
+            by_micro(norm.shape, first),
+            by_micro(passed.shape),
+            by_micro(latent.shape, first),
+            by_micro(grad.shape, first),
+            by_micro(halo.shape, first),
+            whole(kernel.shape),
+            whole(mix.shape),
+        ],
+        out_specs=by_micro((size, pixels, channels)),
+        out_shape=jax.ShapeDtypeStruct((size, pixels, channels), BF16),
+        scratch_shapes=[
+            pltpu.VMEM(((rows + 2) * cols, 3 * channels), BF16),
+            pltpu.VMEM((3, channels, 3 * channels), BF16),
+            pltpu.VMEM((pixels, channels), F32),
+        ],
+        compiler_params=PARAMS,
+        name="redo_upper",
+    )(me, sums, totals, acts, norm, passed, latent, grad, halo, kernel, mix)
+
+
+def pad_rows(value, rows):
+    return jnp.pad(value, ((0, 0),) * (value.ndim - 2) + ((0, rows - value.shape[-2]), (0, 0)))
+
+
+def pair_body(
+    activations, latent, recon, target, boxes, kernel, mod_weight, scale_bias, shift_bias, out_weight
+):
+    micros, rows, cols, channels = activations.shape[1:]
+    colors = recon.shape[1]
+    pixels = rows * cols
+    bands = lax.axis_size("rows")
+    total_rows, total_cols = rows * bands, cols * 2
+    count = float(total_rows * total_cols * (channels // GROUPS))
+    segment = lax.axis_index("segment")
+    band = lax.axis_index("rows")
+    side = lax.axis_index("sub")
+    row_start, col_start = band * rows, side * cols
+    me = segment.astype(jnp.int32).reshape(1)
+    acts = activations[0].reshape(micros, pixels, channels)
+
+    mix = jnp.concatenate(
+        [mod_weight[0], jnp.concatenate([scale_bias, shift_bias], axis=1), jnp.zeros((3, 2 * channels), BF16)]
+    )
+    half = kernel.shape[1] // 2
+    mine = jnp.concatenate(
+        [lax.dynamic_slice_in_dim(kernel[0], side * half, half), mix.reshape(2 * mix.shape[0], channels)]
+    )
+    mine = swap(mine, "segment")
+    half_passed, mix_passed = mine[:half], mine[half:].reshape(mix.shape)
+    other = swap(half_passed, "sub")
+    kernel_passed = jnp.where(
+        side == 0, jnp.concatenate([half_passed, other]), jnp.concatenate([other, half_passed])
+    )
+    passed = [swap(acts[m : m + 1], "segment") for m in range(micros)]
+
+    sums = pl.pallas_call(
+        sums_kernel,
+        grid=(micros,),
+        in_specs=[by_micro(acts.shape)],
+        out_specs=whole((2 * micros, channels)),
+        out_shape=jax.ShapeDtypeStruct((2 * micros, channels), F32),
+        name="input_sums",
+    )(acts)
+    diff = (recon.astype(F32) - target.astype(F32)).reshape(micros * colors, rows, cols)
+    planes = micros * colors
+    edge = jnp.where(side == 0, diff[:, :, cols - 1], diff[:, :, 0])
+    lines = -(-planes * rows // channels)
+    flat = jnp.pad(edge.reshape(-1), (0, lines * channels - planes * rows)).reshape(lines, channels)
+    got = swap(jnp.concatenate([sums, flat]), "sub")
+    sums = sums + got[: 2 * micros]
+    edge = got[2 * micros :].reshape(-1)[: planes * rows].reshape(planes, rows)
+
+    def with_row(r):
+        corner = jnp.pad(edge[:, r], (0, channels - planes)).reshape(1, channels)
+        return jnp.concatenate([sums, diff[:, r], corner])
+
+    from_up = shift(with_row(rows - 1), "rows", 1)
+    from_down = shift(with_row(0), "rows", bands - 1)
+    across = shift(sums, "rows", 2)
+    sums = (sums + across) + (from_up[: 2 * micros] + from_down[: 2 * micros])
+    up, down = from_up[2 * micros : 2 * micros + planes], from_down[2 * micros : 2 * micros + planes]
+    inner = jnp.concatenate(
+        [from_up[-1, :planes, None], edge, from_down[-1, :planes, None], jnp.zeros((planes, HALO // 2 - rows - 2), F32)], axis=1
+    )
+    blank = jnp.zeros_like(inner)
+    lanes = -(-(pixels + 2 * cols + HALO) // 128) * 128
+    diff = jnp.concatenate(
+        [
+            diff.reshape(planes, pixels),
+            up,
+            down,
+            jnp.where(side == 1, inner, blank),
+            jnp.where(side == 0, inner, blank),
+            jnp.zeros((planes, lanes - pixels - 2 * cols - HALO), F32),
+        ],
+        axis=1,
+    ).reshape(micros, colors, lanes)
+    lane = jnp.arange(lanes, dtype=jnp.int32)
+    tail = lane - pixels - 2 * cols
+    low, high = tail < HALO // 2, tail < HALO
+    lane_row = jnp.where(
+        lane < pixels,
+        lane // cols,
+        jnp.where(lane < pixels + cols, -1, jnp.where(tail < 0, rows, tail % (HALO // 2) - 1)),
+    )
+    lane_col = jnp.where(tail < 0, lane % cols, jnp.where(low, -1, cols))
+    row_tile, col_tile = (row_start + lane_row) // TILE, (col_start + lane_col) // TILE
+    row_0, col_0, height, width = [boxes[:, :, i : i + 1] for i in range(4)]
+    contains = (row_tile >= row_0) & (row_tile < row_0 + height) & (col_tile >= col_0) & (col_tile < col_0 + width)
+    contains = contains & ((tail < 0) | (high & (tail % (HALO // 2) < rows + 2)))
+    tiles = total_rows // TILE * (total_cols // TILE)
+    share = tiles / (boxes.shape[1] * (height * width).astype(F32))
+    cropped = jnp.sum(jnp.where(contains, share, 0.0), axis=1)
+    diff = pad_rows(2.0 * diff * cropped[:, None], 8)
+    halo_rows = 2 * cols + HALO
+    top, top_halo = pl.pallas_call(
+        functools.partial(top_kernel, pixels),
+        grid=(micros,),
+        in_specs=[by_micro(diff.shape), whole((8, channels))],
+        out_specs=[by_micro((micros, pixels, channels)), by_micro((micros, halo_rows, channels))],
+        out_shape=[
+            jax.ShapeDtypeStruct((micros, pixels, channels), BF16),
+            jax.ShapeDtypeStruct((micros, halo_rows, channels), BF16),
+        ],
+        name="top_gradient",
+    )(diff, pad_rows(out_weight, 8))
+
+    latent = latent.reshape(micros, latent.shape[1], pixels)
+    latents = latent.shape[1]
+    latent = jnp.concatenate(
+        [latent, jnp.ones((micros, 1, pixels), BF16), jnp.zeros((micros, 7 - latents, pixels), BF16)], axis=1
+    )
+
+    fixed = (micros, rows, cols, count, me)
+    norm_upper, reduced, kernel_grad = run_block(
+        1, 0, micros, *fixed, sums, acts, latent, top, top_halo, kernel[0], mix, jnp.zeros(kernel.shape[1:], F32)
+    )
+    totals_own = pixel_total(reduced.reshape(micros * 8, 2 * channels))
+    from_above = swap(jnp.concatenate([sums, totals_own.reshape(-1, channels)]), "segment")
+    lower = segment == 0
+    sums_upper = jnp.where(lower, from_above[: 2 * micros], sums)
+    totals_upper = jnp.where(lower, from_above[2 * micros :].reshape(totals_own.shape), totals_own)
+    totals_upper = totals_upper.reshape(micros, 8, 2 * channels)
+    kernel_upper = jnp.where(lower, kernel_passed, kernel[0])
+    mix_upper = jnp.where(lower, mix_passed, mix)
+
+    def with_border(value):
+        size = value.shape[0]
+        value = value.reshape(size, rows, cols, channels)
+        near = jnp.where(side == 0, value[:, :, cols - 1], value[:, :, 0])
+        near = swap(near, "sub")
+
+        def payload(r):
+            return jnp.concatenate([value[:, r], near[:, r : r + 1], jnp.zeros((size, 15, channels), BF16)], axis=1)
+
+        above = shift(payload(rows - 1), "rows", 1)
+        below = shift(payload(0), "rows", bands - 1)
+        above = jnp.where(band == 0, jnp.zeros_like(above), above)
+        below = jnp.where(band == bands - 1, jnp.zeros_like(below), below)
+        column = jnp.concatenate(
+            [
+                above[:, cols : cols + 1],
+                near,
+                below[:, cols : cols + 1],
+                jnp.zeros((size, HALO // 2 - rows - 2, channels), BF16),
+            ],
+            axis=1,
+        )
+        nothing = jnp.zeros_like(column)
+        return jnp.concatenate(
+            [above[:, :cols], below[:, :cols], jnp.where(side == 1, column, nothing), jnp.where(side == 0, column, nothing)],
+            axis=1,
+        )
+
+    results, norms, parts = [], [], []
+    early = micros - 1
+    for first, size in ((0, early), (early, micros - early)):
+        given = passed[first] if size == 1 else jnp.concatenate(passed[first : first + size])
+        result = run_redo(
+            first, size, *fixed, sums_upper, totals_upper, acts, norm_upper, given, latent, top, top_halo, kernel_upper, mix_upper
+        )
+        norm, part, kernel_grad = run_block(
+            0, first, size, *fixed, sums, acts, latent, result, with_border(result), kernel[0], mix, kernel_grad
+        )
+        results.append(result)
+        norms.append(norm)
+        parts.append(part)
+    parts = jnp.concatenate(parts)
+    totals = pixel_total(parts.reshape(micros * 8, 2 * channels))
+    totals = jnp.where(lower, totals, totals_own).reshape(micros, 8, 2 * channels)
+    grads = []
+    for first, size, norm, result in ((0, early, norms[0], results[0]), (early, micros - early, norms[1], results[1])):
+        grads.append(
+            pl.pallas_call(
+                functools.partial(last_kernel, first, micros, rows, cols, count),
+                grid=(size,),
+                in_specs=[
+                    SCALAR,
+                    whole(sums.shape),
+                    by_micro(totals.shape, first),
+                    by_micro(acts.shape, first),
+                    by_micro(norm.shape),
+                    by_micro(result.shape),
+                    whole(mix.shape),
+                ],
+                out_specs=by_micro(result.shape),
+                out_shape=jax.ShapeDtypeStruct(result.shape, BF16),
+                name="input_gradient",
+            )(me, sums, totals, acts, norm, result, mix)
+        )
+    grads = jnp.concatenate(grads).reshape(activations.shape)
+
+    give = lax.dynamic_slice_in_dim(kernel_grad, (1 - side) * half, half)
+    keep = lax.dynamic_slice_in_dim(kernel_grad, side * half, half)
+    keep = (keep + swap(give, "sub")).astype(BF16)
+    one, two, three = [shift(keep, "rows", steps).astype(F32) for steps in (1, 2, 3)]
+    keep = (keep.astype(F32) + two) + (one + three)
+    give = swap(keep, "sub")
+    kernel_grad = jnp.where(side == 0, jnp.concatenate([keep, give]), jnp.concatenate([give, keep]))
+    parameter = jnp.sum(totals, axis=0)
+    return (grads, kernel_grad[None], parameter[None, :latents], parameter[None, latents])
+
+
 def solution(mesh):
+    pair = mesh.shape["segment"] == 2 and mesh.shape["rows"] == 4 and mesh.shape["sub"] == 2
+    body = pair_body if pair else general_body
     placed = (
         P("segment", "groups", "rows", "sub", None),
         P("groups", None, "rows", "sub"),

time: 402 us -> 151 us (0.38)
  blocking collectives: 157 us -> 0 us
  starting transfers between devices: 101 us -> 51.9 us
  Pallas kernels: 0 us -> 39.3 us
  matrix products: 22.8 us -> 0 us
  waiting for transfers between devices: 54.1 us -> 31.9 us
  between operations: 14.1 us -> 1.36 us
  other arithmetic: 25.6 us -> 13.9 us
  local copies, waits for them, and re-layouts: 22.2 us -> 12 us
    psum x11 -> x0, blocking collectives: 157 us -> none  [the longest x5 73.8 us: section_backward(): sum_one, sum_two = lax.psum((sum_one, sum_two), ('rows', 'sub'))]
    ppermute x45 -> x30, starting transfers between devices: 101 us -> 51.9 us  [the longest x16 26.7 us: shift(): lax.ppermute(value, axis, [(i, (i + steps) % count) for i in range(count)])]
    psum x1 -> x0, waiting for transfers between devices: 41 us -> none  [body(): lax.psum((kernel_grad, mod_grad, bias_grad), ('rows', 'sub'))]
    pallas_call x0 -> x9, Pallas kernels: none -> 39.3 us  [the longest x3 14 us: run_block(): pl.pallas_call(functools.partial(block_kernel, segment, first, micros, ro...]
    dot_general x22 -> x0, matrix products: 22.8 us -> none  [the longest x5 13.9 us: section_backward(): jnp.dot(taps(padded_g, row_count, col_count, True), weights_t, preferred_...]
    ppermute x45 -> x30, waiting for transfers between devices: 13.1 us -> 31.9 us  [the longest x14 20.8 us: swap(): return lax.ppermute(value, axis, [(0, 1), (1, 0)])]
    dynamic_update_slice x5 -> x0, other arithmetic: 10.7 us -> none  [tick(): lax.dynamic_update_slice_in_dim(grads_out, jnp.where(valid, result, curre...]
    reduce_sum x30 -> x2, other arithmetic: 8.56 us -> 0.81 us  [the longest x1 0.62 us: pair_body(): parameter = jnp.sum(totals, axis=0)]
  transfers between devices with their start and end apart: 46 -> 30, of which waited for: 16 -> 10; matrix products, arithmetic and copies ran while one was open for 8% -> 11% of each run, Pallas kernels for 0% -> 7%
where the time goes in v1:
time: 151 us; the launch traced here: 150 us
  starting transfers between devices  51.9 us (34%)
  Pallas kernels  39.3 us (26%)
  waiting for transfers between devices  31.9 us (21%)
  other arithmetic  13.9 us (9%)
  local copies, waits for them, and re-layouts  12 us (8%)
    ppermute x16, starting transfers between devices, shift(): lax.ppermute(value, axis, [(i, (i + steps) % count) for i in range(count)])  26.7 us
    ppermute x14, starting transfers between devices, swap(): return lax.ppermute(value, axis, [(0, 1), (1, 0)])  25.2 us
    ppermute x14, waiting for transfers between devices, swap(): return lax.ppermute(value, axis, [(0, 1), (1, 0)])  20.8 us
    pallas_call x3, Pallas kernels, run_block(): pl.pallas_call(functools.partial(block_kernel, segment, first, micros, ro...  14 us
    pallas_call x2, Pallas kernels, run_redo(): pl.pallas_call(functools.partial(redo_kernel, first, micros, rows, cols,...  11.8 us
    ppermute x16, waiting for transfers between devices, shift(): lax.ppermute(value, axis, [(i, (i + steps) % count) for i in range(count)])  11.1 us
    pallas_call x2, Pallas kernels, pair_body(): pl.pallas_call(functools.partial(last_kernel, first, micros, rows, cols,...  6.53 us
    unnamed x44, local copies, waits for them, and re-layouts  5.62 us
  transfers between devices with their start and end apart: 30, of which 10 were waited for; matrix products, arithmetic and copies ran while one was open for 11% of the time, Pallas kernels for 7%

profile of v1, /device:TPU:0, one launch (start us, length us, event | category | flops | bytes accessed | tf_op | source)
XLA Modules:
  0.0 150.3 jit_solution(14769236996719739136)
XLA Ops:
  0.7 3.1 %input_sums.1 = f32[8,128]{1,0:T(8,128)} custom-call(bf16[4,1024,128]{2,1,0:T(8,128)(2,1)} %bitcast.59), custom_call_target="tpu_custom_call" | custom-call | tf_op jit(solution)/shard_map/input_sums/pallas_call | solution.py:659
  3.7 0.8 convert_subtract_fusion
  4.8 0.7 pad_maximum_fusion.8
  5.4 0.5 collective-permute-start
  5.9 0.9 fusion.29
  6.9 1.2 slice_reduce_fusion.3
  8.3 0.2 select_reduce_fusion
  8.5 0.8 reshape.365
  9.5 0.2 slice_reduce_fusion.1
  9.7 0.7 slice_add_fusion.1
  10.4 2.6 %collective-permute-start.2 = (f32[21,128]{1,0:T(8,128)S(1)}, f32[21,128]{1,0:T(8,128)S(1)}, u32[]{:S(2)}, u32[]{:S(2)}) collective-permute-start(f32[21,128]{1,0:T(8,128)S(1)} %get-tuple-element.56), channel_id=1, source_target_pairs={{0,4},{4,8},{8,12},{12,0},{1,5},{5,9},{9,13},{13,1},{2,6},{6,10},{... | collective-permute-start | bytes 32264 | tf_op jit(solution)/shard_map/ppermute | solution.py:267
  13.0 0.8 maximum_maximum_fusion.7.mix_ref
  13.8 1.3 pad.23.out_weight_ref
  15.2 2.6 %collective-permute-start.1 = (f32[8,128]{1,0:T(8,128)S(1)}, f32[8,128]{1,0:T(8,128)S(1)}, u32[]{:S(2)}, u32[]{:S(2)}) collective-permute-start(f32[8,128]{1,0:T(8,128)S(1)} %slice_add_fusion.1), channel_id=1, source_target_pairs={{0,8},{4,12},{8,0},{12,4},{1,9},{5,13},{9,1},{13,5},{2,10},{6,14},... | collective-permute-start | bytes 12296 | tf_op jit(solution)/shard_map/ppermute | solution.py:267
  17.9 1.4 collective-permute-start.3
  19.4 2.2 %collective-permute-done.3 = f32[21,128]{1,0:T(8,128)S(1)} collective-permute-done((f32[21,128]{1,0:T(8,128)S(1)}, f32[21,128]{1,0:T(8,128)S(1)}, u32[]{:S(2)}, u32[]{:S(2)}) %collective-permute-start.3) | collective-permute-done | bytes 10784 | tf_op jit(solution)/shard_map/ppermute | solution.py:267
  22.0 0.7 pad.22.diff_ref
  22.6 3.9 %top_gradient.1 = (bf16[4,1024,128]{2,1,0:T(8,128)(2,1)}, bf16[4,288,128]{2,1,0:T(8,128)(2,1)}) custom-call(f32[4,8,1408]{2,1,0:T(8,128)} %pad.22.diff_ref, bf16[8,128]{1,0:T(8,128)(2,1)} %pad.23.out_weight_ref), custom_call_target="tpu_custom_call" | custom-call | tf_op jit(solution)/shard_map/top_gradient/pallas_call | solution.py:719
  26.6 1.2 copy-done.1
  27.9 1.0 copy-done.8
  28.9 1.4 copy-done.4
  30.3 0.8 copy-done.12
  31.1 1.2 collective-permute-done.4
  32.3 3.1 %collective-permute-start.7 = (f32[32,256]{1,0:T(8,128)S(1)}, f32[32,256]{1,0:T(8,128)S(1)}, u32[]{:S(2)}, u32[]{:S(2)}) collective-permute-start(f32[32,256]{1,0:T(8,128)S(1)} %bitcast_add_fusion), channel_id=1, source_target_pairs={{0,12},{4,0},{8,4},{12,8},{1,13},{5,1},{9,5},{13,9},{2,14},{6,2},{... | collective-permute-start | bytes 98312 | tf_op jit(solution)/shard_map/ppermute | solution.py:267
  35.4 0.6 collective-permute-start.5
  36.1 0.7 pad_maximum_fusion.3
  36.7 15.0 %collective-permute-start.12 = (bf16[592,128]{1,0:T(8,128)(2,1)}, bf16[592,128]{1,0:T(8,128)(2,1)S(1)}, u32[]{:S(2)}, u32[]{:S(2)}) collective-permute-start(bf16[592,128]{1,0:T(8,128)(2,1)} %pad_maximum_fusion.3), channel_id=1, source_target_pairs={{0,2},{2,0},{1,3},{3,1},{4,6},{6,4},{5,7},{7,5},{8,10},{10,8},{9,1... | collective-permute-start | bytes 454664 | tf_op jit(solution)/shard_map/ppermute | solution.py:262
  51.8 0.6 pad_maximum_fusion.5
  52.4 4.4 %collective-permute-start.8 = (f32[72,128]{1,0:T(8,128)}, f32[72,128]{1,0:T(8,128)S(1)}, u32[]{:S(2)}, u32[]{:S(2)}) collective-permute-start(f32[72,128]{1,0:T(8,128)} %pad_maximum_fusion.5), channel_id=1, source_target_pairs={{0,2},{2,0},{1,3},{3,1},{4,6},{6,4},{5,7},{7,5},{8,10},{10,8},{9,1... | collective-permute-start | bytes 110600 | tf_op jit(solution)/shard_map/ppermute | solution.py:262
  56.8 1.0 fusion.35
  57.8 2.0 %collective-permute-start.9 = (bf16[1,1024,128]{2,1,0:T(8,128)(2,1)}, bf16[1,1024,128]{2,1,0:T(8,128)(2,1)}, u32[]{:S(2)}, u32[]{:S(2)}) collective-permute-start(bf16[1,1024,128]{2,1,0:T(8,128)(2,1)} %bitcast.12), channel_id=1, source_target_pairs={{0,2},{2,0},{1,3},{3,1},{4,6},{6,4},{5,7},{7,5},{8,10},{10,8},{9,1... | collective-permute-start | bytes 786440 | tf_op jit(solution)/shard_map/ppermute | solution.py:262
  60.1 2.0 %collective-permute-start.11 = (bf16[1,1024,128]{2,1,0:T(8,128)(2,1)}, bf16[1,1024,128]{2,1,0:T(8,128)(2,1)}, u32[]{:S(2)}, u32[]{:S(2)}) collective-permute-start(bf16[1,1024,128]{2,1,0:T(8,128)(2,1)} %bitcast.80), channel_id=1, source_target_pairs={{0,2},{2,0},{1,3},{3,1},{4,6},{6,4},{5,7},{7,5},{8,10},{10,8},{9,1... | collective-permute-start | bytes 786440 | tf_op jit(solution)/shard_map/ppermute | solution.py:262
  62.1 0.7 slice_select_fusion.1.sums_ref
  62.9 0.9 broadcast_select_fusion.10.mix_ref
  63.8 3.5 %collective-permute-done.10 = bf16[1,1024,128]{2,1,0:T(8,128)(2,1)S(1)} collective-permute-done((bf16[1,1024,128]{2,1,0:T(8,128)(2,1)}, bf16[1,1024,128]{2,1,0:T(8,128)(2,1)S(1)}, u32[]{:S(2)}, u32[]{:S(2)}) %collective-permute-start.10) | collective-permute-done | bytes 262176 | tf_op jit(solution)/shard_map/ppermute | solution.py:262
  67.3 5.7 %collective-permute-done.9 = bf16[1,1024,128]{2,1,0:T(8,128)(2,1)} collective-permute-done((bf16[1,1024,128]{2,1,0:T(8,128)(2,1)}, bf16[1,1024,128]{2,1,0:T(8,128)(2,1)}, u32[]{:S(2)}, u32[]{:S(2)}) %collective-permute-start.9) | collective-permute-done | bytes 262176 | tf_op jit(solution)/shard_map/ppermute | solution.py:262
  73.0 8.7 %collective-permute-done.11 = bf16[1,1024,128]{2,1,0:T(8,128)(2,1)} collective-permute-done((bf16[1,1024,128]{2,1,0:T(8,128)(2,1)}, bf16[1,1024,128]{2,1,0:T(8,128)(2,1)}, u32[]{:S(2)}, u32[]{:S(2)}) %collective-permute-start.11) | collective-permute-done | bytes 262176 | tf_op jit(solution)/shard_map/ppermute | solution.py:262
  81.7 1.1 pad_maximum_fusion.1.passed_ref
  83.0 3.0 %redo_upper.3.grad_ref = bf16[1,1024,128]{2,1,0:T(8,128)(2,1)S(1)} custom-call(s32[1]{0:T(128)} %bitcast.segment_ref, f32[8,128]{1,0:T(8,128)S(1)} %slice_select_fusion.1.sums_ref, f32[4,8,256]{2,1,0:T(8,128)S(1)} %select_bitcast_fusion.1.total_ref, bf16[4,1024,128]{2,1,0:T(8,128)(2,1)S(1)} %bitcast.63, f32[4,1024,128]{2,1,0:T(8,128)S(1)} %copy-done.5, ...), custom_call_target="tpu_custom_call" | custom-call | tf_op jit(solution)/shard_map/redo_upper/pallas_call | solution.py:596
  86.0 8.8 %redo_upper.2.grad_ref = bf16[3,1024,128]{2,1,0:T(8,128)(2,1)S(1)} custom-call(s32[1]{0:T(128)} %bitcast.segment_ref, f32[8,128]{1,0:T(8,128)S(1)} %slice_select_fusion.1.sums_ref, f32[4,8,256]{2,1,0:T(8,128)S(1)} %select_bitcast_fusion.1.total_ref, bf16[4,1024,128]{2,1,0:T(8,128)(2,1)S(1)} %bitcast.64, f32[4,1024,128]{2,1,0:T(8,128)S(1)} %copy-done.5, ...), custom_call_target="tpu_custom_call" | custom-call | tf_op jit(solution)/shard_map/redo_upper/pallas_call | solution.py:596
  95.0 0.5 collective-permute-start.14
  95.5 0.6 collective-permute-done.18
  96.2 1.3 collective-permute-start.19
  97.5 2.6 %collective-permute-start.20 = (bf16[1,144,128]{2,1,0:T(8,128)(2,1)S(1)}, bf16[1,144,128]{2,1,0:T(8,128)(2,1)S(1)}, u32[]{:S(2)}, u32[]{:S(2)}) collective-permute-start(bf16[1,144,128]{2,1,0:T(8,128)(2,1)S(1)} %get-tuple-element.65), channel_id=1, source_target_pairs={{0,12},{4,0},{8,4},{12,8},{1,13},{5,1},{9,5},{13,9},{2,14},{6,2},{... | collective-permute-start | bytes 110600 | tf_op jit(solution)/shard_map/ppermute | solution.py:267
  100.3 3.8 %collective-permute-start.16 = (bf16[3,144,128]{2,1,0:T(8,128)(2,1)S(1)}, bf16[3,144,128]{2,1,0:T(8,128)(2,1)S(1)}, u32[]{:S(2)}, u32[]{:S(2)}) collective-permute-start(bf16[3,144,128]{2,1,0:T(8,128)(2,1)S(1)} %get-tuple-element.63), channel_id=1, source_target_pairs={{0,12},{4,0},{8,4},{12,8},{1,13},{5,1},{9,5},{13,9},{2,14},{6,2},{... | collective-permute-start | bytes 331784 | tf_op jit(solution)/shard_map/ppermute | solution.py:267
  104.3 3.6 %collective-permute-done.15 = bf16[3,144,128]{2,1,0:T(8,128)(2,1)S(1)} collective-permute-done((bf16[3,144,128]{2,1,0:T(8,128)(2,1)S(1)}, bf16[3,144,128]{2,1,0:T(8,128)(2,1)S(1)}, u32[]{:S(2)}, u32[]{:S(2)}) %collective-permute-start.15) | collective-permute-done | bytes 110624 | tf_op jit(solution)/shard_map/ppermute | solution.py:267
  108.1 10.3 %block_backward.4 = (f32[3,1024,128]{2,1,0:T(8,128)S(1)}, f32[3,8,256]{2,1,0:T(8,128)S(1)}, f32[1152,128]{1,0:T(8,128)S(1)}) custom-call(s32[1]{0:T(128)} %bitcast.segment_ref, f32[8,128]{1,0:T(8,128)S(1)} %fusion.31.sums_ref, bf16[4,1024,128]{2,1,0:T(8,128)(2,1)S(1)} %bitcast.65, bf16[4,8,1024]{2,1,0:T(8,128)(2,1)S(1)} %maximum_maximum_fusion.2.latent_ref, ...), custom_call_target="tpu_custom_call" | custom-call | tf_op jit(solution)/shard_map/block_backward/pallas_call | solution.py:556
  118.4 1.2 copy-done.11
  119.6 3.7 %block_backward.5 = (f32[1,1024,128]{2,1,0:T(8,128)S(1)}, f32[1,8,256]{2,1,0:T(8,128)S(1)}, f32[1152,128]{1,0:T(8,128)S(1)}) custom-call(s32[1]{0:T(128)} %bitcast.segment_ref, f32[8,128]{1,0:T(8,128)S(1)} %fusion.31.sums_ref, bf16[4,1024,128]{2,1,0:T(8,128)(2,1)S(1)} %bitcast.66, bf16[4,8,1024]{2,1,0:T(8,128)(2,1)S(1)} %maximum_maximum_fusion.2.latent_ref, ...), custom_call_target="tpu_custom_call" | custom-call | tf_op jit(solution)/shard_map/block_backward/pallas_call | solution.py:556
  123.5 0.5 collective-permute-start.21
  124.0 1.1 collective-permute-done.21
  125.1 2.7 %collective-permute-start.24 = (f32[32,256]{1,0:T(8,128)S(1)}, f32[32,256]{1,0:T(8,128)S(1)}, u32[]{:S(2)}, u32[]{:S(2)}) collective-permute-start(f32[32,256]{1,0:T(8,128)S(1)} %fusion.33), channel_id=1, source_target_pairs={{0,12},{4,0},{8,4},{12,8},{1,13},{5,1},{9,5},{13,9},{2,14},{6,2},{... | collective-permute-start | bytes 98312 | tf_op jit(solution)/shard_map/ppermute | solution.py:267
  127.8 1.0 collective-permute-start.22
  128.8 2.9 %collective-permute-start.28 = (bf16[576,128]{1,0:T(8,128)(2,1)S(1)}, bf16[576,128]{1,0:T(8,128)(2,1)S(1)}, u32[]{:S(2)}, u32[]{:S(2)}) collective-permute-start(bf16[576,128]{1,0:T(8,128)(2,1)S(1)} %add_convert_fusion), channel_id=1, source_target_pairs={{0,12},{4,0},{8,4},{12,8},{1,13},{5,1},{9,5},{13,9},{2,14},{6,2},{... | collective-permute-start | bytes 442376 | tf_op jit(solution)/shard_map/ppermute | solution.py:267
  131.7 0.6 collective-permute-start.27
  132.3 1.4 collective-permute-start.26
  133.9 0.6 fusion.34
  134.5 4.1 %input_gradient.2 = bf16[3,1024,128]{2,1,0:T(8,128)(2,1)} custom-call(s32[1]{0:T(128)} %bitcast.segment_ref, f32[8,128]{1,0:T(8,128)} %copy-done.15, f32[4,8,256]{2,1,0:T(8,128)} %get-tuple-element.33.total_ref, bf16[4,1024,128]{2,1,0:T(8,128)(2,1)} %bitcast.60, f32[3,1024,128]{2,1,0:T(8,128)} %copy-done.11, bf16[3,1024,128]{2,1,0:T(8,128)(2,1)} %copy-done.3, ...), custom_call_target="tpu_custom_call" | custom-call | tf_op jit(solution)/shard_map/input_gradient/pallas_call | solution.py:797
  138.6 2.4 %input_gradient.3 = bf16[1,1024,128]{2,1,0:T(8,128)(2,1)} custom-call(s32[1]{0:T(128)} %bitcast.segment_ref, f32[8,128]{1,0:T(8,128)} %copy-done.15, f32[4,8,256]{2,1,0:T(8,128)} %get-tuple-element.33.total_ref, bf16[4,1024,128]{2,1,0:T(8,128)(2,1)} %bitcast.61, f32[1,1024,128]{2,1,0:T(8,128)} %copy-done.14, bf16[1,1024,128]{2,1,0:T(8,128)(2,1)} %copy-done.7, ...), custom_call_target="tpu_custom_call" | custom-call | tf_op jit(solution)/shard_map/input_gradient/pallas_call | solution.py:797
  141.0 0.6 slice.248
  141.6 5.1 %collective-permute-done.26 = bf16[576,128]{1,0:T(8,128)(2,1)S(1)} collective-permute-done((bf16[576,128]{1,0:T(8,128)(2,1)S(1)}, bf16[576,128]{1,0:T(8,128)(2,1)S(1)}, u32[]{:S(2)}, u32[]{:S(2)}) %collective-permute-start.26) | collective-permute-done | bytes 147488 | tf_op jit(solution)/shard_map/ppermute | solution.py:267
  146.9 2.0 %pad_maximum_fusion = bf16[4,1024,128]{2,1,0:T(8,128)(2,1)} fusion(bf16[1,1024,128]{2,1,0:T(8,128)(2,1)} %input_gradient.3, bf16[3,1024,128]{2,1,0:T(8,128)(2,1)S(1)} %copy-done.17), kind=kLoop, calls=%fused_computation | loop fusion | flops 524288 | bytes 2097152 | tf_op jit(solution)/shard_map/concatenate | solution.py:814
  148.9 0.6 slice_bitcast_fusion.4
  149.5 0.9 maximum_select_fusion
  (153 shorter events, 3.1 us)
Async XLA Ops:
  0.6 26.0 %copy-start = (bf16[1,4,8,128,128]{4,3,2,1,0:T(8,128)(2,1)S(1)}, bf16[1,4,8,128,128]{4,3,2,1,0:T(8,128)(2,1)}, u32[]{:S(2)}) copy-start(bf16[1,4,8,128,128]{4,3,2,1,0:T(8,128)(2,1)} %param.10) | copy-start | bytes 3145732
  0.6 26.0 %copy-start.6 = (bf16[1,1152,128]{2,1,0:T(8,128)(2,1)S(1)}, bf16[1,1152,128]{2,1,0:T(8,128)(2,1)}, u32[]{:S(2)}) copy-start(bf16[1,1152,128]{2,1,0:T(8,128)(2,1)} %param.15) | copy-start | bytes 884740
  5.4 3.9 %collective-permute-start = (f32[9,128]{1,0:T(8,128)S(1)}, f32[9,128]{1,0:T(8,128)S(1)}, u32[]{:S(2)}, u32[]{:S(2)}) collective-permute-start(f32[9,128]{1,0:T(8,128)S(1)} %pad_maximum_fusion.8), channel_id=1, source_target_pairs={{0,1},{1,0},{2,3},{3,2},{4,5},{5,4},{6,7},{7,6},{8,9},{9,8},{10,11... | collective-permute-start | bytes 13832 | tf_op jit(solution)/shard_map/ppermute | solution.py:262
  10.4 8.8 %collective-permute-start.2 = (f32[21,128]{1,0:T(8,128)S(1)}, f32[21,128]{1,0:T(8,128)S(1)}, u32[]{:S(2)}, u32[]{:S(2)}) collective-permute-start(f32[21,128]{1,0:T(8,128)S(1)} %get-tuple-element.56), channel_id=1, source_target_pairs={{0,4},{4,8},{8,12},{12,0},{1,5},{5,9},{9,13},{13,1},{2,6},{6,10},{... | collective-permute-start | bytes 32264 | tf_op jit(solution)/shard_map/ppermute | solution.py:267
  13.8 105.8 %copy-start.16 = (bf16[8,256]{1,0:T(8,128)(2,1)}, bf16[8,256]{1,0:T(8,128)(2,1)S(1)}, u32[]{:S(2)}) copy-start(bf16[8,256]{1,0:T(8,128)(2,1)S(1)} %maximum_maximum_fusion.7.mix_ref) | copy-start | bytes 12292
  15.2 11.3 %collective-permute-start.1 = (f32[8,128]{1,0:T(8,128)S(1)}, f32[8,128]{1,0:T(8,128)S(1)}, u32[]{:S(2)}, u32[]{:S(2)}) collective-permute-start(f32[8,128]{1,0:T(8,128)S(1)} %slice_add_fusion.1), channel_id=1, source_target_pairs={{0,8},{4,12},{8,0},{12,4},{1,9},{5,13},{9,1},{13,5},{2,10},{6,14},... | collective-permute-start | bytes 12296 | tf_op jit(solution)/shard_map/ppermute | solution.py:267
  17.9 3.7 %collective-permute-start.3 = (f32[21,128]{1,0:T(8,128)S(1)}, f32[21,128]{1,0:T(8,128)S(1)}, u32[]{:S(2)}, u32[]{:S(2)}) collective-permute-start(f32[21,128]{1,0:T(8,128)S(1)} %get-tuple-element.57), channel_id=1, source_target_pairs={{0,12},{4,0},{8,4},{12,8},{1,13},{5,1},{9,5},{13,9},{2,14},{6,2},{... | collective-permute-start | bytes 32264 | tf_op jit(solution)/shard_map/ppermute | solution.py:267
  26.5 93.1 %copy-start.15 = (f32[8,128]{1,0:T(8,128)}, f32[8,128]{1,0:T(8,128)S(1)}, u32[]{:S(2)}) copy-start(f32[8,128]{1,0:T(8,128)S(1)} %fusion.31.sums_ref) | copy-start | bytes 12292
  26.6 1.2 copy-start.1
  27.9 1.0 copy-start.8
  28.9 1.4 copy-start.4
  30.3 0.8 copy-start.12
  31.1 31.9 %copy-start.21 = (bf16[1,4,256]{2,1,0:T(4,128)(2,1)S(1)}, bf16[1,4,256]{2,1,0:T(4,128)(2,1)}, u32[]{:S(2)}) copy-start(bf16[1,4,256]{2,1,0:T(4,128)(2,1)} %param.16) | copy-start | bytes 6148
  31.1 1.2 collective-permute-start.4
  32.3 19.5 %collective-permute-start.7 = (f32[32,256]{1,0:T(8,128)S(1)}, f32[32,256]{1,0:T(8,128)S(1)}, u32[]{:S(2)}, u32[]{:S(2)}) collective-permute-start(f32[32,256]{1,0:T(8,128)S(1)} %bitcast_add_fusion), channel_id=1, source_target_pairs={{0,12},{4,0},{8,4},{12,8},{1,13},{5,1},{9,5},{13,9},{2,14},{6,2},{... | collective-permute-start | bytes 98312 | tf_op jit(solution)/shard_map/ppermute | solution.py:267
  35.4 16.3 %collective-permute-start.6 = (f32[32,256]{1,0:T(8,128)S(1)}, f32[32,256]{1,0:T(8,128)S(1)}, u32[]{:S(2)}, u32[]{:S(2)}) collective-permute-start(f32[32,256]{1,0:T(8,128)S(1)} %bitcast_add_fusion), channel_id=1, source_target_pairs={{0,4},{4,8},{8,12},{12,0},{1,5},{5,9},{9,13},{13,1},{2,6},{6,10},{... | collective-permute-start | bytes 98312 | tf_op jit(solution)/shard_map/ppermute | solution.py:267
  35.4 16.3 %collective-permute-start.5 = (f32[32,256]{1,0:T(8,128)S(1)}, f32[32,256]{1,0:T(8,128)S(1)}, u32[]{:S(2)}, u32[]{:S(2)}) collective-permute-start(f32[32,256]{1,0:T(8,128)S(1)} %bitcast_add_fusion), channel_id=1, source_target_pairs={{0,8},{4,12},{8,0},{12,4},{1,9},{5,13},{9,1},{13,5},{2,10},{6,14},... | collective-permute-start | bytes 98312 | tf_op jit(solution)/shard_map/ppermute | solution.py:267
  36.7 26.1 %collective-permute-start.12 = (bf16[592,128]{1,0:T(8,128)(2,1)}, bf16[592,128]{1,0:T(8,128)(2,1)S(1)}, u32[]{:S(2)}, u32[]{:S(2)}) collective-permute-start(bf16[592,128]{1,0:T(8,128)(2,1)} %pad_maximum_fusion.3), channel_id=1, source_target_pairs={{0,2},{2,0},{1,3},{3,1},{4,6},{6,4},{5,7},{7,5},{8,10},{10,8},{9,1... | collective-permute-start | bytes 454664 | tf_op jit(solution)/shard_map/ppermute | solution.py:262
  51.8 11.0 %copy-start.18 = (f32[32,256]{1,0:T(8,128)}, f32[32,256]{1,0:T(8,128)S(1)}, u32[]{:S(2)}) copy-start(f32[32,256]{1,0:T(8,128)S(1)} %add_add_fusion.1) | copy-start | bytes 98308
  52.4 30.5 %copy-start.2 = (bf16[4,1024,128]{2,1,0:T(8,128)(2,1)S(1)}, bf16[4,1024,128]{2,1,0:T(8,128)(2,1)}, u32[]{:S(2)}) copy-start(bf16[4,1024,128]{2,1,0:T(8,128)(2,1)} %get-tuple-element.15.grad_ref) | copy-start | bytes 3145732
  52.4 30.5 %copy-start.9 = (bf16[4,288,128]{2,1,0:T(8,128)(2,1)S(1)}, bf16[4,288,128]{2,1,0:T(8,128)(2,1)}, u32[]{:S(2)}) copy-start(bf16[4,288,128]{2,1,0:T(8,128)(2,1)} %get-tuple-element.16.halo_ref) | copy-start | bytes 884740
  52.4 7.6 %collective-permute-start.8 = (f32[72,128]{1,0:T(8,128)}, f32[72,128]{1,0:T(8,128)S(1)}, u32[]{:S(2)}, u32[]{:S(2)}) collective-permute-start(f32[72,128]{1,0:T(8,128)} %pad_maximum_fusion.5), channel_id=1, source_target_pairs={{0,2},{2,0},{1,3},{3,1},{4,6},{6,4},{5,7},{7,5},{8,10},{10,8},{9,1... | collective-permute-start | bytes 110600 | tf_op jit(solution)/shard_map/ppermute | solution.py:262
  57.8 9.5 %collective-permute-start.10 = (bf16[1,1024,128]{2,1,0:T(8,128)(2,1)}, bf16[1,1024,128]{2,1,0:T(8,128)(2,1)S(1)}, u32[]{:S(2)}, u32[]{:S(2)}) collective-permute-start(bf16[1,1024,128]{2,1,0:T(8,128)(2,1)} %bitcast.13), channel_id=1, source_target_pairs={{0,2},{2,0},{1,3},{3,1},{4,6},{6,4},{5,7},{7,5},{8,10},{10,8},{9,1... | collective-permute-start | bytes 786440 | tf_op jit(solution)/shard_map/ppermute | solution.py:262
  57.8 15.2 %collective-permute-start.9 = (bf16[1,1024,128]{2,1,0:T(8,128)(2,1)}, bf16[1,1024,128]{2,1,0:T(8,128)(2,1)}, u32[]{:S(2)}, u32[]{:S(2)}) collective-permute-start(bf16[1,1024,128]{2,1,0:T(8,128)(2,1)} %bitcast.12), channel_id=1, source_target_pairs={{0,2},{2,0},{1,3},{3,1},{4,6},{6,4},{5,7},{7,5},{8,10},{10,8},{9,1... | collective-permute-start | bytes 786440 | tf_op jit(solution)/shard_map/ppermute | solution.py:262
  59.9 23.1 %collective-permute-start.17 = (bf16[1,1024,128]{2,1,0:T(8,128)(2,1)}, bf16[1,1024,128]{2,1,0:T(8,128)(2,1)S(1)}, u32[]{:S(2)}, u32[]{:S(2)}) collective-permute-start(bf16[1,1024,128]{2,1,0:T(8,128)(2,1)} %bitcast.20), channel_id=1, source_target_pairs={{0,2},{2,0},{1,3},{3,1},{4,6},{6,4},{5,7},{7,5},{8,10},{10,8},{9,1... | collective-permute-start | bytes 786440 | tf_op jit(solution)/shard_map/ppermute | solution.py:262
  60.1 2.0 %copy-start.20 = (f32[72,128]{1,0:T(8,128)}, f32[72,128]{1,0:T(8,128)S(1)}, u32[]{:S(2)}) copy-start(f32[72,128]{1,0:T(8,128)S(1)} %collective-permute-done.8) | copy-start | bytes 110596
  60.1 21.6 %collective-permute-start.11 = (bf16[1,1024,128]{2,1,0:T(8,128)(2,1)}, bf16[1,1024,128]{2,1,0:T(8,128)(2,1)}, u32[]{:S(2)}, u32[]{:S(2)}) collective-permute-start(bf16[1,1024,128]{2,1,0:T(8,128)(2,1)} %bitcast.80), channel_id=1, source_target_pairs={{0,2},{2,0},{1,3},{3,1},{4,6},{6,4},{5,7},{7,5},{8,10},{10,8},{9,1... | collective-permute-start | bytes 786440 | tf_op jit(solution)/shard_map/ppermute | solution.py:262
  62.8 20.2 %copy-start.5 = (f32[4,1024,128]{2,1,0:T(8,128)S(1)}, f32[4,1024,128]{2,1,0:T(8,128)}, u32[]{:S(2)}) copy-start(f32[4,1024,128]{2,1,0:T(8,128)} %copy-done.4) | copy-start | bytes 6291460
  62.9 20.0 %collective-permute-start.13 = (bf16[576,128]{1,0:T(8,128)(2,1)S(1)}, bf16[576,128]{1,0:T(8,128)(2,1)S(1)}, u32[]{:S(2)}, u32[]{:S(2)}) collective-permute-start(bf16[576,128]{1,0:T(8,128)(2,1)S(1)} %slice.227), channel_id=1, source_target_pairs={{0,1},{1,0},{2,3},{3,2},{4,5},{5,4},{6,7},{7,6},{8,9},{9,8},{10,11... | collective-permute-start | bytes 442376 | tf_op jit(solution)/shard_map/ppermute | solution.py:262
  83.0 3.0 %copy-start.10 = (bf16[4,288,128]{2,1,0:T(8,128)(2,1)S(1)}, bf16[4,288,128]{2,1,0:T(8,128)(2,1)}, u32[]{:S(2)}) copy-start(bf16[4,288,128]{2,1,0:T(8,128)(2,1)} %get-tuple-element.16.halo_ref) | copy-start | bytes 884740
  86.0 33.7 %copy-start.7 = (bf16[1,1024,128]{2,1,0:T(8,128)(2,1)}, bf16[1,1024,128]{2,1,0:T(8,128)(2,1)S(1)}, u32[]{:S(2)}) copy-start(bf16[1,1024,128]{2,1,0:T(8,128)(2,1)S(1)} %redo_upper.3.grad_ref) | copy-start | bytes 786436
  94.8 23.6 %copy-start.3 = (bf16[3,1024,128]{2,1,0:T(8,128)(2,1)}, bf16[3,1024,128]{2,1,0:T(8,128)(2,1)S(1)}, u32[]{:S(2)}) copy-start(bf16[3,1024,128]{2,1,0:T(8,128)(2,1)S(1)} %redo_upper.2.grad_ref) | copy-start | bytes 2359300
  94.8 13.3 %copy-start.13 = (f32[1152,128]{1,0:T(8,128)S(1)}, f32[1152,128]{1,0:T(8,128)}, u32[]{:S(2)}) copy-start(f32[1152,128]{1,0:T(8,128)} %copy-done.12) | copy-start | bytes 1769476
  94.9 1.2 collective-permute-start.18
  95.0 5.1 %collective-permute-start.14 = (bf16[3,8,128]{2,1,0:T(8,128)(2,1)S(1)}, bf16[3,8,128]{2,1,0:T(8,128)(2,1)S(1)}, u32[]{:S(2)}, u32[]{:S(2)}) collective-permute-start(bf16[3,8,128]{2,1,0:T(8,128)(2,1)S(1)} %fusion.30), channel_id=1, source_target_pairs={{0,1},{1,0},{2,3},{3,2},{4,5},{5,4},{6,7},{7,6},{8,9},{9,8},{10,11... | collective-permute-start | bytes 18440 | tf_op jit(solution)/shard_map/ppermute | solution.py:262
  96.2 7.9 %collective-permute-start.19 = (bf16[1,144,128]{2,1,0:T(8,128)(2,1)S(1)}, bf16[1,144,128]{2,1,0:T(8,128)(2,1)S(1)}, u32[]{:S(2)}, u32[]{:S(2)}) collective-permute-start(bf16[1,144,128]{2,1,0:T(8,128)(2,1)S(1)} %get-tuple-element.64), channel_id=1, source_target_pairs={{0,4},{4,8},{8,12},{12,0},{1,5},{5,9},{9,13},{13,1},{2,6},{6,10},{... | collective-permute-start | bytes 110600 | tf_op jit(solution)/shard_map/ppermute | solution.py:267
  97.5 6.6 %collective-permute-start.20 = (bf16[1,144,128]{2,1,0:T(8,128)(2,1)S(1)}, bf16[1,144,128]{2,1,0:T(8,128)(2,1)S(1)}, u32[]{:S(2)}, u32[]{:S(2)}) collective-permute-start(bf16[1,144,128]{2,1,0:T(8,128)(2,1)S(1)} %get-tuple-element.65), channel_id=1, source_target_pairs={{0,12},{4,0},{8,4},{12,8},{1,13},{5,1},{9,5},{13,9},{2,14},{6,2},{... | collective-permute-start | bytes 110600 | tf_op jit(solution)/shard_map/ppermute | solution.py:267
  100.2 7.7 %collective-permute-start.15 = (bf16[3,144,128]{2,1,0:T(8,128)(2,1)S(1)}, bf16[3,144,128]{2,1,0:T(8,128)(2,1)S(1)}, u32[]{:S(2)}, u32[]{:S(2)}) collective-permute-start(bf16[3,144,128]{2,1,0:T(8,128)(2,1)S(1)} %get-tuple-element.62), channel_id=1, source_target_pairs={{0,4},{4,8},{8,12},{12,0},{1,5},{5,9},{9,13},{13,1},{2,6},{6,10},{... | collective-permute-start | bytes 331784 | tf_op jit(solution)/shard_map/ppermute | solution.py:267
  100.3 7.6 %collective-permute-start.16 = (bf16[3,144,128]{2,1,0:T(8,128)(2,1)S(1)}, bf16[3,144,128]{2,1,0:T(8,128)(2,1)S(1)}, u32[]{:S(2)}, u32[]{:S(2)}) collective-permute-start(bf16[3,144,128]{2,1,0:T(8,128)(2,1)S(1)} %get-tuple-element.63), channel_id=1, source_target_pairs={{0,12},{4,0},{8,4},{12,8},{1,13},{5,1},{9,5},{13,9},{2,14},{6,2},{... | collective-permute-start | bytes 331784 | tf_op jit(solution)/shard_map/ppermute | solution.py:267
  118.4 1.2 copy-start.11
  119.6 14.2 %copy-start.19 = (f32[32,256]{1,0:T(8,128)S(1)}, f32[32,256]{1,0:T(8,128)}, u32[]{:S(2)}) copy-start(f32[32,256]{1,0:T(8,128)} %copy-done.18) | copy-start | bytes 98308
  123.3 5.5 %copy-start.14 = (f32[1,1024,128]{2,1,0:T(8,128)}, f32[1,1024,128]{2,1,0:T(8,128)S(1)}, u32[]{:S(2)}) copy-start(f32[1,1024,128]{2,1,0:T(8,128)S(1)} %get-tuple-element.24.norm_ref) | copy-start | bytes 1572868
  123.4 5.4 %collective-permute-start.25 = (f32[576,128]{1,0:T(8,128)S(1)}, f32[576,128]{1,0:T(8,128)S(1)}, u32[]{:S(2)}, u32[]{:S(2)}) collective-permute-start(f32[576,128]{1,0:T(8,128)S(1)} %constant_dynamic-slice_fusion), channel_id=1, source_target_pairs={{0,1},{1,0},{2,3},{3,2},{4,5},{5,4},{6,7},{7,6},{8,9},{9,8},{10,11... | collective-permute-start | bytes 884744 | tf_op jit(solution)/shard_map/ppermute | solution.py:262
  123.5 1.6 %collective-permute-start.21 = (f32[32,256]{1,0:T(8,128)S(1)}, f32[32,256]{1,0:T(8,128)S(1)}, u32[]{:S(2)}, u32[]{:S(2)}) collective-permute-start(f32[32,256]{1,0:T(8,128)S(1)} %maximum_bitcast_fusion), channel_id=1, source_target_pairs={{0,1},{1,0},{2,3},{3,2},{4,5},{5,4},{6,7},{7,6},{8,9},{9,8},{10,11... | collective-permute-start | bytes 98312 | tf_op jit(solution)/shard_map/ppermute | solution.py:262
  125.1 7.3 %collective-permute-start.24 = (f32[32,256]{1,0:T(8,128)S(1)}, f32[32,256]{1,0:T(8,128)S(1)}, u32[]{:S(2)}, u32[]{:S(2)}) collective-permute-start(f32[32,256]{1,0:T(8,128)S(1)} %fusion.33), channel_id=1, source_target_pairs={{0,12},{4,0},{8,4},{12,8},{1,13},{5,1},{9,5},{13,9},{2,14},{6,2},{... | collective-permute-start | bytes 98312 | tf_op jit(solution)/shard_map/ppermute | solution.py:267
  127.8 6.1 %collective-permute-start.23 = (f32[32,256]{1,0:T(8,128)S(1)}, f32[32,256]{1,0:T(8,128)S(1)}, u32[]{:S(2)}, u32[]{:S(2)}) collective-permute-start(f32[32,256]{1,0:T(8,128)S(1)} %fusion.33), channel_id=1, source_target_pairs={{0,4},{4,8},{8,12},{12,0},{1,5},{5,9},{9,13},{13,1},{2,6},{6,10},{... | collective-permute-start | bytes 98312 | tf_op jit(solution)/shard_map/ppermute | solution.py:267
  127.8 6.1 %collective-permute-start.22 = (f32[32,256]{1,0:T(8,128)S(1)}, f32[32,256]{1,0:T(8,128)S(1)}, u32[]{:S(2)}, u32[]{:S(2)}) collective-permute-start(f32[32,256]{1,0:T(8,128)S(1)} %fusion.33), channel_id=1, source_target_pairs={{0,8},{4,12},{8,0},{12,4},{1,9},{5,13},{9,1},{13,5},{2,10},{6,14},... | collective-permute-start | bytes 98312 | tf_op jit(solution)/shard_map/ppermute | solution.py:267
  128.8 12.7 %collective-permute-start.28 = (bf16[576,128]{1,0:T(8,128)(2,1)S(1)}, bf16[576,128]{1,0:T(8,128)(2,1)S(1)}, u32[]{:S(2)}, u32[]{:S(2)}) collective-permute-start(bf16[576,128]{1,0:T(8,128)(2,1)S(1)} %add_convert_fusion), channel_id=1, source_target_pairs={{0,12},{4,0},{8,4},{12,8},{1,13},{5,1},{9,5},{13,9},{2,14},{6,2},{... | collective-permute-start | bytes 442376 | tf_op jit(solution)/shard_map/ppermute | solution.py:267
  131.7 9.9 %collective-permute-start.27 = (bf16[576,128]{1,0:T(8,128)(2,1)S(1)}, bf16[576,128]{1,0:T(8,128)(2,1)S(1)}, u32[]{:S(2)}, u32[]{:S(2)}) collective-permute-start(bf16[576,128]{1,0:T(8,128)(2,1)S(1)} %add_convert_fusion), channel_id=1, source_target_pairs={{0,4},{4,8},{8,12},{12,0},{1,5},{5,9},{9,13},{13,1},{2,6},{6,10},{... | collective-permute-start | bytes 442376 | tf_op jit(solution)/shard_map/ppermute | solution.py:267
  132.3 14.4 %collective-permute-start.26 = (bf16[576,128]{1,0:T(8,128)(2,1)S(1)}, bf16[576,128]{1,0:T(8,128)(2,1)S(1)}, u32[]{:S(2)}, u32[]{:S(2)}) collective-permute-start(bf16[576,128]{1,0:T(8,128)(2,1)S(1)} %add_convert_fusion), channel_id=1, source_target_pairs={{0,8},{4,12},{8,0},{12,4},{1,9},{5,13},{9,1},{13,5},{2,10},{6,14},... | collective-permute-start | bytes 442376 | tf_op jit(solution)/shard_map/ppermute | solution.py:267
  138.6 8.3 %copy-start.17 = (bf16[3,1024,128]{2,1,0:T(8,128)(2,1)S(1)}, bf16[3,1024,128]{2,1,0:T(8,128)(2,1)}, u32[]{:S(2)}) copy-start(bf16[3,1024,128]{2,1,0:T(8,128)(2,1)} %input_gradient.2) | copy-start | bytes 2359300
  146.8 2.7 %collective-permute-start.29 = (f32[576,128]{1,0:T(8,128)S(1)}, f32[576,128]{1,0:T(8,128)S(1)}, u32[]{:S(2)}, u32[]{:S(2)}) collective-permute-start(f32[576,128]{1,0:T(8,128)S(1)} %add_add_fusion), channel_id=1, source_target_pairs={{0,1},{1,0},{2,3},{3,2},{4,5},{5,4},{6,7},{7,6},{8,9},{9,8},{10,11... | collective-permute-start | bytes 884744 | tf_op jit(solution)/shard_map/ppermute | solution.py:262

commit v2 on v0

--- a/solution.py
+++ b/solution.py
@@ -1,6 +1,10 @@
+import functools
+
 import jax
 import jax.numpy as jnp
 from jax import lax
+from jax.experimental import pallas as pl
+from jax.experimental.pallas import tpu as pltpu
 from jax.sharding import PartitionSpec as P
 
 GROUPS = 32
@@ -166,7 +170,7 @@
     return (result, kernel_term, mod_term, bias_term)
 
 
-def body(
+def general_body(
     activations,
     latent,
     recon,
@@ -246,7 +250,587 @@
     return (grads_out, kernel_grad, mod_grad, bias_grad)
 
 
+EXACT = lax.Precision.HIGHEST
+TN = (((0,), (0,)), ((), ()))
+NT = (((1,), (1,)), ((), ()))
+F32 = jnp.float32
+BF16 = jnp.bfloat16
+
+
+def swap(value, axis):
+    return lax.ppermute(value, axis, [(0, 1), (1, 0)])
+
+
+def shift(value, axis, steps):
+    count = lax.axis_size(axis)
+    return lax.ppermute(value, axis, [(i, (i + steps) % count) for i in range(count)])
+
+
+def swap_and_shift(value, steps):
+    count = lax.axis_size("rows")
+    pairs = [(2 * i + s, 2 * ((i + steps) % count) + 1 - s) for i in range(count) for s in range(2)]
+    return lax.ppermute(value, ("rows", "segment"), pairs)
+
+
+def pixel_total(value):
+    value = value + swap(value, "sub")
+    one, two, three = [shift(value, "rows", steps) for steps in (1, 2, 3)]
+    return (value + two) + (one + three)
+
+
+def same_group(channels):
+    per = channels // GROUPS
+    left = lax.broadcasted_iota(jnp.int32, (channels, channels), 0) // per
+    right = lax.broadcasted_iota(jnp.int32, (channels, channels), 1) // per
+    return (left == right).astype(F32)
+
+
+def statistics(sums_ref, micro, micros, member, count):
+    both = jnp.concatenate([sums_ref[pl.ds(micro, 1), :], sums_ref[pl.ds(micros + micro, 1), :]], axis=0)
+    both = jnp.dot(both, member, precision=EXACT, preferred_element_type=F32) / count
+    mean = both[0:1]
+    return mean, lax.rsqrt(both[1:2] - mean * mean + EPS)
+
+
+def gradient_means(total, mix, member, count):
+    mean_grad = jnp.sum(mix[:8] * total[8:], axis=0, keepdims=True)
+    mean_cross = jnp.sum(mix[:8] * total[:8], axis=0, keepdims=True)
+    both = jnp.concatenate([mean_grad, mean_cross], axis=0)
+    both = jnp.dot(both, member, precision=EXACT, preferred_element_type=F32) / count
+    return both[0:1], both[1:2]
+
+
+def side_by_side(mix):
+    return jnp.concatenate([mix[:8], mix[8:]], axis=1).astype(BF16)
+
+
+def sums_kernel(acts_ref, out_ref):
+    micro, micros = pl.program_id(0), pl.num_programs(0)
+    value = acts_ref[0].astype(F32)
+    out_ref[pl.ds(micro, 1), :] = jnp.sum(value, axis=0, keepdims=True)
+    out_ref[pl.ds(micros + micro, 1), :] = jnp.sum(value * value, axis=0, keepdims=True)
+
+
+class Top:
+    def __init__(self, shape, micro, place_ref, boxes_ref, weight_ref, up_ref, diff_ref, down_ref):
+        self.rows, self.cols, total_rows, total_cols, crops = shape
+        self.refs = (up_ref, diff_ref, down_ref)
+        self.side, self.row_start = place_ref[1], place_ref[2]
+        lane = lax.broadcasted_iota(jnp.int32, (1, self.cols), 1)
+        tiles = total_rows // TILE * (total_cols // TILE)
+        self.boxes = []
+        for k in range(crops):
+            row, col, height, width = [boxes_ref[micro, k, i] for i in range(4)]
+            area = jnp.full((1, self.cols), crops * height * width, jnp.int32).astype(F32)
+            share = tiles / area
+            inside = []
+            for side in (self.side, 1 - self.side):
+                at = lane + side * self.cols
+                inside.append(jnp.where((at >= col * TILE) & (at < (col + width) * TILE), share, 0.0))
+            self.boxes.append((row * TILE, (row + height) * TILE, inside[0], inside[1]))
+        weight = weight_ref[...].astype(F32)
+        blank = jnp.zeros((8 - weight.shape[0], weight.shape[1]), F32)
+        own = jnp.concatenate([weight, blank])
+        other = jnp.concatenate([blank[:3], weight, blank[3:]])
+        self.own = jnp.concatenate([own] * 3).astype(BF16)
+        self.other = jnp.concatenate([other] * 3).astype(BF16)
+
+    def row(self, index):
+        up_ref, diff_ref, down_ref = self.refs
+        if index < 2:
+            diff = up_ref[0, index]
+        elif index < self.rows + 2:
+            diff = diff_ref[0, index - 2]
+        else:
+            diff = down_ref[0, index - self.rows - 2]
+        at = self.row_start + (index - 2)
+        own = jnp.zeros((1, self.cols), F32)
+        other = jnp.zeros((1, self.cols), F32)
+        for first, end, own_share, other_share in self.boxes:
+            here = (at >= first) & (at < end)
+            own = own + jnp.where(here, own_share, 0.0)
+            other = other + jnp.where(here, other_share, 0.0)
+        plane = lax.broadcasted_iota(jnp.int32, (8, self.cols), 0)
+        diff = 2.0 * diff * jnp.where(plane < 3, own, other)
+        high = diff.astype(BF16).astype(F32)
+        middle = (diff - high).astype(BF16).astype(F32)
+        parts = jnp.concatenate([high, middle, diff - high - middle]).astype(BF16)
+        value = lax.dot_general(parts, self.own, TN, preferred_element_type=F32).astype(BF16)
+        beside = lax.dot_general(parts, self.other, TN, preferred_element_type=F32).astype(BF16).astype(F32)
+        return value, jnp.where(self.side == 0, beside[0:1], beside[self.cols - 1 : self.cols])
+
+    def main_row(self, r):
+        return self.row(r + 2)[0]
+
+
+def spread(index, cols, value, near, side, shifted):
+    channels = value.shape[-1]
+    at = slice(index * cols, (index + 1) * cols)
+    place = lax.broadcasted_iota(jnp.int32, (cols, channels), 0)
+    wide = value.astype(F32)
+    before = jnp.where(side == 1, near, 0.0)
+    behind = jnp.where(side == 0, near, 0.0)
+    shifted[at, 0:channels] = jnp.where(place == 0, before, pltpu.roll(wide, 1, 0)).astype(BF16)
+    shifted[at, channels : 2 * channels] = value
+    shifted[at, 2 * channels :] = jnp.where(place == cols - 1, behind, pltpu.roll(wide, cols - 1, 0)).astype(BF16)
+
+
+def tap_of(row, col):
+    return 3 * (2 - row) + (2 - col)
+
+
+def arrange_weights(kernel_ref, weights):
+    channels = kernel_ref.shape[-1]
+    for row in range(3):
+        for col in range(3):
+            tap = tap_of(row, col)
+            weights[row, :, col * channels : (col + 1) * channels] = kernel_ref[tap * channels : (tap + 1) * channels, :]
+
+
+def hidden_gradient(rows, cols, shifted, weights, hidden_grad):
+    pixels = rows * cols
+    total = lax.dot_general(shifted[0:pixels, :], weights[0], NT, preferred_element_type=F32)
+    total = total + lax.dot_general(shifted[cols : cols + pixels, :], weights[1], NT, preferred_element_type=F32)
+    hidden_grad[0:pixels, :] = total + lax.dot_general(
+        shifted[2 * cols : 2 * cols + pixels, :], weights[2], NT, preferred_element_type=F32
+    )
+
+
+def pixel_values(acts, latent, mix, mean, rstd):
+    channels = mean.shape[-1]
+    xhat = (acts.astype(F32) - mean) * rstd
+    mixed = lax.dot_general(latent, mix, TN, preferred_element_type=F32)
+    scale = mixed[:, :channels]
+    pre = xhat * scale + mixed[:, channels:]
+    sig = 0.5 * jnp.tanh(0.5 * pre) + 0.5
+    hidden = pre * sig
+    return xhat, scale, hidden, sig + hidden * (1.0 - sig)
+
+
+def block_step(
+    rows, cols, mean, rstd, mix, acts_ref, latent_ref, norm_ref, reduced_ref, shifted, weights, hidden_grad, hidden_keep, pairs, total_kernel
+):
+    channels = acts_ref.shape[-1]
+    pixels = rows * cols
+    hidden_gradient(rows, cols, shifted, weights, hidden_grad)
+    for r in range(rows):
+        at = slice(r * cols, (r + 1) * cols)
+        latent = latent_ref[0, :, (r + 1) * cols : (r + 2) * cols]
+        xhat, scale, hidden, slope = pixel_values(acts_ref[0, at, :], latent, mix, mean, rstd)
+        hidden_keep[at, :] = hidden.astype(BF16)
+        pre_grad = hidden_grad[at, :] * slope
+        norm_ref[0, at, :] = (pre_grad * scale).astype(BF16)
+        pairs[at, 0:channels] = (pre_grad * xhat).astype(BF16)
+        pairs[at, channels:] = pre_grad.astype(BF16)
+    reduced = jnp.dot(latent_ref[0, :, cols : cols + pixels], pairs[...], preferred_element_type=F32)
+    reduced_ref[0, 0:8, :] = reduced[:, :channels]
+    reduced_ref[0, 8:16, :] = reduced[:, channels:]
+    for row in range(3):
+        total_kernel[row] += lax.dot_general(
+            hidden_keep[...], shifted[row * cols : row * cols + pixels, :], TN, preferred_element_type=F32
+        )
+
+
+def write_kernel_grad(total_kernel, kernel_grad_ref):
+    channels = kernel_grad_ref.shape[-1]
+    for row in range(3):
+        for col in range(3):
+            tap = tap_of(row, col)
+            kernel_grad_ref[tap * channels : (tap + 1) * channels, :] = total_kernel[row, :, col * channels : (col + 1) * channels]
+
+
+def upper_kernel(
+    shape,
+    micros,
+    count,
+    place_ref,
+    boxes_ref,
+    sums_ref,
+    mix_ref,
+    weight_ref,
+    kernel_ref,
+    up_ref,
+    diff_ref,
+    down_ref,
+    acts_ref,
+    latent_ref,
+    norm_ref,
+    reduced_ref,
+    kernel_grad_ref,
+    shifted,
+    weights,
+    hidden_grad,
+    hidden_keep,
+    pairs,
+    total_kernel,
+):
+    step = pl.program_id(0)
+    rows, cols = shape[:2]
+    active = place_ref[0] == 1
+
+    @pl.when(active)
+    def _():
+        @pl.when(step == 0)
+        def _():
+            arrange_weights(kernel_ref, weights)
+            total_kernel[...] = jnp.zeros_like(total_kernel)
+
+        mean, rstd = statistics(sums_ref, step, micros, same_group(acts_ref.shape[-1]), count)
+        top = Top(shape, step, place_ref, boxes_ref, weight_ref, up_ref, diff_ref, down_ref)
+        for r in range(rows + 2):
+            spread(r, cols, *top.row(r + 1), place_ref[1], shifted)
+        block_step(
+            rows,
+            cols,
+            mean,
+            rstd,
+            side_by_side(mix_ref[...]),
+            acts_ref,
+            latent_ref,
+            norm_ref,
+            reduced_ref,
+            shifted,
+            weights,
+            hidden_grad,
+            hidden_keep,
+            pairs,
+            total_kernel,
+        )
+
+        @pl.when(step == micros - 1)
+        def _():
+            write_kernel_grad(total_kernel, kernel_grad_ref)
+
+    @pl.when(jnp.logical_not(active))
+    def _():
+        reduced_ref[...] = jnp.zeros_like(reduced_ref)
+
+
+def redo_kernel(
+    shape,
+    micros,
+    count,
+    place_ref,
+    boxes_ref,
+    packed_ref,
+    weight_ref,
+    kernel_ref,
+    up_ref,
+    diff_ref,
+    down_ref,
+    acts_ref,
+    norm_ref,
+    passed_ref,
+    above_ref,
+    below_ref,
+    latent_ref,
+    result_ref,
+    edge_ref,
+    shifted,
+    weights,
+    hidden_grad,
+):
+    step = pl.program_id(0)
+    rows, cols, total_rows = shape[:3]
+    channels = acts_ref.shape[-1]
+    upper = place_ref[0] == 1
+    side = place_ref[1]
+    member = same_group(channels)
+    mean, rstd = statistics(packed_ref, step, micros, member, count)
+    mix = packed_ref[2 * micros + 16 * micros :, :]
+    total = packed_ref[pl.ds(pl.multiple_of(2 * micros + 16 * step, 8), 16), :]
+    mean_grad, mean_cross = gradient_means(total, mix, member, count)
+    top = Top(shape, step, place_ref, boxes_ref, weight_ref, up_ref, diff_ref, down_ref)
+
+    @pl.when(upper)
+    def _():
+        for r in range(rows):
+            at = slice(r * cols, (r + 1) * cols)
+            xhat = (acts_ref[0, at, :].astype(F32) - mean) * rstd
+            change = rstd * (norm_ref[0, at, :].astype(F32) - mean_grad - xhat * mean_cross)
+            result_ref[0, (r + 1) * cols : (r + 2) * cols, :] = (top.main_row(r).astype(F32) + change).astype(BF16)
+
+    @pl.when(jnp.logical_not(upper))
+    def _():
+        @pl.when(step == 0)
+        def _():
+            arrange_weights(kernel_ref, weights)
+
+        for r in range(rows + 4):
+            spread(r, cols, *top.row(r), side, shifted)
+        hidden_gradient(rows + 2, cols, shifted, weights, hidden_grad)
+        wide_mix = side_by_side(mix)
+        edges = []
+        for r in range(rows + 2):
+            at = slice(r * cols, (r + 1) * cols)
+            if r == 0:
+                acts = above_ref[0]
+            elif r == rows + 1:
+                acts = below_ref[0]
+            else:
+                acts = passed_ref[0, (r - 1) * cols : r * cols, :]
+            xhat, scale, _, slope = pixel_values(acts, latent_ref[0, :, at], wide_mix, mean, rstd)
+            change = rstd * (hidden_grad[at, :] * slope * scale - mean_grad - xhat * mean_cross)
+            middle = shifted[(r + 1) * cols : (r + 2) * cols, channels : 2 * channels]
+            value = middle.astype(F32) + change
+            if r == 0 or r == rows + 1:
+                row = place_ref[2] + (r - 1)
+                value = jnp.where((row >= 0) & (row < total_rows), value, 0.0)
+            result_ref[0, at, :] = value.astype(BF16)
+            edges.append(jnp.where(side == 0, value[cols - 1 : cols], value[0:1]))
+        edges.append(jnp.zeros((16 - rows - 2, channels), F32))
+        edge_ref[0] = jnp.concatenate(edges).astype(BF16)
+
+
+def lower_kernel(
+    shape,
+    micros,
+    count,
+    place_ref,
+    sums_ref,
+    mix_ref,
+    kernel_ref,
+    grad_ref,
+    near_ref,
+    acts_ref,
+    latent_ref,
+    before_ref,
+    norm_ref,
+    reduced_ref,
+    kernel_grad_ref,
+    shifted,
+    weights,
+    hidden_grad,
+    hidden_keep,
+    pairs,
+    total_kernel,
+):
+    step = pl.program_id(0)
+    rows, cols = shape[:2]
+    active = place_ref[0] == 0
+
+    @pl.when(active)
+    def _():
+        @pl.when(step == 0)
+        def _():
+            arrange_weights(kernel_ref, weights)
+            total_kernel[...] = jnp.zeros_like(total_kernel)
+
+        mean, rstd = statistics(sums_ref, step, micros, same_group(acts_ref.shape[-1]), count)
+        near = near_ref[0].astype(F32)
+        for r in range(rows + 2):
+            spread(r, cols, grad_ref[0, r * cols : (r + 1) * cols, :], near[r : r + 1], place_ref[1], shifted)
+        block_step(
+            rows,
+            cols,
+            mean,
+            rstd,
+            side_by_side(mix_ref[...]),
+            acts_ref,
+            latent_ref,
+            norm_ref,
+            reduced_ref,
+            shifted,
+            weights,
+            hidden_grad,
+            hidden_keep,
+            pairs,
+            total_kernel,
+        )
+
+        @pl.when(step == micros - 1)
+        def _():
+            write_kernel_grad(total_kernel, kernel_grad_ref)
+
+    @pl.when(jnp.logical_not(active))
+    def _():
+        reduced_ref[...] = jnp.zeros_like(reduced_ref)
+
+        @pl.when(step == micros - 1)
+        def _():
+            kernel_grad_ref[...] = before_ref[...]
+
+
+def last_kernel(rows, cols, micros, count, place_ref, sums_ref, mix_ref, total_ref, acts_ref, norm_ref, grad_ref, result_ref):
+    step = pl.program_id(0)
+    lower = place_ref[0] == 0
+
+    @pl.when(lower)
+    def _():
+        member = same_group(acts_ref.shape[-1])
+        mean, rstd = statistics(sums_ref, step, micros, member, count)
+        mean_grad, mean_cross = gradient_means(total_ref[0], mix_ref[...], member, count)
+        for r in range(rows):
+            at = slice(r * cols, (r + 1) * cols)
+            xhat = (acts_ref[0, at, :].astype(F32) - mean) * rstd
+            change = rstd * (norm_ref[0, at, :].astype(F32) - mean_grad - xhat * mean_cross)
+            result_ref[0, at, :] = (grad_ref[0, (r + 1) * cols : (r + 2) * cols, :].astype(F32) + change).astype(BF16)
+
+    @pl.when(jnp.logical_not(lower))
+    def _():
+        result_ref[0] = grad_ref[0, cols : (rows + 1) * cols, :]
+
+
+def by_micro(value):
+    rest = (0,) * (len(value.shape) - 1)
+    return pl.BlockSpec((1,) + tuple(value.shape[1:]), lambda m: (m,) + rest)
+
+
+def whole(value):
+    return pl.BlockSpec(tuple(value.shape), lambda m: (0,) * len(value.shape))
+
+
+def call(kernel, name, micros, scalars, fixed, per_micro, outs, fixed_outs=(), scratch=(), tail=()):
+    out_shape = [jax.ShapeDtypeStruct(s, d) for s, d in outs] + [jax.ShapeDtypeStruct(s, d) for s, d in fixed_outs]
+    return pl.pallas_call(
+        kernel,
+        grid=(micros,),
+        in_specs=[pl.BlockSpec(memory_space=pltpu.SMEM) for _ in scalars]
+        + [whole(v) for v in fixed]
+        + [by_micro(v) for v in per_micro]
+        + [whole(v) for v in tail],
+        out_specs=[by_micro(s) for s in out_shape[: len(outs)]] + [whole(s) for s in out_shape[len(outs) :]],
+        out_shape=out_shape,
+        scratch_shapes=[pltpu.VMEM(s, d) for s, d in scratch],
+        compiler_params=pltpu.CompilerParams(vmem_limit_bytes=20 * 1024 * 1024),
+        cost_estimate=pl.CostEstimate(flops=1, bytes_accessed=1, transcendentals=0),
+        name=name,
+    )(*scalars, *fixed, *per_micro, *tail)
+
+
+def pair_body(
+    activations, latent, recon, target, boxes, kernel, mod_weight, scale_bias, shift_bias, out_weight
+):
+    micros, rows, cols, channels = activations.shape[1:]
+    latents, colors = latent.shape[1], recon.shape[1]
+    pixels = rows * cols
+    bands = lax.axis_size("rows")
+    total_rows, total_cols = rows * bands, cols * 2
+    count = float(total_rows * total_cols * (channels // GROUPS))
+    segment = lax.axis_index("segment")
+    side = lax.axis_index("sub")
+    place = jnp.stack([segment, side, lax.axis_index("rows") * rows]).astype(jnp.int32)
+    acts = activations[0].reshape(micros, pixels, channels)
+
+    passed = swap(acts, "segment")
+    above = swap_and_shift(acts[:, pixels - cols :], 1)
+    below = swap_and_shift(acts[:, :cols], bands - 1)
+    kernel_passed = swap(kernel[0], "segment")
+
+    (sums,) = call(sums_kernel, "input_sums", micros, [], [], [acts], [], [((2 * micros, channels), F32)])
+    diff = (recon.astype(F32) - target.astype(F32)).transpose(0, 2, 1, 3)
+    flat = diff.reshape(micros * rows * colors, channels)
+    got = swap(jnp.concatenate([sums, flat]), "sub")
+    sums = sums + got[: 2 * micros]
+    other = got[2 * micros :].reshape(diff.shape)
+
+    def border(first, r):
+        extra = latent[:, :, r].astype(F32).reshape(micros, 2, latents // 2, cols)
+        two = jnp.concatenate([diff[:, first : first + 2], other[:, first : first + 2], extra], axis=2)
+        return jnp.concatenate([sums, two.reshape(micros * 16, cols)])
+
+    from_up = shift(border(rows - 2, rows - 1), "rows", 1)
+    from_down = shift(border(0, 0), "rows", bands - 1)
+    across = shift(sums, "rows", 2)
+    sums = (sums + across) + (from_up[: 2 * micros] + from_down[: 2 * micros])
+    up = from_up[2 * micros :].reshape(micros, 2, 8, cols)
+    down = from_down[2 * micros :].reshape(micros, 2, 8, cols)
+    diff = jnp.concatenate([diff, other, jnp.zeros((micros, rows, 2, cols), F32)], axis=2)
+    beyond = [v[:, :, 6:8].reshape(micros, latents, cols).astype(BF16) for v in (up, down)]
+    wide = (rows + 2) * cols
+    latent = jnp.concatenate([beyond[0], latent.reshape(micros, latents, pixels), beyond[1]], axis=2)
+    latent = jnp.concatenate(
+        [latent, jnp.ones((micros, 1, wide), BF16), jnp.zeros((micros, 7 - latents, wide), BF16)], axis=1
+    )
+    mix = jnp.concatenate([mod_weight[0], jnp.concatenate([scale_bias, shift_bias], axis=1)]).astype(F32)
+    mix = jnp.pad(mix, ((0, 7 - latents), (0, 0)))
+    mix = jnp.concatenate([mix[:, :channels], mix[:, channels:]])
+
+    shape = (rows, cols, total_rows, total_cols, boxes.shape[1])
+    triple = 3 * channels
+    work = [
+        ((wide, triple), BF16),
+        ((3, channels, triple), BF16),
+        ((pixels, channels), F32),
+        ((pixels, channels), BF16),
+        ((pixels, 2 * channels), BF16),
+        ((3, channels, triple), F32),
+    ]
+    produced = [((micros, pixels, channels), BF16), ((micros, 16, channels), F32)]
+    kernel_shape = [(kernel.shape[1:], F32)]
+    norm_upper, reduced, kernel_grad = call(
+        functools.partial(upper_kernel, shape, micros, count),
+        "upper_block",
+        micros,
+        [place, boxes],
+        [sums, mix, out_weight, kernel[0]],
+        [up, diff, down, acts, latent],
+        produced,
+        kernel_shape,
+        work,
+    )
+    totals = pixel_total(reduced.reshape(micros * 16, channels))
+    lower = segment == 0
+    packed = jnp.concatenate([sums, totals, mix])
+    packed = jnp.where(lower, swap(packed, "segment"), packed)
+    result, edge = call(
+        functools.partial(redo_kernel, shape, micros, count),
+        "redo_upper",
+        micros,
+        [place, boxes],
+        [packed, out_weight, kernel_passed],
+        [up, diff, down, acts, norm_upper, passed, above, below, latent],
+        [((micros, wide, channels), BF16), ((micros, 16, channels), BF16)],
+        (),
+        [(((rows + 4) * cols, triple), BF16), ((3, channels, triple), BF16), ((wide, channels), F32)],
+    )
+    near = swap(edge, "sub")
+    norm, reduced, kernel_grad = call(
+        functools.partial(lower_kernel, shape, micros, count),
+        "lower_block",
+        micros,
+        [place],
+        [sums, mix, kernel[0]],
+        [result, near, acts, latent],
+        produced,
+        kernel_shape,
+        work,
+        [kernel_grad],
+    )
+
+    half = kernel.shape[1] // 2
+    give = lax.dynamic_slice_in_dim(kernel_grad, (1 - side) * half, half)
+    keep = lax.dynamic_slice_in_dim(kernel_grad, side * half, half)
+    keep = (keep + swap(give, "sub")).astype(BF16)
+    one, two, three = [shift(keep, "rows", steps).astype(F32) for steps in (1, 2, 3)]
+    keep = (keep.astype(F32) + two) + (one + three)
+    give = swap(keep, "sub")
+    kernel_grad = jnp.where(side == 0, jnp.concatenate([keep, give]), jnp.concatenate([give, keep]))
+
+    totals = jnp.where(lower, pixel_total(reduced.reshape(micros * 16, channels)), totals)
+    totals = totals.reshape(micros, 16, channels)
+    (grads,) = call(
+        functools.partial(last_kernel, rows, cols, micros, count),
+        "input_gradient",
+        micros,
+        [place],
+        [sums, mix],
+        [totals, acts, norm, result],
+        [((micros, pixels, channels), BF16)],
+    )
+    parameter = jnp.sum(totals, axis=0)
+    parameter = jnp.concatenate([parameter[:8], parameter[8:]], axis=1)
+    return (
+        grads.reshape(activations.shape),
+        kernel_grad[None],
+        parameter[None, :latents],
+        parameter[None, latents],
+    )
+
+
 def solution(mesh):
+    pair = mesh.shape["segment"] == 2 and mesh.shape["rows"] == 4 and mesh.shape["sub"] == 2
+    body = pair_body if pair else general_body
     placed = (
         P("segment", "groups", "rows", "sub", None),
         P("groups", None, "rows", "sub"),

time: 402 us -> 123 us (0.31)
  blocking collectives: 157 us -> 0 us
  starting transfers between devices: 101 us -> 39.8 us
  matrix products: 22.8 us -> 0 us
  Pallas kernels: 0 us -> 22.7 us
  other arithmetic: 25.6 us -> 8.25 us
  waiting for transfers between devices: 54.1 us -> 37.7 us
  between operations: 14.1 us -> 1 us
  local copies, waits for them, and re-layouts: 22.2 us -> 12.6 us
    psum x11 -> x0, blocking collectives: 157 us -> none  [the longest x5 73.8 us: section_backward(): sum_one, sum_two = lax.psum((sum_one, sum_two), ('rows', 'sub'))]
    ppermute x45 -> x23, starting transfers between devices: 101 us -> 39.8 us  [the longest x12 22.1 us: shift(): lax.ppermute(value, axis, [(i, (i + steps) % count) for i in range(count)])]
    psum x1 -> x0, waiting for transfers between devices: 41 us -> none  [body(): lax.psum((kernel_grad, mod_grad, bias_grad), ('rows', 'sub'))]
    ppermute x45 -> x23, waiting for transfers between devices: 13.1 us -> 37.7 us  [the longest x9 24.4 us: swap(): return lax.ppermute(value, axis, [(0, 1), (1, 0)])]
    dot_general x22 -> x0, matrix products: 22.8 us -> none  [the longest x5 13.9 us: section_backward(): jnp.dot(taps(padded_g, row_count, col_count, True), weights_t, preferred_...]
    pallas_call x0 -> x5, Pallas kernels: none -> 22.7 us  [call(): pl.pallas_call(kernel, grid=(micros,), in_specs=[pl.BlockSpec(memory_spac...]
    dynamic_update_slice x5 -> x0, other arithmetic: 10.7 us -> none  [tick(): lax.dynamic_update_slice_in_dim(grads_out, jnp.where(valid, result, curre...]
    reduce_sum x30 -> x1, other arithmetic: 8.56 us -> 0.01 us  [pair_body(): parameter = jnp.sum(totals, axis=0)]
  transfers between devices with their start and end apart: 46 -> 23, of which waited for: 16 -> 9; matrix products, arithmetic and copies ran while one was open for 8% -> 5% of each run, Pallas kernels for 0% -> 3%
where the time goes in v2:
time: 123 us; the launch traced here: 122 us
  starting transfers between devices  39.8 us (32%)
  waiting for transfers between devices  37.7 us (31%)
  Pallas kernels  22.7 us (18%)
  local copies, waits for them, and re-layouts  12.6 us (10%)
  other arithmetic  8.25 us (7%)
    ppermute x9, waiting for transfers between devices, swap(): return lax.ppermute(value, axis, [(0, 1), (1, 0)])  24.4 us
    pallas_call x5, Pallas kernels, call(): pl.pallas_call(kernel, grid=(micros,), in_specs=[pl.BlockSpec(memory_spac...  22.7 us
    ppermute x12, starting transfers between devices, shift(): lax.ppermute(value, axis, [(i, (i + steps) % count) for i in range(count)])  22.1 us
    ppermute x12, waiting for transfers between devices, shift(): lax.ppermute(value, axis, [(i, (i + steps) % count) for i in range(count)])  13.3 us
    ppermute x9, starting transfers between devices, swap(): return lax.ppermute(value, axis, [(0, 1), (1, 0)])  13 us
    unnamed x44, local copies, waits for them, and re-layouts  9.76 us
    ppermute x2, starting transfers between devices, swap_and_shift(): return lax.ppermute(value, ('rows', 'segment'), pairs)  4.72 us
  transfers between devices with their start and end apart: 23, of which 9 were waited for; matrix products, arithmetic and copies ran while one was open for 5% of the time, Pallas kernels for 3%

profile of v2, /device:TPU:0, one launch (start us, length us, event | category | flops | bytes accessed | tf_op | source)
XLA Modules:
  0.0 122.0 jit_solution(10992104205798576704)
XLA Ops:
  0.7 1.2 %copy-done = bf16[1,4,8,128,128]{4,3,2,1,0:T(8,128)(2,1)S(1)} copy-done((bf16[1,4,8,128,128]{4,3,2,1,0:T(8,128)(2,1)S(1)}, bf16[1,4,8,128,128]{4,3,2,1,0:T(8,128)(2,1)}, u32[]{:S(2)}) %copy-start) | copy-done | bytes 1048600
  1.9 0.6 input_sums.1
  2.6 0.7 convert_element_type.46
  3.3 0.8 fusion
  4.1 0.5 collective-permute-start
  4.7 0.0 copy-start.18
  4.8 0.1 pad_add_fusion.place_ref
  4.9 0.1 pad.23.clone
  4.9 0.1 pad.22.clone
  5.0 0.1 pad.26.clone
  5.1 0.4 collective-permute-done
  5.6 4.0 %collective-permute-start.1 = (f32[8,128]{1,0:T(8,128)S(1)}, f32[8,128]{1,0:T(8,128)S(1)}, u32[]{:S(2)}, u32[]{:S(2)}) collective-permute-start(f32[8,128]{1,0:T(8,128)S(1)} %slice_add_fusion.1), channel_id=1, source_target_pairs={{0,8},{4,12},{8,0},{12,4},{1,9},{5,13},{9,1},{13,5},{2,10},{6,14},... | collective-permute-start | bytes 12296 | tf_op jit(solution)/shard_map/ppermute | solution.py:266
  9.6 1.6 %collective-permute-start.2 = (f32[72,128]{1,0:T(8,128)S(1)}, f32[72,128]{1,0:T(8,128)S(1)}, u32[]{:S(2)}, u32[]{:S(2)}) collective-permute-start(f32[72,128]{1,0:T(8,128)S(1)} %get-tuple-element.32), channel_id=1, source_target_pairs={{0,4},{4,8},{8,12},{12,0},{1,5},{5,9},{9,13},{13,1},{2,6},{6,10},{... | collective-permute-start | bytes 110600 | tf_op jit(solution)/shard_map/ppermute | solution.py:266
  11.3 2.2 %collective-permute-start.3 = (f32[72,128]{1,0:T(8,128)S(1)}, f32[72,128]{1,0:T(8,128)S(1)}, u32[]{:S(2)}, u32[]{:S(2)}) collective-permute-start(f32[72,128]{1,0:T(8,128)S(1)} %get-tuple-element.33), channel_id=1, source_target_pairs={{0,12},{4,0},{8,4},{12,8},{1,13},{5,1},{9,5},{13,9},{2,14},{6,2},{... | collective-permute-start | bytes 110600 | tf_op jit(solution)/shard_map/ppermute | solution.py:266
  13.5 0.1 maximum_maximum_fusion.diff_ref
  13.6 2.0 %collective-permute-done.2 = f32[72,128]{1,0:T(8,128)S(1)} collective-permute-done((f32[72,128]{1,0:T(8,128)S(1)}, f32[72,128]{1,0:T(8,128)S(1)}, u32[]{:S(2)}, u32[]{:S(2)}) %collective-permute-start.2) | collective-permute-done | bytes 36896 | tf_op jit(solution)/shard_map/ppermute | solution.py:266
  15.6 0.1 collective-permute-done.3
  15.6 0.1 maximum_maximum_fusion.1.latent_ref
  15.8 0.9 upper_block.1
  16.7 0.0 copy-start.5
  16.7 1.0 copy-done.5
  17.6 9.6 %collective-permute-start.10 = (bf16[4,1024,128]{2,1,0:T(8,128)(2,1)S(1)}, bf16[4,1024,128]{2,1,0:T(8,128)(2,1)S(1)}, u32[]{:S(2)}, u32[]{:S(2)}) collective-permute-start(bf16[4,1024,128]{2,1,0:T(8,128)(2,1)S(1)} %bitcast.31), channel_id=1, source_target_pairs={{0,2},{2,0},{1,3},{3,1},{4,6},{6,4},{5,7},{7,5},{8,10},{10,8},{9,1... | collective-permute-start | bytes 3145736 | tf_op jit(solution)/shard_map/ppermute | solution.py:261
  27.3 0.9 collective-permute-start.5
  28.1 3.4 %collective-permute-start.6 = (f32[64,128]{1,0:T(8,128)S(1)}, f32[64,128]{1,0:T(8,128)S(1)}, u32[]{:S(2)}, u32[]{:S(2)}) collective-permute-start(f32[64,128]{1,0:T(8,128)S(1)} %bitcast_add_fusion.1), channel_id=1, source_target_pairs={{0,4},{4,8},{8,12},{12,0},{1,5},{5,9},{9,13},{13,1},{2,6},{6,10},{... | collective-permute-start | bytes 98312 | tf_op jit(solution)/shard_map/ppermute | solution.py:266
  31.6 0.4 collective-permute-start.7
  31.9 1.1 collective-permute-start.9
  33.1 1.0 collective-permute-done.6
  34.1 1.4 %collective-permute-done.7 = f32[64,128]{1,0:T(8,128)S(1)} collective-permute-done((f32[64,128]{1,0:T(8,128)S(1)}, f32[64,128]{1,0:T(8,128)S(1)}, u32[]{:S(2)}, u32[]{:S(2)}) %collective-permute-start.7) | collective-permute-done | bytes 32800 | tf_op jit(solution)/shard_map/ppermute | solution.py:266
  35.5 0.6 pad_maximum_fusion.3
  36.1 1.1 collective-permute-start.8
  37.2 0.7 fusion.10
  38.0 0.3 collective-permute-start.11
  38.3 4.4 %collective-permute-start.12 = (bf16[4,128,128]{2,1,0:T(8,128)(2,1)}, bf16[4,128,128]{2,1,0:T(8,128)(2,1)S(1)}, u32[]{:S(2)}, u32[]{:S(2)}) collective-permute-start(bf16[4,128,128]{2,1,0:T(8,128)(2,1)} %get-tuple-element.20), channel_id=1, source_target_pairs={{0,14},{2,12},{4,2},{6,0},{8,6},{10,4},{12,10},{14,8},{1,15},{3,13... | collective-permute-start | bytes 393224 | tf_op jit(solution)/shard_map/ppermute | solution.py:272
  42.7 21.4 %collective-permute-done.8 = f32[88,128]{1,0:T(8,128)} collective-permute-done((f32[88,128]{1,0:T(8,128)}, f32[88,128]{1,0:T(8,128)}, u32[]{:S(2)}, u32[]{:S(2)}) %collective-permute-start.8) | collective-permute-done | bytes 45088 | tf_op jit(solution)/shard_map/ppermute | solution.py:261
  64.1 0.8 broadcast_select_fusion.packed_ref
  64.9 0.6 copy-done.9
  65.6 0.7 copy-done.11
  66.2 1.0 copy-done.7
  67.2 1.2 %copy-done.6 = bf16[4,1024,128]{2,1,0:T(8,128)(2,1)S(1)} copy-done((bf16[4,1024,128]{2,1,0:T(8,128)(2,1)S(1)}, bf16[4,1024,128]{2,1,0:T(8,128)(2,1)}, u32[]{:S(2)}) %copy-start.6) | copy-done | bytes 1048600
  68.4 1.2 %copy-done.8 = bf16[4,1024,128]{2,1,0:T(8,128)(2,1)S(1)} copy-done((bf16[4,1024,128]{2,1,0:T(8,128)(2,1)S(1)}, bf16[4,1024,128]{2,1,0:T(8,128)(2,1)}, u32[]{:S(2)}) %copy-start.8) | copy-done | bytes 1048600
  69.7 0.9 copy-done.10
  70.6 0.9 copy-done.12
  71.5 9.3 %redo_upper.1 = (bf16[4,1280,128]{2,1,0:T(8,128)(2,1)S(1)}, bf16[4,16,128]{2,1,0:T(8,128)(2,1)}) custom-call(s32[3]{0:T(128)S(1)} %pad_add_fusion.place_ref, s32[4,4,4]{2,1,0:T(4,128)S(1)} %copy-done.13, f32[88,128]{1,0:T(8,128)S(1)} %broadcast_select_fusion.packed_ref, bf16[3,128]{1,0:T(4,128)(2,1)S(1)} %copy-done.14, ...), custom_call_target="tpu_custom_call" | custom-call | flops 1 | bytes 1 | tf_op jit(solution)/shard_map/redo_upper/pallas_call | solution.py:685
  80.8 1.4 %collective-permute-done.13.near_ref = bf16[4,16,128]{2,1,0:T(8,128)(2,1)S(1)} collective-permute-done((bf16[4,16,128]{2,1,0:T(8,128)(2,1)}, bf16[4,16,128]{2,1,0:T(8,128)(2,1)S(1)}, u32[]{:S(2)}, u32[]{:S(2)}) %collective-permute-start.13) | collective-permute-done | bytes 16416 | tf_op jit(solution)/shard_map/ppermute | solution.py:261
  82.2 8.6 %lower_block.1 = (bf16[4,1024,128]{2,1,0:T(8,128)(2,1)S(1)}, f32[4,16,128]{2,1,0:T(8,128)S(1)}, f32[1152,128]{1,0:T(8,128)}) custom-call(s32[3]{0:T(128)S(1)} %pad_add_fusion.place_ref, f32[8,128]{1,0:T(8,128)S(1)} %fusion.9.sums_ref, f32[16,128]{1,0:T(8,128)S(1)} %pad_maximum_fusion.6.mix_ref, bf16[1152,128]{1,0:T(8,128)(2,1)S(1)} %bitcast.38, ...), custom_call_target="tpu_custom_call" | custom-call | flops 1 | bytes 1 | tf_op jit(solution)/shard_map/lower_block/pallas_call | solution.py:685
  90.8 1.0 copy-done.3
  91.8 1.8 %constant_dynamic-slice_fusion = f32[576,128]{1,0:T(8,128)} fusion(f32[1152,128]{1,0:T(8,128)} %get-tuple-element.19, s32[]{:T(128)S(6)} %select_n.43), kind=kLoop, calls=%fused_computation.37 | loop fusion | bytes 589828 | tf_op jit(solution)/shard_map/dynamic_slice | solution.py:802
  93.6 0.2 collective-permute-start.18
  93.8 0.3 collective-permute-start.14
  94.1 1.1 collective-permute-done.14
  95.2 0.8 collective-permute-start.15
  96.0 3.4 %collective-permute-start.16 = (f32[64,128]{1,0:T(8,128)S(1)}, f32[64,128]{1,0:T(8,128)S(1)}, u32[]{:S(2)}, u32[]{:S(2)}) collective-permute-start(f32[64,128]{1,0:T(8,128)S(1)} %bitcast_add_fusion), channel_id=1, source_target_pairs={{0,4},{4,8},{8,12},{12,0},{1,5},{5,9},{9,13},{13,1},{2,6},{6,10},{... | collective-permute-start | bytes 98312 | tf_op jit(solution)/shard_map/ppermute | solution.py:266
  99.4 0.4 collective-permute-start.17
  99.8 1.7 %add_convert_fusion = bf16[576,128]{1,0:T(8,128)(2,1)} fusion(f32[576,128]{1,0:T(8,128)} %collective-permute-done.18, f32[1152,128]{1,0:T(8,128)} %get-tuple-element.19, s32[]{:T(128)S(6)} %select_n.42), kind=kLoop, calls=%fused_computation.2 | loop fusion | flops 147456 | bytes 737284 | tf_op jit(solution)/shard_map/convert_element_type | solution.py:804
  101.6 1.1 collective-permute-start.19
  102.7 0.6 collective-permute-start.20
  103.3 3.2 %collective-permute-start.21 = (bf16[576,128]{1,0:T(8,128)(2,1)}, bf16[576,128]{1,0:T(8,128)(2,1)}, u32[]{:S(2)}, u32[]{:S(2)}) collective-permute-start(bf16[576,128]{1,0:T(8,128)(2,1)} %add_convert_fusion), channel_id=1, source_target_pairs={{0,12},{4,0},{8,4},{12,8},{1,13},{5,1},{9,5},{13,9},{2,14},{6,2},{... | collective-permute-start | bytes 442376 | tf_op jit(solution)/shard_map/ppermute | solution.py:266
  106.5 8.9 %collective-permute-done.19 = bf16[576,128]{1,0:T(8,128)(2,1)} collective-permute-done((bf16[576,128]{1,0:T(8,128)(2,1)}, bf16[576,128]{1,0:T(8,128)(2,1)}, u32[]{:S(2)}, u32[]{:S(2)}) %collective-permute-start.19) | collective-permute-done | bytes 147488 | tf_op jit(solution)/shard_map/ppermute | solution.py:266
  115.4 1.2 add_add_fusion
  116.6 0.1 collective-permute-start.22
  116.7 3.3 %input_gradient.1 = bf16[4,1024,128]{2,1,0:T(8,128)(2,1)} custom-call(s32[3]{0:T(128)S(1)} %pad_add_fusion.place_ref, f32[8,128]{1,0:T(8,128)S(1)} %fusion.9.sums_ref, f32[16,128]{1,0:T(8,128)S(1)} %pad_maximum_fusion.6.mix_ref, f32[4,16,128]{2,1,0:T(8,128)S(1)} %bitcast.46, bf16[4,1024,128]{2,1,0:T(8,128)(2,1)S(1)} %bitcast.35, ...), custom_call_target="tpu_custom_call" | custom-call | flops 1 | bytes 1 | tf_op jit(solution)/shard_map/input_gradient/pallas_call | solution.py:685
  120.0 0.6 pad_maximum_fusion.7
  120.6 0.6 fusion.5
  121.2 0.9 maximum_select_fusion
  (75 shorter events, 0.3 us)
Async XLA Ops:
  0.6 4.0 %copy-start.21 = (bf16[1,128]{1,0:T(2,128)(2,1)S(1)}, bf16[1,128]{1,0:T(2,128)(2,1)}, u32[]{:S(2)}) copy-start(bf16[1,128]{1,0:T(2,128)(2,1)} %param.17) | copy-start | bytes 772
  0.6 4.0 %copy-start.20 = (bf16[1,128]{1,0:T(2,128)(2,1)S(1)}, bf16[1,128]{1,0:T(2,128)(2,1)}, u32[]{:S(2)}) copy-start(bf16[1,128]{1,0:T(2,128)(2,1)} %param.18) | copy-start | bytes 772
  0.7 1.2 %copy-start = (bf16[1,4,8,128,128]{4,3,2,1,0:T(8,128)(2,1)S(1)}, bf16[1,4,8,128,128]{4,3,2,1,0:T(8,128)(2,1)}, u32[]{:S(2)}) copy-start(bf16[1,4,8,128,128]{4,3,2,1,0:T(8,128)(2,1)} %param.10) | copy-start | bytes 3145732
  1.9 2.8 %copy-start.17 = (bf16[4,4,8,128]{3,2,1,0:T(8,128)(2,1)S(1)}, bf16[4,4,8,128]{3,2,1,0:T(8,128)(2,1)}, u32[]{:S(2)}) copy-start(bf16[4,4,8,128]{3,2,1,0:T(8,128)(2,1)} %param.11) | copy-start | bytes 98308
  1.9 2.8 %copy-start.19 = (bf16[1,4,256]{2,1,0:T(4,128)(2,1)S(1)}, bf16[1,4,256]{2,1,0:T(4,128)(2,1)}, u32[]{:S(2)}) copy-start(bf16[1,4,256]{2,1,0:T(4,128)(2,1)} %param.16) | copy-start | bytes 6148
  1.9 13.9 %copy-start.1 = (bf16[1,4,8,128,128]{4,3,2,1,0:T(8,128)(2,1)S(1)}, bf16[1,4,8,128,128]{4,3,2,1,0:T(8,128)(2,1)}, u32[]{:S(2)}) copy-start(bf16[1,4,8,128,128]{4,3,2,1,0:T(8,128)(2,1)} %param.10) | copy-start | bytes 3145732
  1.9 13.9 %copy-start.2 = (bf16[1,1152,128]{2,1,0:T(8,128)(2,1)S(1)}, bf16[1,1152,128]{2,1,0:T(8,128)(2,1)}, u32[]{:S(2)}) copy-start(bf16[1,1152,128]{2,1,0:T(8,128)(2,1)} %param.15) | copy-start | bytes 884740
  1.9 13.9 %copy-start.13 = (s32[4,4,4]{2,1,0:T(4,128)S(1)}, s32[4,4,4]{2,1,0:T(4,128)}, u32[]{:S(2)}) copy-start(s32[4,4,4]{2,1,0:T(4,128)} %boxes_ref.3) | copy-start | bytes 772
  1.9 13.9 %copy-start.14 = (bf16[3,128]{1,0:T(4,128)(2,1)S(1)}, bf16[3,128]{1,0:T(4,128)(2,1)}, u32[]{:S(2)}) copy-start(bf16[3,128]{1,0:T(4,128)(2,1)} %weight_ref.3) | copy-start | bytes 2308
  4.1 1.4 %collective-permute-start = (f32[104,128]{1,0:T(8,128)S(1)}, f32[104,128]{1,0:T(8,128)S(1)}, u32[]{:S(2)}, u32[]{:S(2)}) collective-permute-start(f32[104,128]{1,0:T(8,128)S(1)} %pad_maximum_fusion), channel_id=1, source_target_pairs={{0,1},{1,0},{2,3},{3,2},{4,5},{5,4},{6,7},{7,6},{8,9},{9,8},{10,11... | collective-permute-start | bytes 159752 | tf_op jit(solution)/shard_map/ppermute | solution.py:261
  4.7 33.2 %copy-start.18 = (f32[8,128]{1,0:T(8,128)}, f32[8,128]{1,0:T(8,128)S(1)}, u32[]{:S(2)}) copy-start(f32[8,128]{1,0:T(8,128)S(1)} %get-tuple-element.31) | copy-start | bytes 12292
  5.6 10.1 %collective-permute-start.1 = (f32[8,128]{1,0:T(8,128)S(1)}, f32[8,128]{1,0:T(8,128)S(1)}, u32[]{:S(2)}, u32[]{:S(2)}) collective-permute-start(f32[8,128]{1,0:T(8,128)S(1)} %slice_add_fusion.1), channel_id=1, source_target_pairs={{0,8},{4,12},{8,0},{12,4},{1,9},{5,13},{9,1},{13,5},{2,10},{6,14},... | collective-permute-start | bytes 12296 | tf_op jit(solution)/shard_map/ppermute | solution.py:266
  9.6 5.9 %collective-permute-start.2 = (f32[72,128]{1,0:T(8,128)S(1)}, f32[72,128]{1,0:T(8,128)S(1)}, u32[]{:S(2)}, u32[]{:S(2)}) collective-permute-start(f32[72,128]{1,0:T(8,128)S(1)} %get-tuple-element.32), channel_id=1, source_target_pairs={{0,4},{4,8},{8,12},{12,0},{1,5},{5,9},{9,13},{13,1},{2,6},{6,10},{... | collective-permute-start | bytes 110600 | tf_op jit(solution)/shard_map/ppermute | solution.py:266
  11.3 4.4 %collective-permute-start.3 = (f32[72,128]{1,0:T(8,128)S(1)}, f32[72,128]{1,0:T(8,128)S(1)}, u32[]{:S(2)}, u32[]{:S(2)}) collective-permute-start(f32[72,128]{1,0:T(8,128)S(1)} %get-tuple-element.33), channel_id=1, source_target_pairs={{0,12},{4,0},{8,4},{12,8},{1,13},{5,1},{9,5},{13,9},{2,14},{6,2},{... | collective-permute-start | bytes 110600 | tf_op jit(solution)/shard_map/ppermute | solution.py:266
  16.7 1.0 copy-start.5
  17.6 9.6 %collective-permute-start.4 = (f32[64,128]{1,0:T(8,128)S(1)}, f32[64,128]{1,0:T(8,128)S(1)}, u32[]{:S(2)}, u32[]{:S(2)}) collective-permute-start(f32[64,128]{1,0:T(8,128)S(1)} %bitcast.48), channel_id=1, source_target_pairs={{0,1},{1,0},{2,3},{3,2},{4,5},{5,4},{6,7},{7,6},{8,9},{9,8},{10,11... | collective-permute-start | bytes 98312 | tf_op jit(solution)/shard_map/ppermute | solution.py:261
  17.6 48.6 %collective-permute-start.10 = (bf16[4,1024,128]{2,1,0:T(8,128)(2,1)S(1)}, bf16[4,1024,128]{2,1,0:T(8,128)(2,1)S(1)}, u32[]{:S(2)}, u32[]{:S(2)}) collective-permute-start(bf16[4,1024,128]{2,1,0:T(8,128)(2,1)S(1)} %bitcast.31), channel_id=1, source_target_pairs={{0,2},{2,0},{1,3},{3,1},{4,6},{6,4},{5,7},{7,5},{8,10},{10,8},{9,1... | collective-permute-start | bytes 3145736 | tf_op jit(solution)/shard_map/ppermute | solution.py:261
  27.3 5.8 %collective-permute-start.5 = (f32[64,128]{1,0:T(8,128)S(1)}, f32[64,128]{1,0:T(8,128)S(1)}, u32[]{:S(2)}, u32[]{:S(2)}) collective-permute-start(f32[64,128]{1,0:T(8,128)S(1)} %bitcast_add_fusion.1), channel_id=1, source_target_pairs={{0,8},{4,12},{8,0},{12,4},{1,9},{5,13},{9,1},{13,5},{2,10},{6,14},... | collective-permute-start | bytes 98312 | tf_op jit(solution)/shard_map/ppermute | solution.py:266
  28.1 5.9 %collective-permute-start.6 = (f32[64,128]{1,0:T(8,128)S(1)}, f32[64,128]{1,0:T(8,128)S(1)}, u32[]{:S(2)}, u32[]{:S(2)}) collective-permute-start(f32[64,128]{1,0:T(8,128)S(1)} %bitcast_add_fusion.1), channel_id=1, source_target_pairs={{0,4},{4,8},{8,12},{12,0},{1,5},{5,9},{9,13},{13,1},{2,6},{6,10},{... | collective-permute-start | bytes 98312 | tf_op jit(solution)/shard_map/ppermute | solution.py:266
  31.6 3.9 %collective-permute-start.7 = (f32[64,128]{1,0:T(8,128)S(1)}, f32[64,128]{1,0:T(8,128)S(1)}, u32[]{:S(2)}, u32[]{:S(2)}) collective-permute-start(f32[64,128]{1,0:T(8,128)S(1)} %bitcast_add_fusion.1), channel_id=1, source_target_pairs={{0,12},{4,0},{8,4},{12,8},{1,13},{5,1},{9,5},{13,9},{2,14},{6,2},{... | collective-permute-start | bytes 98312 | tf_op jit(solution)/shard_map/ppermute | solution.py:266
  31.9 34.3 %collective-permute-start.9 = (bf16[1152,128]{1,0:T(8,128)(2,1)S(1)}, bf16[1152,128]{1,0:T(8,128)(2,1)}, u32[]{:S(2)}, u32[]{:S(2)}) collective-permute-start(bf16[1152,128]{1,0:T(8,128)(2,1)S(1)} %bitcast.37), channel_id=1, source_target_pairs={{0,2},{2,0},{1,3},{3,1},{4,6},{6,4},{5,7},{7,5},{8,10},{10,8},{9,1... | collective-permute-start | bytes 884744 | tf_op jit(solution)/shard_map/ppermute | solution.py:261
  35.5 2.5 %copy-start.15 = (f32[64,128]{1,0:T(8,128)}, f32[64,128]{1,0:T(8,128)S(1)}, u32[]{:S(2)}) copy-start(f32[64,128]{1,0:T(8,128)S(1)} %add_add_fusion.1) | copy-start | bytes 98308
  36.1 28.0 %collective-permute-start.8 = (f32[88,128]{1,0:T(8,128)}, f32[88,128]{1,0:T(8,128)}, u32[]{:S(2)}, u32[]{:S(2)}) collective-permute-start(f32[88,128]{1,0:T(8,128)} %pad_maximum_fusion.3), channel_id=1, source_target_pairs={{0,2},{2,0},{1,3},{3,1},{4,6},{6,4},{5,7},{7,5},{8,10},{10,8},{9,1... | collective-permute-start | bytes 135176 | tf_op jit(solution)/shard_map/ppermute | solution.py:261
  38.0 26.9 %collective-permute-start.11 = (bf16[4,128,128]{2,1,0:T(8,128)(2,1)}, bf16[4,128,128]{2,1,0:T(8,128)(2,1)S(1)}, u32[]{:S(2)}, u32[]{:S(2)}) collective-permute-start(bf16[4,128,128]{2,1,0:T(8,128)(2,1)} %get-tuple-element.21), channel_id=1, source_target_pairs={{0,6},{2,4},{4,10},{6,8},{8,14},{10,12},{12,2},{14,0},{1,7},{3,5},... | collective-permute-start | bytes 393224 | tf_op jit(solution)/shard_map/ppermute | solution.py:272
  38.3 27.3 %collective-permute-start.12 = (bf16[4,128,128]{2,1,0:T(8,128)(2,1)}, bf16[4,128,128]{2,1,0:T(8,128)(2,1)S(1)}, u32[]{:S(2)}, u32[]{:S(2)}) collective-permute-start(bf16[4,128,128]{2,1,0:T(8,128)(2,1)} %get-tuple-element.20), channel_id=1, source_target_pairs={{0,14},{2,12},{4,2},{6,0},{8,6},{10,4},{12,10},{14,8},{1,15},{3,13... | collective-permute-start | bytes 393224 | tf_op jit(solution)/shard_map/ppermute | solution.py:272
  64.9 0.6 copy-start.9
  65.6 0.7 copy-start.11
  66.2 1.0 copy-start.7
  67.2 1.2 %copy-start.6 = (bf16[4,1024,128]{2,1,0:T(8,128)(2,1)S(1)}, bf16[4,1024,128]{2,1,0:T(8,128)(2,1)}, u32[]{:S(2)}) copy-start(bf16[4,1024,128]{2,1,0:T(8,128)(2,1)} %copy-done.5) | copy-start | bytes 3145732
  68.4 1.2 %copy-start.8 = (bf16[4,1024,128]{2,1,0:T(8,128)(2,1)S(1)}, bf16[4,1024,128]{2,1,0:T(8,128)(2,1)}, u32[]{:S(2)}) copy-start(bf16[4,1024,128]{2,1,0:T(8,128)(2,1)} %copy-done.7) | copy-start | bytes 3145732
  69.7 0.9 copy-start.10
  70.6 0.9 copy-start.12
  80.8 1.4 %collective-permute-start.13 = (bf16[4,16,128]{2,1,0:T(8,128)(2,1)}, bf16[4,16,128]{2,1,0:T(8,128)(2,1)S(1)}, u32[]{:S(2)}, u32[]{:S(2)}) collective-permute-start(bf16[4,16,128]{2,1,0:T(8,128)(2,1)} %get-tuple-element.15), channel_id=1, source_target_pairs={{0,1},{1,0},{2,3},{3,2},{4,5},{5,4},{6,7},{7,6},{8,9},{9,8},{10,11... | collective-permute-start | bytes 49160 | tf_op jit(solution)/shard_map/ppermute | solution.py:261
  90.8 1.0 copy-start.3
  91.8 14.7 %copy-start.16 = (f32[64,128]{1,0:T(8,128)S(1)}, f32[64,128]{1,0:T(8,128)}, u32[]{:S(2)}) copy-start(f32[64,128]{1,0:T(8,128)} %copy-done.15) | copy-start | bytes 98308
  91.8 24.9 %copy-start.4 = (bf16[4,1024,128]{2,1,0:T(8,128)(2,1)S(1)}, bf16[4,1024,128]{2,1,0:T(8,128)(2,1)}, u32[]{:S(2)}) copy-start(bf16[4,1024,128]{2,1,0:T(8,128)(2,1)} %copy-done.3) | copy-start | bytes 3145732
  93.6 6.3 %collective-permute-start.18 = (f32[576,128]{1,0:T(8,128)}, f32[576,128]{1,0:T(8,128)}, u32[]{:S(2)}, u32[]{:S(2)}) collective-permute-start(f32[576,128]{1,0:T(8,128)} %constant_dynamic-slice_fusion), channel_id=1, source_target_pairs={{0,1},{1,0},{2,3},{3,2},{4,5},{5,4},{6,7},{7,6},{8,9},{9,8},{10,11... | collective-permute-start | bytes 884744 | tf_op jit(solution)/shard_map/ppermute | solution.py:261
  93.8 1.5 %collective-permute-start.14 = (f32[64,128]{1,0:T(8,128)S(1)}, f32[64,128]{1,0:T(8,128)S(1)}, u32[]{:S(2)}, u32[]{:S(2)}) collective-permute-start(f32[64,128]{1,0:T(8,128)S(1)} %bitcast.47), channel_id=1, source_target_pairs={{0,1},{1,0},{2,3},{3,2},{4,5},{5,4},{6,7},{7,6},{8,9},{9,8},{10,11... | collective-permute-start | bytes 98312 | tf_op jit(solution)/shard_map/ppermute | solution.py:261
  95.2 8.1 %collective-permute-start.15 = (f32[64,128]{1,0:T(8,128)S(1)}, f32[64,128]{1,0:T(8,128)S(1)}, u32[]{:S(2)}, u32[]{:S(2)}) collective-permute-start(f32[64,128]{1,0:T(8,128)S(1)} %bitcast_add_fusion), channel_id=1, source_target_pairs={{0,8},{4,12},{8,0},{12,4},{1,9},{5,13},{9,1},{13,5},{2,10},{6,14},... | collective-permute-start | bytes 98312 | tf_op jit(solution)/shard_map/ppermute | solution.py:266
  96.0 10.5 %collective-permute-start.16 = (f32[64,128]{1,0:T(8,128)S(1)}, f32[64,128]{1,0:T(8,128)S(1)}, u32[]{:S(2)}, u32[]{:S(2)}) collective-permute-start(f32[64,128]{1,0:T(8,128)S(1)} %bitcast_add_fusion), channel_id=1, source_target_pairs={{0,4},{4,8},{8,12},{12,0},{1,5},{5,9},{9,13},{13,1},{2,6},{6,10},{... | collective-permute-start | bytes 98312 | tf_op jit(solution)/shard_map/ppermute | solution.py:266
  99.4 7.0 %collective-permute-start.17 = (f32[64,128]{1,0:T(8,128)S(1)}, f32[64,128]{1,0:T(8,128)S(1)}, u32[]{:S(2)}, u32[]{:S(2)}) collective-permute-start(f32[64,128]{1,0:T(8,128)S(1)} %bitcast_add_fusion), channel_id=1, source_target_pairs={{0,12},{4,0},{8,4},{12,8},{1,13},{5,1},{9,5},{13,9},{2,14},{6,2},{... | collective-permute-start | bytes 98312 | tf_op jit(solution)/shard_map/ppermute | solution.py:266
  101.6 13.8 %collective-permute-start.19 = (bf16[576,128]{1,0:T(8,128)(2,1)}, bf16[576,128]{1,0:T(8,128)(2,1)}, u32[]{:S(2)}, u32[]{:S(2)}) collective-permute-start(bf16[576,128]{1,0:T(8,128)(2,1)} %add_convert_fusion), channel_id=1, source_target_pairs={{0,8},{4,12},{8,0},{12,4},{1,9},{5,13},{9,1},{13,5},{2,10},{6,14},... | collective-permute-start | bytes 442376 | tf_op jit(solution)/shard_map/ppermute | solution.py:266
  102.7 12.8 %collective-permute-start.20 = (bf16[576,128]{1,0:T(8,128)(2,1)}, bf16[576,128]{1,0:T(8,128)(2,1)}, u32[]{:S(2)}, u32[]{:S(2)}) collective-permute-start(bf16[576,128]{1,0:T(8,128)(2,1)} %add_convert_fusion), channel_id=1, source_target_pairs={{0,4},{4,8},{8,12},{12,0},{1,5},{5,9},{9,13},{13,1},{2,6},{6,10},{... | collective-permute-start | bytes 442376 | tf_op jit(solution)/shard_map/ppermute | solution.py:266
  103.3 12.2 %collective-permute-start.21 = (bf16[576,128]{1,0:T(8,128)(2,1)}, bf16[576,128]{1,0:T(8,128)(2,1)}, u32[]{:S(2)}, u32[]{:S(2)}) collective-permute-start(bf16[576,128]{1,0:T(8,128)(2,1)} %add_convert_fusion), channel_id=1, source_target_pairs={{0,12},{4,0},{8,4},{12,8},{1,13},{5,1},{9,5},{13,9},{2,14},{6,2},{... | collective-permute-start | bytes 442376 | tf_op jit(solution)/shard_map/ppermute | solution.py:266
  116.6 4.5 %collective-permute-start.22 = (f32[576,128]{1,0:T(8,128)S(1)}, f32[576,128]{1,0:T(8,128)S(1)}, u32[]{:S(2)}, u32[]{:S(2)}) collective-permute-start(f32[576,128]{1,0:T(8,128)S(1)} %add_add_fusion), channel_id=1, source_target_pairs={{0,1},{1,0},{2,3},{3,2},{4,5},{5,4},{6,7},{7,6},{8,9},{9,8},{10,11... | collective-permute-start | bytes 884744 | tf_op jit(solution)/shard_map/ppermute | solution.py:261

commit v3 on v2

--- a/solution.py
+++ b/solution.py
@@ -431,12 +431,19 @@
         )
 
 
-def write_kernel_grad(total_kernel, kernel_grad_ref):
-    channels = kernel_grad_ref.shape[-1]
-    for row in range(3):
-        for col in range(3):
-            tap = tap_of(row, col)
-            kernel_grad_ref[tap * channels : (tap + 1) * channels, :] = total_kernel[row, :, col * channels : (col + 1) * channels]
+def write_kernel_grad(total_kernel, side, keep_ref, give_ref):
+    half, channels = keep_ref.shape
+    for which in range(2):
+        for ref, owner in ((keep_ref, which), (give_ref, 1 - which)):
+
+            @pl.when(side == owner)
+            def _(ref=ref, first=which * half):
+                for row in range(3):
+                    for col in range(3):
+                        at = tap_of(row, col) * channels - first
+                        low, high = max(at, 0), min(at + channels, half)
+                        if low < high:
+                            ref[low:high, :] = total_kernel[row, low - at : high - at, col * channels : (col + 1) * channels]
 
 
 def upper_kernel(
@@ -456,7 +463,8 @@
     latent_ref,
     norm_ref,
     reduced_ref,
-    kernel_grad_ref,
+    keep_ref,
+    give_ref,
     shifted,
     weights,
     hidden_grad,
@@ -499,7 +507,7 @@
 
         @pl.when(step == micros - 1)
         def _():
-            write_kernel_grad(total_kernel, kernel_grad_ref)
+            write_kernel_grad(total_kernel, place_ref[1], keep_ref, give_ref)
 
     @pl.when(jnp.logical_not(active))
     def _():
@@ -520,7 +528,8 @@
     down_ref,
     acts_ref,
     norm_ref,
-    passed_ref,
+    passed_early_ref,
+    passed_late_ref,
     above_ref,
     below_ref,
     latent_ref,
@@ -568,7 +577,8 @@
             elif r == rows + 1:
                 acts = below_ref[0]
             else:
-                acts = passed_ref[0, (r - 1) * cols : r * cols, :]
+                row = slice((r - 1) * cols, r * cols)
+                acts = jnp.where(step < micros // 2, passed_early_ref[0, row, :], passed_late_ref[0, row, :])
             xhat, scale, _, slope = pixel_values(acts, latent_ref[0, :, at], wide_mix, mean, rstd)
             change = rstd * (hidden_grad[at, :] * slope * scale - mean_grad - xhat * mean_cross)
             middle = shifted[(r + 1) * cols : (r + 2) * cols, channels : 2 * channels]
@@ -594,10 +604,12 @@
     near_ref,
     acts_ref,
     latent_ref,
-    before_ref,
+    before_keep_ref,
+    before_give_ref,
     norm_ref,
     reduced_ref,
-    kernel_grad_ref,
+    keep_ref,
+    give_ref,
     shifted,
     weights,
     hidden_grad,
@@ -640,7 +652,7 @@
 
         @pl.when(step == micros - 1)
         def _():
-            write_kernel_grad(total_kernel, kernel_grad_ref)
+            write_kernel_grad(total_kernel, place_ref[1], keep_ref, give_ref)
 
     @pl.when(jnp.logical_not(active))
     def _():
@@ -648,7 +660,8 @@
 
         @pl.when(step == micros - 1)
         def _():
-            kernel_grad_ref[...] = before_ref[...]
+            keep_ref[...] = before_keep_ref[...]
+            give_ref[...] = before_give_ref[...]
 
 
 def last_kernel(rows, cols, micros, count, place_ref, sums_ref, mix_ref, total_ref, acts_ref, norm_ref, grad_ref, result_ref):
@@ -672,6 +685,9 @@
 
 
 def by_micro(value):
+    if isinstance(value, tuple):
+        value, first, size = value
+        return pl.BlockSpec((1,) + tuple(value.shape[1:]), lambda m: (jnp.clip(m - first, 0, size - 1), 0, 0))
     rest = (0,) * (len(value.shape) - 1)
     return pl.BlockSpec((1,) + tuple(value.shape[1:]), lambda m: (m,) + rest)
 
@@ -680,7 +696,7 @@
     return pl.BlockSpec(tuple(value.shape), lambda m: (0,) * len(value.shape))
 
 
-def call(kernel, name, micros, scalars, fixed, per_micro, outs, fixed_outs=(), scratch=(), tail=()):
+def call(kernel, name, micros, scalars, fixed, per_micro, outs, fixed_outs=(), scratch=(), tail=(), work=4, room=62):
     out_shape = [jax.ShapeDtypeStruct(s, d) for s, d in outs] + [jax.ShapeDtypeStruct(s, d) for s, d in fixed_outs]
     return pl.pallas_call(
         kernel,
@@ -692,10 +708,10 @@
         out_specs=[by_micro(s) for s in out_shape[: len(outs)]] + [whole(s) for s in out_shape[len(outs) :]],
         out_shape=out_shape,
         scratch_shapes=[pltpu.VMEM(s, d) for s, d in scratch],
-        compiler_params=pltpu.CompilerParams(vmem_limit_bytes=20 * 1024 * 1024),
-        cost_estimate=pl.CostEstimate(flops=1, bytes_accessed=1, transcendentals=0),
+        compiler_params=pltpu.CompilerParams(vmem_limit_bytes=room * 1024 * 1024),
+        cost_estimate=pl.CostEstimate(flops=work, bytes_accessed=work // 4, transcendentals=0),
         name=name,
-    )(*scalars, *fixed, *per_micro, *tail)
+    )(*scalars, *fixed, *[v[0] if isinstance(v, tuple) else v for v in per_micro], *tail)
 
 
 def pair_body(
@@ -712,12 +728,13 @@
     place = jnp.stack([segment, side, lax.axis_index("rows") * rows]).astype(jnp.int32)
     acts = activations[0].reshape(micros, pixels, channels)
 
-    passed = swap(acts, "segment")
+    early = micros // 2
+    passed = [swap(acts[:early], "segment"), swap(acts[early:], "segment")]
     above = swap_and_shift(acts[:, pixels - cols :], 1)
     below = swap_and_shift(acts[:, :cols], bands - 1)
     kernel_passed = swap(kernel[0], "segment")
 
-    (sums,) = call(sums_kernel, "input_sums", micros, [], [], [acts], [], [((2 * micros, channels), F32)])
+    (sums,) = call(sums_kernel, "input_sums", micros, [], [], [acts], [], [((2 * micros, channels), F32)], room=16)
     diff = (recon.astype(F32) - target.astype(F32)).transpose(0, 2, 1, 3)
     flat = diff.reshape(micros * rows * colors, channels)
     got = swap(jnp.concatenate([sums, flat]), "sub")
@@ -757,8 +774,9 @@
         ((3, channels, triple), F32),
     ]
     produced = [((micros, pixels, channels), BF16), ((micros, 16, channels), F32)]
-    kernel_shape = [(kernel.shape[1:], F32)]
-    norm_upper, reduced, kernel_grad = call(
+    kernel_shape = [((kernel.shape[1] // 2, channels), F32)] * 2
+    up, above, below, kernel_passed = lax.optimization_barrier((up, above, below, kernel_passed))
+    norm_upper, reduced, *kernel_grad = call(
         functools.partial(upper_kernel, shape, micros, count),
         "upper_block",
         micros,
@@ -769,9 +787,11 @@
         kernel_shape,
         work,
     )
+    reduced, passed[0] = lax.optimization_barrier((reduced, passed[0]))
     totals = pixel_total(reduced.reshape(micros * 16, channels))
     lower = segment == 0
     packed = jnp.concatenate([sums, totals, mix])
+    packed, passed[1] = lax.optimization_barrier((packed, passed[1]))
     packed = jnp.where(lower, swap(packed, "segment"), packed)
     result, edge = call(
         functools.partial(redo_kernel, shape, micros, count),
@@ -779,13 +799,13 @@
         micros,
         [place, boxes],
         [packed, out_weight, kernel_passed],
-        [up, diff, down, acts, norm_upper, passed, above, below, latent],
+        [up, diff, down, acts, norm_upper, (passed[0], 0, early), (passed[1], early, micros - early), above, below, latent],
         [((micros, wide, channels), BF16), ((micros, 16, channels), BF16)],
         (),
         [(((rows + 4) * cols, triple), BF16), ((3, channels, triple), BF16), ((wide, channels), F32)],
     )
     near = swap(edge, "sub")
-    norm, reduced, kernel_grad = call(
+    norm, reduced, keep, give = call(
         functools.partial(lower_kernel, shape, micros, count),
         "lower_block",
         micros,
@@ -795,18 +815,11 @@
         produced,
         kernel_shape,
         work,
-        [kernel_grad],
-    )
-
-    half = kernel.shape[1] // 2
-    give = lax.dynamic_slice_in_dim(kernel_grad, (1 - side) * half, half)
-    keep = lax.dynamic_slice_in_dim(kernel_grad, side * half, half)
+        kernel_grad,
+    )
+
     keep = (keep + swap(give, "sub")).astype(BF16)
-    one, two, three = [shift(keep, "rows", steps).astype(F32) for steps in (1, 2, 3)]
-    keep = (keep.astype(F32) + two) + (one + three)
-    give = swap(keep, "sub")
-    kernel_grad = jnp.where(side == 0, jnp.concatenate([keep, give]), jnp.concatenate([give, keep]))
-
+    others = [shift(keep, "rows", steps) for steps in (1, 2, 3)]
     totals = jnp.where(lower, pixel_total(reduced.reshape(micros * 16, channels)), totals)
     totals = totals.reshape(micros, 16, channels)
     (grads,) = call(
@@ -817,7 +830,14 @@
         [sums, mix],
         [totals, acts, norm, result],
         [((micros, pixels, channels), BF16)],
-    )
+        work=1 << 25,
+    )
+    grads, *others = lax.optimization_barrier((grads, *others))
+    one, two, three = [value.astype(F32) for value in others]
+    keep = (keep.astype(F32) + two) + (one + three)
+    give = swap(keep, "sub")
+    kernel_grad = jnp.where(side == 0, jnp.concatenate([keep, give]), jnp.concatenate([give, keep]))
+
     parameter = jnp.sum(totals, axis=0)
     parameter = jnp.concatenate([parameter[:8], parameter[8:]], axis=1)
     return (

time: 123 us -> 105 us (0.85)
  waiting for transfers between devices: 37.7 us -> 28 us
  local copies, waits for them, and re-layouts: 12.6 us -> 3.73 us
  starting transfers between devices: 39.8 us -> 32.4 us
  Pallas kernels: 22.7 us -> 29.3 us
  other arithmetic: 8.25 us -> 10.2 us
    ppermute x9 -> x10, waiting for transfers between devices: 24.4 us -> 12.6 us  [swap(): return lax.ppermute(value, axis, [(0, 1), (1, 0)])]
    unnamed x44 -> x28, local copies, waits for them, and re-layouts: 9.76 us -> 2.46 us
    pallas_call x5, Pallas kernels: 22.7 us -> 29.3 us  [call(): pl.pallas_call(kernel, grid=(micros,), in_specs=[pl.BlockSpec(memory_spac...]
    ppermute x12, starting transfers between devices: 22.1 us -> 17.8 us  [shift(): lax.ppermute(value, axis, [(i, (i + steps) % count) for i in range(count)])]
    ppermute x9 -> x10, starting transfers between devices: 13 us -> 9.04 us  [swap(): return lax.ppermute(value, axis, [(0, 1), (1, 0)])]
    ppermute x12, waiting for transfers between devices: 13.3 us -> 15.4 us  [shift(): lax.ppermute(value, axis, [(i, (i + steps) % count) for i in range(count)])]
    dynamic_slice x1 -> x0, local copies, waits for them, and re-layouts: 1.79 us -> none  [pair_body(): give = lax.dynamic_slice_in_dim(kernel_grad, (1 - side) * half, half)]
    add x2, other arithmetic: 0.01 us -> 1.53 us  [pixel_total(): value = value + swap(value, 'sub')]
  transfers between devices with their start and end apart: 23 -> 24, of which waited for: 9 -> 11; matrix products, arithmetic and copies ran while one was open for 5% -> 8% of each run, Pallas kernels for 3% -> 8%
where the time goes in v3:
time: 105 us
  starting transfers between devices  32.4 us (31%)
  Pallas kernels  29.3 us (28%)
  waiting for transfers between devices  28 us (27%)
  other arithmetic  10.2 us (10%)
  local copies, waits for them, and re-layouts  3.73 us (4%)
    pallas_call x5, Pallas kernels, call(): pl.pallas_call(kernel, grid=(micros,), in_specs=[pl.BlockSpec(memory_spac...  29.3 us
    ppermute x12, starting transfers between devices, shift(): lax.ppermute(value, axis, [(i, (i + steps) % count) for i in range(count)])  17.8 us
    ppermute x12, waiting for transfers between devices, shift(): lax.ppermute(value, axis, [(i, (i + steps) % count) for i in range(count)])  15.4 us
    ppermute x10, waiting for transfers between devices, swap(): return lax.ppermute(value, axis, [(0, 1), (1, 0)])  12.6 us
    ppermute x10, starting transfers between devices, swap(): return lax.ppermute(value, axis, [(0, 1), (1, 0)])  9.04 us
    ppermute x2, starting transfers between devices, swap_and_shift(): return lax.ppermute(value, ('rows', 'segment'), pairs)  5.6 us
    unnamed x28, local copies, waits for them, and re-layouts  2.46 us
  transfers between devices with their start and end apart: 24, of which 11 were waited for; matrix products, arithmetic and copies ran while one was open for 8% of the time, Pallas kernels for 8%

profile of v3, /device:TPU:0, one launch (start us, length us, event | category | flops | bytes accessed | tf_op | source)
XLA Modules:
  0.0 104.6 jit_solution(1768517971630122068)
XLA Ops:
  0.6 0.0 copy-start
  0.6 1.2 %copy-done = bf16[1,4,8,128,128]{4,3,2,1,0:T(8,128)(2,1)S(1)} copy-done((bf16[1,4,8,128,128]{4,3,2,1,0:T(8,128)(2,1)S(1)}, bf16[1,4,8,128,128]{4,3,2,1,0:T(8,128)(2,1)}, u32[]{:S(2)}) %copy-start) | copy-done | bytes 1048600
  1.9 0.6 input_sums.1
  2.5 0.7 convert_element_type.46
  3.2 0.8 fusion
  4.0 0.0 copy-start.11
  4.1 0.0 copy-start.12
  4.1 0.0 copy-start.13
  4.1 0.0 copy-start.9
  4.1 0.5 collective-permute-start
  4.6 5.6 %collective-permute-start.5 = (bf16[4,128,128]{2,1,0:T(8,128)(2,1)S(1)}, bf16[4,128,128]{2,1,0:T(8,128)(2,1)}, u32[]{:S(2)}, u32[]{:S(2)}) collective-permute-start(bf16[4,128,128]{2,1,0:T(8,128)(2,1)S(1)} %get-tuple-element.50), channel_id=1, source_target_pairs={{0,14},{2,12},{4,2},{6,0},{8,6},{10,4},{12,10},{14,8},{1,15},{3,13... | collective-permute-start | bytes 393224 | tf_op jit(solution)/shard_map/ppermute | solution.py:272
  10.2 0.5 collective-permute-start.6
  10.8 0.9 fusion.10
  11.8 0.6 pad_maximum_fusion.6.mix_ref
  12.4 0.7 pad_add_fusion.place_ref
  13.0 0.1 pad.23.clone
  13.1 0.1 pad.22.clone
  13.2 0.1 pad.26.clone
  13.3 0.0 collective-permute-done
  13.4 1.0 collective-permute-start.2
  14.4 3.9 %collective-permute-start.3 = (f32[72,128]{1,0:T(8,128)S(1)}, f32[72,128]{1,0:T(8,128)S(1)}, u32[]{:S(2)}, u32[]{:S(2)}) collective-permute-start(f32[72,128]{1,0:T(8,128)S(1)} %get-tuple-element.63), channel_id=1, source_target_pairs={{0,12},{4,0},{8,4},{12,8},{1,13},{5,1},{9,5},{13,9},{2,14},{6,2},{... | collective-permute-start | bytes 110600 | tf_op jit(solution)/shard_map/ppermute | solution.py:266
  18.3 0.7 maximum_maximum_fusion.diff_ref
  19.0 1.2 %collective-permute-done.2 = f32[72,128]{1,0:T(8,128)S(1)} collective-permute-done((f32[72,128]{1,0:T(8,128)S(1)}, f32[72,128]{1,0:T(8,128)S(1)}, u32[]{:S(2)}, u32[]{:S(2)}) %collective-permute-start.2) | collective-permute-done | bytes 36896 | tf_op jit(solution)/shard_map/ppermute | solution.py:266
  20.2 0.5 collective-permute-start.7
  20.8 1.9 %collective-permute-start.1 = (f32[8,128]{1,0:T(8,128)S(1)}, f32[8,128]{1,0:T(8,128)S(1)}, u32[]{:S(2)}, u32[]{:S(2)}) collective-permute-start(f32[8,128]{1,0:T(8,128)S(1)} %slice_add_fusion.1), channel_id=1, source_target_pairs={{0,8},{4,12},{8,0},{12,4},{1,9},{5,13},{9,1},{13,5},{2,10},{6,14},... | collective-permute-start | bytes 12296 | tf_op jit(solution)/shard_map/ppermute | solution.py:266
  22.7 0.7 maximum_maximum_fusion.1.latent_ref
  23.5 1.9 %collective-permute-done.1 = f32[8,128]{1,0:T(8,128)S(1)} collective-permute-done((f32[8,128]{1,0:T(8,128)S(1)}, f32[8,128]{1,0:T(8,128)S(1)}, u32[]{:S(2)}, u32[]{:S(2)}) %collective-permute-start.1) | collective-permute-done | bytes 4128 | tf_op jit(solution)/shard_map/ppermute | solution.py:266
  25.4 0.6 fusion.9.sums_ref
  26.0 4.0 %upper_block.1 = (bf16[4,1024,128]{2,1,0:T(8,128)(2,1)}, f32[4,16,128]{2,1,0:T(8,128)}, f32[576,128]{1,0:T(8,128)}, f32[576,128]{1,0:T(8,128)}) custom-call(s32[3]{0:T(128)} %pad_add_fusion.place_ref, s32[4,4,4]{2,1,0:T(4,128)} %boxes_ref.3, f32[8,128]{1,0:T(8,128)} %fusion.9.sums_ref, f32[16,128]{1,0:T(8,128)} %pad_maximum_fusion.6.mix_ref, ...), custom_call_target="tpu_custom_call" | custom-call | flops 4 | bytes 1 | tf_op jit(solution)/shard_map/upper_block/pallas_call | solution.py:701
  30.0 3.4 %collective-permute-done.7.passed_early_ref = bf16[2,1024,128]{2,1,0:T(8,128)(2,1)S(1)} collective-permute-done((bf16[2,1024,128]{2,1,0:T(8,128)(2,1)}, bf16[2,1024,128]{2,1,0:T(8,128)(2,1)S(1)}, u32[]{:S(2)}, u32[]{:S(2)}) %collective-permute-start.7) | collective-permute-done | bytes 524320 | tf_op jit(solution)/shard_map/ppermute | solution.py:261
  33.4 5.0 %collective-permute-start.12 = (bf16[2,1024,128]{2,1,0:T(8,128)(2,1)S(1)}, bf16[2,1024,128]{2,1,0:T(8,128)(2,1)S(1)}, u32[]{:S(2)}, u32[]{:S(2)}) collective-permute-start(bf16[2,1024,128]{2,1,0:T(8,128)(2,1)S(1)} %bitcast.42), channel_id=1, source_target_pairs={{0,2},{2,0},{1,3},{3,1},{4,6},{6,4},{5,7},{7,5},{8,10},{10,8},{9,1... | collective-permute-start | bytes 1572872 | tf_op jit(solution)/shard_map/ppermute | solution.py:261
  38.4 0.8 bitcast_add_fusion.1
  39.1 2.2 %collective-permute-start.11 = (f32[64,128]{1,0:T(8,128)S(1)}, f32[64,128]{1,0:T(8,128)S(1)}, u32[]{:S(2)}, u32[]{:S(2)}) collective-permute-start(f32[64,128]{1,0:T(8,128)S(1)} %bitcast_add_fusion.1), channel_id=1, source_target_pairs={{0,12},{4,0},{8,4},{12,8},{1,13},{5,1},{9,5},{13,9},{2,14},{6,2},{... | collective-permute-start | bytes 98312 | tf_op jit(solution)/shard_map/ppermute | solution.py:266
  41.3 0.7 collective-permute-start.9
  42.1 1.0 collective-permute-done.11
  43.1 4.0 %collective-permute-done.10 = f32[64,128]{1,0:T(8,128)S(1)} collective-permute-done((f32[64,128]{1,0:T(8,128)S(1)}, f32[64,128]{1,0:T(8,128)S(1)}, u32[]{:S(2)}, u32[]{:S(2)}) %collective-permute-start.10) | collective-permute-done | bytes 32800 | tf_op jit(solution)/shard_map/ppermute | solution.py:266
  47.1 3.8 %collective-permute-done.12.passed_late_ref = bf16[2,1024,128]{2,1,0:T(8,128)(2,1)S(1)} collective-permute-done((bf16[2,1024,128]{2,1,0:T(8,128)(2,1)S(1)}, bf16[2,1024,128]{2,1,0:T(8,128)(2,1)S(1)}, u32[]{:S(2)}, u32[]{:S(2)}) %collective-permute-start.12) | collective-permute-done | bytes 524320 | tf_op jit(solution)/shard_map/ppermute | solution.py:261
  50.9 1.8 %collective-permute-start.13 = (f32[88,128]{1,0:T(8,128)S(1)}, f32[88,128]{1,0:T(8,128)S(1)}, u32[]{:S(2)}, u32[]{:S(2)}) collective-permute-start(f32[88,128]{1,0:T(8,128)S(1)} %pad_maximum_fusion.3), channel_id=1, source_target_pairs={{0,2},{2,0},{1,3},{3,1},{4,6},{6,4},{5,7},{7,5},{8,10},{10,8},{9,1... | collective-permute-start | bytes 135176 | tf_op jit(solution)/shard_map/ppermute | solution.py:261
  52.7 2.3 %collective-permute-done.13 = f32[88,128]{1,0:T(8,128)S(1)} collective-permute-done((f32[88,128]{1,0:T(8,128)S(1)}, f32[88,128]{1,0:T(8,128)S(1)}, u32[]{:S(2)}, u32[]{:S(2)}) %collective-permute-start.13) | collective-permute-done | bytes 45088 | tf_op jit(solution)/shard_map/ppermute | solution.py:261
  54.9 0.6 broadcast_select_fusion.packed_ref
  55.6 10.4 %redo_upper.1 = (bf16[4,1280,128]{2,1,0:T(8,128)(2,1)}, bf16[4,16,128]{2,1,0:T(8,128)(2,1)}) custom-call(s32[3]{0:T(128)} %pad_add_fusion.place_ref, s32[4,4,4]{2,1,0:T(4,128)} %boxes_ref.3, f32[88,128]{1,0:T(8,128)} %broadcast_select_fusion.packed_ref, bf16[3,128]{1,0:T(4,128)(2,1)} %weight_ref.3, bf16[1152,128]{1,0:T(8,128)(2,1)} %collective-permute-done.6.kernel_ref, ...), custom_call_target="tpu_custom_call" | custom-call | flops 4 | bytes 1 | tf_op jit(solution)/shard_map/redo_upper/pallas_call | solution.py:701
  65.9 0.1 collective-permute-start.14
  66.0 1.4 %collective-permute-done.14.near_ref = bf16[4,16,128]{2,1,0:T(8,128)(2,1)S(1)} collective-permute-done((bf16[4,16,128]{2,1,0:T(8,128)(2,1)}, bf16[4,16,128]{2,1,0:T(8,128)(2,1)S(1)}, u32[]{:S(2)}, u32[]{:S(2)}) %collective-permute-start.14) | collective-permute-done | bytes 16416 | tf_op jit(solution)/shard_map/ppermute | solution.py:261
  67.4 0.6 copy-done.10
  68.0 9.7 %lower_block.1 = (bf16[4,1024,128]{2,1,0:T(8,128)(2,1)}, f32[4,16,128]{2,1,0:T(8,128)}, f32[576,128]{1,0:T(8,128)}, f32[576,128]{1,0:T(8,128)}) custom-call(s32[3]{0:T(128)} %pad_add_fusion.place_ref, f32[8,128]{1,0:T(8,128)} %fusion.9.sums_ref, f32[16,128]{1,0:T(8,128)} %pad_maximum_fusion.6.mix_ref, bf16[1152,128]{1,0:T(8,128)(2,1)} %bitcast.39, ...), custom_call_target="tpu_custom_call" | custom-call | flops 4 | bytes 1 | tf_op jit(solution)/shard_map/lower_block/pallas_call | solution.py:701
  77.7 0.2 collective-permute-start.19
  77.9 0.3 collective-permute-start.15
  78.3 1.3 %collective-permute-done.15 = f32[64,128]{1,0:T(8,128)S(1)} collective-permute-done((f32[64,128]{1,0:T(8,128)}, f32[64,128]{1,0:T(8,128)S(1)}, u32[]{:S(2)}, u32[]{:S(2)}) %collective-permute-start.15) | collective-permute-done | bytes 32800 | tf_op jit(solution)/shard_map/ppermute | solution.py:261
  79.6 0.8 bitcast_add_fusion
  80.4 2.2 %collective-permute-start.18 = (f32[64,128]{1,0:T(8,128)S(1)}, f32[64,128]{1,0:T(8,128)S(1)}, u32[]{:S(2)}, u32[]{:S(2)}) collective-permute-start(f32[64,128]{1,0:T(8,128)S(1)} %bitcast_add_fusion), channel_id=1, source_target_pairs={{0,12},{4,0},{8,4},{12,8},{1,13},{5,1},{9,5},{13,9},{2,14},{6,2},{... | collective-permute-start | bytes 98312 | tf_op jit(solution)/shard_map/ppermute | solution.py:266
  82.6 0.7 collective-permute-start.16
  83.3 1.0 add_convert_fusion
  84.3 3.2 %collective-permute-start.22 = (bf16[576,128]{1,0:T(8,128)(2,1)S(1)}, bf16[576,128]{1,0:T(8,128)(2,1)S(1)}, u32[]{:S(2)}, u32[]{:S(2)}) collective-permute-start(bf16[576,128]{1,0:T(8,128)(2,1)S(1)} %add_convert_fusion), channel_id=1, source_target_pairs={{0,12},{4,0},{8,4},{12,8},{1,13},{5,1},{9,5},{13,9},{2,14},{6,2},{... | collective-permute-start | bytes 442376 | tf_op jit(solution)/shard_map/ppermute | solution.py:266
  87.4 2.0 %collective-permute-start.21 = (bf16[576,128]{1,0:T(8,128)(2,1)S(1)}, bf16[576,128]{1,0:T(8,128)(2,1)S(1)}, u32[]{:S(2)}, u32[]{:S(2)}) collective-permute-start(bf16[576,128]{1,0:T(8,128)(2,1)S(1)} %add_convert_fusion), channel_id=1, source_target_pairs={{0,8},{4,12},{8,0},{12,4},{1,9},{5,13},{9,1},{13,5},{2,10},{6,14},... | collective-permute-start | bytes 442376 | tf_op jit(solution)/shard_map/ppermute | solution.py:266
  89.5 0.0 copy-start.7
  89.5 0.6 copy-done.7
  90.1 4.6 %input_gradient.1 = bf16[4,1024,128]{2,1,0:T(8,128)(2,1)} custom-call(s32[3]{0:T(128)} %pad_add_fusion.place_ref, f32[8,128]{1,0:T(8,128)} %fusion.9.sums_ref, f32[16,128]{1,0:T(8,128)} %pad_maximum_fusion.6.mix_ref, f32[4,16,128]{2,1,0:T(8,128)} %bitcast.50, bf16[4,1024,128]{2,1,0:T(8,128)(2,1)} %bitcast.34, ...), custom_call_target="tpu_custom_call" | custom-call | flops 33554432 | bytes 8388608 | tf_op jit(solution)/shard_map/input_gradient/pallas_call | solution.py:701
  94.7 7.2 %collective-permute-done.21 = bf16[576,128]{1,0:T(8,128)(2,1)S(1)} collective-permute-done((bf16[576,128]{1,0:T(8,128)(2,1)S(1)}, bf16[576,128]{1,0:T(8,128)(2,1)S(1)}, u32[]{:S(2)}, u32[]{:S(2)}) %collective-permute-start.21) | collective-permute-done | bytes 147488 | tf_op jit(solution)/shard_map/ppermute | solution.py:266
  102.0 0.1 add_add_fusion
  102.1 0.1 collective-permute-start.23
  102.2 0.6 pad_maximum_fusion.7
  102.7 0.6 fusion.5
  103.3 0.4 collective-permute-done.23
  103.7 0.9 maximum_select_fusion
  (61 shorter events, 0.3 us)
Async XLA Ops:
  0.6 1.2 %copy-start = (bf16[1,4,8,128,128]{4,3,2,1,0:T(8,128)(2,1)S(1)}, bf16[1,4,8,128,128]{4,3,2,1,0:T(8,128)(2,1)}, u32[]{:S(2)}) copy-start(bf16[1,4,8,128,128]{4,3,2,1,0:T(8,128)(2,1)} %param.10) | copy-start | bytes 3145732
  1.9 2.8 %copy-start.1 = (bf16[1,4,8,128,128]{4,3,2,1,0:T(8,128)(2,1)S(1)}, bf16[1,4,8,128,128]{4,3,2,1,0:T(8,128)(2,1)}, u32[]{:S(2)}) copy-start(bf16[1,4,8,128,128]{4,3,2,1,0:T(8,128)(2,1)} %param.10) | copy-start | bytes 3145732
  1.9 8.4 %copy-start.2 = (bf16[1,1152,128]{2,1,0:T(8,128)(2,1)S(1)}, bf16[1,1152,128]{2,1,0:T(8,128)(2,1)}, u32[]{:S(2)}) copy-start(bf16[1,1152,128]{2,1,0:T(8,128)(2,1)} %param.15) | copy-start | bytes 884740
  4.0 7.7 %copy-start.11 = (bf16[1,4,256]{2,1,0:T(4,128)(2,1)S(1)}, bf16[1,4,256]{2,1,0:T(4,128)(2,1)}, u32[]{:S(2)}) copy-start(bf16[1,4,256]{2,1,0:T(4,128)(2,1)} %param.16) | copy-start | bytes 6148
  4.1 7.6 %copy-start.12 = (bf16[1,128]{1,0:T(2,128)(2,1)S(1)}, bf16[1,128]{1,0:T(2,128)(2,1)}, u32[]{:S(2)}) copy-start(bf16[1,128]{1,0:T(2,128)(2,1)} %param.18) | copy-start | bytes 772
  4.1 7.6 %copy-start.13 = (bf16[1,128]{1,0:T(2,128)(2,1)S(1)}, bf16[1,128]{1,0:T(2,128)(2,1)}, u32[]{:S(2)}) copy-start(bf16[1,128]{1,0:T(2,128)(2,1)} %param.17) | copy-start | bytes 772
  4.1 7.6 %copy-start.9 = (bf16[4,4,8,128]{3,2,1,0:T(8,128)(2,1)S(1)}, bf16[4,4,8,128]{3,2,1,0:T(8,128)(2,1)}, u32[]{:S(2)}) copy-start(bf16[4,4,8,128]{3,2,1,0:T(8,128)(2,1)} %param.11) | copy-start | bytes 98308
  4.1 9.2 %collective-permute-start = (f32[104,128]{1,0:T(8,128)S(1)}, f32[104,128]{1,0:T(8,128)S(1)}, u32[]{:S(2)}, u32[]{:S(2)}) collective-permute-start(f32[104,128]{1,0:T(8,128)S(1)} %pad_maximum_fusion), channel_id=1, source_target_pairs={{0,1},{1,0},{2,3},{3,2},{4,5},{5,4},{6,7},{7,6},{8,9},{9,8},{10,11... | collective-permute-start | bytes 159752 | tf_op jit(solution)/shard_map/ppermute | solution.py:261
  4.6 21.4 %collective-permute-start.5 = (bf16[4,128,128]{2,1,0:T(8,128)(2,1)S(1)}, bf16[4,128,128]{2,1,0:T(8,128)(2,1)}, u32[]{:S(2)}, u32[]{:S(2)}) collective-permute-start(bf16[4,128,128]{2,1,0:T(8,128)(2,1)S(1)} %get-tuple-element.50), channel_id=1, source_target_pairs={{0,14},{2,12},{4,2},{6,0},{8,6},{10,4},{12,10},{14,8},{1,15},{3,13... | collective-permute-start | bytes 393224 | tf_op jit(solution)/shard_map/ppermute | solution.py:272
  10.2 15.8 %collective-permute-start.4 = (bf16[4,128,128]{2,1,0:T(8,128)(2,1)S(1)}, bf16[4,128,128]{2,1,0:T(8,128)(2,1)}, u32[]{:S(2)}, u32[]{:S(2)}) collective-permute-start(bf16[4,128,128]{2,1,0:T(8,128)(2,1)S(1)} %get-tuple-element.51), channel_id=1, source_target_pairs={{0,6},{2,4},{4,10},{6,8},{8,14},{10,12},{12,2},{14,0},{1,7},{3,5},... | collective-permute-start | bytes 393224 | tf_op jit(solution)/shard_map/ppermute | solution.py:272
  10.2 15.8 %collective-permute-start.6 = (bf16[1152,128]{1,0:T(8,128)(2,1)S(1)}, bf16[1152,128]{1,0:T(8,128)(2,1)}, u32[]{:S(2)}, u32[]{:S(2)}) collective-permute-start(bf16[1152,128]{1,0:T(8,128)(2,1)S(1)} %bitcast.40), channel_id=1, source_target_pairs={{0,2},{2,0},{1,3},{3,1},{4,6},{6,4},{5,7},{7,5},{8,10},{10,8},{9,1... | collective-permute-start | bytes 884744 | tf_op jit(solution)/shard_map/ppermute | solution.py:261
  13.4 6.8 %collective-permute-start.2 = (f32[72,128]{1,0:T(8,128)S(1)}, f32[72,128]{1,0:T(8,128)S(1)}, u32[]{:S(2)}, u32[]{:S(2)}) collective-permute-start(f32[72,128]{1,0:T(8,128)S(1)} %get-tuple-element.62), channel_id=1, source_target_pairs={{0,4},{4,8},{8,12},{12,0},{1,5},{5,9},{9,13},{13,1},{2,6},{6,10},{... | collective-permute-start | bytes 110600 | tf_op jit(solution)/shard_map/ppermute | solution.py:266
  14.4 6.4 %collective-permute-start.3 = (f32[72,128]{1,0:T(8,128)S(1)}, f32[72,128]{1,0:T(8,128)S(1)}, u32[]{:S(2)}, u32[]{:S(2)}) collective-permute-start(f32[72,128]{1,0:T(8,128)S(1)} %get-tuple-element.63), channel_id=1, source_target_pairs={{0,12},{4,0},{8,4},{12,8},{1,13},{5,1},{9,5},{13,9},{2,14},{6,2},{... | collective-permute-start | bytes 110600 | tf_op jit(solution)/shard_map/ppermute | solution.py:266
  20.2 13.2 %collective-permute-start.7 = (bf16[2,1024,128]{2,1,0:T(8,128)(2,1)}, bf16[2,1024,128]{2,1,0:T(8,128)(2,1)S(1)}, u32[]{:S(2)}, u32[]{:S(2)}) collective-permute-start(bf16[2,1024,128]{2,1,0:T(8,128)(2,1)} %bitcast.15), channel_id=1, source_target_pairs={{0,2},{2,0},{1,3},{3,1},{4,6},{6,4},{5,7},{7,5},{8,10},{10,8},{9,1... | collective-permute-start | bytes 1572872 | tf_op jit(solution)/shard_map/ppermute | solution.py:261
  20.8 5.2 %copy-start.5 = (f32[64,128]{1,0:T(8,128)}, f32[64,128]{1,0:T(8,128)S(1)}, u32[]{:S(2)}) copy-start(f32[64,128]{1,0:T(8,128)S(1)} %slice.116) | copy-start | bytes 98308
  20.8 4.6 %collective-permute-start.1 = (f32[8,128]{1,0:T(8,128)S(1)}, f32[8,128]{1,0:T(8,128)S(1)}, u32[]{:S(2)}, u32[]{:S(2)}) collective-permute-start(f32[8,128]{1,0:T(8,128)S(1)} %slice_add_fusion.1), channel_id=1, source_target_pairs={{0,8},{4,12},{8,0},{12,4},{1,9},{5,13},{9,1},{13,5},{2,10},{6,14},... | collective-permute-start | bytes 12296 | tf_op jit(solution)/shard_map/ppermute | solution.py:266
  22.7 3.3 %copy-start.6 = (f32[64,128]{1,0:T(8,128)}, f32[64,128]{1,0:T(8,128)S(1)}, u32[]{:S(2)}) copy-start(f32[64,128]{1,0:T(8,128)S(1)} %slice.119) | copy-start | bytes 98308
  26.0 21.1 %copy-start.8 = (f32[8,128]{1,0:T(8,128)S(1)}, f32[8,128]{1,0:T(8,128)}, u32[]{:S(2)}) copy-start(f32[8,128]{1,0:T(8,128)} %fusion.9.sums_ref) | copy-start | bytes 12292
  33.4 22.2 %copy-start.3 = (bf16[2,1024,128]{2,1,0:T(8,128)(2,1)}, bf16[2,1024,128]{2,1,0:T(8,128)(2,1)S(1)}, u32[]{:S(2)}) copy-start(bf16[2,1024,128]{2,1,0:T(8,128)(2,1)S(1)} %collective-permute-done.7.passed_early_ref) | copy-start | bytes 1572868
  33.4 5.0 %collective-permute-start.8 = (f32[64,128]{1,0:T(8,128)}, f32[64,128]{1,0:T(8,128)S(1)}, u32[]{:S(2)}, u32[]{:S(2)}) collective-permute-start(f32[64,128]{1,0:T(8,128)} %bitcast.55), channel_id=1, source_target_pairs={{0,1},{1,0},{2,3},{3,2},{4,5},{5,4},{6,7},{7,6},{8,9},{9,8},{10,11... | collective-permute-start | bytes 98312 | tf_op jit(solution)/shard_map/ppermute | solution.py:261
  33.4 17.5 %collective-permute-start.12 = (bf16[2,1024,128]{2,1,0:T(8,128)(2,1)S(1)}, bf16[2,1024,128]{2,1,0:T(8,128)(2,1)S(1)}, u32[]{:S(2)}, u32[]{:S(2)}) collective-permute-start(bf16[2,1024,128]{2,1,0:T(8,128)(2,1)S(1)} %bitcast.42), channel_id=1, source_target_pairs={{0,2},{2,0},{1,3},{3,1},{4,6},{6,4},{5,7},{7,5},{8,10},{10,8},{9,1... | collective-permute-start | bytes 1572872 | tf_op jit(solution)/shard_map/ppermute | solution.py:261
  39.1 3.9 %collective-permute-start.11 = (f32[64,128]{1,0:T(8,128)S(1)}, f32[64,128]{1,0:T(8,128)S(1)}, u32[]{:S(2)}, u32[]{:S(2)}) collective-permute-start(f32[64,128]{1,0:T(8,128)S(1)} %bitcast_add_fusion.1), channel_id=1, source_target_pairs={{0,12},{4,0},{8,4},{12,8},{1,13},{5,1},{9,5},{13,9},{2,14},{6,2},{... | collective-permute-start | bytes 98312 | tf_op jit(solution)/shard_map/ppermute | solution.py:266
  41.3 5.7 %collective-permute-start.10 = (f32[64,128]{1,0:T(8,128)S(1)}, f32[64,128]{1,0:T(8,128)S(1)}, u32[]{:S(2)}, u32[]{:S(2)}) collective-permute-start(f32[64,128]{1,0:T(8,128)S(1)} %bitcast_add_fusion.1), channel_id=1, source_target_pairs={{0,4},{4,8},{8,12},{12,0},{1,5},{5,9},{9,13},{13,1},{2,6},{6,10},{... | collective-permute-start | bytes 98312 | tf_op jit(solution)/shard_map/ppermute | solution.py:266
  41.3 5.7 %collective-permute-start.9 = (f32[64,128]{1,0:T(8,128)S(1)}, f32[64,128]{1,0:T(8,128)S(1)}, u32[]{:S(2)}, u32[]{:S(2)}) collective-permute-start(f32[64,128]{1,0:T(8,128)S(1)} %bitcast_add_fusion.1), channel_id=1, source_target_pairs={{0,8},{4,12},{8,0},{12,4},{1,9},{5,13},{9,1},{13,5},{2,10},{6,14},... | collective-permute-start | bytes 98312 | tf_op jit(solution)/shard_map/ppermute | solution.py:266
  50.9 4.7 %copy-start.4 = (bf16[2,1024,128]{2,1,0:T(8,128)(2,1)}, bf16[2,1024,128]{2,1,0:T(8,128)(2,1)S(1)}, u32[]{:S(2)}) copy-start(bf16[2,1024,128]{2,1,0:T(8,128)(2,1)S(1)} %collective-permute-done.12.passed_late_ref) | copy-start | bytes 1572868
  50.9 4.0 %collective-permute-start.13 = (f32[88,128]{1,0:T(8,128)S(1)}, f32[88,128]{1,0:T(8,128)S(1)}, u32[]{:S(2)}, u32[]{:S(2)}) collective-permute-start(f32[88,128]{1,0:T(8,128)S(1)} %pad_maximum_fusion.3), channel_id=1, source_target_pairs={{0,2},{2,0},{1,3},{3,1},{4,6},{6,4},{5,7},{7,5},{8,10},{10,8},{9,1... | collective-permute-start | bytes 135176 | tf_op jit(solution)/shard_map/ppermute | solution.py:261
  65.9 1.5 %collective-permute-start.14 = (bf16[4,16,128]{2,1,0:T(8,128)(2,1)}, bf16[4,16,128]{2,1,0:T(8,128)(2,1)S(1)}, u32[]{:S(2)}, u32[]{:S(2)}) collective-permute-start(bf16[4,16,128]{2,1,0:T(8,128)(2,1)} %get-tuple-element.37), channel_id=1, source_target_pairs={{0,1},{1,0},{2,3},{3,2},{4,5},{5,4},{6,7},{7,6},{8,9},{9,8},{10,11... | collective-permute-start | bytes 49160 | tf_op jit(solution)/shard_map/ppermute | solution.py:261
  67.4 0.6 copy-start.10
  77.7 5.6 %collective-permute-start.19 = (f32[576,128]{1,0:T(8,128)}, f32[576,128]{1,0:T(8,128)S(1)}, u32[]{:S(2)}, u32[]{:S(2)}) collective-permute-start(f32[576,128]{1,0:T(8,128)} %get-tuple-element.43), channel_id=1, source_target_pairs={{0,1},{1,0},{2,3},{3,2},{4,5},{5,4},{6,7},{7,6},{8,9},{9,8},{10,11... | collective-permute-start | bytes 884744 | tf_op jit(solution)/shard_map/ppermute | solution.py:261
  77.9 1.7 %collective-permute-start.15 = (f32[64,128]{1,0:T(8,128)}, f32[64,128]{1,0:T(8,128)S(1)}, u32[]{:S(2)}, u32[]{:S(2)}) collective-permute-start(f32[64,128]{1,0:T(8,128)} %bitcast.54), channel_id=1, source_target_pairs={{0,1},{1,0},{2,3},{3,2},{4,5},{5,4},{6,7},{7,6},{8,9},{9,8},{10,11... | collective-permute-start | bytes 98312 | tf_op jit(solution)/shard_map/ppermute | solution.py:261
  80.4 9.1 %collective-permute-start.18 = (f32[64,128]{1,0:T(8,128)S(1)}, f32[64,128]{1,0:T(8,128)S(1)}, u32[]{:S(2)}, u32[]{:S(2)}) collective-permute-start(f32[64,128]{1,0:T(8,128)S(1)} %bitcast_add_fusion), channel_id=1, source_target_pairs={{0,12},{4,0},{8,4},{12,8},{1,13},{5,1},{9,5},{13,9},{2,14},{6,2},{... | collective-permute-start | bytes 98312 | tf_op jit(solution)/shard_map/ppermute | solution.py:266
  82.6 6.9 %collective-permute-start.17 = (f32[64,128]{1,0:T(8,128)S(1)}, f32[64,128]{1,0:T(8,128)S(1)}, u32[]{:S(2)}, u32[]{:S(2)}) collective-permute-start(f32[64,128]{1,0:T(8,128)S(1)} %bitcast_add_fusion), channel_id=1, source_target_pairs={{0,4},{4,8},{8,12},{12,0},{1,5},{5,9},{9,13},{13,1},{2,6},{6,10},{... | collective-permute-start | bytes 98312 | tf_op jit(solution)/shard_map/ppermute | solution.py:266
  82.6 6.9 %collective-permute-start.16 = (f32[64,128]{1,0:T(8,128)S(1)}, f32[64,128]{1,0:T(8,128)S(1)}, u32[]{:S(2)}, u32[]{:S(2)}) collective-permute-start(f32[64,128]{1,0:T(8,128)S(1)} %bitcast_add_fusion), channel_id=1, source_target_pairs={{0,8},{4,12},{8,0},{12,4},{1,9},{5,13},{9,1},{13,5},{2,10},{6,14},... | collective-permute-start | bytes 98312 | tf_op jit(solution)/shard_map/ppermute | solution.py:266
  84.3 10.5 %collective-permute-start.22 = (bf16[576,128]{1,0:T(8,128)(2,1)S(1)}, bf16[576,128]{1,0:T(8,128)(2,1)S(1)}, u32[]{:S(2)}, u32[]{:S(2)}) collective-permute-start(bf16[576,128]{1,0:T(8,128)(2,1)S(1)} %add_convert_fusion), channel_id=1, source_target_pairs={{0,12},{4,0},{8,4},{12,8},{1,13},{5,1},{9,5},{13,9},{2,14},{6,2},{... | collective-permute-start | bytes 442376 | tf_op jit(solution)/shard_map/ppermute | solution.py:266
  87.4 14.6 %collective-permute-start.21 = (bf16[576,128]{1,0:T(8,128)(2,1)S(1)}, bf16[576,128]{1,0:T(8,128)(2,1)S(1)}, u32[]{:S(2)}, u32[]{:S(2)}) collective-permute-start(bf16[576,128]{1,0:T(8,128)(2,1)S(1)} %add_convert_fusion), channel_id=1, source_target_pairs={{0,8},{4,12},{8,0},{12,4},{1,9},{5,13},{9,1},{13,5},{2,10},{6,14},... | collective-permute-start | bytes 442376 | tf_op jit(solution)/shard_map/ppermute | solution.py:266
  89.5 12.5 %collective-permute-start.20 = (bf16[576,128]{1,0:T(8,128)(2,1)S(1)}, bf16[576,128]{1,0:T(8,128)(2,1)S(1)}, u32[]{:S(2)}, u32[]{:S(2)}) collective-permute-start(bf16[576,128]{1,0:T(8,128)(2,1)S(1)} %add_convert_fusion), channel_id=1, source_target_pairs={{0,4},{4,8},{8,12},{12,0},{1,5},{5,9},{9,13},{13,1},{2,6},{6,10},{... | collective-permute-start | bytes 442376 | tf_op jit(solution)/shard_map/ppermute | solution.py:266
  89.5 0.6 copy-start.7
  102.1 1.6 %collective-permute-start.23 = (f32[576,128]{1,0:T(8,128)S(1)}, f32[576,128]{1,0:T(8,128)S(1)}, u32[]{:S(2)}, u32[]{:S(2)}) collective-permute-start(f32[576,128]{1,0:T(8,128)S(1)} %add_add_fusion), channel_id=1, source_target_pairs={{0,1},{1,0},{2,3},{3,2},{4,5},{5,4},{6,7},{7,6},{8,9},{9,8},{10,11... | collective-permute-start | bytes 884744 | tf_op jit(solution)/shard_map/ppermute | solution.py:261

commit v4 on v0

--- a/solution.py
+++ b/solution.py
@@ -1,6 +1,11 @@
+import functools
+import types
+
 import jax
 import jax.numpy as jnp
 from jax import lax
+from jax.experimental import pallas as pl
+from jax.experimental.pallas import tpu as pltpu
 from jax.sharding import PartitionSpec as P
 
 GROUPS = 32
@@ -166,7 +171,7 @@
     return (result, kernel_term, mod_term, bias_term)
 
 
-def body(
+def general_body(
     activations,
     latent,
     recon,
@@ -246,7 +251,563 @@
     return (grads_out, kernel_grad, mod_grad, bias_grad)
 
 
+EXACT = lax.Precision.HIGHEST
+TN = (((0,), (0,)), ((), ()))
+NT = (((1,), (1,)), ((), ()))
+F32 = jnp.float32
+BF16 = jnp.bfloat16
+
+
+def swap(value, axis):
+    return lax.ppermute(value, axis, [(0, 1), (1, 0)])
+
+
+def shift(value, axis, steps):
+    count = lax.axis_size(axis)
+    return lax.ppermute(value, axis, [(i, (i + steps) % count) for i in range(count)])
+
+
+def swap_and_shift(value, steps):
+    count = lax.axis_size("rows")
+    pairs = [(2 * i + s, 2 * ((i + steps) % count) + 1 - s) for i in range(count) for s in range(2)]
+    return lax.ppermute(value, ("rows", "segment"), pairs)
+
+
+def pixel_total(value):
+    value = value + swap(value, "sub")
+    one, two, three = [shift(value, "rows", steps) for steps in (1, 2, 3)]
+    return (value + two) + (one + three)
+
+
+def same_group(channels):
+    per = channels // GROUPS
+    left = lax.broadcasted_iota(jnp.int32, (channels, channels), 0) // per
+    right = lax.broadcasted_iota(jnp.int32, (channels, channels), 1) // per
+    return (left == right).astype(F32)
+
+
+def statistics(sums_ref, micro, micros, count):
+    member = same_group(sums_ref.shape[-1])
+    both = jnp.concatenate([sums_ref[pl.ds(micro, 1), :], sums_ref[pl.ds(micros + micro, 1), :]], axis=0)
+    both = jnp.dot(both, member, precision=EXACT, preferred_element_type=F32) / count
+    mean = both[0:1]
+    return mean, lax.rsqrt(both[1:2] - mean * mean + EPS)
+
+
+def gradient_means(total, mix, count):
+    mean_grad = jnp.sum(mix[:8] * total[8:], axis=0, keepdims=True)
+    mean_cross = jnp.sum(mix[:8] * total[:8], axis=0, keepdims=True)
+    both = jnp.concatenate([mean_grad, mean_cross], axis=0)
+    both = jnp.dot(both, same_group(total.shape[-1]), precision=EXACT, preferred_element_type=F32) / count
+    return both[0:1], both[1:2]
+
+
+def side_by_side(mix):
+    return jnp.concatenate([mix[:8], mix[8:]], axis=1).astype(BF16)
+
+
+def sums_kernel(n, micro):
+    micros = n.sums.shape[0] // 2
+    value = n.acts[0].astype(F32)
+    n.sums[pl.ds(micro, 1), :] = jnp.sum(value, axis=0, keepdims=True)
+    n.sums[pl.ds(micros + micro, 1), :] = jnp.sum(value * value, axis=0, keepdims=True)
+
+
+class Band:
+    def __init__(self, n, micro, rows, cols, bands):
+        self.n, self.rows, self.cols = n, rows, cols
+        self.head = n.from_up.shape[0] - 16 * (n.from_up.shape[0] // 16)
+        self.micro = micro
+        self.side = lax.axis_index("sub")
+        self.row_start = lax.axis_index("rows") * rows
+        self.total_rows = rows * bands
+        lane = lax.broadcasted_iota(jnp.int32, (1, cols), 1)
+        crops = n.boxes.shape[1]
+        tiles = self.total_rows // TILE * (2 * cols // TILE)
+        self.boxes = []
+        for k in range(crops):
+            row, col, height, width = [n.boxes[micro, k, i] for i in range(4)]
+            share = tiles / jnp.full((1, cols), crops * height * width, jnp.int32).astype(F32)
+            inside = []
+            for side in (self.side, 1 - self.side):
+                at = lane + side * cols
+                inside.append(jnp.where((at >= col * TILE) & (at < (col + width) * TILE), share, 0.0))
+            self.boxes.append((row * TILE, (row + height) * TILE, inside[0], inside[1]))
+        weight = n.out_weight[...].astype(F32)
+        blank = jnp.zeros((8 - weight.shape[0], weight.shape[1]), F32)
+        self.own = jnp.concatenate([jnp.concatenate([weight, blank])] * 3).astype(BF16)
+        self.other = jnp.concatenate([jnp.concatenate([blank[:3], weight, blank[3:]])] * 3).astype(BF16)
+
+    def border(self, ref, which):
+        return ref[pl.ds(pl.multiple_of(self.head + 16 * self.micro + 8 * which, 8), 8), :]
+
+    def planes(self, r):
+        if r < 0:
+            return self.border(self.n.from_up, r + 2)
+        if r >= self.rows:
+            return self.border(self.n.from_down, r - self.rows)
+        own = self.n.recon[0, :, r, :].astype(F32) - self.n.target[0, :, r, :].astype(F32)
+        beside = self.n.recon_beside[0, :, r, :].astype(F32) - self.n.target_beside[0, :, r, :].astype(F32)
+        return jnp.concatenate([own, beside, jnp.zeros((2, self.cols), F32)])
+
+    def latent(self, r):
+        if r < 0 or r >= self.rows:
+            ref = self.n.from_up if r < 0 else self.n.from_down
+            value = jnp.concatenate([self.border(ref, 0)[6:8], self.border(ref, 1)[6:8]])
+        else:
+            value = self.n.latent[0, :, r, :].astype(F32)
+        count = value.shape[0]
+        return jnp.concatenate([value, jnp.ones((1, self.cols), F32), jnp.zeros((7 - count, self.cols), F32)]).astype(BF16)
+
+    def row(self, r):
+        diff = self.planes(r)
+        at = self.row_start + r
+        own = jnp.zeros((1, self.cols), F32)
+        other = jnp.zeros((1, self.cols), F32)
+        for first, end, own_share, other_share in self.boxes:
+            here = (at >= first) & (at < end)
+            own = own + jnp.where(here, own_share, 0.0)
+            other = other + jnp.where(here, other_share, 0.0)
+        plane = lax.broadcasted_iota(jnp.int32, (8, self.cols), 0)
+        diff = 2.0 * diff * jnp.where(plane < 3, own, other)
+        high = diff.astype(BF16).astype(F32)
+        middle = (diff - high).astype(BF16).astype(F32)
+        parts = jnp.concatenate([high, middle, diff - high - middle]).astype(BF16)
+        value = lax.dot_general(parts, self.own, TN, preferred_element_type=F32).astype(BF16)
+        beside = lax.dot_general(parts, self.other, TN, preferred_element_type=F32).astype(BF16).astype(F32)
+        return value, jnp.where(self.side == 0, beside[0:1], beside[self.cols - 1 : self.cols])
+
+
+def spread(index, cols, value, near, shifted):
+    channels = value.shape[-1]
+    side = lax.axis_index("sub")
+    at = slice(index * cols, (index + 1) * cols)
+    place = lax.broadcasted_iota(jnp.int32, (cols, channels), 0)
+    wide = value.astype(F32)
+    before = jnp.where(side == 1, near, 0.0)
+    behind = jnp.where(side == 0, near, 0.0)
+    shifted[at, 0:channels] = jnp.where(place == 0, before, pltpu.roll(wide, 1, 0)).astype(BF16)
+    shifted[at, channels : 2 * channels] = value
+    shifted[at, 2 * channels :] = jnp.where(place == cols - 1, behind, pltpu.roll(wide, cols - 1, 0)).astype(BF16)
+
+
+def tap_of(row, col):
+    return 3 * (2 - row) + (2 - col)
+
+
+def arrange_weights(kernel_ref, weights):
+    channels = kernel_ref.shape[-1]
+    for row in range(3):
+        for col in range(3):
+            tap = tap_of(row, col)
+            weights[row, :, col * channels : (col + 1) * channels] = kernel_ref[tap * channels : (tap + 1) * channels, :]
+
+
+def hidden_gradient(rows, cols, shifted, weights, hidden_grad):
+    pixels = rows * cols
+    total = lax.dot_general(shifted[0:pixels, :], weights[0], NT, preferred_element_type=F32)
+    total = total + lax.dot_general(shifted[cols : cols + pixels, :], weights[1], NT, preferred_element_type=F32)
+    hidden_grad[0:pixels, :] = total + lax.dot_general(
+        shifted[2 * cols : 2 * cols + pixels, :], weights[2], NT, preferred_element_type=F32
+    )
+
+
+def pixel_values(acts, latent, mix, mean, rstd):
+    channels = mean.shape[-1]
+    xhat = (acts.astype(F32) - mean) * rstd
+    mixed = lax.dot_general(latent, mix, TN, preferred_element_type=F32)
+    scale = mixed[:, :channels]
+    pre = xhat * scale + mixed[:, channels:]
+    sig = 0.5 * jnp.tanh(0.5 * pre) + 0.5
+    hidden = pre * sig
+    return xhat, scale, hidden, sig + hidden * (1.0 - sig)
+
+
+def reduce_block(n, band, mean, rstd, mix):
+    rows, cols = band.rows, band.cols
+    channels = n.acts.shape[-1]
+    hidden_gradient(rows, cols, n.shifted, n.weights, n.hidden_grad)
+    for r in range(rows):
+        at = slice(r * cols, (r + 1) * cols)
+        latent = band.latent(r)
+        n.latent_keep[:, at] = latent
+        xhat, scale, _, slope = pixel_values(n.acts[0, at, :], latent, mix, mean, rstd)
+        pre_grad = n.hidden_grad[at, :] * slope
+        n.norm[0, at, :] = (pre_grad * scale).astype(BF16)
+        n.pairs[at, 0:channels] = (pre_grad * xhat).astype(BF16)
+        n.pairs[at, channels:] = pre_grad.astype(BF16)
+    reduced = jnp.dot(n.latent_keep[...], n.pairs[...], preferred_element_type=F32)
+    n.reduced[0, 0:8, :] = reduced[:, :channels]
+    n.reduced[0, 8:16, :] = reduced[:, channels:]
+
+
+def upper_kernel(rows, cols, bands, micros, count, n, step):
+    active = lax.axis_index("segment") == 1
+
+    @pl.when(active)
+    def _():
+        @pl.when(step == 0)
+        def _():
+            arrange_weights(n.kernel, n.weights)
+            head = 2 * micros
+            n.sums_keep[...] = (n.sums[...] + n.across[...]) + (n.from_up[0:head, :] + n.from_down[0:head, :])
+
+        mean, rstd = statistics(n.sums_keep, step, micros, count)
+        channels = mean.shape[-1]
+        mix = [n.mod_weight[0].astype(F32), jnp.concatenate([n.scale_bias[...], n.shift_bias[...]], axis=1).astype(F32)]
+        mix.append(jnp.zeros((7 - mix[0].shape[0], 2 * channels), F32))
+        band = Band(n, step, rows, cols, bands)
+        for r in range(rows + 2):
+            spread(r, cols, *band.row(r - 1), n.shifted)
+        reduce_block(n, band, mean, rstd, jnp.concatenate(mix).astype(BF16))
+
+    @pl.when(jnp.logical_not(active))
+    def _():
+        n.reduced[...] = jnp.zeros_like(n.reduced)
+
+
+def lower_kernel(rows, cols, bands, micros, count, n, step):
+    active = lax.axis_index("segment") == 0
+
+    @pl.when(active)
+    def _():
+        @pl.when(step == 0)
+        def _():
+            arrange_weights(n.kernel, n.weights)
+
+        mean, rstd = statistics(n.sums, step, micros, count)
+        band = Band(n, step, rows, cols, bands)
+        near = n.near[0].astype(F32)
+        for r in range(rows + 2):
+            spread(r, cols, n.result[0, r * cols : (r + 1) * cols, :], near[r : r + 1], n.shifted)
+        reduce_block(n, band, mean, rstd, side_by_side(n.mix[...]))
+
+    @pl.when(jnp.logical_not(active))
+    def _():
+        n.reduced[...] = jnp.zeros_like(n.reduced)
+
+
+def gradient_kernel(rows, cols, bands, micros, count, n, step):
+    pixels = rows * cols
+    side = lax.axis_index("sub")
+    segment = lax.axis_index("segment")
+
+    @pl.when(step == 0)
+    def _():
+        n.total[...] = jnp.zeros_like(n.total)
+
+    mean, rstd = statistics(n.sums, step, micros, count)
+    band = Band(n, step, rows, cols, bands)
+
+    @pl.when(segment == 1)
+    def _():
+        for r in range(rows + 2):
+            spread(r, cols, *band.row(r - 1), n.shifted)
+
+    @pl.when(segment == 0)
+    def _():
+        near = n.near[0].astype(F32)
+        for r in range(rows + 2):
+            spread(r, cols, n.result[0, r * cols : (r + 1) * cols, :], near[r : r + 1], n.shifted)
+
+    mix = side_by_side(n.mix[...])
+    for r in range(rows):
+        at = slice(r * cols, (r + 1) * cols)
+        n.hidden[at, :] = pixel_values(n.acts[0, at, :], band.latent(r), mix, mean, rstd)[2].astype(BF16)
+    for row in range(3):
+        n.total[row] += lax.dot_general(
+            n.hidden[...], n.shifted[row * cols : row * cols + pixels, :], TN, preferred_element_type=F32
+        )
+
+    @pl.when(step == micros - 1)
+    def _():
+        half, channels = n.keep.shape
+        for which in range(2):
+            for ref, owner in ((n.keep, which), (n.give, 1 - which)):
+
+                @pl.when(side == owner)
+                def _(ref=ref, first=which * half):
+                    for row in range(3):
+                        for col in range(3):
+                            at = tap_of(row, col) * channels - first
+                            low, high = max(at, 0), min(at + channels, half)
+                            if low < high:
+                                ref[low:high, :] = n.total[row, low - at : high - at, col * channels : (col + 1) * channels]
+
+
+def redo_kernel(rows, cols, bands, micros, count, n, step):
+    channels = n.acts.shape[-1]
+    segment = lax.axis_index("segment")
+    side = lax.axis_index("sub")
+    mean, rstd = statistics(n.packed, step, micros, count)
+    mix = n.packed[2 * micros + 16 * micros :, :]
+    total = n.packed[pl.ds(pl.multiple_of(2 * micros + 16 * step, 8), 16), :]
+    mean_grad, mean_cross = gradient_means(total, mix, count)
+    band = Band(n, step, rows, cols, bands)
+
+    @pl.when(segment == 1)
+    def _():
+        for r in range(rows):
+            at = slice(r * cols, (r + 1) * cols)
+            xhat = (n.acts[0, at, :].astype(F32) - mean) * rstd
+            change = rstd * (n.norm[0, at, :].astype(F32) - mean_grad - xhat * mean_cross)
+            n.result[0, (r + 1) * cols : (r + 2) * cols, :] = (band.row(r)[0].astype(F32) + change).astype(BF16)
+
+    @pl.when(segment == 0)
+    def _():
+        @pl.when(step == 0)
+        def _():
+            arrange_weights(n.kernel, n.weights)
+
+        for r in range(rows + 4):
+            spread(r, cols, *band.row(r - 2), n.shifted)
+        hidden_gradient(rows + 2, cols, n.shifted, n.weights, n.hidden_grad)
+        wide_mix = side_by_side(mix)
+        edges = []
+        for r in range(rows + 2):
+            at = slice(r * cols, (r + 1) * cols)
+            if r == 0:
+                acts = n.above[0]
+            elif r == rows + 1:
+                acts = n.below[0]
+            else:
+                row = slice((r - 1) * cols, r * cols)
+                acts = jnp.where(step < micros // 2, n.passed_early[0, row, :], n.passed_late[0, row, :])
+            xhat, scale, _, slope = pixel_values(acts, band.latent(r - 1), wide_mix, mean, rstd)
+            change = rstd * (n.hidden_grad[at, :] * slope * scale - mean_grad - xhat * mean_cross)
+            value = n.shifted[(r + 1) * cols : (r + 2) * cols, channels : 2 * channels].astype(F32) + change
+            if r == 0 or r == rows + 1:
+                row = band.row_start + (r - 1)
+                value = jnp.where((row >= 0) & (row < band.total_rows), value, 0.0)
+            n.result[0, at, :] = value.astype(BF16)
+            edges.append(jnp.where(side == 0, value[cols - 1 : cols], value[0:1]))
+        edges.append(jnp.zeros((16 - rows - 2, channels), F32))
+        n.edge[0] = jnp.concatenate(edges).astype(BF16)
+
+
+def last_kernel(rows, cols, micros, count, n, step):
+    lower = lax.axis_index("segment") == 0
+
+    @pl.when(step == 0)
+    def _():
+        latents, channels = n.mod_grad.shape[1], n.total_lower.shape[-1]
+        total = jnp.zeros((16, channels), F32)
+        for m in range(micros):
+            at = slice(16 * m, 16 * (m + 1))
+            total = total + jnp.where(lower, n.total_lower[at, :], n.total_upper[at, :])
+        total = jnp.concatenate([total[:8], total[8:]], axis=1)
+        n.mod_grad[0] = total[:latents]
+        n.bias_grad[...] = total[latents : latents + 1]
+
+    @pl.when(lower)
+    def _():
+        mean, rstd = statistics(n.sums, step, micros, count)
+        total = n.total_lower[pl.ds(pl.multiple_of(16 * step, 8), 16), :]
+        mean_grad, mean_cross = gradient_means(total, n.mix[...], count)
+        for r in range(rows):
+            at = slice(r * cols, (r + 1) * cols)
+            xhat = (n.acts[0, at, :].astype(F32) - mean) * rstd
+            change = rstd * (n.norm[0, at, :].astype(F32) - mean_grad - xhat * mean_cross)
+            n.grads[0, at, :] = (n.result[0, (r + 1) * cols : (r + 2) * cols, :].astype(F32) + change).astype(BF16)
+
+    @pl.when(jnp.logical_not(lower))
+    def _():
+        n.grads[0] = n.result[0, cols : (rows + 1) * cols, :]
+
+
+def by_micro(value):
+    if isinstance(value, tuple):
+        value, first, size = value
+        return pl.BlockSpec((1,) + tuple(value.shape[1:]), lambda m: (jnp.clip(m - first, 0, size - 1), 0, 0))
+    rest = (0,) * (len(value.shape) - 1)
+    return pl.BlockSpec((1,) + tuple(value.shape[1:]), lambda m: (m,) + rest)
+
+
+def whole(value):
+    return pl.BlockSpec(tuple(value.shape), lambda m: (0,) * len(value.shape))
+
+
+def call(kernel, name, micros, scalars, fixed, cut, outs, fixed_outs, scratch, work=4, room=62):
+    names = [*scalars, *fixed, *cut, *outs, *fixed_outs, *scratch]
+    cut_shape = [jax.ShapeDtypeStruct(s, d) for s, d in outs.values()]
+    fixed_shape = [jax.ShapeDtypeStruct(s, d) for s, d in fixed_outs.values()]
+
+    def body(*refs):
+        kernel(types.SimpleNamespace(**dict(zip(names, refs))), pl.program_id(0))
+
+    return pl.pallas_call(
+        body,
+        grid=(micros,),
+        in_specs=[pl.BlockSpec(memory_space=pltpu.SMEM) for _ in scalars]
+        + [whole(v) for v in fixed.values()]
+        + [by_micro(v) for v in cut.values()],
+        out_specs=[by_micro(s) for s in cut_shape] + [whole(s) for s in fixed_shape],
+        out_shape=cut_shape + fixed_shape,
+        scratch_shapes=[pltpu.VMEM(s, d) for s, d in scratch.values()],
+        compiler_params=pltpu.CompilerParams(vmem_limit_bytes=room * 1024 * 1024),
+        cost_estimate=pl.CostEstimate(flops=work, bytes_accessed=work // 4, transcendentals=0),
+        name=name,
+    )(*scalars.values(), *fixed.values(), *[v[0] if isinstance(v, tuple) else v for v in cut.values()])
+
+
+def pair_body(
+    activations, latent, recon, target, boxes, kernel, mod_weight, scale_bias, shift_bias, out_weight
+):
+    micros, rows, cols, channels = activations.shape[1:]
+    latents = latent.shape[1]
+    pixels = rows * cols
+    bands = lax.axis_size("rows")
+    count = float(pixels * bands * 2 * (channels // GROUPS))
+    segment = lax.axis_index("segment")
+    side = lax.axis_index("sub")
+    acts = activations[0].reshape(micros, pixels, channels)
+
+    early = micros // 2
+    passed = [swap(acts[:early], "segment"), swap(acts[early:], "segment")]
+    above = swap_and_shift(acts[:, pixels - cols :], 1)
+    below = swap_and_shift(acts[:, :cols], bands - 1)
+    kernel_passed = swap(kernel[0], "segment")
+    recon_beside, target_beside = swap(recon, "sub"), swap(target, "sub")
+
+    (sums,) = call(sums_kernel, "input_sums", micros, {}, {}, {"acts": acts}, {}, {"sums": ((2 * micros, channels), F32)}, {}, room=16)
+    sums = sums + swap(sums, "sub")
+
+    def border(first, r):
+        def difference(one, two):
+            part = slice(first, first + 2)
+            return (one[:, :, part].astype(F32) - two[:, :, part].astype(F32)).transpose(0, 2, 1, 3)
+
+        extra = latent[:, :, r].astype(F32).reshape(micros, 2, latents // 2, cols)
+        two = jnp.concatenate([difference(recon, target), difference(recon_beside, target_beside), extra], axis=2)
+        return jnp.concatenate([sums, two.reshape(micros * 16, cols)])
+
+    from_up = shift(border(rows - 2, rows - 1), "rows", 1)
+    from_down = shift(border(0, 0), "rows", bands - 1)
+    across = shift(sums, "rows", 2)
+
+    from_up, above, below, kernel_passed = lax.optimization_barrier((from_up, above, below, kernel_passed))
+    image = {
+        "latent": latent,
+        "recon": recon,
+        "target": target,
+        "recon_beside": recon_beside,
+        "target_beside": target_beside,
+    }
+    borders = {"from_up": from_up, "from_down": from_down, "out_weight": out_weight}
+    wide = (rows + 2) * cols
+    triple = 3 * channels
+    shifted = {"shifted": ((wide, triple), BF16)}
+    work = {
+        **shifted,
+        "weights": ((3, channels, triple), BF16),
+        "hidden_grad": ((pixels, channels), F32),
+        "latent_keep": ((8, pixels), BF16),
+        "pairs": ((pixels, 2 * channels), BF16),
+    }
+    produced = {"norm": ((micros, pixels, channels), BF16), "reduced": ((micros, 16, channels), F32)}
+    size = (rows, cols, bands, micros, count)
+    norm_upper, reduced = call(
+        functools.partial(upper_kernel, *size),
+        "upper_block",
+        micros,
+        {"boxes": boxes},
+        {
+            "sums": sums,
+            "across": across,
+            "mod_weight": mod_weight,
+            "scale_bias": scale_bias,
+            "shift_bias": shift_bias,
+            "kernel": kernel[0],
+            **borders,
+        },
+        {"acts": acts, **image},
+        produced,
+        {},
+        {**work, "sums_keep": ((2 * micros, channels), F32)},
+    )
+    reduced, passed[0] = lax.optimization_barrier((reduced, passed[0]))
+    total_upper = pixel_total(reduced.reshape(micros * 16, channels))
+    sums = (sums + across) + (from_up[: 2 * micros] + from_down[: 2 * micros])
+    mix = jnp.concatenate([mod_weight[0], jnp.concatenate([scale_bias, shift_bias], axis=1)]).astype(F32)
+    mix = jnp.pad(mix, ((0, 7 - latents), (0, 0)))
+    mix = jnp.concatenate([mix[:, :channels], mix[:, channels:]])
+    packed = jnp.concatenate([sums, total_upper, mix])
+    packed, passed[1] = lax.optimization_barrier((packed, passed[1]))
+    packed = jnp.where(segment == 0, swap(packed, "segment"), packed)
+    result, edge = call(
+        functools.partial(redo_kernel, *size),
+        "redo_upper",
+        micros,
+        {"boxes": boxes},
+        {"packed": packed, "kernel": kernel_passed, **borders},
+        {
+            "acts": acts,
+            "norm": norm_upper,
+            "passed_early": (passed[0], 0, early),
+            "passed_late": (passed[1], early, micros - early),
+            "above": above,
+            "below": below,
+            **image,
+        },
+        {"result": ((micros, wide, channels), BF16), "edge": ((micros, 16, channels), BF16)},
+        {},
+        {
+            "shifted": (((rows + 4) * cols, triple), BF16),
+            "weights": ((3, channels, triple), BF16),
+            "hidden_grad": ((wide, channels), F32),
+        },
+    )
+    near = swap(edge, "sub")
+    half = kernel.shape[1] // 2
+    keep, give = call(
+        functools.partial(gradient_kernel, *size),
+        "kernel_gradient",
+        micros,
+        {"boxes": boxes},
+        {"sums": sums, "mix": mix, **borders},
+        {"result": result, "near": near, "acts": acts, **image},
+        {},
+        {"keep": ((half, channels), F32), "give": ((half, channels), F32)},
+        {**shifted, "hidden": ((pixels, channels), BF16), "total": ((3, channels, triple), F32)},
+    )
+    keep = (keep + swap(give, "sub")).astype(BF16)
+    others = [shift(keep, "rows", steps) for steps in (1, 2, 3)]
+    norm, reduced = call(
+        functools.partial(lower_kernel, *size),
+        "lower_block",
+        micros,
+        {"boxes": boxes},
+        {"sums": sums, "mix": mix, "kernel": kernel[0], **borders},
+        {"result": result, "near": near, "acts": acts, **image},
+        produced,
+        {},
+        work,
+        work=1 << 27,
+    )
+    total_lower = pixel_total(reduced.reshape(micros * 16, channels))
+    grads, mod_grad, bias_grad = call(
+        functools.partial(last_kernel, rows, cols, micros, count),
+        "input_gradient",
+        micros,
+        {},
+        {"sums": sums, "mix": mix, "total_lower": total_lower, "total_upper": total_upper},
+        {"acts": acts, "norm": norm, "result": result},
+        {"grads": ((micros, pixels, channels), BF16)},
+        {"mod_grad": ((1, latents, 2 * channels), F32), "bias_grad": ((1, 2 * channels), F32)},
+        {},
+        work=1 << 25,
+    )
+    grads, *others = lax.optimization_barrier((grads, *others))
+    one, two, three = [value.astype(F32) for value in others]
+    keep = (keep.astype(F32) + two) + (one + three)
+    give = swap(keep, "sub")
+    kernel_grad = jnp.where(side == 0, jnp.concatenate([keep, give]), jnp.concatenate([give, keep]))
+    return (grads.reshape(activations.shape), kernel_grad[None], mod_grad, bias_grad)
+
+
 def solution(mesh):
+    pair = mesh.shape["segment"] == 2 and mesh.shape["rows"] == 4 and mesh.shape["sub"] == 2
+    body = pair_body if pair else general_body
     placed = (
         P("segment", "groups", "rows", "sub", None),
         P("groups", None, "rows", "sub"),

time: 402 us -> 104 us (0.26)
  blocking collectives: 157 us -> 0 us
  starting transfers between devices: 101 us -> 24.3 us
  Pallas kernels: 0 us -> 34 us
  matrix products: 22.8 us -> 0 us
  waiting for transfers between devices: 54.1 us -> 33.1 us
  other arithmetic: 25.6 us -> 5.15 us
  local copies, waits for them, and re-layouts: 22.2 us -> 5.84 us
  between operations: 14.1 us -> 0.96 us
    psum x11 -> x0, blocking collectives: 157 us -> none  [the longest x5 73.8 us: section_backward(): sum_one, sum_two = lax.psum((sum_one, sum_two), ('rows', 'sub'))]
    ppermute x45 -> x26, starting transfers between devices: 101 us -> 24.3 us  [the longest x12 13.2 us: shift(): lax.ppermute(value, axis, [(i, (i + steps) % count) for i in range(count)])]
    psum x1 -> x0, waiting for transfers between devices: 41 us -> none  [body(): lax.psum((kernel_grad, mod_grad, bias_grad), ('rows', 'sub'))]
    pallas_call x0 -> x6, Pallas kernels: none -> 34 us  [call(): pl.pallas_call(body, grid=(micros,), in_specs=[pl.BlockSpec(memory_space=...]
    dot_general x22 -> x0, matrix products: 22.8 us -> none  [the longest x5 13.9 us: section_backward(): jnp.dot(taps(padded_g, row_count, col_count, True), weights_t, preferred_...]
    ppermute x45 -> x26, waiting for transfers between devices: 13.1 us -> 33.1 us  [the longest x12 18.6 us: shift(): lax.ppermute(value, axis, [(i, (i + steps) % count) for i in range(count)])]
    dynamic_update_slice x5 -> x0, other arithmetic: 10.7 us -> none  [tick(): lax.dynamic_update_slice_in_dim(grads_out, jnp.where(valid, result, curre...]
    reduce_sum x30 -> x0, other arithmetic: 8.56 us -> none  [the longest x10 6.09 us: group_sums(): jnp.sum(shaped, axis=(-4, -3, -1))]
  transfers between devices with their start and end apart: 46 -> 26, of which waited for: 16 -> 13; matrix products, arithmetic and copies ran while one was open for 8% -> 4% of each run, Pallas kernels for 0% -> 15%
where the time goes in v4:
time: 104 us; the launch traced here: 103 us
  Pallas kernels  34 us (33%)
  waiting for transfers between devices  33.1 us (32%)
  starting transfers between devices  24.3 us (23%)
  local copies, waits for them, and re-layouts  5.84 us (6%)
  other arithmetic  5.15 us (5%)
    pallas_call x6, Pallas kernels, call(): pl.pallas_call(body, grid=(micros,), in_specs=[pl.BlockSpec(memory_space=...  34 us
    ppermute x12, waiting for transfers between devices, shift(): lax.ppermute(value, axis, [(i, (i + steps) % count) for i in range(count)])  18.6 us
    ppermute x12, starting transfers between devices, shift(): lax.ppermute(value, axis, [(i, (i + steps) % count) for i in range(count)])  13.2 us
    ppermute x12, waiting for transfers between devices, swap(): return lax.ppermute(value, axis, [(0, 1), (1, 0)])  12.9 us
    ppermute x2, starting transfers between devices, swap_and_shift(): return lax.ppermute(value, ('rows', 'segment'), pairs)  5.66 us
    ppermute x12, starting transfers between devices, swap(): return lax.ppermute(value, axis, [(0, 1), (1, 0)])  5.45 us
    unnamed x46, local copies, waits for them, and re-layouts  4.92 us
  transfers between devices with their start and end apart: 26, of which 13 were waited for; matrix products, arithmetic and copies ran while one was open for 4% of the time, Pallas kernels for 15%

profile of v4, /device:TPU:0, one launch (start us, length us, event | category | flops | bytes accessed | tf_op | source)
XLA Modules:
  0.0 103.3 jit_solution(12778494681521379202)
XLA Ops:
  0.6 0.0 copy-start
  0.6 1.2 %copy-done = bf16[1,4,8,128,128]{4,3,2,1,0:T(8,128)(2,1)S(1)} copy-done((bf16[1,4,8,128,128]{4,3,2,1,0:T(8,128)(2,1)S(1)}, bf16[1,4,8,128,128]{4,3,2,1,0:T(8,128)(2,1)}, u32[]{:S(2)}) %copy-start) | copy-done | bytes 1048600
  1.9 0.6 input_sums.1
  2.5 0.0 copy-start.2
  2.5 0.5 collective-permute-start
  3.0 0.1 collective-permute-start.2
  3.1 0.4 collective-permute-start.3
  3.6 5.7 %collective-permute-start.6 = (bf16[4,128,128]{2,1,0:T(8,128)(2,1)S(1)}, bf16[4,128,128]{2,1,0:T(8,128)(2,1)S(1)}, u32[]{:S(2)}, u32[]{:S(2)}) collective-permute-start(bf16[4,128,128]{2,1,0:T(8,128)(2,1)S(1)} %get-tuple-element.52), channel_id=1, source_target_pairs={{0,14},{2,12},{4,2},{6,0},{8,6},{10,4},{12,10},{14,8},{1,15},{3,13... | collective-permute-start | bytes 393224 | tf_op jit(solution)/shard_map/ppermute | solution.py:273
  9.2 0.5 collective-permute-start.7
  9.8 0.0 copy-start.20
  9.8 0.0 copy-start.21
  9.8 0.0 copy-start.22
  9.8 0.9 fusion.7
  10.7 0.0 collective-permute-done
  10.7 1.6 %collective-permute-start.9 = (bf16[2,1024,128]{2,1,0:T(8,128)(2,1)}, bf16[2,1024,128]{2,1,0:T(8,128)(2,1)S(1)}, u32[]{:S(2)}, u32[]{:S(2)}) collective-permute-start(bf16[2,1024,128]{2,1,0:T(8,128)(2,1)} %bitcast.11), channel_id=1, source_target_pairs={{0,2},{2,0},{1,3},{3,1},{4,6},{6,4},{5,7},{7,5},{8,10},{10,8},{9,1... | collective-permute-start | bytes 1572872 | tf_op jit(solution)/shard_map/ppermute | solution.py:262
  12.3 0.0 collective-permute-done.2.refs_14_.refs_15_.refs_13_.refs_12_
  12.3 0.0 collective-permute-done.3.refs_15_.refs_16_.refs_14_.refs_13_
  12.5 0.5 copy-done.10
  12.9 0.0 collective-permute-start.4
  12.9 0.0 collective-permute-start.5
  12.9 6.2 %collective-permute-done.4.refs_7_.refs_3_.refs_4_ = f32[72,128]{1,0:T(8,128)S(1)} collective-permute-done((f32[72,128]{1,0:T(8,128)S(1)}, f32[72,128]{1,0:T(8,128)S(1)}, u32[]{:S(2)}, u32[]{:S(2)}) %collective-permute-start.4) | collective-permute-done | bytes 36896 | tf_op jit(solution)/shard_map/ppermute | solution.py:267
  19.2 0.5 collective-permute-start.8
  19.7 1.5 %collective-permute-done.5.refs_10_ = bf16[4,128,128]{2,1,0:T(8,128)(2,1)S(1)} collective-permute-done((bf16[4,128,128]{2,1,0:T(8,128)(2,1)S(1)}, bf16[4,128,128]{2,1,0:T(8,128)(2,1)S(1)}, u32[]{:S(2)}, u32[]{:S(2)}) %collective-permute-start.5) | collective-permute-done | bytes 131104 | tf_op jit(solution)/shard_map/ppermute | solution.py:273
  21.2 0.6 copy-done.15
  21.9 0.9 collective-permute-start.14
  22.8 0.7 copy-done.12
  23.6 0.1 collective-permute-done.1.refs_2_
  23.7 0.6 copy-done.19
  24.3 0.6 copy-done.4
  24.9 3.7 %upper_block.1 = (bf16[4,1024,128]{2,1,0:T(8,128)(2,1)}, f32[4,16,128]{2,1,0:T(8,128)}) custom-call(s32[4,4,4]{2,1,0:T(4,128)} %refs_0_.7, f32[8,128]{1,0:T(8,128)} %copy-done.18, f32[8,128]{1,0:T(8,128)} %copy-done.19, bf16[1,4,256]{2,1,0:T(4,128)(2,1)} %refs_3_.1, bf16[1,128]{1,0:T(2,128)(2,1)} %refs_4_.1, bf16[1,128]{1,0:T(2,128)(2,1)} %refs_5_.3, ...), custom_call_target="tpu_custom_call" | custom-call | flops 4 | bytes 1 | tf_op jit(solution)/shard_map/upper_block/pallas_call | solution.py:638
  28.6 4.5 %collective-permute-done.9.refs_8_ = bf16[2,1024,128]{2,1,0:T(8,128)(2,1)S(1)} collective-permute-done((bf16[2,1024,128]{2,1,0:T(8,128)(2,1)}, bf16[2,1024,128]{2,1,0:T(8,128)(2,1)S(1)}, u32[]{:S(2)}, u32[]{:S(2)}) %collective-permute-start.9) | collective-permute-done | bytes 524320 | tf_op jit(solution)/shard_map/ppermute | solution.py:262
  33.1 1.4 %collective-permute-done.10 = f32[64,128]{1,0:T(8,128)S(1)} collective-permute-done((f32[64,128]{1,0:T(8,128)}, f32[64,128]{1,0:T(8,128)S(1)}, u32[]{:S(2)}, u32[]{:S(2)}) %collective-permute-start.10) | collective-permute-done | bytes 32800 | tf_op jit(solution)/shard_map/ppermute | solution.py:262
  34.5 0.8 bitcast_add_fusion.1
  35.3 3.3 %collective-permute-start.13 = (f32[64,128]{1,0:T(8,128)S(1)}, f32[64,128]{1,0:T(8,128)S(1)}, u32[]{:S(2)}, u32[]{:S(2)}) collective-permute-start(f32[64,128]{1,0:T(8,128)S(1)} %bitcast_add_fusion.1), channel_id=1, source_target_pairs={{0,12},{4,0},{8,4},{12,8},{1,13},{5,1},{9,5},{13,9},{2,14},{6,2},{... | collective-permute-start | bytes 98312 | tf_op jit(solution)/shard_map/ppermute | solution.py:267
  38.6 0.6 collective-permute-start.11
  39.2 0.7 fusion.6.refs_1_.refs_0_
  39.9 0.3 collective-permute-done.13
  40.2 4.0 %collective-permute-done.12 = f32[64,128]{1,0:T(8,128)S(1)} collective-permute-done((f32[64,128]{1,0:T(8,128)S(1)}, f32[64,128]{1,0:T(8,128)S(1)}, u32[]{:S(2)}, u32[]{:S(2)}) %collective-permute-start.12) | collective-permute-done | bytes 32800 | tf_op jit(solution)/shard_map/ppermute | solution.py:267
  44.3 0.6 collective-permute-start.15
  44.9 3.5 %collective-permute-done.15 = f32[88,128]{1,0:T(8,128)S(1)} collective-permute-done((f32[88,128]{1,0:T(8,128)S(1)}, f32[88,128]{1,0:T(8,128)S(1)}, u32[]{:S(2)}, u32[]{:S(2)}) %collective-permute-start.15) | collective-permute-done | bytes 45088 | tf_op jit(solution)/shard_map/ppermute | solution.py:262
  48.4 0.6 broadcast_select_fusion.refs_1_
  49.1 10.3 %redo_upper.1 = (bf16[4,1280,128]{2,1,0:T(8,128)(2,1)}, bf16[4,16,128]{2,1,0:T(8,128)(2,1)}) custom-call(s32[4,4,4]{2,1,0:T(4,128)} %refs_0_.7, f32[88,128]{1,0:T(8,128)} %broadcast_select_fusion.refs_1_, bf16[1152,128]{1,0:T(8,128)(2,1)} %copy-done.12, f32[72,128]{1,0:T(8,128)} %copy-done.3, f32[72,128]{1,0:T(8,128)} %copy-done.4, bf16[3,128]{1,0:T(4,128)(2,1)} %refs_5_.5, ...), custom_call_target="tpu_custom_call" | custom-call | flops 4 | bytes 1 | tf_op jit(solution)/shard_map/redo_upper/pallas_call | solution.py:638
  59.4 0.1 collective-permute-start.16
  59.5 0.6 pad_maximum_fusion.5.refs_2_.refs_1_
  60.1 0.8 collective-permute-done.16.refs_8_.refs_7_
  60.8 0.6 copy-done.17
  61.4 7.4 %kernel_gradient.1 = (f32[576,128]{1,0:T(8,128)}, f32[576,128]{1,0:T(8,128)}) custom-call(s32[4,4,4]{2,1,0:T(4,128)} %refs_0_.7, f32[8,128]{1,0:T(8,128)} %copy-done.16, f32[16,128]{1,0:T(8,128)} %pad_maximum_fusion.5.refs_2_.refs_1_, f32[72,128]{1,0:T(8,128)} %copy-done.3, f32[72,128]{1,0:T(8,128)} %copy-done.4, bf16[3,128]{1,0:T(4,128)(2,1)} %refs_5_.5, ...), custom_call_target="tpu_custom_call" | custom-call | flops 4 | bytes 1 | tf_op jit(solution)/shard_map/kernel_gradient/pallas_call | solution.py:638
  68.9 0.2 collective-permute-start.21
  69.1 7.4 %lower_block.1 = (bf16[4,1024,128]{2,1,0:T(8,128)(2,1)}, f32[4,16,128]{2,1,0:T(8,128)}) custom-call(s32[4,4,4]{2,1,0:T(4,128)} %refs_0_.7, f32[8,128]{1,0:T(8,128)} %copy-done.16, f32[16,128]{1,0:T(8,128)} %pad_maximum_fusion.5.refs_2_.refs_1_, bf16[1152,128]{1,0:T(8,128)(2,1)} %bitcast.33, f32[72,128]{1,0:T(8,128)} %copy-done.3, f32[72,128]{1,0:T(8,128)} %copy-done.4, ...), custom_call_target="tpu_custom_call" | custom-call | flops 134217728 | bytes 33554432 | tf_op jit(solution)/shard_map/lower_block/pallas_call | solution.py:638
  76.5 0.4 collective-permute-start.17
  76.9 1.1 %collective-permute-done.17 = f32[64,128]{1,0:T(8,128)S(1)} collective-permute-done((f32[64,128]{1,0:T(8,128)}, f32[64,128]{1,0:T(8,128)S(1)}, u32[]{:S(2)}, u32[]{:S(2)}) %collective-permute-start.17) | collective-permute-done | bytes 32800 | tf_op jit(solution)/shard_map/ppermute | solution.py:262
  78.0 0.8 bitcast_add_fusion
  78.8 2.9 %collective-permute-start.20 = (f32[64,128]{1,0:T(8,128)S(1)}, f32[64,128]{1,0:T(8,128)S(1)}, u32[]{:S(2)}, u32[]{:S(2)}) collective-permute-start(f32[64,128]{1,0:T(8,128)S(1)} %bitcast_add_fusion), channel_id=1, source_target_pairs={{0,12},{4,0},{8,4},{12,8},{1,13},{5,1},{9,5},{13,9},{2,14},{6,2},{... | collective-permute-start | bytes 98312 | tf_op jit(solution)/shard_map/ppermute | solution.py:267
  81.7 0.6 collective-permute-start.18
  82.4 3.3 %collective-permute-start.24 = (bf16[576,128]{1,0:T(8,128)(2,1)S(1)}, bf16[576,128]{1,0:T(8,128)(2,1)S(1)}, u32[]{:S(2)}, u32[]{:S(2)}) collective-permute-start(bf16[576,128]{1,0:T(8,128)(2,1)S(1)} %add_convert_fusion), channel_id=1, source_target_pairs={{0,12},{4,0},{8,4},{12,8},{1,13},{5,1},{9,5},{13,9},{2,14},{6,2},{... | collective-permute-start | bytes 442376 | tf_op jit(solution)/shard_map/ppermute | solution.py:267
  85.6 2.0 %collective-permute-start.23 = (bf16[576,128]{1,0:T(8,128)(2,1)S(1)}, bf16[576,128]{1,0:T(8,128)(2,1)S(1)}, u32[]{:S(2)}, u32[]{:S(2)}) collective-permute-start(bf16[576,128]{1,0:T(8,128)(2,1)S(1)} %add_convert_fusion), channel_id=1, source_target_pairs={{0,8},{4,12},{8,0},{12,4},{1,9},{5,13},{9,1},{13,5},{2,10},{6,14},... | collective-permute-start | bytes 442376 | tf_op jit(solution)/shard_map/ppermute | solution.py:267
  87.6 0.1 collective-permute-done.19
  87.8 0.6 add_add_fusion.1.refs_2_
  88.4 4.6 %input_gradient.1 = (bf16[4,1024,128]{2,1,0:T(8,128)(2,1)}, f32[1,4,256]{2,1,0:T(4,128)}, f32[1,256]{1,0:T(1,128)}) custom-call(f32[8,128]{1,0:T(8,128)} %copy-done.16, f32[16,128]{1,0:T(8,128)} %pad_maximum_fusion.5.refs_2_.refs_1_, f32[64,128]{1,0:T(8,128)} %add_add_fusion.1.refs_2_, f32[64,128]{1,0:T(8,128)} %copy-done.11, ...), custom_call_target="tpu_custom_call" | custom-call | flops 33554432 | bytes 8388608 | tf_op jit(solution)/shard_map/input_gradient/pallas_call | solution.py:638
  93.0 7.8 %collective-permute-done.23 = bf16[576,128]{1,0:T(8,128)(2,1)S(1)} collective-permute-done((bf16[576,128]{1,0:T(8,128)(2,1)S(1)}, bf16[576,128]{1,0:T(8,128)(2,1)S(1)}, u32[]{:S(2)}, u32[]{:S(2)}) %collective-permute-start.23) | collective-permute-done | bytes 147488 | tf_op jit(solution)/shard_map/ppermute | solution.py:267
  100.7 0.1 add_add_fusion
  100.8 0.1 collective-permute-start.25
  100.9 1.6 %collective-permute-done.25 = f32[576,128]{1,0:T(8,128)S(1)} collective-permute-done((f32[576,128]{1,0:T(8,128)S(1)}, f32[576,128]{1,0:T(8,128)S(1)}, u32[]{:S(2)}, u32[]{:S(2)}) %collective-permute-start.25) | collective-permute-done | bytes 294944 | tf_op jit(solution)/shard_map/ppermute | solution.py:262
  102.4 0.9 maximum_select_fusion
  (65 shorter events, 0.3 us)
Async XLA Ops:
  0.6 1.2 %copy-start = (bf16[1,4,8,128,128]{4,3,2,1,0:T(8,128)(2,1)S(1)}, bf16[1,4,8,128,128]{4,3,2,1,0:T(8,128)(2,1)}, u32[]{:S(2)}) copy-start(bf16[1,4,8,128,128]{4,3,2,1,0:T(8,128)(2,1)} %param.10) | copy-start | bytes 3145732
  1.9 7.4 %copy-start.1 = (bf16[1,1152,128]{2,1,0:T(8,128)(2,1)S(1)}, bf16[1,1152,128]{2,1,0:T(8,128)(2,1)}, u32[]{:S(2)}) copy-start(bf16[1,1152,128]{2,1,0:T(8,128)(2,1)} %param.15) | copy-start | bytes 884740
  1.9 7.9 %copy-start.7 = (bf16[4,3,8,128]{3,2,1,0:T(8,128)(2,1)S(1)}, bf16[4,3,8,128]{3,2,1,0:T(8,128)(2,1)}, u32[]{:S(2)}) copy-start(bf16[4,3,8,128]{3,2,1,0:T(8,128)(2,1)} %refs_11_.5) | copy-start | bytes 73732
  1.9 7.9 %copy-start.8 = (bf16[4,3,8,128]{3,2,1,0:T(8,128)(2,1)S(1)}, bf16[4,3,8,128]{3,2,1,0:T(8,128)(2,1)}, u32[]{:S(2)}) copy-start(bf16[4,3,8,128]{3,2,1,0:T(8,128)(2,1)} %refs_10_.3) | copy-start | bytes 73732
  2.5 8.2 %copy-start.2 = (bf16[4,4,8,128]{3,2,1,0:T(8,128)(2,1)S(1)}, bf16[4,4,8,128]{3,2,1,0:T(8,128)(2,1)}, u32[]{:S(2)}) copy-start(bf16[4,4,8,128]{3,2,1,0:T(8,128)(2,1)} %refs_9_.3) | copy-start | bytes 98308
  2.5 8.2 %collective-permute-start = (f32[8,128]{1,0:T(8,128)S(1)}, f32[8,128]{1,0:T(8,128)S(1)}, u32[]{:S(2)}, u32[]{:S(2)}) collective-permute-start(f32[8,128]{1,0:T(8,128)S(1)} %input_sums.1), channel_id=1, source_target_pairs={{0,1},{1,0},{2,3},{3,2},{4,5},{5,4},{6,7},{7,6},{8,9},{9,8},{10,11... | collective-permute-start | bytes 12296 | tf_op jit(solution)/shard_map/ppermute | solution.py:262
  3.0 9.3 %collective-permute-start.2 = (bf16[4,3,8,128]{3,2,1,0:T(8,128)(2,1)}, bf16[4,3,8,128]{3,2,1,0:T(8,128)(2,1)S(1)}, u32[]{:S(2)}, u32[]{:S(2)}) collective-permute-start(bf16[4,3,8,128]{3,2,1,0:T(8,128)(2,1)} %refs_10_.3), channel_id=1, source_target_pairs={{0,1},{1,0},{2,3},{3,2},{4,5},{5,4},{6,7},{7,6},{8,9},{9,8},{10,11... | collective-permute-start | bytes 73736 | tf_op jit(solution)/shard_map/ppermute | solution.py:262
  3.1 9.2 %collective-permute-start.3 = (bf16[4,3,8,128]{3,2,1,0:T(8,128)(2,1)}, bf16[4,3,8,128]{3,2,1,0:T(8,128)(2,1)S(1)}, u32[]{:S(2)}, u32[]{:S(2)}) collective-permute-start(bf16[4,3,8,128]{3,2,1,0:T(8,128)(2,1)} %refs_11_.5), channel_id=1, source_target_pairs={{0,1},{1,0},{2,3},{3,2},{4,5},{5,4},{6,7},{7,6},{8,9},{9,8},{10,11... | collective-permute-start | bytes 73736 | tf_op jit(solution)/shard_map/ppermute | solution.py:262
  3.6 15.6 %collective-permute-start.6 = (bf16[4,128,128]{2,1,0:T(8,128)(2,1)S(1)}, bf16[4,128,128]{2,1,0:T(8,128)(2,1)S(1)}, u32[]{:S(2)}, u32[]{:S(2)}) collective-permute-start(bf16[4,128,128]{2,1,0:T(8,128)(2,1)S(1)} %get-tuple-element.52), channel_id=1, source_target_pairs={{0,14},{2,12},{4,2},{6,0},{8,6},{10,4},{12,10},{14,8},{1,15},{3,13... | collective-permute-start | bytes 393224 | tf_op jit(solution)/shard_map/ppermute | solution.py:273
  9.2 13.6 %collective-permute-start.7 = (bf16[1152,128]{1,0:T(8,128)(2,1)S(1)}, bf16[1152,128]{1,0:T(8,128)(2,1)S(1)}, u32[]{:S(2)}, u32[]{:S(2)}) collective-permute-start(bf16[1152,128]{1,0:T(8,128)(2,1)S(1)} %bitcast.34), channel_id=1, source_target_pairs={{0,2},{2,0},{1,3},{3,1},{4,6},{6,4},{5,7},{7,5},{8,10},{10,8},{9,1... | collective-permute-start | bytes 884744 | tf_op jit(solution)/shard_map/ppermute | solution.py:262
  9.8 9.9 %copy-start.20 = (bf16[1,4,256]{2,1,0:T(4,128)(2,1)S(1)}, bf16[1,4,256]{2,1,0:T(4,128)(2,1)}, u32[]{:S(2)}) copy-start(bf16[1,4,256]{2,1,0:T(4,128)(2,1)} %refs_3_.1) | copy-start | bytes 6148
  9.8 9.9 %copy-start.21 = (bf16[1,128]{1,0:T(2,128)(2,1)S(1)}, bf16[1,128]{1,0:T(2,128)(2,1)}, u32[]{:S(2)}) copy-start(bf16[1,128]{1,0:T(2,128)(2,1)} %refs_5_.3) | copy-start | bytes 772
  9.8 9.9 %copy-start.22 = (bf16[1,128]{1,0:T(2,128)(2,1)S(1)}, bf16[1,128]{1,0:T(2,128)(2,1)}, u32[]{:S(2)}) copy-start(bf16[1,128]{1,0:T(2,128)(2,1)} %refs_4_.1) | copy-start | bytes 772
  10.7 22.4 %collective-permute-start.9 = (bf16[2,1024,128]{2,1,0:T(8,128)(2,1)}, bf16[2,1024,128]{2,1,0:T(8,128)(2,1)S(1)}, u32[]{:S(2)}, u32[]{:S(2)}) collective-permute-start(bf16[2,1024,128]{2,1,0:T(8,128)(2,1)} %bitcast.11), channel_id=1, source_target_pairs={{0,2},{2,0},{1,3},{3,1},{4,6},{6,4},{5,7},{7,5},{8,10},{10,8},{9,1... | collective-permute-start | bytes 1572872 | tf_op jit(solution)/shard_map/ppermute | solution.py:262
  12.3 11.4 %copy-start.18 = (f32[8,128]{1,0:T(8,128)}, f32[8,128]{1,0:T(8,128)S(1)}, u32[]{:S(2)}) copy-start(f32[8,128]{1,0:T(8,128)S(1)} %add.50.refs_1_) | copy-start | bytes 12292
  12.3 11.4 %copy-start.9 = (bf16[4,3,8,128]{3,2,1,0:T(8,128)(2,1)}, bf16[4,3,8,128]{3,2,1,0:T(8,128)(2,1)S(1)}, u32[]{:S(2)}) copy-start(bf16[4,3,8,128]{3,2,1,0:T(8,128)(2,1)S(1)} %collective-permute-done.2.refs_14_.refs_15_.refs_13_.refs_12_) | copy-start | bytes 73732
  12.3 0.6 copy-start.10
  12.9 6.2 %collective-permute-start.4 = (f32[72,128]{1,0:T(8,128)S(1)}, f32[72,128]{1,0:T(8,128)S(1)}, u32[]{:S(2)}, u32[]{:S(2)}) collective-permute-start(f32[72,128]{1,0:T(8,128)S(1)} %get-tuple-element.62), channel_id=1, source_target_pairs={{0,4},{4,8},{8,12},{12,0},{1,5},{5,9},{9,13},{13,1},{2,6},{6,10},{... | collective-permute-start | bytes 110600 | tf_op jit(solution)/shard_map/ppermute | solution.py:267
  12.9 8.3 %collective-permute-start.5 = (bf16[4,128,128]{2,1,0:T(8,128)(2,1)S(1)}, bf16[4,128,128]{2,1,0:T(8,128)(2,1)S(1)}, u32[]{:S(2)}, u32[]{:S(2)}) collective-permute-start(bf16[4,128,128]{2,1,0:T(8,128)(2,1)S(1)} %get-tuple-element.53), channel_id=1, source_target_pairs={{0,6},{2,4},{4,10},{6,8},{8,14},{10,12},{12,2},{14,0},{1,7},{3,5},... | collective-permute-start | bytes 393224 | tf_op jit(solution)/shard_map/ppermute | solution.py:273
  19.2 4.5 %copy-start.3 = (f32[72,128]{1,0:T(8,128)}, f32[72,128]{1,0:T(8,128)S(1)}, u32[]{:S(2)}) copy-start(f32[72,128]{1,0:T(8,128)S(1)} %collective-permute-done.4.refs_7_.refs_3_.refs_4_) | copy-start | bytes 110596
  19.2 4.5 %collective-permute-start.1 = (f32[8,128]{1,0:T(8,128)S(1)}, f32[8,128]{1,0:T(8,128)S(1)}, u32[]{:S(2)}, u32[]{:S(2)}) collective-permute-start(f32[8,128]{1,0:T(8,128)S(1)} %add.50.refs_1_), channel_id=1, source_target_pairs={{0,8},{4,12},{8,0},{12,4},{1,9},{5,13},{9,1},{13,5},{2,10},{6,14},... | collective-permute-start | bytes 12296 | tf_op jit(solution)/shard_map/ppermute | solution.py:267
  19.2 2.0 %copy-start.14 = (bf16[4,128,128]{2,1,0:T(8,128)(2,1)}, bf16[4,128,128]{2,1,0:T(8,128)(2,1)S(1)}, u32[]{:S(2)}) copy-start(bf16[4,128,128]{2,1,0:T(8,128)(2,1)S(1)} %collective-permute-done.6.refs_11_) | copy-start | bytes 393220
  19.2 4.5 %collective-permute-start.8 = (f32[72,128]{1,0:T(8,128)S(1)}, f32[72,128]{1,0:T(8,128)S(1)}, u32[]{:S(2)}, u32[]{:S(2)}) collective-permute-start(f32[72,128]{1,0:T(8,128)S(1)} %get-tuple-element.63), channel_id=1, source_target_pairs={{0,12},{4,0},{8,4},{12,8},{1,13},{5,1},{9,5},{13,9},{2,14},{6,2},{... | collective-permute-start | bytes 110600 | tf_op jit(solution)/shard_map/ppermute | solution.py:267
  21.2 0.6 copy-start.15
  21.9 22.4 %collective-permute-start.14 = (bf16[2,1024,128]{2,1,0:T(8,128)(2,1)S(1)}, bf16[2,1024,128]{2,1,0:T(8,128)(2,1)S(1)}, u32[]{:S(2)}, u32[]{:S(2)}) collective-permute-start(bf16[2,1024,128]{2,1,0:T(8,128)(2,1)S(1)} %bitcast.35), channel_id=1, source_target_pairs={{0,2},{2,0},{1,3},{3,1},{4,6},{6,4},{5,7},{7,5},{8,10},{10,8},{9,1... | collective-permute-start | bytes 1572872 | tf_op jit(solution)/shard_map/ppermute | solution.py:262
  22.8 0.7 copy-start.12
  23.7 0.6 copy-start.19
  24.3 0.6 copy-start.4
  33.1 15.9 %copy-start.5 = (bf16[2,1024,128]{2,1,0:T(8,128)(2,1)}, bf16[2,1024,128]{2,1,0:T(8,128)(2,1)S(1)}, u32[]{:S(2)}) copy-start(bf16[2,1024,128]{2,1,0:T(8,128)(2,1)S(1)} %collective-permute-done.9.refs_8_) | copy-start | bytes 1572868
  33.1 1.4 %collective-permute-start.10 = (f32[64,128]{1,0:T(8,128)}, f32[64,128]{1,0:T(8,128)S(1)}, u32[]{:S(2)}, u32[]{:S(2)}) collective-permute-start(f32[64,128]{1,0:T(8,128)} %bitcast.39), channel_id=1, source_target_pairs={{0,1},{1,0},{2,3},{3,2},{4,5},{5,4},{6,7},{7,6},{8,9},{9,8},{10,11... | collective-permute-start | bytes 98312 | tf_op jit(solution)/shard_map/ppermute | solution.py:262
  35.3 4.9 %collective-permute-start.13 = (f32[64,128]{1,0:T(8,128)S(1)}, f32[64,128]{1,0:T(8,128)S(1)}, u32[]{:S(2)}, u32[]{:S(2)}) collective-permute-start(f32[64,128]{1,0:T(8,128)S(1)} %bitcast_add_fusion.1), channel_id=1, source_target_pairs={{0,12},{4,0},{8,4},{12,8},{1,13},{5,1},{9,5},{13,9},{2,14},{6,2},{... | collective-permute-start | bytes 98312 | tf_op jit(solution)/shard_map/ppermute | solution.py:267
  38.6 5.7 %collective-permute-start.12 = (f32[64,128]{1,0:T(8,128)S(1)}, f32[64,128]{1,0:T(8,128)S(1)}, u32[]{:S(2)}, u32[]{:S(2)}) collective-permute-start(f32[64,128]{1,0:T(8,128)S(1)} %bitcast_add_fusion.1), channel_id=1, source_target_pairs={{0,4},{4,8},{8,12},{12,0},{1,5},{5,9},{9,13},{13,1},{2,6},{6,10},{... | collective-permute-start | bytes 98312 | tf_op jit(solution)/shard_map/ppermute | solution.py:267
  38.6 5.7 %collective-permute-start.11 = (f32[64,128]{1,0:T(8,128)S(1)}, f32[64,128]{1,0:T(8,128)S(1)}, u32[]{:S(2)}, u32[]{:S(2)}) collective-permute-start(f32[64,128]{1,0:T(8,128)S(1)} %bitcast_add_fusion.1), channel_id=1, source_target_pairs={{0,8},{4,12},{8,0},{12,4},{1,9},{5,13},{9,1},{13,5},{2,10},{6,14},... | collective-permute-start | bytes 98312 | tf_op jit(solution)/shard_map/ppermute | solution.py:267
  39.9 19.5 %copy-start.16 = (f32[8,128]{1,0:T(8,128)}, f32[8,128]{1,0:T(8,128)S(1)}, u32[]{:S(2)}) copy-start(f32[8,128]{1,0:T(8,128)S(1)} %fusion.6.refs_1_.refs_0_) | copy-start | bytes 12292
  44.3 32.2 %copy-start.11 = (f32[64,128]{1,0:T(8,128)}, f32[64,128]{1,0:T(8,128)S(1)}, u32[]{:S(2)}) copy-start(f32[64,128]{1,0:T(8,128)S(1)} %add_add_fusion.2.refs_3_) | copy-start | bytes 98308
  44.3 4.7 %copy-start.6 = (bf16[2,1024,128]{2,1,0:T(8,128)(2,1)}, bf16[2,1024,128]{2,1,0:T(8,128)(2,1)S(1)}, u32[]{:S(2)}) copy-start(bf16[2,1024,128]{2,1,0:T(8,128)(2,1)S(1)} %collective-permute-done.14.refs_9_) | copy-start | bytes 1572868
  44.3 4.1 %collective-permute-start.15 = (f32[88,128]{1,0:T(8,128)S(1)}, f32[88,128]{1,0:T(8,128)S(1)}, u32[]{:S(2)}, u32[]{:S(2)}) collective-permute-start(f32[88,128]{1,0:T(8,128)S(1)} %pad_maximum_fusion.2), channel_id=1, source_target_pairs={{0,2},{2,0},{1,3},{3,1},{4,6},{6,4},{5,7},{7,5},{8,10},{10,8},{9,1... | collective-permute-start | bytes 135176 | tf_op jit(solution)/shard_map/ppermute | solution.py:262
  59.4 1.5 %collective-permute-start.16 = (bf16[4,16,128]{2,1,0:T(8,128)(2,1)}, bf16[4,16,128]{2,1,0:T(8,128)(2,1)S(1)}, u32[]{:S(2)}, u32[]{:S(2)}) collective-permute-start(bf16[4,16,128]{2,1,0:T(8,128)(2,1)} %get-tuple-element.38), channel_id=1, source_target_pairs={{0,1},{1,0},{2,3},{3,2},{4,5},{5,4},{6,7},{7,6},{8,9},{9,8},{10,11... | collective-permute-start | bytes 49160 | tf_op jit(solution)/shard_map/ppermute | solution.py:262
  60.8 0.6 copy-start.17
  68.9 13.4 %copy-start.13 = (f32[576,128]{1,0:T(8,128)S(1)}, f32[576,128]{1,0:T(8,128)}, u32[]{:S(2)}) copy-start(f32[576,128]{1,0:T(8,128)} %get-tuple-element.42) | copy-start | bytes 884740
  68.9 13.4 %collective-permute-start.21 = (f32[576,128]{1,0:T(8,128)}, f32[576,128]{1,0:T(8,128)S(1)}, u32[]{:S(2)}, u32[]{:S(2)}) collective-permute-start(f32[576,128]{1,0:T(8,128)} %get-tuple-element.43), channel_id=1, source_target_pairs={{0,1},{1,0},{2,3},{3,2},{4,5},{5,4},{6,7},{7,6},{8,9},{9,8},{10,11... | collective-permute-start | bytes 884744 | tf_op jit(solution)/shard_map/ppermute | solution.py:262
  76.5 1.5 %collective-permute-start.17 = (f32[64,128]{1,0:T(8,128)}, f32[64,128]{1,0:T(8,128)S(1)}, u32[]{:S(2)}, u32[]{:S(2)}) collective-permute-start(f32[64,128]{1,0:T(8,128)} %bitcast.40), channel_id=1, source_target_pairs={{0,1},{1,0},{2,3},{3,2},{4,5},{5,4},{6,7},{7,6},{8,9},{9,8},{10,11... | collective-permute-start | bytes 98312 | tf_op jit(solution)/shard_map/ppermute | solution.py:262
  78.8 8.9 %collective-permute-start.20 = (f32[64,128]{1,0:T(8,128)S(1)}, f32[64,128]{1,0:T(8,128)S(1)}, u32[]{:S(2)}, u32[]{:S(2)}) collective-permute-start(f32[64,128]{1,0:T(8,128)S(1)} %bitcast_add_fusion), channel_id=1, source_target_pairs={{0,12},{4,0},{8,4},{12,8},{1,13},{5,1},{9,5},{13,9},{2,14},{6,2},{... | collective-permute-start | bytes 98312 | tf_op jit(solution)/shard_map/ppermute | solution.py:267
  81.7 6.1 %collective-permute-start.19 = (f32[64,128]{1,0:T(8,128)S(1)}, f32[64,128]{1,0:T(8,128)S(1)}, u32[]{:S(2)}, u32[]{:S(2)}) collective-permute-start(f32[64,128]{1,0:T(8,128)S(1)} %bitcast_add_fusion), channel_id=1, source_target_pairs={{0,4},{4,8},{8,12},{12,0},{1,5},{5,9},{9,13},{13,1},{2,6},{6,10},{... | collective-permute-start | bytes 98312 | tf_op jit(solution)/shard_map/ppermute | solution.py:267
  81.7 6.1 %collective-permute-start.18 = (f32[64,128]{1,0:T(8,128)S(1)}, f32[64,128]{1,0:T(8,128)S(1)}, u32[]{:S(2)}, u32[]{:S(2)}) collective-permute-start(f32[64,128]{1,0:T(8,128)S(1)} %bitcast_add_fusion), channel_id=1, source_target_pairs={{0,8},{4,12},{8,0},{12,4},{1,9},{5,13},{9,1},{13,5},{2,10},{6,14},... | collective-permute-start | bytes 98312 | tf_op jit(solution)/shard_map/ppermute | solution.py:267
  82.4 10.6 %collective-permute-start.24 = (bf16[576,128]{1,0:T(8,128)(2,1)S(1)}, bf16[576,128]{1,0:T(8,128)(2,1)S(1)}, u32[]{:S(2)}, u32[]{:S(2)}) collective-permute-start(bf16[576,128]{1,0:T(8,128)(2,1)S(1)} %add_convert_fusion), channel_id=1, source_target_pairs={{0,12},{4,0},{8,4},{12,8},{1,13},{5,1},{9,5},{13,9},{2,14},{6,2},{... | collective-permute-start | bytes 442376 | tf_op jit(solution)/shard_map/ppermute | solution.py:267
  85.6 15.1 %collective-permute-start.23 = (bf16[576,128]{1,0:T(8,128)(2,1)S(1)}, bf16[576,128]{1,0:T(8,128)(2,1)S(1)}, u32[]{:S(2)}, u32[]{:S(2)}) collective-permute-start(bf16[576,128]{1,0:T(8,128)(2,1)S(1)} %add_convert_fusion), channel_id=1, source_target_pairs={{0,8},{4,12},{8,0},{12,4},{1,9},{5,13},{9,1},{13,5},{2,10},{6,14},... | collective-permute-start | bytes 442376 | tf_op jit(solution)/shard_map/ppermute | solution.py:267
  87.6 13.1 %collective-permute-start.22 = (bf16[576,128]{1,0:T(8,128)(2,1)S(1)}, bf16[576,128]{1,0:T(8,128)(2,1)S(1)}, u32[]{:S(2)}, u32[]{:S(2)}) collective-permute-start(bf16[576,128]{1,0:T(8,128)(2,1)S(1)} %add_convert_fusion), channel_id=1, source_target_pairs={{0,4},{4,8},{8,12},{12,0},{1,5},{5,9},{9,13},{13,1},{2,6},{6,10},{... | collective-permute-start | bytes 442376 | tf_op jit(solution)/shard_map/ppermute | solution.py:267
  100.8 1.6 %collective-permute-start.25 = (f32[576,128]{1,0:T(8,128)S(1)}, f32[576,128]{1,0:T(8,128)S(1)}, u32[]{:S(2)}, u32[]{:S(2)}) collective-permute-start(f32[576,128]{1,0:T(8,128)S(1)} %add_add_fusion), channel_id=1, source_target_pairs={{0,1},{1,0},{2,3},{3,2},{4,5},{5,4},{6,7},{7,6},{8,9},{9,8},{10,11... | collective-permute-start | bytes 884744 | tf_op jit(solution)/shard_map/ppermute | solution.py:262

commit v5 on v4

--- a/solution.py
+++ b/solution.py
@@ -423,7 +423,7 @@
     return xhat, scale, hidden, sig + hidden * (1.0 - sig)
 
 
-def reduce_block(n, band, mean, rstd, mix):
+def reduce_block(n, band, mean, rstd, mix, base=False):
     rows, cols = band.rows, band.cols
     channels = n.acts.shape[-1]
     hidden_gradient(rows, cols, n.shifted, n.weights, n.hidden_grad)
@@ -431,9 +431,15 @@
         at = slice(r * cols, (r + 1) * cols)
         latent = band.latent(r)
         n.latent_keep[:, at] = latent
-        xhat, scale, _, slope = pixel_values(n.acts[0, at, :], latent, mix, mean, rstd)
+        xhat, scale, hidden, slope = pixel_values(n.acts[0, at, :], latent, mix, mean, rstd)
         pre_grad = n.hidden_grad[at, :] * slope
-        n.norm[0, at, :] = (pre_grad * scale).astype(BF16)
+        norm = pre_grad * scale
+        if base:
+            norm = n.shifted[(r + 1) * cols : (r + 2) * cols, channels : 2 * channels].astype(F32) + rstd * norm
+            n.base[0, (r + 1) * cols : (r + 2) * cols, :] = norm.astype(BF16)
+        else:
+            n.norm[0, at, :] = norm.astype(BF16)
+            n.hidden[at, :] = hidden.astype(BF16)
         n.pairs[at, 0:channels] = (pre_grad * xhat).astype(BF16)
         n.pairs[at, channels:] = pre_grad.astype(BF16)
     reduced = jnp.dot(n.latent_keep[...], n.pairs[...], preferred_element_type=F32)
@@ -459,61 +465,55 @@
         band = Band(n, step, rows, cols, bands)
         for r in range(rows + 2):
             spread(r, cols, *band.row(r - 1), n.shifted)
-        reduce_block(n, band, mean, rstd, jnp.concatenate(mix).astype(BF16))
+        reduce_block(n, band, mean, rstd, jnp.concatenate(mix).astype(BF16), base=True)
 
     @pl.when(jnp.logical_not(active))
-    def _():
-        n.reduced[...] = jnp.zeros_like(n.reduced)
-
-
-def lower_kernel(rows, cols, bands, micros, count, n, step):
-    active = lax.axis_index("segment") == 0
-
-    @pl.when(active)
     def _():
         @pl.when(step == 0)
         def _():
+            arrange_weights(n.kernel_passed, n.weights)
+
+        n.reduced[...] = jnp.zeros_like(n.reduced)
+        band = Band(n, step, rows, cols, bands)
+        for r in range(rows + 4):
+            spread(r, cols, *band.row(r - 2), n.shifted)
+        hidden_gradient(rows + 2, cols, n.shifted, n.weights, n.hidden_grad)
+        n.base[0] = n.hidden_grad[...].astype(BF16)
+
+
+def own_kernel(rows, cols, bands, micros, count, n, step):
+    pixels = rows * cols
+    side = lax.axis_index("sub")
+    segment = lax.axis_index("segment")
+
+    @pl.when(step == 0)
+    def _():
+        n.total[...] = jnp.zeros_like(n.total)
+
+        @pl.when(segment == 0)
+        def _():
             arrange_weights(n.kernel, n.weights)
 
-        mean, rstd = statistics(n.sums, step, micros, count)
-        band = Band(n, step, rows, cols, bands)
+    mean, rstd = statistics(n.sums, step, micros, count)
+    band = Band(n, step, rows, cols, bands)
+    mix = side_by_side(n.mix[...])
+
+    @pl.when(segment == 1)
+    def _():
+        n.reduced[...] = jnp.zeros_like(n.reduced)
+        for r in range(rows + 2):
+            spread(r, cols, *band.row(r - 1), n.shifted)
+        for r in range(rows):
+            at = slice(r * cols, (r + 1) * cols)
+            n.hidden[at, :] = pixel_values(n.acts[0, at, :], band.latent(r), mix, mean, rstd)[2].astype(BF16)
+
+    @pl.when(segment == 0)
+    def _():
         near = n.near[0].astype(F32)
         for r in range(rows + 2):
             spread(r, cols, n.result[0, r * cols : (r + 1) * cols, :], near[r : r + 1], n.shifted)
-        reduce_block(n, band, mean, rstd, side_by_side(n.mix[...]))
-
-    @pl.when(jnp.logical_not(active))
-    def _():
-        n.reduced[...] = jnp.zeros_like(n.reduced)
-
-
-def gradient_kernel(rows, cols, bands, micros, count, n, step):
-    pixels = rows * cols
-    side = lax.axis_index("sub")
-    segment = lax.axis_index("segment")
-
-    @pl.when(step == 0)
-    def _():
-        n.total[...] = jnp.zeros_like(n.total)
-
-    mean, rstd = statistics(n.sums, step, micros, count)
-    band = Band(n, step, rows, cols, bands)
-
-    @pl.when(segment == 1)
-    def _():
-        for r in range(rows + 2):
-            spread(r, cols, *band.row(r - 1), n.shifted)
-
-    @pl.when(segment == 0)
-    def _():
-        near = n.near[0].astype(F32)
-        for r in range(rows + 2):
-            spread(r, cols, n.result[0, r * cols : (r + 1) * cols, :], near[r : r + 1], n.shifted)
-
-    mix = side_by_side(n.mix[...])
-    for r in range(rows):
-        at = slice(r * cols, (r + 1) * cols)
-        n.hidden[at, :] = pixel_values(n.acts[0, at, :], band.latent(r), mix, mean, rstd)[2].astype(BF16)
+        reduce_block(n, band, mean, rstd, mix)
+
     for row in range(3):
         n.total[row] += lax.dot_general(
             n.hidden[...], n.shifted[row * cols : row * cols + pixels, :], TN, preferred_element_type=F32
@@ -535,34 +535,29 @@
                                 ref[low:high, :] = n.total[row, low - at : high - at, col * channels : (col + 1) * channels]
 
 
-def redo_kernel(rows, cols, bands, micros, count, n, step):
+def finish_kernel(rows, cols, bands, micros, count, n, step):
     channels = n.acts.shape[-1]
     segment = lax.axis_index("segment")
     side = lax.axis_index("sub")
-    mean, rstd = statistics(n.packed, step, micros, count)
-    mix = n.packed[2 * micros + 16 * micros :, :]
-    total = n.packed[pl.ds(pl.multiple_of(2 * micros + 16 * step, 8), 16), :]
-    mean_grad, mean_cross = gradient_means(total, mix, count)
-    band = Band(n, step, rows, cols, bands)
 
     @pl.when(segment == 1)
     def _():
+        mean, rstd = statistics(n.sums, step, micros, count)
+        total = n.total[pl.ds(pl.multiple_of(16 * step, 8), 16), :]
+        mean_grad, mean_cross = gradient_means(total, n.mix[...], count)
         for r in range(rows):
-            at = slice(r * cols, (r + 1) * cols)
-            xhat = (n.acts[0, at, :].astype(F32) - mean) * rstd
-            change = rstd * (n.norm[0, at, :].astype(F32) - mean_grad - xhat * mean_cross)
-            n.result[0, (r + 1) * cols : (r + 2) * cols, :] = (band.row(r)[0].astype(F32) + change).astype(BF16)
+            at = slice((r + 1) * cols, (r + 2) * cols)
+            xhat = (n.acts[0, r * cols : (r + 1) * cols, :].astype(F32) - mean) * rstd
+            n.result[0, at, :] = (n.base[0, at, :].astype(F32) - rstd * (mean_grad + xhat * mean_cross)).astype(BF16)
 
     @pl.when(segment == 0)
     def _():
-        @pl.when(step == 0)
-        def _():
-            arrange_weights(n.kernel, n.weights)
-
-        for r in range(rows + 4):
-            spread(r, cols, *band.row(r - 2), n.shifted)
-        hidden_gradient(rows + 2, cols, n.shifted, n.weights, n.hidden_grad)
+        mean, rstd = statistics(n.packed, step, micros, count)
+        total = n.packed[pl.ds(pl.multiple_of(2 * micros + 16 * step, 8), 16), :]
+        mix = n.packed[2 * micros + 16 * micros :, :]
+        mean_grad, mean_cross = gradient_means(total, mix, count)
         wide_mix = side_by_side(mix)
+        band = Band(n, step, rows, cols, bands)
         edges = []
         for r in range(rows + 2):
             at = slice(r * cols, (r + 1) * cols)
@@ -572,10 +567,10 @@
                 acts = n.below[0]
             else:
                 row = slice((r - 1) * cols, r * cols)
-                acts = jnp.where(step < micros // 2, n.passed_early[0, row, :], n.passed_late[0, row, :])
+                acts = jnp.where(step < 1, n.passed_early[0, row, :], n.passed_late[0, row, :])
             xhat, scale, _, slope = pixel_values(acts, band.latent(r - 1), wide_mix, mean, rstd)
-            change = rstd * (n.hidden_grad[at, :] * slope * scale - mean_grad - xhat * mean_cross)
-            value = n.shifted[(r + 1) * cols : (r + 2) * cols, channels : 2 * channels].astype(F32) + change
+            change = rstd * (n.base[0, at, :].astype(F32) * slope * scale - mean_grad - xhat * mean_cross)
+            value = band.row(r - 1)[0].astype(F32) + change
             if r == 0 or r == rows + 1:
                 row = band.row_start + (r - 1)
                 value = jnp.where((row >= 0) & (row < band.total_rows), value, 0.0)
@@ -618,7 +613,8 @@
 def by_micro(value):
     if isinstance(value, tuple):
         value, first, size = value
-        return pl.BlockSpec((1,) + tuple(value.shape[1:]), lambda m: (jnp.clip(m - first, 0, size - 1), 0, 0))
+        rest = (0,) * (len(value.shape) - 1)
+        return pl.BlockSpec((1,) + tuple(value.shape[1:]), lambda m: (jnp.clip(m - first, 0, size - 1),) + rest)
     rest = (0,) * (len(value.shape) - 1)
     return pl.BlockSpec((1,) + tuple(value.shape[1:]), lambda m: (m,) + rest)
 
@@ -627,7 +623,7 @@
     return pl.BlockSpec(tuple(value.shape), lambda m: (0,) * len(value.shape))
 
 
-def call(kernel, name, micros, scalars, fixed, cut, outs, fixed_outs, scratch, work=4, room=62):
+def call(kernel, name, micros, scalars, fixed, cut, outs, fixed_outs, scratch, work=4, room=16):
     names = [*scalars, *fixed, *cut, *outs, *fixed_outs, *scratch]
     cut_shape = [jax.ShapeDtypeStruct(s, d) for s, d in outs.values()]
     fixed_shape = [jax.ShapeDtypeStruct(s, d) for s, d in fixed_outs.values()]
@@ -662,14 +658,14 @@
     side = lax.axis_index("sub")
     acts = activations[0].reshape(micros, pixels, channels)
 
-    early = micros // 2
+    early = 1
     passed = [swap(acts[:early], "segment"), swap(acts[early:], "segment")]
     above = swap_and_shift(acts[:, pixels - cols :], 1)
     below = swap_and_shift(acts[:, :cols], bands - 1)
     kernel_passed = swap(kernel[0], "segment")
     recon_beside, target_beside = swap(recon, "sub"), swap(target, "sub")
 
-    (sums,) = call(sums_kernel, "input_sums", micros, {}, {}, {"acts": acts}, {}, {"sums": ((2 * micros, channels), F32)}, {}, room=16)
+    (sums,) = call(sums_kernel, "input_sums", micros, {}, {}, {"acts": acts}, {}, {"sums": ((2 * micros, channels), F32)}, {})
     sums = sums + swap(sums, "sub")
 
     def border(first, r):
@@ -685,7 +681,7 @@
     from_down = shift(border(0, 0), "rows", bands - 1)
     across = shift(sums, "rows", 2)
 
-    from_up, above, below, kernel_passed = lax.optimization_barrier((from_up, above, below, kernel_passed))
+    from_up, kernel_passed = lax.optimization_barrier((from_up, kernel_passed))
     image = {
         "latent": latent,
         "recon": recon,
@@ -704,9 +700,12 @@
         "latent_keep": ((8, pixels), BF16),
         "pairs": ((pixels, 2 * channels), BF16),
     }
-    produced = {"norm": ((micros, pixels, channels), BF16), "reduced": ((micros, 16, channels), F32)}
     size = (rows, cols, bands, micros, count)
-    norm_upper, reduced = call(
+    sums_own = (sums + across) + (from_up[: 2 * micros] + from_down[: 2 * micros])
+    mix = jnp.concatenate([mod_weight[0], jnp.concatenate([scale_bias, shift_bias], axis=1)]).astype(F32)
+    mix = jnp.pad(mix, ((0, 7 - latents), (0, 0)))
+    mix = jnp.concatenate([mix[:, :channels], mix[:, channels:]])
+    base, reduced = call(
         functools.partial(upper_kernel, *size),
         "upper_block",
         micros,
@@ -718,31 +717,34 @@
             "scale_bias": scale_bias,
             "shift_bias": shift_bias,
             "kernel": kernel[0],
+            "kernel_passed": kernel_passed,
             **borders,
         },
         {"acts": acts, **image},
-        produced,
+        {"base": ((micros, wide, channels), BF16), "reduced": ((micros, 16, channels), F32)},
         {},
-        {**work, "sums_keep": ((2 * micros, channels), F32)},
-    )
+        {
+            **work,
+            "shifted": (((rows + 4) * cols, triple), BF16),
+            "hidden_grad": ((wide, channels), F32),
+            "sums_keep": ((2 * micros, channels), F32),
+        },
+    )
+    sums = sums_own
     reduced, passed[0] = lax.optimization_barrier((reduced, passed[0]))
     total_upper = pixel_total(reduced.reshape(micros * 16, channels))
-    sums = (sums + across) + (from_up[: 2 * micros] + from_down[: 2 * micros])
-    mix = jnp.concatenate([mod_weight[0], jnp.concatenate([scale_bias, shift_bias], axis=1)]).astype(F32)
-    mix = jnp.pad(mix, ((0, 7 - latents), (0, 0)))
-    mix = jnp.concatenate([mix[:, :channels], mix[:, channels:]])
     packed = jnp.concatenate([sums, total_upper, mix])
-    packed, passed[1] = lax.optimization_barrier((packed, passed[1]))
-    packed = jnp.where(segment == 0, swap(packed, "segment"), packed)
+    packed, passed[1], above, below = lax.optimization_barrier((packed, passed[1], above, below))
+    packed = swap(packed, "segment")
     result, edge = call(
-        functools.partial(redo_kernel, *size),
-        "redo_upper",
+        functools.partial(finish_kernel, *size),
+        "finish_upper",
         micros,
         {"boxes": boxes},
-        {"packed": packed, "kernel": kernel_passed, **borders},
+        {"sums": sums, "mix": mix, "packed": packed, "total": total_upper, **borders},
         {
+            "base": base,
             "acts": acts,
-            "norm": norm_upper,
             "passed_early": (passed[0], 0, early),
             "passed_late": (passed[1], early, micros - early),
             "above": above,
@@ -751,39 +753,23 @@
         },
         {"result": ((micros, wide, channels), BF16), "edge": ((micros, 16, channels), BF16)},
         {},
-        {
-            "shifted": (((rows + 4) * cols, triple), BF16),
-            "weights": ((3, channels, triple), BF16),
-            "hidden_grad": ((wide, channels), F32),
-        },
+        {},
     )
     near = swap(edge, "sub")
     half = kernel.shape[1] // 2
-    keep, give = call(
-        functools.partial(gradient_kernel, *size),
-        "kernel_gradient",
-        micros,
-        {"boxes": boxes},
-        {"sums": sums, "mix": mix, **borders},
-        {"result": result, "near": near, "acts": acts, **image},
-        {},
-        {"keep": ((half, channels), F32), "give": ((half, channels), F32)},
-        {**shifted, "hidden": ((pixels, channels), BF16), "total": ((3, channels, triple), F32)},
-    )
-    keep = (keep + swap(give, "sub")).astype(BF16)
-    others = [shift(keep, "rows", steps) for steps in (1, 2, 3)]
-    norm, reduced = call(
-        functools.partial(lower_kernel, *size),
-        "lower_block",
+    norm, reduced, keep, give = call(
+        functools.partial(own_kernel, *size),
+        "own_block",
         micros,
         {"boxes": boxes},
         {"sums": sums, "mix": mix, "kernel": kernel[0], **borders},
         {"result": result, "near": near, "acts": acts, **image},
-        produced,
-        {},
-        work,
-        work=1 << 27,
-    )
+        {"norm": ((micros, pixels, channels), BF16), "reduced": ((micros, 16, channels), F32)},
+        {"keep": ((half, channels), F32), "give": ((half, channels), F32)},
+        {**work, "hidden": ((pixels, channels), BF16), "total": ((3, channels, triple), F32)},
+    )
+    keep = (keep + swap(give, "sub")).astype(BF16)
+    others = [shift(keep, "rows", steps) for steps in (1, 2, 3)]
     total_lower = pixel_total(reduced.reshape(micros * 16, channels))
     grads, mod_grad, bias_grad = call(
         functools.partial(last_kernel, rows, cols, micros, count),

time: 104 us -> 85.4 us (0.82)
  Pallas kernels: 34 us -> 23 us
  starting transfers between devices: 24.3 us -> 33.7 us
  waiting for transfers between devices: 33.1 us -> 25.1 us
  local copies, waits for them, and re-layouts: 5.84 us -> 1.38 us
  other arithmetic: 5.15 us -> 1.12 us
    pallas_call x6 -> x5, Pallas kernels: 34 us -> 23 us  [call(): pl.pallas_call(body, grid=(micros,), in_specs=[pl.BlockSpec(memory_space=...]
    ppermute x12, starting transfers between devices: 13.2 us -> 22.2 us  [shift(): lax.ppermute(value, axis, [(i, (i + steps) % count) for i in range(count)])]
    ppermute x12, waiting for transfers between devices: 18.6 us -> 10.1 us  [shift(): lax.ppermute(value, axis, [(i, (i + steps) % count) for i in range(count)])]
    unnamed x46 -> x20, local copies, waits for them, and re-layouts: 4.92 us -> 1.27 us
    ppermute x12, starting transfers between devices: 5.45 us -> 7.19 us  [swap(): return lax.ppermute(value, axis, [(0, 1), (1, 0)])]
    add x2, other arithmetic: 1.53 us -> 0.01 us  [pixel_total(): value = value + swap(value, 'sub')]
    ppermute x2, starting transfers between devices: 5.66 us -> 4.32 us  [swap_and_shift(): return lax.ppermute(value, ('rows', 'segment'), pairs)]
    ppermute x2, waiting for transfers between devices: 1.54 us -> 2.66 us  [swap_and_shift(): return lax.ppermute(value, ('rows', 'segment'), pairs)]
  transfers between devices with their start and end apart: 26 -> 26, of which waited for: 13 -> 11; matrix products, arithmetic and copies ran while one was open for 4% -> 0% of each run, Pallas kernels for 15% -> 11%
where the time goes in v5:
time: 85.4 us; the launch traced here: 85.3 us
  starting transfers between devices  33.7 us (39%)
  waiting for transfers between devices  25.1 us (29%)
  Pallas kernels  23 us (27%)
  local copies, waits for them, and re-layouts  1.38 us (2%)
  other arithmetic  1.12 us (1%)
  between operations  0.96 us (1%)
    pallas_call x5, Pallas kernels, call(): pl.pallas_call(body, grid=(micros,), in_specs=[pl.BlockSpec(memory_space=...  23 us
    ppermute x12, starting transfers between devices, shift(): lax.ppermute(value, axis, [(i, (i + steps) % count) for i in range(count)])  22.2 us
    ppermute x12, waiting for transfers between devices, swap(): return lax.ppermute(value, axis, [(0, 1), (1, 0)])  12.4 us
    ppermute x12, waiting for transfers between devices, shift(): lax.ppermute(value, axis, [(i, (i + steps) % count) for i in range(count)])  10.1 us
    ppermute x12, starting transfers between devices, swap(): return lax.ppermute(value, axis, [(0, 1), (1, 0)])  7.19 us
    ppermute x2, starting transfers between devices, swap_and_shift(): return lax.ppermute(value, ('rows', 'segment'), pairs)  4.32 us
    ppermute x2, waiting for transfers between devices, swap_and_shift(): return lax.ppermute(value, ('rows', 'segment'), pairs)  2.66 us
  transfers between devices with their start and end apart: 26, of which 11 were waited for; matrix products, arithmetic and copies ran while one was open for 0% of the time, Pallas kernels for 11%

profile of v5, /device:TPU:0, one launch (start us, length us, event | category | flops | bytes accessed | tf_op | source)
XLA Modules:
  0.0 85.3 jit_solution(13918887255253810249)
XLA Ops:
  0.6 0.5 collective-permute-start.2
  1.2 0.1 collective-permute-start.3
  1.2 1.2 %copy-done = bf16[1,4,8,128,128]{4,3,2,1,0:T(8,128)(2,1)S(1)} copy-done((bf16[1,4,8,128,128]{4,3,2,1,0:T(8,128)(2,1)S(1)}, bf16[1,4,8,128,128]{4,3,2,1,0:T(8,128)(2,1)}, u32[]{:S(2)}) %copy-start) | copy-done | bytes 1048600
  2.5 0.6 input_sums.1
  3.1 0.5 collective-permute-start
  3.6 2.6 %collective-permute-start.5 = (bf16[1152,128]{1,0:T(8,128)(2,1)}, bf16[1152,128]{1,0:T(8,128)(2,1)S(1)}, u32[]{:S(2)}, u32[]{:S(2)}) collective-permute-start(bf16[1152,128]{1,0:T(8,128)(2,1)} %bitcast.30), channel_id=1, source_target_pairs={{0,2},{2,0},{1,3},{3,1},{4,6},{6,4},{5,7},{7,5},{8,10},{10,8},{9,1... | collective-permute-start | bytes 884744 | tf_op jit(solution)/shard_map/ppermute | solution.py:262
  6.2 0.1 collective-permute-start.7
  6.3 0.0 copy-start.1
  6.4 0.0 copy-start.5
  6.4 0.0 copy-start.6
  6.5 0.0 collective-permute-done
  6.5 3.2 %collective-permute-start.1 = (f32[8,128]{1,0:T(8,128)S(1)}, f32[8,128]{1,0:T(8,128)S(1)}, u32[]{:S(2)}, u32[]{:S(2)}) collective-permute-start(f32[8,128]{1,0:T(8,128)S(1)} %add.50.refs_1_), channel_id=1, source_target_pairs={{0,8},{4,12},{8,0},{12,4},{1,9},{5,13},{9,1},{13,5},{2,10},{6,14},... | collective-permute-start | bytes 12296 | tf_op jit(solution)/shard_map/ppermute | solution.py:267
  9.6 0.0 collective-permute-done.2.refs_15_.refs_17_.refs_13_
  9.6 0.0 collective-permute-done.3.refs_16_.refs_18_.refs_14_
  9.8 1.6 %collective-permute-start.4 = (f32[72,128]{1,0:T(8,128)S(1)}, f32[72,128]{1,0:T(8,128)S(1)}, u32[]{:S(2)}, u32[]{:S(2)}) collective-permute-start(f32[72,128]{1,0:T(8,128)S(1)} %get-tuple-element.60), channel_id=1, source_target_pairs={{0,4},{4,8},{8,12},{12,0},{1,5},{5,9},{9,13},{13,1},{2,6},{6,10},{... | collective-permute-start | bytes 110600 | tf_op jit(solution)/shard_map/ppermute | solution.py:267
  11.4 2.2 %collective-permute-start.6 = (f32[72,128]{1,0:T(8,128)S(1)}, f32[72,128]{1,0:T(8,128)S(1)}, u32[]{:S(2)}, u32[]{:S(2)}) collective-permute-start(f32[72,128]{1,0:T(8,128)S(1)} %get-tuple-element.61), channel_id=1, source_target_pairs={{0,12},{4,0},{8,4},{12,8},{1,13},{5,1},{9,5},{13,9},{2,14},{6,2},{... | collective-permute-start | bytes 110600 | tf_op jit(solution)/shard_map/ppermute | solution.py:267
  13.7 0.1 slice.76
  13.7 2.0 %collective-permute-done.4.refs_8_.refs_5_.refs_4_ = f32[72,128]{1,0:T(8,128)S(1)} collective-permute-done((f32[72,128]{1,0:T(8,128)S(1)}, f32[72,128]{1,0:T(8,128)S(1)}, u32[]{:S(2)}, u32[]{:S(2)}) %collective-permute-start.4) | collective-permute-done | bytes 36896 | tf_op jit(solution)/shard_map/ppermute | solution.py:267
  15.7 0.6 collective-permute-start.13
  16.3 0.0 collective-permute-done.5.refs_7_
  16.3 0.9 %collective-permute-start.12 = (bf16[3,1024,128]{2,1,0:T(8,128)(2,1)S(1)}, bf16[3,1024,128]{2,1,0:T(8,128)(2,1)S(1)}, u32[]{:S(2)}, u32[]{:S(2)}) collective-permute-start(bf16[3,1024,128]{2,1,0:T(8,128)(2,1)S(1)} %bitcast.37), channel_id=1, source_target_pairs={{0,2},{2,0},{1,3},{3,1},{4,6},{6,4},{5,7},{7,5},{8,10},{10,8},{9,1... | collective-permute-start | bytes 2359304 | tf_op jit(solution)/shard_map/ppermute | solution.py:262
  17.2 0.0 collective-permute-done.1.refs_2_
  17.2 0.0 collective-permute-done.6.refs_9_.refs_6_.refs_5_
  17.2 6.2 %upper_block.1 = (bf16[4,1280,128]{2,1,0:T(8,128)(2,1)S(1)}, f32[4,16,128]{2,1,0:T(8,128)S(1)}) custom-call(s32[4,4,4]{2,1,0:T(4,128)S(1)} %copy-done.5, f32[8,128]{1,0:T(8,128)S(1)} %add.50.refs_1_, f32[8,128]{1,0:T(8,128)S(1)} %collective-permute-done.1.refs_2_, bf16[1,4,256]{2,1,0:T(4,128)(2,1)S(1)} %copy-done.7, bf16[1,128]{1,0:T(2,128)(2,1)S(1)} %copy-done.9, ...), custom_call_target="tpu_custom_call" | custom-call | flops 4 | bytes 1 | tf_op jit(solution)/shard_map/upper_block/pallas_call | solution.py:634
  23.4 0.0 collective-permute-done.7.refs_10_
  23.4 0.1 collective-permute-start.8
  23.5 1.2 %collective-permute-done.8 = f32[64,128]{1,0:T(8,128)S(1)} collective-permute-done((f32[64,128]{1,0:T(8,128)S(1)}, f32[64,128]{1,0:T(8,128)S(1)}, u32[]{:S(2)}, u32[]{:S(2)}) %collective-permute-start.8) | collective-permute-done | bytes 32800 | tf_op jit(solution)/shard_map/ppermute | solution.py:262
  24.7 1.3 %collective-permute-start.10 = (f32[64,128]{1,0:T(8,128)S(1)}, f32[64,128]{1,0:T(8,128)S(1)}, u32[]{:S(2)}, u32[]{:S(2)}) collective-permute-start(f32[64,128]{1,0:T(8,128)S(1)} %bitcast_add_fusion.1), channel_id=1, source_target_pairs={{0,4},{4,8},{8,12},{12,0},{1,5},{5,9},{9,13},{13,1},{2,6},{6,10},{... | collective-permute-start | bytes 98312 | tf_op jit(solution)/shard_map/ppermute | solution.py:267
  25.9 2.8 %collective-permute-start.11 = (f32[64,128]{1,0:T(8,128)S(1)}, f32[64,128]{1,0:T(8,128)S(1)}, u32[]{:S(2)}, u32[]{:S(2)}) collective-permute-start(f32[64,128]{1,0:T(8,128)S(1)} %bitcast_add_fusion.1), channel_id=1, source_target_pairs={{0,12},{4,0},{8,4},{12,8},{1,13},{5,1},{9,5},{13,9},{2,14},{6,2},{... | collective-permute-start | bytes 98312 | tf_op jit(solution)/shard_map/ppermute | solution.py:267
  28.8 0.5 collective-permute-start.9
  29.3 1.4 %collective-permute-done.10 = f32[64,128]{1,0:T(8,128)S(1)} collective-permute-done((f32[64,128]{1,0:T(8,128)S(1)}, f32[64,128]{1,0:T(8,128)S(1)}, u32[]{:S(2)}, u32[]{:S(2)}) %collective-permute-start.10) | collective-permute-done | bytes 32800 | tf_op jit(solution)/shard_map/ppermute | solution.py:267
  30.6 3.7 %collective-permute-start.14 = (bf16[4,128,128]{2,1,0:T(8,128)(2,1)S(1)}, bf16[4,128,128]{2,1,0:T(8,128)(2,1)S(1)}, u32[]{:S(2)}, u32[]{:S(2)}) collective-permute-start(bf16[4,128,128]{2,1,0:T(8,128)(2,1)S(1)} %get-tuple-element.50), channel_id=1, source_target_pairs={{0,14},{2,12},{4,2},{6,0},{8,6},{10,4},{12,10},{14,8},{1,15},{3,13... | collective-permute-start | bytes 393224 | tf_op jit(solution)/shard_map/ppermute | solution.py:273
  34.4 0.0 collective-permute-done.11
  34.4 0.0 collective-permute-done.9
  34.4 0.0 collective-permute-done.13.refs_12_
  34.4 2.7 %collective-permute-done.14.refs_13_ = bf16[4,128,128]{2,1,0:T(8,128)(2,1)S(1)} collective-permute-done((bf16[4,128,128]{2,1,0:T(8,128)(2,1)S(1)}, bf16[4,128,128]{2,1,0:T(8,128)(2,1)S(1)}, u32[]{:S(2)}, u32[]{:S(2)}) %collective-permute-start.14) | collective-permute-done | bytes 131104 | tf_op jit(solution)/shard_map/ppermute | solution.py:273
  37.1 5.0 %collective-permute-done.12.refs_11_ = bf16[3,1024,128]{2,1,0:T(8,128)(2,1)S(1)} collective-permute-done((bf16[3,1024,128]{2,1,0:T(8,128)(2,1)S(1)}, bf16[3,1024,128]{2,1,0:T(8,128)(2,1)S(1)}, u32[]{:S(2)}, u32[]{:S(2)}) %collective-permute-start.12) | collective-permute-done | bytes 786464 | tf_op jit(solution)/shard_map/ppermute | solution.py:262
  42.1 1.8 %collective-permute-start.15 = (f32[88,128]{1,0:T(8,128)S(1)}, f32[88,128]{1,0:T(8,128)S(1)}, u32[]{:S(2)}, u32[]{:S(2)}) collective-permute-start(f32[88,128]{1,0:T(8,128)S(1)} %pad_maximum_fusion.2), channel_id=1, source_target_pairs={{0,2},{2,0},{1,3},{3,1},{4,6},{6,4},{5,7},{7,5},{8,10},{10,8},{9,1... | collective-permute-start | bytes 135176 | tf_op jit(solution)/shard_map/ppermute | solution.py:262
  43.9 2.3 %collective-permute-done.15.refs_3_ = f32[88,128]{1,0:T(8,128)S(1)} collective-permute-done((f32[88,128]{1,0:T(8,128)S(1)}, f32[88,128]{1,0:T(8,128)S(1)}, u32[]{:S(2)}, u32[]{:S(2)}) %collective-permute-start.15) | collective-permute-done | bytes 45088 | tf_op jit(solution)/shard_map/ppermute | solution.py:262
  46.1 4.1 %finish_upper.1 = (bf16[4,1280,128]{2,1,0:T(8,128)(2,1)S(1)}, bf16[4,16,128]{2,1,0:T(8,128)(2,1)S(1)}) custom-call(s32[4,4,4]{2,1,0:T(4,128)S(1)} %copy-done.5, f32[8,128]{1,0:T(8,128)S(1)} %fusion.6.refs_1_.refs_0_, f32[16,128]{1,0:T(8,128)S(1)} %pad_maximum_fusion.5.refs_2_.refs_1_, f32[88,128]{1,0:T(8,128)S(1)} %collective-permute-done.15.refs_3_, ...), custom_call_target="tpu_custom_call" | custom-call | flops 4 | bytes 1 | tf_op jit(solution)/shard_map/finish_upper/pallas_call | solution.py:634
  50.3 0.1 collective-permute-start.16
  50.3 1.2 %collective-permute-done.16.refs_8_ = bf16[4,16,128]{2,1,0:T(8,128)(2,1)S(1)} collective-permute-done((bf16[4,16,128]{2,1,0:T(8,128)(2,1)S(1)}, bf16[4,16,128]{2,1,0:T(8,128)(2,1)S(1)}, u32[]{:S(2)}, u32[]{:S(2)}) %collective-permute-start.16) | collective-permute-done | bytes 16416 | tf_op jit(solution)/shard_map/ppermute | solution.py:262
  51.5 9.3 %own_block.1 = (bf16[4,1024,128]{2,1,0:T(8,128)(2,1)S(1)}, f32[4,16,128]{2,1,0:T(8,128)S(1)}, f32[576,128]{1,0:T(8,128)S(1)}, f32[576,128]{1,0:T(8,128)S(1)}) custom-call(s32[4,4,4]{2,1,0:T(4,128)S(1)} %copy-done.5, f32[8,128]{1,0:T(8,128)S(1)} %fusion.6.refs_1_.refs_0_, f32[16,128]{1,0:T(8,128)S(1)} %pad_maximum_fusion.5.refs_2_.refs_1_, ...), custom_call_target="tpu_custom_call" | custom-call | flops 4 | bytes 1 | tf_op jit(solution)/shard_map/own_block/pallas_call | solution.py:634
  60.8 0.2 collective-permute-start.21
  61.1 0.3 collective-permute-start.17
  61.4 1.1 %collective-permute-done.17 = f32[64,128]{1,0:T(8,128)S(1)} collective-permute-done((f32[64,128]{1,0:T(8,128)S(1)}, f32[64,128]{1,0:T(8,128)S(1)}, u32[]{:S(2)}, u32[]{:S(2)}) %collective-permute-start.17) | collective-permute-done | bytes 32800 | tf_op jit(solution)/shard_map/ppermute | solution.py:262
  62.5 2.8 %collective-permute-start.18 = (f32[64,128]{1,0:T(8,128)S(1)}, f32[64,128]{1,0:T(8,128)S(1)}, u32[]{:S(2)}, u32[]{:S(2)}) collective-permute-start(f32[64,128]{1,0:T(8,128)S(1)} %bitcast_add_fusion), channel_id=1, source_target_pairs={{0,8},{4,12},{8,0},{12,4},{1,9},{5,13},{9,1},{13,5},{2,10},{6,14},... | collective-permute-start | bytes 98312 | tf_op jit(solution)/shard_map/ppermute | solution.py:267
  65.4 1.6 %collective-permute-start.19 = (f32[64,128]{1,0:T(8,128)S(1)}, f32[64,128]{1,0:T(8,128)S(1)}, u32[]{:S(2)}, u32[]{:S(2)}) collective-permute-start(f32[64,128]{1,0:T(8,128)S(1)} %bitcast_add_fusion), channel_id=1, source_target_pairs={{0,4},{4,8},{8,12},{12,0},{1,5},{5,9},{9,13},{13,1},{2,6},{6,10},{... | collective-permute-start | bytes 98312 | tf_op jit(solution)/shard_map/ppermute | solution.py:267
  67.0 2.2 %collective-permute-start.20 = (f32[64,128]{1,0:T(8,128)S(1)}, f32[64,128]{1,0:T(8,128)S(1)}, u32[]{:S(2)}, u32[]{:S(2)}) collective-permute-start(f32[64,128]{1,0:T(8,128)S(1)} %bitcast_add_fusion), channel_id=1, source_target_pairs={{0,12},{4,0},{8,4},{12,8},{1,13},{5,1},{9,5},{13,9},{2,14},{6,2},{... | collective-permute-start | bytes 98312 | tf_op jit(solution)/shard_map/ppermute | solution.py:267
  69.2 0.0 collective-permute-done.21
  69.3 0.1 collective-permute-start.22
  69.3 0.6 collective-permute-start.23
  69.9 0.0 collective-permute-done.18
  69.9 3.3 %collective-permute-start.24 = (bf16[576,128]{1,0:T(8,128)(2,1)S(1)}, bf16[576,128]{1,0:T(8,128)(2,1)S(1)}, u32[]{:S(2)}, u32[]{:S(2)}) collective-permute-start(bf16[576,128]{1,0:T(8,128)(2,1)S(1)} %add_convert_fusion), channel_id=1, source_target_pairs={{0,12},{4,0},{8,4},{12,8},{1,13},{5,1},{9,5},{13,9},{2,14},{6,2},{... | collective-permute-start | bytes 442376 | tf_op jit(solution)/shard_map/ppermute | solution.py:267
  73.2 0.0 collective-permute-done.19
  73.2 0.0 collective-permute-done.20
  73.2 2.8 %input_gradient.1 = (bf16[4,1024,128]{2,1,0:T(8,128)(2,1)}, f32[1,4,256]{2,1,0:T(4,128)}, f32[1,256]{1,0:T(1,128)}) custom-call(f32[8,128]{1,0:T(8,128)S(1)} %fusion.6.refs_1_.refs_0_, f32[16,128]{1,0:T(8,128)S(1)} %pad_maximum_fusion.5.refs_2_.refs_1_, f32[64,128]{1,0:T(8,128)S(1)} %add_add_fusion.1.refs_2_, f32[64,128]{1,0:T(8,128)S(1)} %add_add_fusion.2.refs_4_.refs_3_, ...), custom_call_target="tpu_custom_call" | custom-call | flops 33554432 | bytes 8388608 | tf_op jit(solution)/shard_map/input_gradient/pallas_call | solution.py:634
  75.9 2.0 %collective-permute-done.22 = bf16[576,128]{1,0:T(8,128)(2,1)S(1)} collective-permute-done((bf16[576,128]{1,0:T(8,128)(2,1)S(1)}, bf16[576,128]{1,0:T(8,128)(2,1)S(1)}, u32[]{:S(2)}, u32[]{:S(2)}) %collective-permute-start.22) | collective-permute-done | bytes 147488 | tf_op jit(solution)/shard_map/ppermute | solution.py:267
  77.9 4.8 %collective-permute-done.23 = bf16[576,128]{1,0:T(8,128)(2,1)S(1)} collective-permute-done((bf16[576,128]{1,0:T(8,128)(2,1)S(1)}, bf16[576,128]{1,0:T(8,128)(2,1)S(1)}, u32[]{:S(2)}, u32[]{:S(2)}) %collective-permute-start.23) | collective-permute-done | bytes 147488 | tf_op jit(solution)/shard_map/ppermute | solution.py:267
  82.7 0.0 collective-permute-done.24
  82.7 0.1 add_add_fusion
  82.8 0.1 collective-permute-start.25
  82.8 1.6 %collective-permute-done.25 = f32[576,128]{1,0:T(8,128)S(1)} collective-permute-done((f32[576,128]{1,0:T(8,128)S(1)}, f32[576,128]{1,0:T(8,128)S(1)}, u32[]{:S(2)}, u32[]{:S(2)}) %collective-permute-start.25) | collective-permute-done | bytes 294944 | tf_op jit(solution)/shard_map/ppermute | solution.py:262
  84.4 0.9 %maximum_select_fusion = f32[1,1152,128]{2,1,0:T(8,128)} fusion(f32[1,576,128]{2,1,0:T(8,128)S(1)} %bitcast.38, f32[1,576,128]{2,1,0:T(8,128)S(1)} %bitcast.36, pred[]{:T(512)S(6)} %eq.3), kind=kLoop, calls=%fused_computation | loop fusion | flops 442368 | bytes 1179649 | tf_op jit(solution)/shard_map/jit(_where)/select_n | solution.py:790
  (38 shorter events, 0.3 us)
Async XLA Ops:
  0.6 9.0 %collective-permute-start.2 = (bf16[4,3,8,128]{3,2,1,0:T(8,128)(2,1)}, bf16[4,3,8,128]{3,2,1,0:T(8,128)(2,1)S(1)}, u32[]{:S(2)}, u32[]{:S(2)}) collective-permute-start(bf16[4,3,8,128]{3,2,1,0:T(8,128)(2,1)} %refs_11_.1), channel_id=1, source_target_pairs={{0,1},{1,0},{2,3},{3,2},{4,5},{5,4},{6,7},{7,6},{8,9},{9,8},{10,11... | collective-permute-start | bytes 73736 | tf_op jit(solution)/shard_map/ppermute | solution.py:262
  1.2 8.5 %collective-permute-start.3 = (bf16[4,3,8,128]{3,2,1,0:T(8,128)(2,1)}, bf16[4,3,8,128]{3,2,1,0:T(8,128)(2,1)S(1)}, u32[]{:S(2)}, u32[]{:S(2)}) collective-permute-start(bf16[4,3,8,128]{3,2,1,0:T(8,128)(2,1)} %refs_12_.3), channel_id=1, source_target_pairs={{0,1},{1,0},{2,3},{3,2},{4,5},{5,4},{6,7},{7,6},{8,9},{9,8},{10,11... | collective-permute-start | bytes 73736 | tf_op jit(solution)/shard_map/ppermute | solution.py:262
  1.2 1.2 %copy-start = (bf16[1,4,8,128,128]{4,3,2,1,0:T(8,128)(2,1)S(1)}, bf16[1,4,8,128,128]{4,3,2,1,0:T(8,128)(2,1)}, u32[]{:S(2)}) copy-start(bf16[1,4,8,128,128]{4,3,2,1,0:T(8,128)(2,1)} %param.10) | copy-start | bytes 3145732
  2.5 3.9 %copy-start.3 = (bf16[4,3,8,128]{3,2,1,0:T(8,128)(2,1)S(1)}, bf16[4,3,8,128]{3,2,1,0:T(8,128)(2,1)}, u32[]{:S(2)}) copy-start(bf16[4,3,8,128]{3,2,1,0:T(8,128)(2,1)} %refs_12_.3) | copy-start | bytes 73732
  2.5 3.9 %copy-start.4 = (bf16[4,3,8,128]{3,2,1,0:T(8,128)(2,1)S(1)}, bf16[4,3,8,128]{3,2,1,0:T(8,128)(2,1)}, u32[]{:S(2)}) copy-start(bf16[4,3,8,128]{3,2,1,0:T(8,128)(2,1)} %refs_11_.1) | copy-start | bytes 73732
  2.5 3.9 %copy-start.2 = (bf16[4,4,8,128]{3,2,1,0:T(8,128)(2,1)S(1)}, bf16[4,4,8,128]{3,2,1,0:T(8,128)(2,1)}, u32[]{:S(2)}) copy-start(bf16[4,4,8,128]{3,2,1,0:T(8,128)(2,1)} %refs_10_.3) | copy-start | bytes 98308
  2.5 11.2 %copy-start.7 = (bf16[1,4,256]{2,1,0:T(4,128)(2,1)S(1)}, bf16[1,4,256]{2,1,0:T(4,128)(2,1)}, u32[]{:S(2)}) copy-start(bf16[1,4,256]{2,1,0:T(4,128)(2,1)} %refs_3_.1) | copy-start | bytes 6148
  2.5 11.2 %copy-start.8 = (bf16[1,128]{1,0:T(2,128)(2,1)S(1)}, bf16[1,128]{1,0:T(2,128)(2,1)}, u32[]{:S(2)}) copy-start(bf16[1,128]{1,0:T(2,128)(2,1)} %refs_5_.1) | copy-start | bytes 772
  2.5 11.2 %copy-start.9 = (bf16[1,128]{1,0:T(2,128)(2,1)S(1)}, bf16[1,128]{1,0:T(2,128)(2,1)}, u32[]{:S(2)}) copy-start(bf16[1,128]{1,0:T(2,128)(2,1)} %refs_4_.1) | copy-start | bytes 772
  3.1 3.3 %collective-permute-start = (f32[8,128]{1,0:T(8,128)S(1)}, f32[8,128]{1,0:T(8,128)S(1)}, u32[]{:S(2)}, u32[]{:S(2)}) collective-permute-start(f32[8,128]{1,0:T(8,128)S(1)} %input_sums.1), channel_id=1, source_target_pairs={{0,1},{1,0},{2,3},{3,2},{4,5},{5,4},{6,7},{7,6},{8,9},{9,8},{10,11... | collective-permute-start | bytes 12296 | tf_op jit(solution)/shard_map/ppermute | solution.py:262
  3.6 12.6 %collective-permute-start.5 = (bf16[1152,128]{1,0:T(8,128)(2,1)}, bf16[1152,128]{1,0:T(8,128)(2,1)S(1)}, u32[]{:S(2)}, u32[]{:S(2)}) collective-permute-start(bf16[1152,128]{1,0:T(8,128)(2,1)} %bitcast.30), channel_id=1, source_target_pairs={{0,2},{2,0},{1,3},{3,1},{4,6},{6,4},{5,7},{7,5},{8,10},{10,8},{9,1... | collective-permute-start | bytes 884744 | tf_op jit(solution)/shard_map/ppermute | solution.py:262
  6.2 17.2 %collective-permute-start.7 = (bf16[1,1024,128]{2,1,0:T(8,128)(2,1)S(1)}, bf16[1,1024,128]{2,1,0:T(8,128)(2,1)S(1)}, u32[]{:S(2)}, u32[]{:S(2)}) collective-permute-start(bf16[1,1024,128]{2,1,0:T(8,128)(2,1)S(1)} %bitcast.39), channel_id=1, source_target_pairs={{0,2},{2,0},{1,3},{3,1},{4,6},{6,4},{5,7},{7,5},{8,10},{10,8},{9,1... | collective-permute-start | bytes 786440 | tf_op jit(solution)/shard_map/ppermute | solution.py:262
  6.3 10.8 %copy-start.1 = (bf16[1,1152,128]{2,1,0:T(8,128)(2,1)S(1)}, bf16[1,1152,128]{2,1,0:T(8,128)(2,1)}, u32[]{:S(2)}) copy-start(bf16[1,1152,128]{2,1,0:T(8,128)(2,1)} %param.15) | copy-start | bytes 884740
  6.4 10.8 %copy-start.5 = (s32[4,4,4]{2,1,0:T(4,128)S(1)}, s32[4,4,4]{2,1,0:T(4,128)}, u32[]{:S(2)}) copy-start(s32[4,4,4]{2,1,0:T(4,128)} %refs_0_.5) | copy-start | bytes 772
  6.4 10.8 %copy-start.6 = (bf16[3,128]{1,0:T(4,128)(2,1)S(1)}, bf16[3,128]{1,0:T(4,128)(2,1)}, u32[]{:S(2)}) copy-start(bf16[3,128]{1,0:T(4,128)(2,1)} %refs_6_.1) | copy-start | bytes 2308
  6.5 10.7 %collective-permute-start.1 = (f32[8,128]{1,0:T(8,128)S(1)}, f32[8,128]{1,0:T(8,128)S(1)}, u32[]{:S(2)}, u32[]{:S(2)}) collective-permute-start(f32[8,128]{1,0:T(8,128)S(1)} %add.50.refs_1_), channel_id=1, source_target_pairs={{0,8},{4,12},{8,0},{12,4},{1,9},{5,13},{9,1},{13,5},{2,10},{6,14},... | collective-permute-start | bytes 12296 | tf_op jit(solution)/shard_map/ppermute | solution.py:267
  9.8 5.9 %collective-permute-start.4 = (f32[72,128]{1,0:T(8,128)S(1)}, f32[72,128]{1,0:T(8,128)S(1)}, u32[]{:S(2)}, u32[]{:S(2)}) collective-permute-start(f32[72,128]{1,0:T(8,128)S(1)} %get-tuple-element.60), channel_id=1, source_target_pairs={{0,4},{4,8},{8,12},{12,0},{1,5},{5,9},{9,13},{13,1},{2,6},{6,10},{... | collective-permute-start | bytes 110600 | tf_op jit(solution)/shard_map/ppermute | solution.py:267
  11.4 5.8 %collective-permute-start.6 = (f32[72,128]{1,0:T(8,128)S(1)}, f32[72,128]{1,0:T(8,128)S(1)}, u32[]{:S(2)}, u32[]{:S(2)}) collective-permute-start(f32[72,128]{1,0:T(8,128)S(1)} %get-tuple-element.61), channel_id=1, source_target_pairs={{0,12},{4,0},{8,4},{12,8},{1,13},{5,1},{9,5},{13,9},{2,14},{6,2},{... | collective-permute-start | bytes 110600 | tf_op jit(solution)/shard_map/ppermute | solution.py:267
  15.7 18.7 %collective-permute-start.13 = (bf16[4,128,128]{2,1,0:T(8,128)(2,1)S(1)}, bf16[4,128,128]{2,1,0:T(8,128)(2,1)S(1)}, u32[]{:S(2)}, u32[]{:S(2)}) collective-permute-start(bf16[4,128,128]{2,1,0:T(8,128)(2,1)S(1)} %get-tuple-element.51), channel_id=1, source_target_pairs={{0,6},{2,4},{4,10},{6,8},{8,14},{10,12},{12,2},{14,0},{1,7},{3,5},... | collective-permute-start | bytes 393224 | tf_op jit(solution)/shard_map/ppermute | solution.py:273
  16.3 25.8 %collective-permute-start.12 = (bf16[3,1024,128]{2,1,0:T(8,128)(2,1)S(1)}, bf16[3,1024,128]{2,1,0:T(8,128)(2,1)S(1)}, u32[]{:S(2)}, u32[]{:S(2)}) collective-permute-start(bf16[3,1024,128]{2,1,0:T(8,128)(2,1)S(1)} %bitcast.37), channel_id=1, source_target_pairs={{0,2},{2,0},{1,3},{3,1},{4,6},{6,4},{5,7},{7,5},{8,10},{10,8},{9,1... | collective-permute-start | bytes 2359304 | tf_op jit(solution)/shard_map/ppermute | solution.py:262
  23.4 1.3 %collective-permute-start.8 = (f32[64,128]{1,0:T(8,128)S(1)}, f32[64,128]{1,0:T(8,128)S(1)}, u32[]{:S(2)}, u32[]{:S(2)}) collective-permute-start(f32[64,128]{1,0:T(8,128)S(1)} %bitcast.34), channel_id=1, source_target_pairs={{0,1},{1,0},{2,3},{3,2},{4,5},{5,4},{6,7},{7,6},{8,9},{9,8},{10,11... | collective-permute-start | bytes 98312 | tf_op jit(solution)/shard_map/ppermute | solution.py:262
  24.7 6.0 %collective-permute-start.10 = (f32[64,128]{1,0:T(8,128)S(1)}, f32[64,128]{1,0:T(8,128)S(1)}, u32[]{:S(2)}, u32[]{:S(2)}) collective-permute-start(f32[64,128]{1,0:T(8,128)S(1)} %bitcast_add_fusion.1), channel_id=1, source_target_pairs={{0,4},{4,8},{8,12},{12,0},{1,5},{5,9},{9,13},{13,1},{2,6},{6,10},{... | collective-permute-start | bytes 98312 | tf_op jit(solution)/shard_map/ppermute | solution.py:267
  25.9 8.4 %collective-permute-start.11 = (f32[64,128]{1,0:T(8,128)S(1)}, f32[64,128]{1,0:T(8,128)S(1)}, u32[]{:S(2)}, u32[]{:S(2)}) collective-permute-start(f32[64,128]{1,0:T(8,128)S(1)} %bitcast_add_fusion.1), channel_id=1, source_target_pairs={{0,12},{4,0},{8,4},{12,8},{1,13},{5,1},{9,5},{13,9},{2,14},{6,2},{... | collective-permute-start | bytes 98312 | tf_op jit(solution)/shard_map/ppermute | solution.py:267
  28.8 5.6 %collective-permute-start.9 = (f32[64,128]{1,0:T(8,128)S(1)}, f32[64,128]{1,0:T(8,128)S(1)}, u32[]{:S(2)}, u32[]{:S(2)}) collective-permute-start(f32[64,128]{1,0:T(8,128)S(1)} %bitcast_add_fusion.1), channel_id=1, source_target_pairs={{0,8},{4,12},{8,0},{12,4},{1,9},{5,13},{9,1},{13,5},{2,10},{6,14},... | collective-permute-start | bytes 98312 | tf_op jit(solution)/shard_map/ppermute | solution.py:267
  30.6 6.4 %collective-permute-start.14 = (bf16[4,128,128]{2,1,0:T(8,128)(2,1)S(1)}, bf16[4,128,128]{2,1,0:T(8,128)(2,1)S(1)}, u32[]{:S(2)}, u32[]{:S(2)}) collective-permute-start(bf16[4,128,128]{2,1,0:T(8,128)(2,1)S(1)} %get-tuple-element.50), channel_id=1, source_target_pairs={{0,14},{2,12},{4,2},{6,0},{8,6},{10,4},{12,10},{14,8},{1,15},{3,13... | collective-permute-start | bytes 393224 | tf_op jit(solution)/shard_map/ppermute | solution.py:273
  42.1 4.0 %collective-permute-start.15 = (f32[88,128]{1,0:T(8,128)S(1)}, f32[88,128]{1,0:T(8,128)S(1)}, u32[]{:S(2)}, u32[]{:S(2)}) collective-permute-start(f32[88,128]{1,0:T(8,128)S(1)} %pad_maximum_fusion.2), channel_id=1, source_target_pairs={{0,2},{2,0},{1,3},{3,1},{4,6},{6,4},{5,7},{7,5},{8,10},{10,8},{9,1... | collective-permute-start | bytes 135176 | tf_op jit(solution)/shard_map/ppermute | solution.py:262
  50.3 1.2 %collective-permute-start.16 = (bf16[4,16,128]{2,1,0:T(8,128)(2,1)S(1)}, bf16[4,16,128]{2,1,0:T(8,128)(2,1)S(1)}, u32[]{:S(2)}, u32[]{:S(2)}) collective-permute-start(bf16[4,16,128]{2,1,0:T(8,128)(2,1)S(1)} %get-tuple-element.38), channel_id=1, source_target_pairs={{0,1},{1,0},{2,3},{3,2},{4,5},{5,4},{6,7},{7,6},{8,9},{9,8},{10,11... | collective-permute-start | bytes 49160 | tf_op jit(solution)/shard_map/ppermute | solution.py:262
  60.8 8.4 %collective-permute-start.21 = (f32[576,128]{1,0:T(8,128)S(1)}, f32[576,128]{1,0:T(8,128)S(1)}, u32[]{:S(2)}, u32[]{:S(2)}) collective-permute-start(f32[576,128]{1,0:T(8,128)S(1)} %get-tuple-element.43), channel_id=1, source_target_pairs={{0,1},{1,0},{2,3},{3,2},{4,5},{5,4},{6,7},{7,6},{8,9},{9,8},{10,11... | collective-permute-start | bytes 884744 | tf_op jit(solution)/shard_map/ppermute | solution.py:262
  61.1 1.5 %collective-permute-start.17 = (f32[64,128]{1,0:T(8,128)S(1)}, f32[64,128]{1,0:T(8,128)S(1)}, u32[]{:S(2)}, u32[]{:S(2)}) collective-permute-start(f32[64,128]{1,0:T(8,128)S(1)} %bitcast.33), channel_id=1, source_target_pairs={{0,1},{1,0},{2,3},{3,2},{4,5},{5,4},{6,7},{7,6},{8,9},{9,8},{10,11... | collective-permute-start | bytes 98312 | tf_op jit(solution)/shard_map/ppermute | solution.py:262
  62.5 7.3 %collective-permute-start.18 = (f32[64,128]{1,0:T(8,128)S(1)}, f32[64,128]{1,0:T(8,128)S(1)}, u32[]{:S(2)}, u32[]{:S(2)}) collective-permute-start(f32[64,128]{1,0:T(8,128)S(1)} %bitcast_add_fusion), channel_id=1, source_target_pairs={{0,8},{4,12},{8,0},{12,4},{1,9},{5,13},{9,1},{13,5},{2,10},{6,14},... | collective-permute-start | bytes 98312 | tf_op jit(solution)/shard_map/ppermute | solution.py:267
  65.4 7.8 %collective-permute-start.19 = (f32[64,128]{1,0:T(8,128)S(1)}, f32[64,128]{1,0:T(8,128)S(1)}, u32[]{:S(2)}, u32[]{:S(2)}) collective-permute-start(f32[64,128]{1,0:T(8,128)S(1)} %bitcast_add_fusion), channel_id=1, source_target_pairs={{0,4},{4,8},{8,12},{12,0},{1,5},{5,9},{9,13},{13,1},{2,6},{6,10},{... | collective-permute-start | bytes 98312 | tf_op jit(solution)/shard_map/ppermute | solution.py:267
  67.0 6.2 %collective-permute-start.20 = (f32[64,128]{1,0:T(8,128)S(1)}, f32[64,128]{1,0:T(8,128)S(1)}, u32[]{:S(2)}, u32[]{:S(2)}) collective-permute-start(f32[64,128]{1,0:T(8,128)S(1)} %bitcast_add_fusion), channel_id=1, source_target_pairs={{0,12},{4,0},{8,4},{12,8},{1,13},{5,1},{9,5},{13,9},{2,14},{6,2},{... | collective-permute-start | bytes 98312 | tf_op jit(solution)/shard_map/ppermute | solution.py:267
  69.3 8.6 %collective-permute-start.22 = (bf16[576,128]{1,0:T(8,128)(2,1)S(1)}, bf16[576,128]{1,0:T(8,128)(2,1)S(1)}, u32[]{:S(2)}, u32[]{:S(2)}) collective-permute-start(bf16[576,128]{1,0:T(8,128)(2,1)S(1)} %add_convert_fusion), channel_id=1, source_target_pairs={{0,4},{4,8},{8,12},{12,0},{1,5},{5,9},{9,13},{13,1},{2,6},{6,10},{... | collective-permute-start | bytes 442376 | tf_op jit(solution)/shard_map/ppermute | solution.py:267
  69.3 13.3 %collective-permute-start.23 = (bf16[576,128]{1,0:T(8,128)(2,1)S(1)}, bf16[576,128]{1,0:T(8,128)(2,1)S(1)}, u32[]{:S(2)}, u32[]{:S(2)}) collective-permute-start(bf16[576,128]{1,0:T(8,128)(2,1)S(1)} %add_convert_fusion), channel_id=1, source_target_pairs={{0,8},{4,12},{8,0},{12,4},{1,9},{5,13},{9,1},{13,5},{2,10},{6,14},... | collective-permute-start | bytes 442376 | tf_op jit(solution)/shard_map/ppermute | solution.py:267
  69.9 12.8 %collective-permute-start.24 = (bf16[576,128]{1,0:T(8,128)(2,1)S(1)}, bf16[576,128]{1,0:T(8,128)(2,1)S(1)}, u32[]{:S(2)}, u32[]{:S(2)}) collective-permute-start(bf16[576,128]{1,0:T(8,128)(2,1)S(1)} %add_convert_fusion), channel_id=1, source_target_pairs={{0,12},{4,0},{8,4},{12,8},{1,13},{5,1},{9,5},{13,9},{2,14},{6,2},{... | collective-permute-start | bytes 442376 | tf_op jit(solution)/shard_map/ppermute | solution.py:267
  82.8 1.6 %collective-permute-start.25 = (f32[576,128]{1,0:T(8,128)S(1)}, f32[576,128]{1,0:T(8,128)S(1)}, u32[]{:S(2)}, u32[]{:S(2)}) collective-permute-start(f32[576,128]{1,0:T(8,128)S(1)} %add_add_fusion), channel_id=1, source_target_pairs={{0,1},{1,0},{2,3},{3,2},{4,5},{5,4},{6,7},{7,6},{8,9},{9,8},{10,11... | collective-permute-start | bytes 884744 | tf_op jit(solution)/shard_map/ppermute | solution.py:262

commit v6 on v5

--- a/solution.py
+++ b/solution.py
@@ -267,14 +267,11 @@
     return lax.ppermute(value, axis, [(i, (i + steps) % count) for i in range(count)])
 
 
-def swap_and_shift(value, steps):
-    count = lax.axis_size("rows")
-    pairs = [(2 * i + s, 2 * ((i + steps) % count) + 1 - s) for i in range(count) for s in range(2)]
-    return lax.ppermute(value, ("rows", "segment"), pairs)
-
-
 def pixel_total(value):
-    value = value + swap(value, "sub")
+    return rows_total(value + swap(value, "sub"))
+
+
+def rows_total(value):
     one, two, three = [shift(value, "rows", steps) for steps in (1, 2, 3)]
     return (value + two) + (one + three)
 
@@ -423,7 +420,7 @@
     return xhat, scale, hidden, sig + hidden * (1.0 - sig)
 
 
-def reduce_block(n, band, mean, rstd, mix, base=False):
+def reduce_block(n, band, mean, rstd, mix, step, base=False):
     rows, cols = band.rows, band.cols
     channels = n.acts.shape[-1]
     hidden_gradient(rows, cols, n.shifted, n.weights, n.hidden_grad)
@@ -443,8 +440,10 @@
         n.pairs[at, 0:channels] = (pre_grad * xhat).astype(BF16)
         n.pairs[at, channels:] = pre_grad.astype(BF16)
     reduced = jnp.dot(n.latent_keep[...], n.pairs[...], preferred_element_type=F32)
-    n.reduced[0, 0:8, :] = reduced[:, :channels]
-    n.reduced[0, 8:16, :] = reduced[:, channels:]
+    reduced = jnp.concatenate([reduced[:, :channels], reduced[:, channels:]])
+    n.reduced[0] = reduced
+    if not base:
+        n.give[pl.ds(pl.multiple_of(n.keep.shape[0] + 16 * step, 8), 16), :] = reduced
 
 
 def upper_kernel(rows, cols, bands, micros, count, n, step):
@@ -465,7 +464,7 @@
         band = Band(n, step, rows, cols, bands)
         for r in range(rows + 2):
             spread(r, cols, *band.row(r - 1), n.shifted)
-        reduce_block(n, band, mean, rstd, jnp.concatenate(mix).astype(BF16), base=True)
+        reduce_block(n, band, mean, rstd, jnp.concatenate(mix).astype(BF16), step, base=True)
 
     @pl.when(jnp.logical_not(active))
     def _():
@@ -501,6 +500,7 @@
     @pl.when(segment == 1)
     def _():
         n.reduced[...] = jnp.zeros_like(n.reduced)
+        n.give[pl.ds(pl.multiple_of(n.keep.shape[0] + 16 * step, 8), 16), :] = jnp.zeros_like(n.reduced[0])
         for r in range(rows + 2):
             spread(r, cols, *band.row(r - 1), n.shifted)
         for r in range(rows):
@@ -512,7 +512,7 @@
         near = n.near[0].astype(F32)
         for r in range(rows + 2):
             spread(r, cols, n.result[0, r * cols : (r + 1) * cols, :], near[r : r + 1], n.shifted)
-        reduce_block(n, band, mean, rstd, mix)
+        reduce_block(n, band, mean, rstd, mix, step)
 
     for row in range(3):
         n.total[row] += lax.dot_general(
@@ -565,9 +565,10 @@
                 acts = n.above[0]
             elif r == rows + 1:
                 acts = n.below[0]
+            elif r == 1 or r == rows:
+                acts = n.outer[0, 0:cols, :] if r == 1 else n.outer[0, cols:, :]
             else:
-                row = slice((r - 1) * cols, r * cols)
-                acts = jnp.where(step < 1, n.passed_early[0, row, :], n.passed_late[0, row, :])
+                acts = n.inner[0, (r - 2) * cols : (r - 1) * cols, :]
             xhat, scale, _, slope = pixel_values(acts, band.latent(r - 1), wide_mix, mean, rstd)
             change = rstd * (n.base[0, at, :].astype(F32) * slope * scale - mean_grad - xhat * mean_cross)
             value = band.row(r - 1)[0].astype(F32) + change
@@ -611,10 +612,6 @@
 
 
 def by_micro(value):
-    if isinstance(value, tuple):
-        value, first, size = value
-        rest = (0,) * (len(value.shape) - 1)
-        return pl.BlockSpec((1,) + tuple(value.shape[1:]), lambda m: (jnp.clip(m - first, 0, size - 1),) + rest)
     rest = (0,) * (len(value.shape) - 1)
     return pl.BlockSpec((1,) + tuple(value.shape[1:]), lambda m: (m,) + rest)
 
@@ -643,7 +640,7 @@
         compiler_params=pltpu.CompilerParams(vmem_limit_bytes=room * 1024 * 1024),
         cost_estimate=pl.CostEstimate(flops=work, bytes_accessed=work // 4, transcendentals=0),
         name=name,
-    )(*scalars.values(), *fixed.values(), *[v[0] if isinstance(v, tuple) else v for v in cut.values()])
+    )(*scalars.values(), *fixed.values(), *cut.values())
 
 
 def pair_body(
@@ -658,10 +655,8 @@
     side = lax.axis_index("sub")
     acts = activations[0].reshape(micros, pixels, channels)
 
-    early = 1
-    passed = [swap(acts[:early], "segment"), swap(acts[early:], "segment")]
-    above = swap_and_shift(acts[:, pixels - cols :], 1)
-    below = swap_and_shift(acts[:, :cols], bands - 1)
+    outer = swap(jnp.concatenate([acts[:, :cols], acts[:, pixels - cols :]], axis=1), "segment")
+    inner = swap(acts[:, cols : pixels - cols], "segment")
     kernel_passed = swap(kernel[0], "segment")
     recon_beside, target_beside = swap(recon, "sub"), swap(target, "sub")
 
@@ -731,10 +726,12 @@
         },
     )
     sums = sums_own
-    reduced, passed[0] = lax.optimization_barrier((reduced, passed[0]))
+    reduced, outer = lax.optimization_barrier((reduced, outer))
+    above = shift(outer[:, cols:], "rows", 1)
+    below = shift(outer[:, :cols], "rows", bands - 1)
     total_upper = pixel_total(reduced.reshape(micros * 16, channels))
     packed = jnp.concatenate([sums, total_upper, mix])
-    packed, passed[1], above, below = lax.optimization_barrier((packed, passed[1], above, below))
+    packed, inner, above = lax.optimization_barrier((packed, inner, above))
     packed = swap(packed, "segment")
     result, edge = call(
         functools.partial(finish_kernel, *size),
@@ -745,8 +742,8 @@
         {
             "base": base,
             "acts": acts,
-            "passed_early": (passed[0], 0, early),
-            "passed_late": (passed[1], early, micros - early),
+            "outer": outer,
+            "inner": inner,
             "above": above,
             "below": below,
             **image,
@@ -765,12 +762,13 @@
         {"sums": sums, "mix": mix, "kernel": kernel[0], **borders},
         {"result": result, "near": near, "acts": acts, **image},
         {"norm": ((micros, pixels, channels), BF16), "reduced": ((micros, 16, channels), F32)},
-        {"keep": ((half, channels), F32), "give": ((half, channels), F32)},
+        {"keep": ((half, channels), F32), "give": ((half + micros * 16, channels), F32)},
         {**work, "hidden": ((pixels, channels), BF16), "total": ((3, channels, triple), F32)},
     )
-    keep = (keep + swap(give, "sub")).astype(BF16)
+    got = swap(give, "sub")
+    keep = (keep + got[:half]).astype(BF16)
     others = [shift(keep, "rows", steps) for steps in (1, 2, 3)]
-    total_lower = pixel_total(reduced.reshape(micros * 16, channels))
+    total_lower = rows_total(reduced.reshape(micros * 16, channels) + got[half:])
     grads, mod_grad, bias_grad = call(
         functools.partial(last_kernel, rows, cols, micros, count),
         "input_gradient",

time: 85.4 us -> 79.7 us (0.933)
  starting transfers between devices: 33.7 us -> 28.9 us
  waiting for transfers between devices: 25.1 us -> 24.2 us
    ppermute x2 -> x0, starting transfers between devices: 4.32 us -> none  [swap_and_shift(): return lax.ppermute(value, ('rows', 'segment'), pairs)]
    ppermute x12 -> x14, waiting for transfers between devices: 10.1 us -> 14.4 us  [shift(): lax.ppermute(value, axis, [(i, (i + steps) % count) for i in range(count)])]
    ppermute x2 -> x0, waiting for transfers between devices: 2.66 us -> none  [swap_and_shift(): return lax.ppermute(value, ('rows', 'segment'), pairs)]
    ppermute x12 -> x11, waiting for transfers between devices: 12.4 us -> 9.86 us  [swap(): return lax.ppermute(value, axis, [(0, 1), (1, 0)])]
    ppermute x12 -> x14, starting transfers between devices: 22.2 us -> 21.4 us  [shift(): lax.ppermute(value, axis, [(i, (i + steps) % count) for i in range(count)])]
    ppermute x12 -> x11, starting transfers between devices: 7.19 us -> 7.43 us  [swap(): return lax.ppermute(value, axis, [(0, 1), (1, 0)])]
  transfers between devices with their start and end apart: 26 -> 25, of which waited for: 11 -> 11; matrix products, arithmetic and copies ran while one was open for 0% -> 0% of each run, Pallas kernels for 11% -> 12%
where the time goes in v6:
time: 79.7 us; the launch traced here: 79.5 us
  starting transfers between devices  28.9 us (36%)
  waiting for transfers between devices  24.2 us (30%)
  Pallas kernels  22.9 us (29%)
  local copies, waits for them, and re-layouts  1.38 us (2%)
  other arithmetic  1.13 us (1%)
  between operations  1 us (1%)
    pallas_call x5, Pallas kernels, call(): pl.pallas_call(body, grid=(micros,), in_specs=[pl.BlockSpec(memory_space=...  22.9 us
    ppermute x14, starting transfers between devices, shift(): lax.ppermute(value, axis, [(i, (i + steps) % count) for i in range(count)])  21.4 us
    ppermute x14, waiting for transfers between devices, shift(): lax.ppermute(value, axis, [(i, (i + steps) % count) for i in range(count)])  14.4 us
    ppermute x11, waiting for transfers between devices, swap(): return lax.ppermute(value, axis, [(0, 1), (1, 0)])  9.86 us
    ppermute x11, starting transfers between devices, swap(): return lax.ppermute(value, axis, [(0, 1), (1, 0)])  7.43 us
  transfers between devices with their start and end apart: 25, of which 11 were waited for; matrix products, arithmetic and copies ran while one was open for 0% of the time, Pallas kernels for 12%

profile of v6, /device:TPU:0, one launch (start us, length us, event | category | flops | bytes accessed | tf_op | source)
XLA Modules:
  0.0 79.5 jit_solution(6568068261498380800)
XLA Ops:
  0.6 0.0 copy-start.9
  0.7 0.5 collective-permute-start.2
  1.2 0.1 collective-permute-start.3
  1.3 1.2 %copy-done = bf16[1,4,8,128,128]{4,3,2,1,0:T(8,128)(2,1)S(1)} copy-done((bf16[1,4,8,128,128]{4,3,2,1,0:T(8,128)(2,1)S(1)}, bf16[1,4,8,128,128]{4,3,2,1,0:T(8,128)(2,1)}, u32[]{:S(2)}) %copy-start) | copy-done | bytes 1048600
  2.5 0.6 input_sums.1
  3.1 0.5 collective-permute-start
  3.6 2.6 %collective-permute-start.5 = (bf16[1152,128]{1,0:T(8,128)(2,1)}, bf16[1152,128]{1,0:T(8,128)(2,1)S(1)}, u32[]{:S(2)}, u32[]{:S(2)}) collective-permute-start(bf16[1152,128]{1,0:T(8,128)(2,1)} %bitcast.29), channel_id=1, source_target_pairs={{0,2},{2,0},{1,3},{3,1},{4,6},{6,4},{5,7},{7,5},{8,10},{10,8},{9,1... | collective-permute-start | bytes 884744 | tf_op jit(solution)/shard_map/ppermute | solution.py:262
  6.2 0.0 copy-start.1
  6.2 0.0 copy-start.5
  6.2 0.0 copy-start.6
  6.3 0.1 collective-permute-start.7
  6.4 0.0 copy-done.2
  6.5 0.0 collective-permute-done
  6.5 3.2 %collective-permute-start.1 = (f32[8,128]{1,0:T(8,128)S(1)}, f32[8,128]{1,0:T(8,128)S(1)}, u32[]{:S(2)}, u32[]{:S(2)}) collective-permute-start(f32[8,128]{1,0:T(8,128)S(1)} %add.50.refs_1_), channel_id=1, source_target_pairs={{0,8},{4,12},{8,0},{12,4},{1,9},{5,13},{9,1},{13,5},{2,10},{6,14},... | collective-permute-start | bytes 12296 | tf_op jit(solution)/shard_map/ppermute | solution.py:267
  9.7 0.0 collective-permute-done.2.refs_15_.refs_17_.refs_13_
  9.7 0.0 collective-permute-done.3.refs_16_.refs_18_.refs_14_
  9.8 1.6 %collective-permute-start.4 = (f32[72,128]{1,0:T(8,128)S(1)}, f32[72,128]{1,0:T(8,128)S(1)}, u32[]{:S(2)}, u32[]{:S(2)}) collective-permute-start(f32[72,128]{1,0:T(8,128)S(1)} %get-tuple-element.60), channel_id=1, source_target_pairs={{0,4},{4,8},{8,12},{12,0},{1,5},{5,9},{9,13},{13,1},{2,6},{6,10},{... | collective-permute-start | bytes 110600 | tf_op jit(solution)/shard_map/ppermute | solution.py:267
  11.4 2.2 %collective-permute-start.6 = (f32[72,128]{1,0:T(8,128)S(1)}, f32[72,128]{1,0:T(8,128)S(1)}, u32[]{:S(2)}, u32[]{:S(2)}) collective-permute-start(f32[72,128]{1,0:T(8,128)S(1)} %get-tuple-element.61), channel_id=1, source_target_pairs={{0,12},{4,0},{8,4},{12,8},{1,13},{5,1},{9,5},{13,9},{2,14},{6,2},{... | collective-permute-start | bytes 110600 | tf_op jit(solution)/shard_map/ppermute | solution.py:267
  13.7 0.1 slice.93
  13.7 2.0 %collective-permute-done.4.refs_8_.refs_5_.refs_4_ = f32[72,128]{1,0:T(8,128)S(1)} collective-permute-done((f32[72,128]{1,0:T(8,128)S(1)}, f32[72,128]{1,0:T(8,128)S(1)}, u32[]{:S(2)}, u32[]{:S(2)}) %collective-permute-start.4) | collective-permute-done | bytes 36896 | tf_op jit(solution)/shard_map/ppermute | solution.py:267
  15.7 1.5 %collective-permute-start.12 = (bf16[4,768,128]{2,1,0:T(8,128)(2,1)S(1)}, bf16[4,768,128]{2,1,0:T(8,128)(2,1)S(1)}, u32[]{:S(2)}, u32[]{:S(2)}) collective-permute-start(bf16[4,768,128]{2,1,0:T(8,128)(2,1)S(1)} %slice.93), channel_id=1, source_target_pairs={{0,2},{2,0},{1,3},{3,1},{4,6},{6,4},{5,7},{7,5},{8,10},{10,8},{9,1... | collective-permute-start | bytes 2359304 | tf_op jit(solution)/shard_map/ppermute | solution.py:262
  17.2 0.0 collective-permute-done.5.refs_7_
  17.2 0.0 collective-permute-done.1.refs_2_
  17.2 0.0 collective-permute-done.6.refs_9_.refs_6_.refs_5_
  17.3 6.2 %upper_block.1 = (bf16[4,1280,128]{2,1,0:T(8,128)(2,1)S(1)}, f32[4,16,128]{2,1,0:T(8,128)S(1)}) custom-call(s32[4,4,4]{2,1,0:T(4,128)S(1)} %copy-done.5, f32[8,128]{1,0:T(8,128)S(1)} %add.50.refs_1_, f32[8,128]{1,0:T(8,128)S(1)} %collective-permute-done.1.refs_2_, bf16[1,4,256]{2,1,0:T(4,128)(2,1)S(1)} %copy-done.7, bf16[1,128]{1,0:T(2,128)(2,1)S(1)} %copy-done.9, ...), custom_call_target="tpu_custom_call" | custom-call | flops 4 | bytes 1 | tf_op jit(solution)/shard_map/upper_block/pallas_call | solution.py:631
  23.4 0.0 collective-permute-done.7.refs_10_
  23.4 0.1 collective-permute-start.8
  23.5 0.1 collective-permute-start.13
  23.6 1.1 %collective-permute-done.8 = f32[64,128]{1,0:T(8,128)S(1)} collective-permute-done((f32[64,128]{1,0:T(8,128)S(1)}, f32[64,128]{1,0:T(8,128)S(1)}, u32[]{:S(2)}, u32[]{:S(2)}) %collective-permute-start.8) | collective-permute-done | bytes 32800 | tf_op jit(solution)/shard_map/ppermute | solution.py:262
  24.7 0.0 collective-permute-start.10
  24.7 3.8 %collective-permute-start.11 = (f32[64,128]{1,0:T(8,128)S(1)}, f32[64,128]{1,0:T(8,128)S(1)}, u32[]{:S(2)}, u32[]{:S(2)}) collective-permute-start(f32[64,128]{1,0:T(8,128)S(1)} %bitcast_add_fusion), channel_id=1, source_target_pairs={{0,12},{4,0},{8,4},{12,8},{1,13},{5,1},{9,5},{13,9},{2,14},{6,2},{... | collective-permute-start | bytes 98312 | tf_op jit(solution)/shard_map/ppermute | solution.py:267
  28.5 0.0 collective-permute-start.9
  28.5 3.9 %collective-permute-done.10 = f32[64,128]{1,0:T(8,128)S(1)} collective-permute-done((f32[64,128]{1,0:T(8,128)S(1)}, f32[64,128]{1,0:T(8,128)S(1)}, u32[]{:S(2)}, u32[]{:S(2)}) %collective-permute-start.10) | collective-permute-done | bytes 32800 | tf_op jit(solution)/shard_map/ppermute | solution.py:267
  32.4 0.0 collective-permute-start.15
  32.4 0.0 collective-permute-done.11
  32.4 1.7 %collective-permute-done.9 = f32[64,128]{1,0:T(8,128)S(1)} collective-permute-done((f32[64,128]{1,0:T(8,128)S(1)}, f32[64,128]{1,0:T(8,128)S(1)}, u32[]{:S(2)}, u32[]{:S(2)}) %collective-permute-start.9) | collective-permute-done | bytes 32800 | tf_op jit(solution)/shard_map/ppermute | solution.py:267
  34.2 0.0 collective-permute-done.13.refs_12_
  34.2 2.3 %collective-permute-done.12.refs_11_ = bf16[4,768,128]{2,1,0:T(8,128)(2,1)S(1)} collective-permute-done((bf16[4,768,128]{2,1,0:T(8,128)(2,1)S(1)}, bf16[4,768,128]{2,1,0:T(8,128)(2,1)S(1)}, u32[]{:S(2)}, u32[]{:S(2)}) %collective-permute-start.12) | collective-permute-done | bytes 786464 | tf_op jit(solution)/shard_map/ppermute | solution.py:262
  36.5 1.8 %collective-permute-start.14 = (f32[88,128]{1,0:T(8,128)S(1)}, f32[88,128]{1,0:T(8,128)S(1)}, u32[]{:S(2)}, u32[]{:S(2)}) collective-permute-start(f32[88,128]{1,0:T(8,128)S(1)} %pad_maximum_fusion.3), channel_id=1, source_target_pairs={{0,2},{2,0},{1,3},{3,1},{4,6},{6,4},{5,7},{7,5},{8,10},{10,8},{9,1... | collective-permute-start | bytes 135176 | tf_op jit(solution)/shard_map/ppermute | solution.py:262
  38.2 0.0 collective-permute-done.15.refs_13_
  38.2 2.3 %collective-permute-done.14.refs_3_ = f32[88,128]{1,0:T(8,128)S(1)} collective-permute-done((f32[88,128]{1,0:T(8,128)S(1)}, f32[88,128]{1,0:T(8,128)S(1)}, u32[]{:S(2)}, u32[]{:S(2)}) %collective-permute-start.14) | collective-permute-done | bytes 45088 | tf_op jit(solution)/shard_map/ppermute | solution.py:262
  40.5 4.0 %finish_upper.1 = (bf16[4,1280,128]{2,1,0:T(8,128)(2,1)S(1)}, bf16[4,16,128]{2,1,0:T(8,128)(2,1)S(1)}) custom-call(s32[4,4,4]{2,1,0:T(4,128)S(1)} %copy-done.5, f32[8,128]{1,0:T(8,128)S(1)} %fusion.7.refs_1_.refs_0_, f32[16,128]{1,0:T(8,128)S(1)} %pad_maximum_fusion.6.refs_2_.refs_1_, f32[88,128]{1,0:T(8,128)S(1)} %collective-permute-done.14.refs_3_, ...), custom_call_target="tpu_custom_call" | custom-call | flops 4 | bytes 1 | tf_op jit(solution)/shard_map/finish_upper/pallas_call | solution.py:631
  44.5 0.1 collective-permute-start.16
  44.6 1.2 %collective-permute-done.16.refs_8_ = bf16[4,16,128]{2,1,0:T(8,128)(2,1)S(1)} collective-permute-done((bf16[4,16,128]{2,1,0:T(8,128)(2,1)S(1)}, bf16[4,16,128]{2,1,0:T(8,128)(2,1)S(1)}, u32[]{:S(2)}, u32[]{:S(2)}) %collective-permute-start.16) | collective-permute-done | bytes 16416 | tf_op jit(solution)/shard_map/ppermute | solution.py:262
  45.8 9.3 %own_block.1 = (bf16[4,1024,128]{2,1,0:T(8,128)(2,1)S(1)}, f32[4,16,128]{2,1,0:T(8,128)S(1)}, f32[576,128]{1,0:T(8,128)S(1)}, f32[640,128]{1,0:T(8,128)S(1)}) custom-call(s32[4,4,4]{2,1,0:T(4,128)S(1)} %copy-done.5, f32[8,128]{1,0:T(8,128)S(1)} %fusion.7.refs_1_.refs_0_, f32[16,128]{1,0:T(8,128)S(1)} %pad_maximum_fusion.6.refs_2_.refs_1_, ...), custom_call_target="tpu_custom_call" | custom-call | flops 4 | bytes 1 | tf_op jit(solution)/shard_map/own_block/pallas_call | solution.py:631
  55.1 0.2 collective-permute-start.17
  55.4 1.5 %collective-permute-done.17 = f32[640,128]{1,0:T(8,128)S(1)} collective-permute-done((f32[640,128]{1,0:T(8,128)S(1)}, f32[640,128]{1,0:T(8,128)S(1)}, u32[]{:S(2)}, u32[]{:S(2)}) %collective-permute-start.17) | collective-permute-done | bytes 327712 | tf_op jit(solution)/shard_map/ppermute | solution.py:262
  56.8 2.8 %collective-permute-start.18 = (f32[64,128]{1,0:T(8,128)S(1)}, f32[64,128]{1,0:T(8,128)S(1)}, u32[]{:S(2)}, u32[]{:S(2)}) collective-permute-start(f32[64,128]{1,0:T(8,128)S(1)} %slice_add_fusion.1), channel_id=1, source_target_pairs={{0,8},{4,12},{8,0},{12,4},{1,9},{5,13},{9,1},{13,5},{2,10},{6,14},... | collective-permute-start | bytes 98312 | tf_op jit(solution)/shard_map/ppermute | solution.py:267
  59.7 1.6 %collective-permute-start.19 = (f32[64,128]{1,0:T(8,128)S(1)}, f32[64,128]{1,0:T(8,128)S(1)}, u32[]{:S(2)}, u32[]{:S(2)}) collective-permute-start(f32[64,128]{1,0:T(8,128)S(1)} %slice_add_fusion.1), channel_id=1, source_target_pairs={{0,4},{4,8},{8,12},{12,0},{1,5},{5,9},{9,13},{13,1},{2,6},{6,10},{... | collective-permute-start | bytes 98312 | tf_op jit(solution)/shard_map/ppermute | solution.py:267
  61.2 2.2 %collective-permute-start.20 = (f32[64,128]{1,0:T(8,128)S(1)}, f32[64,128]{1,0:T(8,128)S(1)}, u32[]{:S(2)}, u32[]{:S(2)}) collective-permute-start(f32[64,128]{1,0:T(8,128)S(1)} %slice_add_fusion.1), channel_id=1, source_target_pairs={{0,12},{4,0},{8,4},{12,8},{1,13},{5,1},{9,5},{13,9},{2,14},{6,2},{... | collective-permute-start | bytes 98312 | tf_op jit(solution)/shard_map/ppermute | solution.py:267
  63.5 0.1 collective-permute-start.21
  63.6 0.6 collective-permute-start.22
  64.1 0.0 collective-permute-done.18
  64.1 3.3 %collective-permute-start.23 = (bf16[576,128]{1,0:T(8,128)(2,1)S(1)}, bf16[576,128]{1,0:T(8,128)(2,1)S(1)}, u32[]{:S(2)}, u32[]{:S(2)}) collective-permute-start(bf16[576,128]{1,0:T(8,128)(2,1)S(1)} %fusion), channel_id=1, source_target_pairs={{0,12},{4,0},{8,4},{12,8},{1,13},{5,1},{9,5},{13,9},{2,14},{6,2},{... | collective-permute-start | bytes 442376 | tf_op jit(solution)/shard_map/ppermute | solution.py:267
  67.4 0.0 collective-permute-done.19
  67.4 0.0 collective-permute-done.20
  67.4 2.8 %input_gradient.1 = (bf16[4,1024,128]{2,1,0:T(8,128)(2,1)}, f32[1,4,256]{2,1,0:T(4,128)}, f32[1,256]{1,0:T(1,128)}) custom-call(f32[8,128]{1,0:T(8,128)S(1)} %fusion.7.refs_1_.refs_0_, f32[16,128]{1,0:T(8,128)S(1)} %pad_maximum_fusion.6.refs_2_.refs_1_, f32[64,128]{1,0:T(8,128)S(1)} %add_add_fusion.1.refs_2_, f32[64,128]{1,0:T(8,128)S(1)} %add_add_fusion.2.refs_4_.refs_3_, ...), custom_call_target="tpu_custom_call" | custom-call | flops 33554432 | bytes 8388608 | tf_op jit(solution)/shard_map/input_gradient/pallas_call | solution.py:631
  70.2 2.0 %collective-permute-done.21 = bf16[576,128]{1,0:T(8,128)(2,1)S(1)} collective-permute-done((bf16[576,128]{1,0:T(8,128)(2,1)S(1)}, bf16[576,128]{1,0:T(8,128)(2,1)S(1)}, u32[]{:S(2)}, u32[]{:S(2)}) %collective-permute-start.21) | collective-permute-done | bytes 147488 | tf_op jit(solution)/shard_map/ppermute | solution.py:267
  72.2 4.8 %collective-permute-done.22 = bf16[576,128]{1,0:T(8,128)(2,1)S(1)} collective-permute-done((bf16[576,128]{1,0:T(8,128)(2,1)S(1)}, bf16[576,128]{1,0:T(8,128)(2,1)S(1)}, u32[]{:S(2)}, u32[]{:S(2)}) %collective-permute-start.22) | collective-permute-done | bytes 147488 | tf_op jit(solution)/shard_map/ppermute | solution.py:267
  76.9 0.0 collective-permute-done.23
  76.9 0.1 add_add_fusion
  77.0 0.1 collective-permute-start.24
  77.1 1.6 %collective-permute-done.24 = f32[576,128]{1,0:T(8,128)S(1)} collective-permute-done((f32[576,128]{1,0:T(8,128)S(1)}, f32[576,128]{1,0:T(8,128)S(1)}, u32[]{:S(2)}, u32[]{:S(2)}) %collective-permute-start.24) | collective-permute-done | bytes 294944 | tf_op jit(solution)/shard_map/ppermute | solution.py:262
  78.7 0.9 %maximum_select_fusion = f32[1,1152,128]{2,1,0:T(8,128)} fusion(f32[1,576,128]{2,1,0:T(8,128)S(1)} %bitcast.35, f32[1,576,128]{2,1,0:T(8,128)S(1)} %bitcast.34, pred[]{:T(512)S(6)} %eq.3), kind=kLoop, calls=%fused_computation | loop fusion | flops 442368 | bytes 1179649 | tf_op jit(solution)/shard_map/jit(_where)/select_n | solution.py:788
  (37 shorter events, 0.3 us)
Async XLA Ops:
  0.6 5.8 %copy-start.9 = (bf16[1,128]{1,0:T(2,128)(2,1)S(1)}, bf16[1,128]{1,0:T(2,128)(2,1)}, u32[]{:S(2)}) copy-start(bf16[1,128]{1,0:T(2,128)(2,1)} %refs_4_.1) | copy-start | bytes 772
  0.6 5.8 %copy-start.8 = (bf16[1,128]{1,0:T(2,128)(2,1)S(1)}, bf16[1,128]{1,0:T(2,128)(2,1)}, u32[]{:S(2)}) copy-start(bf16[1,128]{1,0:T(2,128)(2,1)} %refs_5_.1) | copy-start | bytes 772
  0.7 9.0 %collective-permute-start.2 = (bf16[4,3,8,128]{3,2,1,0:T(8,128)(2,1)}, bf16[4,3,8,128]{3,2,1,0:T(8,128)(2,1)S(1)}, u32[]{:S(2)}, u32[]{:S(2)}) collective-permute-start(bf16[4,3,8,128]{3,2,1,0:T(8,128)(2,1)} %refs_11_.1), channel_id=1, source_target_pairs={{0,1},{1,0},{2,3},{3,2},{4,5},{5,4},{6,7},{7,6},{8,9},{9,8},{10,11... | collective-permute-start | bytes 73736 | tf_op jit(solution)/shard_map/ppermute | solution.py:262
  1.2 8.5 %collective-permute-start.3 = (bf16[4,3,8,128]{3,2,1,0:T(8,128)(2,1)}, bf16[4,3,8,128]{3,2,1,0:T(8,128)(2,1)S(1)}, u32[]{:S(2)}, u32[]{:S(2)}) collective-permute-start(bf16[4,3,8,128]{3,2,1,0:T(8,128)(2,1)} %refs_12_.3), channel_id=1, source_target_pairs={{0,1},{1,0},{2,3},{3,2},{4,5},{5,4},{6,7},{7,6},{8,9},{9,8},{10,11... | collective-permute-start | bytes 73736 | tf_op jit(solution)/shard_map/ppermute | solution.py:262
  1.2 1.2 %copy-start = (bf16[1,4,8,128,128]{4,3,2,1,0:T(8,128)(2,1)S(1)}, bf16[1,4,8,128,128]{4,3,2,1,0:T(8,128)(2,1)}, u32[]{:S(2)}) copy-start(bf16[1,4,8,128,128]{4,3,2,1,0:T(8,128)(2,1)} %param.10) | copy-start | bytes 3145732
  2.5 3.9 %copy-start.3 = (bf16[4,3,8,128]{3,2,1,0:T(8,128)(2,1)S(1)}, bf16[4,3,8,128]{3,2,1,0:T(8,128)(2,1)}, u32[]{:S(2)}) copy-start(bf16[4,3,8,128]{3,2,1,0:T(8,128)(2,1)} %refs_12_.3) | copy-start | bytes 73732
  2.5 3.9 %copy-start.4 = (bf16[4,3,8,128]{3,2,1,0:T(8,128)(2,1)S(1)}, bf16[4,3,8,128]{3,2,1,0:T(8,128)(2,1)}, u32[]{:S(2)}) copy-start(bf16[4,3,8,128]{3,2,1,0:T(8,128)(2,1)} %refs_11_.1) | copy-start | bytes 73732
  2.5 3.9 %copy-start.2 = (bf16[4,4,8,128]{3,2,1,0:T(8,128)(2,1)S(1)}, bf16[4,4,8,128]{3,2,1,0:T(8,128)(2,1)}, u32[]{:S(2)}) copy-start(bf16[4,4,8,128]{3,2,1,0:T(8,128)(2,1)} %refs_10_.3) | copy-start | bytes 98308
  2.5 4.0 %copy-start.7 = (bf16[1,4,256]{2,1,0:T(4,128)(2,1)S(1)}, bf16[1,4,256]{2,1,0:T(4,128)(2,1)}, u32[]{:S(2)}) copy-start(bf16[1,4,256]{2,1,0:T(4,128)(2,1)} %refs_3_.1) | copy-start | bytes 6148
  3.1 3.4 %collective-permute-start = (f32[8,128]{1,0:T(8,128)S(1)}, f32[8,128]{1,0:T(8,128)S(1)}, u32[]{:S(2)}, u32[]{:S(2)}) collective-permute-start(f32[8,128]{1,0:T(8,128)S(1)} %input_sums.1), channel_id=1, source_target_pairs={{0,1},{1,0},{2,3},{3,2},{4,5},{5,4},{6,7},{7,6},{8,9},{9,8},{10,11... | collective-permute-start | bytes 12296 | tf_op jit(solution)/shard_map/ppermute | solution.py:262
  3.6 13.6 %collective-permute-start.5 = (bf16[1152,128]{1,0:T(8,128)(2,1)}, bf16[1152,128]{1,0:T(8,128)(2,1)S(1)}, u32[]{:S(2)}, u32[]{:S(2)}) collective-permute-start(bf16[1152,128]{1,0:T(8,128)(2,1)} %bitcast.29), channel_id=1, source_target_pairs={{0,2},{2,0},{1,3},{3,1},{4,6},{6,4},{5,7},{7,5},{8,10},{10,8},{9,1... | collective-permute-start | bytes 884744 | tf_op jit(solution)/shard_map/ppermute | solution.py:262
  6.2 11.0 %copy-start.1 = (bf16[1,1152,128]{2,1,0:T(8,128)(2,1)S(1)}, bf16[1,1152,128]{2,1,0:T(8,128)(2,1)}, u32[]{:S(2)}) copy-start(bf16[1,1152,128]{2,1,0:T(8,128)(2,1)} %param.15) | copy-start | bytes 884740
  6.2 11.0 %copy-start.5 = (s32[4,4,4]{2,1,0:T(4,128)S(1)}, s32[4,4,4]{2,1,0:T(4,128)}, u32[]{:S(2)}) copy-start(s32[4,4,4]{2,1,0:T(4,128)} %refs_0_.5) | copy-start | bytes 772
  6.2 11.0 %copy-start.6 = (bf16[3,128]{1,0:T(4,128)(2,1)S(1)}, bf16[3,128]{1,0:T(4,128)(2,1)}, u32[]{:S(2)}) copy-start(bf16[3,128]{1,0:T(4,128)(2,1)} %refs_6_.1) | copy-start | bytes 2308
  6.3 17.1 %collective-permute-start.7 = (bf16[4,256,128]{2,1,0:T(8,128)(2,1)S(1)}, bf16[4,256,128]{2,1,0:T(8,128)(2,1)S(1)}, u32[]{:S(2)}, u32[]{:S(2)}) collective-permute-start(bf16[4,256,128]{2,1,0:T(8,128)(2,1)S(1)} %pad_maximum_fusion), channel_id=1, source_target_pairs={{0,2},{2,0},{1,3},{3,1},{4,6},{6,4},{5,7},{7,5},{8,10},{10,8},{9,1... | collective-permute-start | bytes 786440 | tf_op jit(solution)/shard_map/ppermute | solution.py:262
  6.5 10.7 %collective-permute-start.1 = (f32[8,128]{1,0:T(8,128)S(1)}, f32[8,128]{1,0:T(8,128)S(1)}, u32[]{:S(2)}, u32[]{:S(2)}) collective-permute-start(f32[8,128]{1,0:T(8,128)S(1)} %add.50.refs_1_), channel_id=1, source_target_pairs={{0,8},{4,12},{8,0},{12,4},{1,9},{5,13},{9,1},{13,5},{2,10},{6,14},... | collective-permute-start | bytes 12296 | tf_op jit(solution)/shard_map/ppermute | solution.py:267
  9.8 5.9 %collective-permute-start.4 = (f32[72,128]{1,0:T(8,128)S(1)}, f32[72,128]{1,0:T(8,128)S(1)}, u32[]{:S(2)}, u32[]{:S(2)}) collective-permute-start(f32[72,128]{1,0:T(8,128)S(1)} %get-tuple-element.60), channel_id=1, source_target_pairs={{0,4},{4,8},{8,12},{12,0},{1,5},{5,9},{9,13},{13,1},{2,6},{6,10},{... | collective-permute-start | bytes 110600 | tf_op jit(solution)/shard_map/ppermute | solution.py:267
  11.4 5.8 %collective-permute-start.6 = (f32[72,128]{1,0:T(8,128)S(1)}, f32[72,128]{1,0:T(8,128)S(1)}, u32[]{:S(2)}, u32[]{:S(2)}) collective-permute-start(f32[72,128]{1,0:T(8,128)S(1)} %get-tuple-element.61), channel_id=1, source_target_pairs={{0,12},{4,0},{8,4},{12,8},{1,13},{5,1},{9,5},{13,9},{2,14},{6,2},{... | collective-permute-start | bytes 110600 | tf_op jit(solution)/shard_map/ppermute | solution.py:267
  15.7 20.8 %collective-permute-start.12 = (bf16[4,768,128]{2,1,0:T(8,128)(2,1)S(1)}, bf16[4,768,128]{2,1,0:T(8,128)(2,1)S(1)}, u32[]{:S(2)}, u32[]{:S(2)}) collective-permute-start(bf16[4,768,128]{2,1,0:T(8,128)(2,1)S(1)} %slice.93), channel_id=1, source_target_pairs={{0,2},{2,0},{1,3},{3,1},{4,6},{6,4},{5,7},{7,5},{8,10},{10,8},{9,1... | collective-permute-start | bytes 2359304 | tf_op jit(solution)/shard_map/ppermute | solution.py:262
  23.4 1.3 %collective-permute-start.8 = (f32[64,128]{1,0:T(8,128)S(1)}, f32[64,128]{1,0:T(8,128)S(1)}, u32[]{:S(2)}, u32[]{:S(2)}) collective-permute-start(f32[64,128]{1,0:T(8,128)S(1)} %bitcast.32), channel_id=1, source_target_pairs={{0,1},{1,0},{2,3},{3,2},{4,5},{5,4},{6,7},{7,6},{8,9},{9,8},{10,11... | collective-permute-start | bytes 98312 | tf_op jit(solution)/shard_map/ppermute | solution.py:262
  23.5 10.7 %collective-permute-start.13 = (bf16[4,128,128]{2,1,0:T(8,128)(2,1)S(1)}, bf16[4,128,128]{2,1,0:T(8,128)(2,1)S(1)}, u32[]{:S(2)}, u32[]{:S(2)}) collective-permute-start(bf16[4,128,128]{2,1,0:T(8,128)(2,1)S(1)} %get-tuple-element.51), channel_id=1, source_target_pairs={{0,4},{4,8},{8,12},{12,0},{1,5},{5,9},{9,13},{13,1},{2,6},{6,10},{... | collective-permute-start | bytes 393224 | tf_op jit(solution)/shard_map/ppermute | solution.py:267
  24.7 7.7 %collective-permute-start.10 = (f32[64,128]{1,0:T(8,128)S(1)}, f32[64,128]{1,0:T(8,128)S(1)}, u32[]{:S(2)}, u32[]{:S(2)}) collective-permute-start(f32[64,128]{1,0:T(8,128)S(1)} %bitcast_add_fusion), channel_id=1, source_target_pairs={{0,4},{4,8},{8,12},{12,0},{1,5},{5,9},{9,13},{13,1},{2,6},{6,10},{... | collective-permute-start | bytes 98312 | tf_op jit(solution)/shard_map/ppermute | solution.py:267
  24.7 7.7 %collective-permute-start.11 = (f32[64,128]{1,0:T(8,128)S(1)}, f32[64,128]{1,0:T(8,128)S(1)}, u32[]{:S(2)}, u32[]{:S(2)}) collective-permute-start(f32[64,128]{1,0:T(8,128)S(1)} %bitcast_add_fusion), channel_id=1, source_target_pairs={{0,12},{4,0},{8,4},{12,8},{1,13},{5,1},{9,5},{13,9},{2,14},{6,2},{... | collective-permute-start | bytes 98312 | tf_op jit(solution)/shard_map/ppermute | solution.py:267
  28.5 5.6 %collective-permute-start.9 = (f32[64,128]{1,0:T(8,128)S(1)}, f32[64,128]{1,0:T(8,128)S(1)}, u32[]{:S(2)}, u32[]{:S(2)}) collective-permute-start(f32[64,128]{1,0:T(8,128)S(1)} %bitcast_add_fusion), channel_id=1, source_target_pairs={{0,8},{4,12},{8,0},{12,4},{1,9},{5,13},{9,1},{13,5},{2,10},{6,14},... | collective-permute-start | bytes 98312 | tf_op jit(solution)/shard_map/ppermute | solution.py:267
  32.4 5.8 %collective-permute-start.15 = (bf16[4,128,128]{2,1,0:T(8,128)(2,1)S(1)}, bf16[4,128,128]{2,1,0:T(8,128)(2,1)S(1)}, u32[]{:S(2)}, u32[]{:S(2)}) collective-permute-start(bf16[4,128,128]{2,1,0:T(8,128)(2,1)S(1)} %get-tuple-element.50), channel_id=1, source_target_pairs={{0,12},{4,0},{8,4},{12,8},{1,13},{5,1},{9,5},{13,9},{2,14},{6,2},{... | collective-permute-start | bytes 393224 | tf_op jit(solution)/shard_map/ppermute | solution.py:267
  36.5 4.0 %collective-permute-start.14 = (f32[88,128]{1,0:T(8,128)S(1)}, f32[88,128]{1,0:T(8,128)S(1)}, u32[]{:S(2)}, u32[]{:S(2)}) collective-permute-start(f32[88,128]{1,0:T(8,128)S(1)} %pad_maximum_fusion.3), channel_id=1, source_target_pairs={{0,2},{2,0},{1,3},{3,1},{4,6},{6,4},{5,7},{7,5},{8,10},{10,8},{9,1... | collective-permute-start | bytes 135176 | tf_op jit(solution)/shard_map/ppermute | solution.py:262
  44.5 1.2 %collective-permute-start.16 = (bf16[4,16,128]{2,1,0:T(8,128)(2,1)S(1)}, bf16[4,16,128]{2,1,0:T(8,128)(2,1)S(1)}, u32[]{:S(2)}, u32[]{:S(2)}) collective-permute-start(bf16[4,16,128]{2,1,0:T(8,128)(2,1)S(1)} %get-tuple-element.36), channel_id=1, source_target_pairs={{0,1},{1,0},{2,3},{3,2},{4,5},{5,4},{6,7},{7,6},{8,9},{9,8},{10,11... | collective-permute-start | bytes 49160 | tf_op jit(solution)/shard_map/ppermute | solution.py:262
  55.1 1.7 %collective-permute-start.17 = (f32[640,128]{1,0:T(8,128)S(1)}, f32[640,128]{1,0:T(8,128)S(1)}, u32[]{:S(2)}, u32[]{:S(2)}) collective-permute-start(f32[640,128]{1,0:T(8,128)S(1)} %get-tuple-element.38), channel_id=1, source_target_pairs={{0,1},{1,0},{2,3},{3,2},{4,5},{5,4},{6,7},{7,6},{8,9},{9,8},{10,11... | collective-permute-start | bytes 983048 | tf_op jit(solution)/shard_map/ppermute | solution.py:262
  56.8 7.3 %collective-permute-start.18 = (f32[64,128]{1,0:T(8,128)S(1)}, f32[64,128]{1,0:T(8,128)S(1)}, u32[]{:S(2)}, u32[]{:S(2)}) collective-permute-start(f32[64,128]{1,0:T(8,128)S(1)} %slice_add_fusion.1), channel_id=1, source_target_pairs={{0,8},{4,12},{8,0},{12,4},{1,9},{5,13},{9,1},{13,5},{2,10},{6,14},... | collective-permute-start | bytes 98312 | tf_op jit(solution)/shard_map/ppermute | solution.py:267
  59.7 7.7 %collective-permute-start.19 = (f32[64,128]{1,0:T(8,128)S(1)}, f32[64,128]{1,0:T(8,128)S(1)}, u32[]{:S(2)}, u32[]{:S(2)}) collective-permute-start(f32[64,128]{1,0:T(8,128)S(1)} %slice_add_fusion.1), channel_id=1, source_target_pairs={{0,4},{4,8},{8,12},{12,0},{1,5},{5,9},{9,13},{13,1},{2,6},{6,10},{... | collective-permute-start | bytes 98312 | tf_op jit(solution)/shard_map/ppermute | solution.py:267
  61.2 6.2 %collective-permute-start.20 = (f32[64,128]{1,0:T(8,128)S(1)}, f32[64,128]{1,0:T(8,128)S(1)}, u32[]{:S(2)}, u32[]{:S(2)}) collective-permute-start(f32[64,128]{1,0:T(8,128)S(1)} %slice_add_fusion.1), channel_id=1, source_target_pairs={{0,12},{4,0},{8,4},{12,8},{1,13},{5,1},{9,5},{13,9},{2,14},{6,2},{... | collective-permute-start | bytes 98312 | tf_op jit(solution)/shard_map/ppermute | solution.py:267
  63.5 8.6 %collective-permute-start.21 = (bf16[576,128]{1,0:T(8,128)(2,1)S(1)}, bf16[576,128]{1,0:T(8,128)(2,1)S(1)}, u32[]{:S(2)}, u32[]{:S(2)}) collective-permute-start(bf16[576,128]{1,0:T(8,128)(2,1)S(1)} %fusion), channel_id=1, source_target_pairs={{0,4},{4,8},{8,12},{12,0},{1,5},{5,9},{9,13},{13,1},{2,6},{6,10},{... | collective-permute-start | bytes 442376 | tf_op jit(solution)/shard_map/ppermute | solution.py:267
  63.6 13.3 %collective-permute-start.22 = (bf16[576,128]{1,0:T(8,128)(2,1)S(1)}, bf16[576,128]{1,0:T(8,128)(2,1)S(1)}, u32[]{:S(2)}, u32[]{:S(2)}) collective-permute-start(bf16[576,128]{1,0:T(8,128)(2,1)S(1)} %fusion), channel_id=1, source_target_pairs={{0,8},{4,12},{8,0},{12,4},{1,9},{5,13},{9,1},{13,5},{2,10},{6,14},... | collective-permute-start | bytes 442376 | tf_op jit(solution)/shard_map/ppermute | solution.py:267
  64.1 12.8 %collective-permute-start.23 = (bf16[576,128]{1,0:T(8,128)(2,1)S(1)}, bf16[576,128]{1,0:T(8,128)(2,1)S(1)}, u32[]{:S(2)}, u32[]{:S(2)}) collective-permute-start(bf16[576,128]{1,0:T(8,128)(2,1)S(1)} %fusion), channel_id=1, source_target_pairs={{0,12},{4,0},{8,4},{12,8},{1,13},{5,1},{9,5},{13,9},{2,14},{6,2},{... | collective-permute-start | bytes 442376 | tf_op jit(solution)/shard_map/ppermute | solution.py:267
  77.0 1.6 %collective-permute-start.24 = (f32[576,128]{1,0:T(8,128)S(1)}, f32[576,128]{1,0:T(8,128)S(1)}, u32[]{:S(2)}, u32[]{:S(2)}) collective-permute-start(f32[576,128]{1,0:T(8,128)S(1)} %add_add_fusion), channel_id=1, source_target_pairs={{0,1},{1,0},{2,3},{3,2},{4,5},{5,4},{6,7},{7,6},{8,9},{9,8},{10,11... | collective-permute-start | bytes 884744 | tf_op jit(solution)/shard_map/ppermute | solution.py:262

commit v7 on v6

--- a/solution.py
+++ b/solution.py
@@ -265,6 +265,11 @@
 def shift(value, axis, steps):
     count = lax.axis_size(axis)
     return lax.ppermute(value, axis, [(i, (i + steps) % count) for i in range(count)])
+
+
+def pair(value, mask):
+    count = lax.axis_size("rows")
+    return lax.ppermute(value, "rows", [(i, i ^ mask) for i in range(count)])
 
 
 def pixel_total(value):
@@ -767,7 +772,8 @@
     )
     got = swap(give, "sub")
     keep = (keep + got[:half]).astype(BF16)
-    others = [shift(keep, "rows", steps) for steps in (1, 2, 3)]
+    keep = (keep.astype(F32) + pair(keep, 1).astype(F32)).astype(BF16)
+    other_pair = pair(keep, 2)
     total_lower = rows_total(reduced.reshape(micros * 16, channels) + got[half:])
     grads, mod_grad, bias_grad = call(
         functools.partial(last_kernel, rows, cols, micros, count),
@@ -781,9 +787,8 @@
         {},
         work=1 << 25,
     )
-    grads, *others = lax.optimization_barrier((grads, *others))
-    one, two, three = [value.astype(F32) for value in others]
-    keep = (keep.astype(F32) + two) + (one + three)
+    grads, other_pair = lax.optimization_barrier((grads, other_pair))
+    keep = keep.astype(F32) + other_pair.astype(F32)
     give = swap(keep, "sub")
     kernel_grad = jnp.where(side == 0, jnp.concatenate([keep, give]), jnp.concatenate([give, keep]))
     return (grads.reshape(activations.shape), kernel_grad[None], mod_grad, bias_grad)

time: 79.7 us -> 76.7 us (0.962)
  waiting for transfers between devices: 24.2 us -> 22.5 us
  starting transfers between devices: 28.9 us -> 27.6 us
    ppermute x14 -> x11, waiting for transfers between devices: 14.4 us -> 8.54 us  [shift(): lax.ppermute(value, axis, [(i, (i + steps) % count) for i in range(count)])]
    ppermute x0 -> x2, waiting for transfers between devices: none -> 4.12 us  [pair(): return lax.ppermute(value, 'rows', [(i, i ^ mask) for i in range(count)])]
    ppermute x14 -> x11, starting transfers between devices: 21.4 us -> 17.4 us  [shift(): lax.ppermute(value, axis, [(i, (i + steps) % count) for i in range(count)])]
    ppermute x0 -> x2, starting transfers between devices: none -> 2.82 us  [pair(): return lax.ppermute(value, 'rows', [(i, i ^ mask) for i in range(count)])]
  transfers between devices with their start and end apart: 25 -> 24, of which waited for: 11 -> 11; matrix products, arithmetic and copies ran while one was open for 0% -> 0% of each run, Pallas kernels for 12% -> 12%
where the time goes in v7:
time: 76.7 us; the launch traced here: 76.5 us
  starting transfers between devices  27.6 us (36%)
  Pallas kernels  22.9 us (30%)
  waiting for transfers between devices  22.5 us (29%)
  local copies, waits for them, and re-layouts  1.38 us (2%)
  other arithmetic  1.14 us (1%)
  between operations  1 us (1%)
    pallas_call x5, Pallas kernels, call(): pl.pallas_call(body, grid=(micros,), in_specs=[pl.BlockSpec(memory_space=...  22.9 us
    ppermute x11, starting transfers between devices, shift(): lax.ppermute(value, axis, [(i, (i + steps) % count) for i in range(count)])  17.4 us
    ppermute x11, waiting for transfers between devices, swap(): return lax.ppermute(value, axis, [(0, 1), (1, 0)])  9.86 us
    ppermute x11, waiting for transfers between devices, shift(): lax.ppermute(value, axis, [(i, (i + steps) % count) for i in range(count)])  8.54 us
    ppermute x11, starting transfers between devices, swap(): return lax.ppermute(value, axis, [(0, 1), (1, 0)])  7.43 us
    ppermute x2, waiting for transfers between devices, pair(): return lax.ppermute(value, 'rows', [(i, i ^ mask) for i in range(count)])  4.12 us
    ppermute x2, starting transfers between devices, pair(): return lax.ppermute(value, 'rows', [(i, i ^ mask) for i in range(count)])  2.82 us
  transfers between devices with their start and end apart: 24, of which 11 were waited for; matrix products, arithmetic and copies ran while one was open for 0% of the time, Pallas kernels for 12%

profile of v7, /device:TPU:0, one launch (start us, length us, event | category | flops | bytes accessed | tf_op | source)
XLA Modules:
  0.0 76.5 jit_solution(4290206912966667451)
XLA Ops:
  0.6 0.0 copy-start.9
  0.7 0.5 collective-permute-start.2
  1.2 0.1 collective-permute-start.3
  1.3 1.2 %copy-done = bf16[1,4,8,128,128]{4,3,2,1,0:T(8,128)(2,1)S(1)} copy-done((bf16[1,4,8,128,128]{4,3,2,1,0:T(8,128)(2,1)S(1)}, bf16[1,4,8,128,128]{4,3,2,1,0:T(8,128)(2,1)}, u32[]{:S(2)}) %copy-start) | copy-done | bytes 1048600
  2.5 0.6 input_sums.1
  3.1 0.5 collective-permute-start
  3.6 2.6 %collective-permute-start.5 = (bf16[1152,128]{1,0:T(8,128)(2,1)}, bf16[1152,128]{1,0:T(8,128)(2,1)S(1)}, u32[]{:S(2)}, u32[]{:S(2)}) collective-permute-start(bf16[1152,128]{1,0:T(8,128)(2,1)} %bitcast.30), channel_id=1, source_target_pairs={{0,2},{2,0},{1,3},{3,1},{4,6},{6,4},{5,7},{7,5},{8,10},{10,8},{9,1... | collective-permute-start | bytes 884744 | tf_op jit(solution)/shard_map/ppermute | solution.py:262
  6.2 0.0 copy-start.1
  6.2 0.0 copy-start.5
  6.2 0.0 copy-start.6
  6.3 0.1 collective-permute-start.7
  6.4 0.0 copy-done.3
  6.4 0.0 copy-done.9
  6.4 0.0 copy-done.8
  6.5 0.0 copy-done.7
  6.5 0.0 collective-permute-done
  6.5 3.2 %collective-permute-start.1 = (f32[8,128]{1,0:T(8,128)S(1)}, f32[8,128]{1,0:T(8,128)S(1)}, u32[]{:S(2)}, u32[]{:S(2)}) collective-permute-start(f32[8,128]{1,0:T(8,128)S(1)} %add.47.refs_1_), channel_id=1, source_target_pairs={{0,8},{4,12},{8,0},{12,4},{1,9},{5,13},{9,1},{13,5},{2,10},{6,14},... | collective-permute-start | bytes 12296 | tf_op jit(solution)/shard_map/ppermute | solution.py:267
  9.7 0.0 collective-permute-done.2.refs_15_.refs_17_.refs_13_
  9.7 0.0 collective-permute-done.3.refs_16_.refs_18_.refs_14_
  9.8 1.6 %collective-permute-start.4 = (f32[72,128]{1,0:T(8,128)S(1)}, f32[72,128]{1,0:T(8,128)S(1)}, u32[]{:S(2)}, u32[]{:S(2)}) collective-permute-start(f32[72,128]{1,0:T(8,128)S(1)} %get-tuple-element.58), channel_id=1, source_target_pairs={{0,4},{4,8},{8,12},{12,0},{1,5},{5,9},{9,13},{13,1},{2,6},{6,10},{... | collective-permute-start | bytes 110600 | tf_op jit(solution)/shard_map/ppermute | solution.py:267
  11.4 2.2 %collective-permute-start.6 = (f32[72,128]{1,0:T(8,128)S(1)}, f32[72,128]{1,0:T(8,128)S(1)}, u32[]{:S(2)}, u32[]{:S(2)}) collective-permute-start(f32[72,128]{1,0:T(8,128)S(1)} %get-tuple-element.59), channel_id=1, source_target_pairs={{0,12},{4,0},{8,4},{12,8},{1,13},{5,1},{9,5},{13,9},{2,14},{6,2},{... | collective-permute-start | bytes 110600 | tf_op jit(solution)/shard_map/ppermute | solution.py:267
  13.7 0.1 slice.93
  13.7 2.0 %collective-permute-done.4.refs_8_.refs_5_.refs_4_ = f32[72,128]{1,0:T(8,128)S(1)} collective-permute-done((f32[72,128]{1,0:T(8,128)S(1)}, f32[72,128]{1,0:T(8,128)S(1)}, u32[]{:S(2)}, u32[]{:S(2)}) %collective-permute-start.4) | collective-permute-done | bytes 36896 | tf_op jit(solution)/shard_map/ppermute | solution.py:267
  15.7 1.5 %collective-permute-start.12 = (bf16[4,768,128]{2,1,0:T(8,128)(2,1)S(1)}, bf16[4,768,128]{2,1,0:T(8,128)(2,1)S(1)}, u32[]{:S(2)}, u32[]{:S(2)}) collective-permute-start(bf16[4,768,128]{2,1,0:T(8,128)(2,1)S(1)} %slice.93), channel_id=1, source_target_pairs={{0,2},{2,0},{1,3},{3,1},{4,6},{6,4},{5,7},{7,5},{8,10},{10,8},{9,1... | collective-permute-start | bytes 2359304 | tf_op jit(solution)/shard_map/ppermute | solution.py:262
  17.2 0.0 collective-permute-done.5.refs_7_
  17.2 0.0 collective-permute-done.1.refs_2_
  17.2 0.0 collective-permute-done.6.refs_9_.refs_6_.refs_5_
  17.3 6.2 %upper_block.1 = (bf16[4,1280,128]{2,1,0:T(8,128)(2,1)S(1)}, f32[4,16,128]{2,1,0:T(8,128)S(1)}) custom-call(s32[4,4,4]{2,1,0:T(4,128)S(1)} %copy-done.5, f32[8,128]{1,0:T(8,128)S(1)} %add.47.refs_1_, f32[8,128]{1,0:T(8,128)S(1)} %collective-permute-done.1.refs_2_, bf16[1,4,256]{2,1,0:T(4,128)(2,1)S(1)} %copy-done.7, bf16[1,128]{1,0:T(2,128)(2,1)S(1)} %copy-done.9, ...), custom_call_target="tpu_custom_call" | custom-call | flops 4 | bytes 1 | tf_op jit(solution)/shard_map/upper_block/pallas_call | solution.py:636
  23.4 0.0 collective-permute-done.7.refs_10_
  23.4 0.1 collective-permute-start.8
  23.5 0.1 collective-permute-start.13
  23.6 1.1 %collective-permute-done.8 = f32[64,128]{1,0:T(8,128)S(1)} collective-permute-done((f32[64,128]{1,0:T(8,128)S(1)}, f32[64,128]{1,0:T(8,128)S(1)}, u32[]{:S(2)}, u32[]{:S(2)}) %collective-permute-start.8) | collective-permute-done | bytes 32800 | tf_op jit(solution)/shard_map/ppermute | solution.py:262
  24.7 0.0 collective-permute-start.10
  24.7 3.8 %collective-permute-start.11 = (f32[64,128]{1,0:T(8,128)S(1)}, f32[64,128]{1,0:T(8,128)S(1)}, u32[]{:S(2)}, u32[]{:S(2)}) collective-permute-start(f32[64,128]{1,0:T(8,128)S(1)} %bitcast_add_fusion), channel_id=1, source_target_pairs={{0,12},{4,0},{8,4},{12,8},{1,13},{5,1},{9,5},{13,9},{2,14},{6,2},{... | collective-permute-start | bytes 98312 | tf_op jit(solution)/shard_map/ppermute | solution.py:267
  28.5 0.0 collective-permute-start.9
  28.5 3.9 %collective-permute-done.10 = f32[64,128]{1,0:T(8,128)S(1)} collective-permute-done((f32[64,128]{1,0:T(8,128)S(1)}, f32[64,128]{1,0:T(8,128)S(1)}, u32[]{:S(2)}, u32[]{:S(2)}) %collective-permute-start.10) | collective-permute-done | bytes 32800 | tf_op jit(solution)/shard_map/ppermute | solution.py:267
  32.4 0.0 collective-permute-start.15
  32.4 0.0 collective-permute-done.11
  32.4 1.7 %collective-permute-done.9 = f32[64,128]{1,0:T(8,128)S(1)} collective-permute-done((f32[64,128]{1,0:T(8,128)S(1)}, f32[64,128]{1,0:T(8,128)S(1)}, u32[]{:S(2)}, u32[]{:S(2)}) %collective-permute-start.9) | collective-permute-done | bytes 32800 | tf_op jit(solution)/shard_map/ppermute | solution.py:267
  34.2 0.0 collective-permute-done.13.refs_12_
  34.2 2.3 %collective-permute-done.12.refs_11_ = bf16[4,768,128]{2,1,0:T(8,128)(2,1)S(1)} collective-permute-done((bf16[4,768,128]{2,1,0:T(8,128)(2,1)S(1)}, bf16[4,768,128]{2,1,0:T(8,128)(2,1)S(1)}, u32[]{:S(2)}, u32[]{:S(2)}) %collective-permute-start.12) | collective-permute-done | bytes 786464 | tf_op jit(solution)/shard_map/ppermute | solution.py:262
  36.5 1.8 %collective-permute-start.14 = (f32[88,128]{1,0:T(8,128)S(1)}, f32[88,128]{1,0:T(8,128)S(1)}, u32[]{:S(2)}, u32[]{:S(2)}) collective-permute-start(f32[88,128]{1,0:T(8,128)S(1)} %pad_maximum_fusion.3), channel_id=1, source_target_pairs={{0,2},{2,0},{1,3},{3,1},{4,6},{6,4},{5,7},{7,5},{8,10},{10,8},{9,1... | collective-permute-start | bytes 135176 | tf_op jit(solution)/shard_map/ppermute | solution.py:262
  38.2 0.0 collective-permute-done.15.refs_13_
  38.2 2.3 %collective-permute-done.14.refs_3_ = f32[88,128]{1,0:T(8,128)S(1)} collective-permute-done((f32[88,128]{1,0:T(8,128)S(1)}, f32[88,128]{1,0:T(8,128)S(1)}, u32[]{:S(2)}, u32[]{:S(2)}) %collective-permute-start.14) | collective-permute-done | bytes 45088 | tf_op jit(solution)/shard_map/ppermute | solution.py:262
  40.5 4.0 %finish_upper.1 = (bf16[4,1280,128]{2,1,0:T(8,128)(2,1)S(1)}, bf16[4,16,128]{2,1,0:T(8,128)(2,1)S(1)}) custom-call(s32[4,4,4]{2,1,0:T(4,128)S(1)} %copy-done.5, f32[8,128]{1,0:T(8,128)S(1)} %fusion.7.refs_1_.refs_0_, f32[16,128]{1,0:T(8,128)S(1)} %pad_maximum_fusion.6.refs_2_.refs_1_, f32[88,128]{1,0:T(8,128)S(1)} %collective-permute-done.14.refs_3_, ...), custom_call_target="tpu_custom_call" | custom-call | flops 4 | bytes 1 | tf_op jit(solution)/shard_map/finish_upper/pallas_call | solution.py:636
  44.5 0.1 collective-permute-start.16
  44.6 1.2 %collective-permute-done.16.refs_8_ = bf16[4,16,128]{2,1,0:T(8,128)(2,1)S(1)} collective-permute-done((bf16[4,16,128]{2,1,0:T(8,128)(2,1)S(1)}, bf16[4,16,128]{2,1,0:T(8,128)(2,1)S(1)}, u32[]{:S(2)}, u32[]{:S(2)}) %collective-permute-start.16) | collective-permute-done | bytes 16416 | tf_op jit(solution)/shard_map/ppermute | solution.py:262
  45.8 9.3 %own_block.1 = (bf16[4,1024,128]{2,1,0:T(8,128)(2,1)S(1)}, f32[4,16,128]{2,1,0:T(8,128)S(1)}, f32[576,128]{1,0:T(8,128)S(1)}, f32[640,128]{1,0:T(8,128)S(1)}) custom-call(s32[4,4,4]{2,1,0:T(4,128)S(1)} %copy-done.5, f32[8,128]{1,0:T(8,128)S(1)} %fusion.7.refs_1_.refs_0_, f32[16,128]{1,0:T(8,128)S(1)} %pad_maximum_fusion.6.refs_2_.refs_1_, ...), custom_call_target="tpu_custom_call" | custom-call | flops 4 | bytes 1 | tf_op jit(solution)/shard_map/own_block/pallas_call | solution.py:636
  55.1 0.2 collective-permute-start.17
  55.4 1.5 %collective-permute-done.17 = f32[640,128]{1,0:T(8,128)S(1)} collective-permute-done((f32[640,128]{1,0:T(8,128)S(1)}, f32[640,128]{1,0:T(8,128)S(1)}, u32[]{:S(2)}, u32[]{:S(2)}) %collective-permute-start.17) | collective-permute-done | bytes 327712 | tf_op jit(solution)/shard_map/ppermute | solution.py:262
  56.9 1.9 %collective-permute-start.21 = (bf16[576,128]{1,0:T(8,128)(2,1)S(1)}, bf16[576,128]{1,0:T(8,128)(2,1)S(1)}, u32[]{:S(2)}, u32[]{:S(2)}) collective-permute-start(bf16[576,128]{1,0:T(8,128)(2,1)S(1)} %fusion), channel_id=1, source_target_pairs={{0,4},{4,0},{8,12},{12,8},{1,5},{5,1},{9,13},{13,9},{2,6},{6,2},{1... | collective-permute-start | bytes 442376 | tf_op jit(solution)/shard_map/ppermute | solution.py:272
  58.8 2.6 %collective-permute-start.18 = (f32[64,128]{1,0:T(8,128)S(1)}, f32[64,128]{1,0:T(8,128)S(1)}, u32[]{:S(2)}, u32[]{:S(2)}) collective-permute-start(f32[64,128]{1,0:T(8,128)S(1)} %slice_add_fusion.1), channel_id=1, source_target_pairs={{0,8},{4,12},{8,0},{12,4},{1,9},{5,13},{9,1},{13,5},{2,10},{6,14},... | collective-permute-start | bytes 98312 | tf_op jit(solution)/shard_map/ppermute | solution.py:267
  61.4 0.4 collective-permute-start.19
  61.8 3.4 %collective-permute-start.20 = (f32[64,128]{1,0:T(8,128)S(1)}, f32[64,128]{1,0:T(8,128)S(1)}, u32[]{:S(2)}, u32[]{:S(2)}) collective-permute-start(f32[64,128]{1,0:T(8,128)S(1)} %slice_add_fusion.1), channel_id=1, source_target_pairs={{0,12},{4,0},{8,4},{12,8},{1,13},{5,1},{9,5},{13,9},{2,14},{6,2},{... | collective-permute-start | bytes 98312 | tf_op jit(solution)/shard_map/ppermute | solution.py:267
  65.2 0.0 collective-permute-done.21
  65.3 0.9 %collective-permute-start.22 = (bf16[576,128]{1,0:T(8,128)(2,1)S(1)}, bf16[576,128]{1,0:T(8,128)(2,1)S(1)}, u32[]{:S(2)}, u32[]{:S(2)}) collective-permute-start(bf16[576,128]{1,0:T(8,128)(2,1)S(1)} %add_convert_fusion), channel_id=1, source_target_pairs={{0,8},{4,12},{8,0},{12,4},{1,9},{5,13},{9,1},{13,5},{2,10},{6,14},... | collective-permute-start | bytes 442376 | tf_op jit(solution)/shard_map/ppermute | solution.py:272
  66.2 0.0 collective-permute-done.18
  66.2 0.9 %collective-permute-done.19 = f32[64,128]{1,0:T(8,128)S(1)} collective-permute-done((f32[64,128]{1,0:T(8,128)S(1)}, f32[64,128]{1,0:T(8,128)S(1)}, u32[]{:S(2)}, u32[]{:S(2)}) %collective-permute-start.19) | collective-permute-done | bytes 32800 | tf_op jit(solution)/shard_map/ppermute | solution.py:267
  67.1 0.0 collective-permute-done.20
  67.1 2.8 %input_gradient.1 = (bf16[4,1024,128]{2,1,0:T(8,128)(2,1)}, f32[1,4,256]{2,1,0:T(4,128)}, f32[1,256]{1,0:T(1,128)}) custom-call(f32[8,128]{1,0:T(8,128)S(1)} %fusion.7.refs_1_.refs_0_, f32[16,128]{1,0:T(8,128)S(1)} %pad_maximum_fusion.6.refs_2_.refs_1_, f32[64,128]{1,0:T(8,128)S(1)} %add_add_fusion.refs_2_, f32[64,128]{1,0:T(8,128)S(1)} %add_add_fusion.1.refs_4_.refs_3_, ...), custom_call_target="tpu_custom_call" | custom-call | flops 33554432 | bytes 8388608 | tf_op jit(solution)/shard_map/input_gradient/pallas_call | solution.py:636
  69.9 4.1 %collective-permute-done.22 = bf16[576,128]{1,0:T(8,128)(2,1)S(1)} collective-permute-done((bf16[576,128]{1,0:T(8,128)(2,1)S(1)}, bf16[576,128]{1,0:T(8,128)(2,1)S(1)}, u32[]{:S(2)}, u32[]{:S(2)}) %collective-permute-start.22) | collective-permute-done | bytes 147488 | tf_op jit(solution)/shard_map/ppermute | solution.py:272
  74.0 0.1 collective-permute-start.23
  74.1 1.6 %collective-permute-done.23 = f32[576,128]{1,0:T(8,128)S(1)} collective-permute-done((f32[576,128]{1,0:T(8,128)S(1)}, f32[576,128]{1,0:T(8,128)S(1)}, u32[]{:S(2)}, u32[]{:S(2)}) %collective-permute-start.23) | collective-permute-done | bytes 294944 | tf_op jit(solution)/shard_map/ppermute | solution.py:262
  75.7 0.9 %maximum_select_fusion = f32[1,1152,128]{2,1,0:T(8,128)} fusion(f32[1,576,128]{2,1,0:T(8,128)S(1)} %bitcast.35, f32[1,576,128]{2,1,0:T(8,128)S(1)} %get-tuple-element.46, pred[]{:T(512)S(6)} %eq.3), kind=kLoop, calls=%fused_computation | loop fusion | flops 442368 | bytes 1179649 | tf_op jit(solution)/shard_map/jit(_where)/select_n | solution.py:793
  (36 shorter events, 0.4 us)
Async XLA Ops:
  0.6 5.8 %copy-start.9 = (bf16[1,128]{1,0:T(2,128)(2,1)S(1)}, bf16[1,128]{1,0:T(2,128)(2,1)}, u32[]{:S(2)}) copy-start(bf16[1,128]{1,0:T(2,128)(2,1)} %refs_4_.1) | copy-start | bytes 772
  0.6 5.8 %copy-start.8 = (bf16[1,128]{1,0:T(2,128)(2,1)S(1)}, bf16[1,128]{1,0:T(2,128)(2,1)}, u32[]{:S(2)}) copy-start(bf16[1,128]{1,0:T(2,128)(2,1)} %refs_5_.1) | copy-start | bytes 772
  0.7 9.0 %collective-permute-start.2 = (bf16[4,3,8,128]{3,2,1,0:T(8,128)(2,1)}, bf16[4,3,8,128]{3,2,1,0:T(8,128)(2,1)S(1)}, u32[]{:S(2)}, u32[]{:S(2)}) collective-permute-start(bf16[4,3,8,128]{3,2,1,0:T(8,128)(2,1)} %refs_11_.1), channel_id=1, source_target_pairs={{0,1},{1,0},{2,3},{3,2},{4,5},{5,4},{6,7},{7,6},{8,9},{9,8},{10,11... | collective-permute-start | bytes 73736 | tf_op jit(solution)/shard_map/ppermute | solution.py:262
  1.2 8.5 %collective-permute-start.3 = (bf16[4,3,8,128]{3,2,1,0:T(8,128)(2,1)}, bf16[4,3,8,128]{3,2,1,0:T(8,128)(2,1)S(1)}, u32[]{:S(2)}, u32[]{:S(2)}) collective-permute-start(bf16[4,3,8,128]{3,2,1,0:T(8,128)(2,1)} %refs_12_.3), channel_id=1, source_target_pairs={{0,1},{1,0},{2,3},{3,2},{4,5},{5,4},{6,7},{7,6},{8,9},{9,8},{10,11... | collective-permute-start | bytes 73736 | tf_op jit(solution)/shard_map/ppermute | solution.py:262
  1.2 1.2 %copy-start = (bf16[1,4,8,128,128]{4,3,2,1,0:T(8,128)(2,1)S(1)}, bf16[1,4,8,128,128]{4,3,2,1,0:T(8,128)(2,1)}, u32[]{:S(2)}) copy-start(bf16[1,4,8,128,128]{4,3,2,1,0:T(8,128)(2,1)} %param.10) | copy-start | bytes 3145732
  2.5 3.9 %copy-start.3 = (bf16[4,3,8,128]{3,2,1,0:T(8,128)(2,1)S(1)}, bf16[4,3,8,128]{3,2,1,0:T(8,128)(2,1)}, u32[]{:S(2)}) copy-start(bf16[4,3,8,128]{3,2,1,0:T(8,128)(2,1)} %refs_12_.3) | copy-start | bytes 73732
  2.5 3.9 %copy-start.4 = (bf16[4,3,8,128]{3,2,1,0:T(8,128)(2,1)S(1)}, bf16[4,3,8,128]{3,2,1,0:T(8,128)(2,1)}, u32[]{:S(2)}) copy-start(bf16[4,3,8,128]{3,2,1,0:T(8,128)(2,1)} %refs_11_.1) | copy-start | bytes 73732
  2.5 3.9 %copy-start.2 = (bf16[4,4,8,128]{3,2,1,0:T(8,128)(2,1)S(1)}, bf16[4,4,8,128]{3,2,1,0:T(8,128)(2,1)}, u32[]{:S(2)}) copy-start(bf16[4,4,8,128]{3,2,1,0:T(8,128)(2,1)} %refs_10_.3) | copy-start | bytes 98308
  2.5 4.0 %copy-start.7 = (bf16[1,4,256]{2,1,0:T(4,128)(2,1)S(1)}, bf16[1,4,256]{2,1,0:T(4,128)(2,1)}, u32[]{:S(2)}) copy-start(bf16[1,4,256]{2,1,0:T(4,128)(2,1)} %refs_3_.1) | copy-start | bytes 6148
  3.1 3.4 %collective-permute-start = (f32[8,128]{1,0:T(8,128)S(1)}, f32[8,128]{1,0:T(8,128)S(1)}, u32[]{:S(2)}, u32[]{:S(2)}) collective-permute-start(f32[8,128]{1,0:T(8,128)S(1)} %input_sums.1), channel_id=1, source_target_pairs={{0,1},{1,0},{2,3},{3,2},{4,5},{5,4},{6,7},{7,6},{8,9},{9,8},{10,11... | collective-permute-start | bytes 12296 | tf_op jit(solution)/shard_map/ppermute | solution.py:262
  3.6 13.6 %collective-permute-start.5 = (bf16[1152,128]{1,0:T(8,128)(2,1)}, bf16[1152,128]{1,0:T(8,128)(2,1)S(1)}, u32[]{:S(2)}, u32[]{:S(2)}) collective-permute-start(bf16[1152,128]{1,0:T(8,128)(2,1)} %bitcast.30), channel_id=1, source_target_pairs={{0,2},{2,0},{1,3},{3,1},{4,6},{6,4},{5,7},{7,5},{8,10},{10,8},{9,1... | collective-permute-start | bytes 884744 | tf_op jit(solution)/shard_map/ppermute | solution.py:262
  6.2 11.0 %copy-start.1 = (bf16[1,1152,128]{2,1,0:T(8,128)(2,1)S(1)}, bf16[1,1152,128]{2,1,0:T(8,128)(2,1)}, u32[]{:S(2)}) copy-start(bf16[1,1152,128]{2,1,0:T(8,128)(2,1)} %param.15) | copy-start | bytes 884740
  6.2 11.0 %copy-start.5 = (s32[4,4,4]{2,1,0:T(4,128)S(1)}, s32[4,4,4]{2,1,0:T(4,128)}, u32[]{:S(2)}) copy-start(s32[4,4,4]{2,1,0:T(4,128)} %refs_0_.5) | copy-start | bytes 772
  6.2 11.0 %copy-start.6 = (bf16[3,128]{1,0:T(4,128)(2,1)S(1)}, bf16[3,128]{1,0:T(4,128)(2,1)}, u32[]{:S(2)}) copy-start(bf16[3,128]{1,0:T(4,128)(2,1)} %refs_6_.1) | copy-start | bytes 2308
  6.3 17.1 %collective-permute-start.7 = (bf16[4,256,128]{2,1,0:T(8,128)(2,1)S(1)}, bf16[4,256,128]{2,1,0:T(8,128)(2,1)S(1)}, u32[]{:S(2)}, u32[]{:S(2)}) collective-permute-start(bf16[4,256,128]{2,1,0:T(8,128)(2,1)S(1)} %pad_maximum_fusion), channel_id=1, source_target_pairs={{0,2},{2,0},{1,3},{3,1},{4,6},{6,4},{5,7},{7,5},{8,10},{10,8},{9,1... | collective-permute-start | bytes 786440 | tf_op jit(solution)/shard_map/ppermute | solution.py:262
  6.5 10.7 %collective-permute-start.1 = (f32[8,128]{1,0:T(8,128)S(1)}, f32[8,128]{1,0:T(8,128)S(1)}, u32[]{:S(2)}, u32[]{:S(2)}) collective-permute-start(f32[8,128]{1,0:T(8,128)S(1)} %add.47.refs_1_), channel_id=1, source_target_pairs={{0,8},{4,12},{8,0},{12,4},{1,9},{5,13},{9,1},{13,5},{2,10},{6,14},... | collective-permute-start | bytes 12296 | tf_op jit(solution)/shard_map/ppermute | solution.py:267
  9.8 5.9 %collective-permute-start.4 = (f32[72,128]{1,0:T(8,128)S(1)}, f32[72,128]{1,0:T(8,128)S(1)}, u32[]{:S(2)}, u32[]{:S(2)}) collective-permute-start(f32[72,128]{1,0:T(8,128)S(1)} %get-tuple-element.58), channel_id=1, source_target_pairs={{0,4},{4,8},{8,12},{12,0},{1,5},{5,9},{9,13},{13,1},{2,6},{6,10},{... | collective-permute-start | bytes 110600 | tf_op jit(solution)/shard_map/ppermute | solution.py:267
  11.4 5.8 %collective-permute-start.6 = (f32[72,128]{1,0:T(8,128)S(1)}, f32[72,128]{1,0:T(8,128)S(1)}, u32[]{:S(2)}, u32[]{:S(2)}) collective-permute-start(f32[72,128]{1,0:T(8,128)S(1)} %get-tuple-element.59), channel_id=1, source_target_pairs={{0,12},{4,0},{8,4},{12,8},{1,13},{5,1},{9,5},{13,9},{2,14},{6,2},{... | collective-permute-start | bytes 110600 | tf_op jit(solution)/shard_map/ppermute | solution.py:267
  15.7 20.8 %collective-permute-start.12 = (bf16[4,768,128]{2,1,0:T(8,128)(2,1)S(1)}, bf16[4,768,128]{2,1,0:T(8,128)(2,1)S(1)}, u32[]{:S(2)}, u32[]{:S(2)}) collective-permute-start(bf16[4,768,128]{2,1,0:T(8,128)(2,1)S(1)} %slice.93), channel_id=1, source_target_pairs={{0,2},{2,0},{1,3},{3,1},{4,6},{6,4},{5,7},{7,5},{8,10},{10,8},{9,1... | collective-permute-start | bytes 2359304 | tf_op jit(solution)/shard_map/ppermute | solution.py:262
  23.4 1.3 %collective-permute-start.8 = (f32[64,128]{1,0:T(8,128)S(1)}, f32[64,128]{1,0:T(8,128)S(1)}, u32[]{:S(2)}, u32[]{:S(2)}) collective-permute-start(f32[64,128]{1,0:T(8,128)S(1)} %bitcast.33), channel_id=1, source_target_pairs={{0,1},{1,0},{2,3},{3,2},{4,5},{5,4},{6,7},{7,6},{8,9},{9,8},{10,11... | collective-permute-start | bytes 98312 | tf_op jit(solution)/shard_map/ppermute | solution.py:262
  23.5 10.7 %collective-permute-start.13 = (bf16[4,128,128]{2,1,0:T(8,128)(2,1)S(1)}, bf16[4,128,128]{2,1,0:T(8,128)(2,1)S(1)}, u32[]{:S(2)}, u32[]{:S(2)}) collective-permute-start(bf16[4,128,128]{2,1,0:T(8,128)(2,1)S(1)} %get-tuple-element.49), channel_id=1, source_target_pairs={{0,4},{4,8},{8,12},{12,0},{1,5},{5,9},{9,13},{13,1},{2,6},{6,10},{... | collective-permute-start | bytes 393224 | tf_op jit(solution)/shard_map/ppermute | solution.py:267
  24.7 7.7 %collective-permute-start.10 = (f32[64,128]{1,0:T(8,128)S(1)}, f32[64,128]{1,0:T(8,128)S(1)}, u32[]{:S(2)}, u32[]{:S(2)}) collective-permute-start(f32[64,128]{1,0:T(8,128)S(1)} %bitcast_add_fusion), channel_id=1, source_target_pairs={{0,4},{4,8},{8,12},{12,0},{1,5},{5,9},{9,13},{13,1},{2,6},{6,10},{... | collective-permute-start | bytes 98312 | tf_op jit(solution)/shard_map/ppermute | solution.py:267
  24.7 7.7 %collective-permute-start.11 = (f32[64,128]{1,0:T(8,128)S(1)}, f32[64,128]{1,0:T(8,128)S(1)}, u32[]{:S(2)}, u32[]{:S(2)}) collective-permute-start(f32[64,128]{1,0:T(8,128)S(1)} %bitcast_add_fusion), channel_id=1, source_target_pairs={{0,12},{4,0},{8,4},{12,8},{1,13},{5,1},{9,5},{13,9},{2,14},{6,2},{... | collective-permute-start | bytes 98312 | tf_op jit(solution)/shard_map/ppermute | solution.py:267
  28.5 5.6 %collective-permute-start.9 = (f32[64,128]{1,0:T(8,128)S(1)}, f32[64,128]{1,0:T(8,128)S(1)}, u32[]{:S(2)}, u32[]{:S(2)}) collective-permute-start(f32[64,128]{1,0:T(8,128)S(1)} %bitcast_add_fusion), channel_id=1, source_target_pairs={{0,8},{4,12},{8,0},{12,4},{1,9},{5,13},{9,1},{13,5},{2,10},{6,14},... | collective-permute-start | bytes 98312 | tf_op jit(solution)/shard_map/ppermute | solution.py:267
  32.4 5.8 %collective-permute-start.15 = (bf16[4,128,128]{2,1,0:T(8,128)(2,1)S(1)}, bf16[4,128,128]{2,1,0:T(8,128)(2,1)S(1)}, u32[]{:S(2)}, u32[]{:S(2)}) collective-permute-start(bf16[4,128,128]{2,1,0:T(8,128)(2,1)S(1)} %get-tuple-element.48), channel_id=1, source_target_pairs={{0,12},{4,0},{8,4},{12,8},{1,13},{5,1},{9,5},{13,9},{2,14},{6,2},{... | collective-permute-start | bytes 393224 | tf_op jit(solution)/shard_map/ppermute | solution.py:267
  36.5 4.0 %collective-permute-start.14 = (f32[88,128]{1,0:T(8,128)S(1)}, f32[88,128]{1,0:T(8,128)S(1)}, u32[]{:S(2)}, u32[]{:S(2)}) collective-permute-start(f32[88,128]{1,0:T(8,128)S(1)} %pad_maximum_fusion.3), channel_id=1, source_target_pairs={{0,2},{2,0},{1,3},{3,1},{4,6},{6,4},{5,7},{7,5},{8,10},{10,8},{9,1... | collective-permute-start | bytes 135176 | tf_op jit(solution)/shard_map/ppermute | solution.py:262
  44.5 1.2 %collective-permute-start.16 = (bf16[4,16,128]{2,1,0:T(8,128)(2,1)S(1)}, bf16[4,16,128]{2,1,0:T(8,128)(2,1)S(1)}, u32[]{:S(2)}, u32[]{:S(2)}) collective-permute-start(bf16[4,16,128]{2,1,0:T(8,128)(2,1)S(1)} %get-tuple-element.34), channel_id=1, source_target_pairs={{0,1},{1,0},{2,3},{3,2},{4,5},{5,4},{6,7},{7,6},{8,9},{9,8},{10,11... | collective-permute-start | bytes 49160 | tf_op jit(solution)/shard_map/ppermute | solution.py:262
  55.1 1.7 %collective-permute-start.17 = (f32[640,128]{1,0:T(8,128)S(1)}, f32[640,128]{1,0:T(8,128)S(1)}, u32[]{:S(2)}, u32[]{:S(2)}) collective-permute-start(f32[640,128]{1,0:T(8,128)S(1)} %get-tuple-element.36), channel_id=1, source_target_pairs={{0,1},{1,0},{2,3},{3,2},{4,5},{5,4},{6,7},{7,6},{8,9},{9,8},{10,11... | collective-permute-start | bytes 983048 | tf_op jit(solution)/shard_map/ppermute | solution.py:262
  56.9 8.3 %collective-permute-start.21 = (bf16[576,128]{1,0:T(8,128)(2,1)S(1)}, bf16[576,128]{1,0:T(8,128)(2,1)S(1)}, u32[]{:S(2)}, u32[]{:S(2)}) collective-permute-start(bf16[576,128]{1,0:T(8,128)(2,1)S(1)} %fusion), channel_id=1, source_target_pairs={{0,4},{4,0},{8,12},{12,8},{1,5},{5,1},{9,13},{13,9},{2,6},{6,2},{1... | collective-permute-start | bytes 442376 | tf_op jit(solution)/shard_map/ppermute | solution.py:272
  58.8 7.4 %collective-permute-start.18 = (f32[64,128]{1,0:T(8,128)S(1)}, f32[64,128]{1,0:T(8,128)S(1)}, u32[]{:S(2)}, u32[]{:S(2)}) collective-permute-start(f32[64,128]{1,0:T(8,128)S(1)} %slice_add_fusion.1), channel_id=1, source_target_pairs={{0,8},{4,12},{8,0},{12,4},{1,9},{5,13},{9,1},{13,5},{2,10},{6,14},... | collective-permute-start | bytes 98312 | tf_op jit(solution)/shard_map/ppermute | solution.py:267
  61.4 5.7 %collective-permute-start.19 = (f32[64,128]{1,0:T(8,128)S(1)}, f32[64,128]{1,0:T(8,128)S(1)}, u32[]{:S(2)}, u32[]{:S(2)}) collective-permute-start(f32[64,128]{1,0:T(8,128)S(1)} %slice_add_fusion.1), channel_id=1, source_target_pairs={{0,4},{4,8},{8,12},{12,0},{1,5},{5,9},{9,13},{13,1},{2,6},{6,10},{... | collective-permute-start | bytes 98312 | tf_op jit(solution)/shard_map/ppermute | solution.py:267
  61.8 5.3 %collective-permute-start.20 = (f32[64,128]{1,0:T(8,128)S(1)}, f32[64,128]{1,0:T(8,128)S(1)}, u32[]{:S(2)}, u32[]{:S(2)}) collective-permute-start(f32[64,128]{1,0:T(8,128)S(1)} %slice_add_fusion.1), channel_id=1, source_target_pairs={{0,12},{4,0},{8,4},{12,8},{1,13},{5,1},{9,5},{13,9},{2,14},{6,2},{... | collective-permute-start | bytes 98312 | tf_op jit(solution)/shard_map/ppermute | solution.py:267
  65.3 8.7 %collective-permute-start.22 = (bf16[576,128]{1,0:T(8,128)(2,1)S(1)}, bf16[576,128]{1,0:T(8,128)(2,1)S(1)}, u32[]{:S(2)}, u32[]{:S(2)}) collective-permute-start(bf16[576,128]{1,0:T(8,128)(2,1)S(1)} %add_convert_fusion), channel_id=1, source_target_pairs={{0,8},{4,12},{8,0},{12,4},{1,9},{5,13},{9,1},{13,5},{2,10},{6,14},... | collective-permute-start | bytes 442376 | tf_op jit(solution)/shard_map/ppermute | solution.py:272
  74.0 1.6 %collective-permute-start.23 = (f32[576,128]{1,0:T(8,128)S(1)}, f32[576,128]{1,0:T(8,128)S(1)}, u32[]{:S(2)}, u32[]{:S(2)}) collective-permute-start(f32[576,128]{1,0:T(8,128)S(1)} %get-tuple-element.47), channel_id=1, source_target_pairs={{0,1},{1,0},{2,3},{3,2},{4,5},{5,4},{6,7},{7,6},{8,9},{9,8},{10,11... | collective-permute-start | bytes 884744 | tf_op jit(solution)/shard_map/ppermute | solution.py:262

commit v8 on v7

--- a/solution.py
+++ b/solution.py
@@ -402,16 +402,25 @@
     for row in range(3):
         for col in range(3):
             tap = tap_of(row, col)
-            weights[row, :, col * channels : (col + 1) * channels] = kernel_ref[tap * channels : (tap + 1) * channels, :]
+            for at in range(2):
+                weights[row + at, at * channels : (at + 1) * channels, col * channels : (col + 1) * channels] = kernel_ref[
+                    tap * channels : (tap + 1) * channels, :
+                ]
+    for at in range(2):
+        unused = weights[3 * (1 - at), at * channels : (at + 1) * channels, :]
+        weights[3 * (1 - at), at * channels : (at + 1) * channels, :] = jnp.zeros_like(unused)
 
 
 def hidden_gradient(rows, cols, shifted, weights, hidden_grad):
-    pixels = rows * cols
-    total = lax.dot_general(shifted[0:pixels, :], weights[0], NT, preferred_element_type=F32)
-    total = total + lax.dot_general(shifted[cols : cols + pixels, :], weights[1], NT, preferred_element_type=F32)
-    hidden_grad[0:pixels, :] = total + lax.dot_general(
-        shifted[2 * cols : 2 * cols + pixels, :], weights[2], NT, preferred_element_type=F32
-    )
+    channels = hidden_grad.shape[-1]
+    total = None
+    for k in range(4):
+        left = jnp.concatenate([shifted[(r + k) * cols : (r + k + 1) * cols, :] for r in range(0, rows, 2)])
+        part = lax.dot_general(left, weights[k], NT, preferred_element_type=F32)
+        total = part if total is None else total + part
+    for r in range(rows):
+        half = (r % 2) * channels
+        hidden_grad[r * cols : (r + 1) * cols, :] = total[r // 2 * cols : (r // 2 + 1) * cols, half : half + channels]
 
 
 def pixel_values(acts, latent, mix, mean, rstd):
@@ -695,7 +704,7 @@
     shifted = {"shifted": ((wide, triple), BF16)}
     work = {
         **shifted,
-        "weights": ((3, channels, triple), BF16),
+        "weights": ((4, 2 * channels, triple), BF16),
         "hidden_grad": ((pixels, channels), F32),
         "latent_keep": ((8, pixels), BF16),
         "pairs": ((pixels, 2 * channels), BF16),

time: 76.7 us -> 76.1 us (level)
  Pallas kernels: 22.9 us -> 21.8 us
    pallas_call x5, Pallas kernels: 22.9 us -> 21.8 us  [call(): pl.pallas_call(body, grid=(micros,), in_specs=[pl.BlockSpec(memory_space=...]
where the time goes in v8:
time: 76.1 us; the launch traced here: 75.9 us
  starting transfers between devices  27.6 us (36%)
  waiting for transfers between devices  23 us (30%)
  Pallas kernels  21.8 us (29%)
  local copies, waits for them, and re-layouts  1.38 us (2%)
  other arithmetic  1.14 us (1%)
  between operations  1 us (1%)
    pallas_call x5, Pallas kernels, call(): pl.pallas_call(body, grid=(micros,), in_specs=[pl.BlockSpec(memory_space=...  21.8 us
    ppermute x11, starting transfers between devices, shift(): lax.ppermute(value, axis, [(i, (i + steps) % count) for i in range(count)])  17.4 us
    ppermute x11, waiting for transfers between devices, swap(): return lax.ppermute(value, axis, [(0, 1), (1, 0)])  10.3 us
    ppermute x11, waiting for transfers between devices, shift(): lax.ppermute(value, axis, [(i, (i + steps) % count) for i in range(count)])  8.54 us
    ppermute x11, starting transfers between devices, swap(): return lax.ppermute(value, axis, [(0, 1), (1, 0)])  7.43 us
    ppermute x2, waiting for transfers between devices, pair(): return lax.ppermute(value, 'rows', [(i, i ^ mask) for i in range(count)])  4.12 us
    ppermute x2, starting transfers between devices, pair(): return lax.ppermute(value, 'rows', [(i, i ^ mask) for i in range(count)])  2.82 us
  transfers between devices with their start and end apart: 24, of which 11 were waited for; matrix products, arithmetic and copies ran while one was open for 0% of the time, Pallas kernels for 12%

profile of v8, /device:TPU:0, one launch (start us, length us, event | category | flops | bytes accessed | tf_op | source)
XLA Modules:
  0.0 75.9 jit_solution(4697356417456956379)
XLA Ops:
  0.6 0.0 copy-start.9
  0.7 0.5 collective-permute-start.2
  1.2 0.1 collective-permute-start.3
  1.3 1.2 %copy-done = bf16[1,4,8,128,128]{4,3,2,1,0:T(8,128)(2,1)S(1)} copy-done((bf16[1,4,8,128,128]{4,3,2,1,0:T(8,128)(2,1)S(1)}, bf16[1,4,8,128,128]{4,3,2,1,0:T(8,128)(2,1)}, u32[]{:S(2)}) %copy-start) | copy-done | bytes 1048600
  2.5 0.6 input_sums.1
  3.1 0.5 collective-permute-start
  3.6 2.6 %collective-permute-start.5 = (bf16[1152,128]{1,0:T(8,128)(2,1)}, bf16[1152,128]{1,0:T(8,128)(2,1)S(1)}, u32[]{:S(2)}, u32[]{:S(2)}) collective-permute-start(bf16[1152,128]{1,0:T(8,128)(2,1)} %bitcast.30), channel_id=1, source_target_pairs={{0,2},{2,0},{1,3},{3,1},{4,6},{6,4},{5,7},{7,5},{8,10},{10,8},{9,1... | collective-permute-start | bytes 884744 | tf_op jit(solution)/shard_map/ppermute | solution.py:262
  6.2 0.0 copy-start.1
  6.2 0.0 copy-start.5
  6.2 0.0 copy-start.6
  6.3 0.1 collective-permute-start.7
  6.4 0.0 copy-done.3
  6.4 0.0 copy-done.9
  6.4 0.0 copy-done.8
  6.5 0.0 copy-done.7
  6.5 0.0 collective-permute-done
  6.5 3.2 %collective-permute-start.1 = (f32[8,128]{1,0:T(8,128)S(1)}, f32[8,128]{1,0:T(8,128)S(1)}, u32[]{:S(2)}, u32[]{:S(2)}) collective-permute-start(f32[8,128]{1,0:T(8,128)S(1)} %add.47.refs_1_), channel_id=1, source_target_pairs={{0,8},{4,12},{8,0},{12,4},{1,9},{5,13},{9,1},{13,5},{2,10},{6,14},... | collective-permute-start | bytes 12296 | tf_op jit(solution)/shard_map/ppermute | solution.py:267
  9.7 0.0 collective-permute-done.2.refs_15_.refs_17_.refs_13_
  9.7 0.0 collective-permute-done.3.refs_16_.refs_18_.refs_14_
  9.8 1.6 %collective-permute-start.4 = (f32[72,128]{1,0:T(8,128)S(1)}, f32[72,128]{1,0:T(8,128)S(1)}, u32[]{:S(2)}, u32[]{:S(2)}) collective-permute-start(f32[72,128]{1,0:T(8,128)S(1)} %get-tuple-element.58), channel_id=1, source_target_pairs={{0,4},{4,8},{8,12},{12,0},{1,5},{5,9},{9,13},{13,1},{2,6},{6,10},{... | collective-permute-start | bytes 110600 | tf_op jit(solution)/shard_map/ppermute | solution.py:267
  11.4 2.2 %collective-permute-start.6 = (f32[72,128]{1,0:T(8,128)S(1)}, f32[72,128]{1,0:T(8,128)S(1)}, u32[]{:S(2)}, u32[]{:S(2)}) collective-permute-start(f32[72,128]{1,0:T(8,128)S(1)} %get-tuple-element.59), channel_id=1, source_target_pairs={{0,12},{4,0},{8,4},{12,8},{1,13},{5,1},{9,5},{13,9},{2,14},{6,2},{... | collective-permute-start | bytes 110600 | tf_op jit(solution)/shard_map/ppermute | solution.py:267
  13.7 0.1 slice.93
  13.7 2.0 %collective-permute-done.4.refs_8_.refs_5_.refs_4_ = f32[72,128]{1,0:T(8,128)S(1)} collective-permute-done((f32[72,128]{1,0:T(8,128)S(1)}, f32[72,128]{1,0:T(8,128)S(1)}, u32[]{:S(2)}, u32[]{:S(2)}) %collective-permute-start.4) | collective-permute-done | bytes 36896 | tf_op jit(solution)/shard_map/ppermute | solution.py:267
  15.7 1.5 %collective-permute-start.12 = (bf16[4,768,128]{2,1,0:T(8,128)(2,1)S(1)}, bf16[4,768,128]{2,1,0:T(8,128)(2,1)S(1)}, u32[]{:S(2)}, u32[]{:S(2)}) collective-permute-start(bf16[4,768,128]{2,1,0:T(8,128)(2,1)S(1)} %slice.93), channel_id=1, source_target_pairs={{0,2},{2,0},{1,3},{3,1},{4,6},{6,4},{5,7},{7,5},{8,10},{10,8},{9,1... | collective-permute-start | bytes 2359304 | tf_op jit(solution)/shard_map/ppermute | solution.py:262
  17.2 0.0 collective-permute-done.5.refs_7_
  17.2 0.0 collective-permute-done.1.refs_2_
  17.2 0.0 collective-permute-done.6.refs_9_.refs_6_.refs_5_
  17.3 5.7 %upper_block.1 = (bf16[4,1280,128]{2,1,0:T(8,128)(2,1)S(1)}, f32[4,16,128]{2,1,0:T(8,128)S(1)}) custom-call(s32[4,4,4]{2,1,0:T(4,128)S(1)} %copy-done.5, f32[8,128]{1,0:T(8,128)S(1)} %add.47.refs_1_, f32[8,128]{1,0:T(8,128)S(1)} %collective-permute-done.1.refs_2_, bf16[1,4,256]{2,1,0:T(4,128)(2,1)S(1)} %copy-done.7, bf16[1,128]{1,0:T(2,128)(2,1)S(1)} %copy-done.9, ...), custom_call_target="tpu_custom_call" | custom-call | flops 4 | bytes 1 | tf_op jit(solution)/shard_map/upper_block/pallas_call | solution.py:645
  22.9 0.0 collective-permute-done.7.refs_10_
  23.0 0.1 collective-permute-start.8
  23.1 0.1 collective-permute-start.13
  23.1 1.1 %collective-permute-done.8 = f32[64,128]{1,0:T(8,128)S(1)} collective-permute-done((f32[64,128]{1,0:T(8,128)S(1)}, f32[64,128]{1,0:T(8,128)S(1)}, u32[]{:S(2)}, u32[]{:S(2)}) %collective-permute-start.8) | collective-permute-done | bytes 32800 | tf_op jit(solution)/shard_map/ppermute | solution.py:262
  24.2 0.0 collective-permute-start.10
  24.2 3.8 %collective-permute-start.11 = (f32[64,128]{1,0:T(8,128)S(1)}, f32[64,128]{1,0:T(8,128)S(1)}, u32[]{:S(2)}, u32[]{:S(2)}) collective-permute-start(f32[64,128]{1,0:T(8,128)S(1)} %bitcast_add_fusion), channel_id=1, source_target_pairs={{0,12},{4,0},{8,4},{12,8},{1,13},{5,1},{9,5},{13,9},{2,14},{6,2},{... | collective-permute-start | bytes 98312 | tf_op jit(solution)/shard_map/ppermute | solution.py:267
  28.1 0.0 collective-permute-start.9
  28.1 3.9 %collective-permute-done.10 = f32[64,128]{1,0:T(8,128)S(1)} collective-permute-done((f32[64,128]{1,0:T(8,128)S(1)}, f32[64,128]{1,0:T(8,128)S(1)}, u32[]{:S(2)}, u32[]{:S(2)}) %collective-permute-start.10) | collective-permute-done | bytes 32800 | tf_op jit(solution)/shard_map/ppermute | solution.py:267
  32.0 0.0 collective-permute-start.15
  32.0 0.0 collective-permute-done.11
  32.0 1.7 %collective-permute-done.9 = f32[64,128]{1,0:T(8,128)S(1)} collective-permute-done((f32[64,128]{1,0:T(8,128)S(1)}, f32[64,128]{1,0:T(8,128)S(1)}, u32[]{:S(2)}, u32[]{:S(2)}) %collective-permute-start.9) | collective-permute-done | bytes 32800 | tf_op jit(solution)/shard_map/ppermute | solution.py:267
  33.7 0.0 collective-permute-done.13.refs_12_
  33.7 2.7 %collective-permute-done.12.refs_11_ = bf16[4,768,128]{2,1,0:T(8,128)(2,1)S(1)} collective-permute-done((bf16[4,768,128]{2,1,0:T(8,128)(2,1)S(1)}, bf16[4,768,128]{2,1,0:T(8,128)(2,1)S(1)}, u32[]{:S(2)}, u32[]{:S(2)}) %collective-permute-start.12) | collective-permute-done | bytes 786464 | tf_op jit(solution)/shard_map/ppermute | solution.py:262
  36.5 1.8 %collective-permute-start.14 = (f32[88,128]{1,0:T(8,128)S(1)}, f32[88,128]{1,0:T(8,128)S(1)}, u32[]{:S(2)}, u32[]{:S(2)}) collective-permute-start(f32[88,128]{1,0:T(8,128)S(1)} %pad_maximum_fusion.3), channel_id=1, source_target_pairs={{0,2},{2,0},{1,3},{3,1},{4,6},{6,4},{5,7},{7,5},{8,10},{10,8},{9,1... | collective-permute-start | bytes 135176 | tf_op jit(solution)/shard_map/ppermute | solution.py:262
  38.2 0.0 collective-permute-done.15.refs_13_
  38.2 2.3 %collective-permute-done.14.refs_3_ = f32[88,128]{1,0:T(8,128)S(1)} collective-permute-done((f32[88,128]{1,0:T(8,128)S(1)}, f32[88,128]{1,0:T(8,128)S(1)}, u32[]{:S(2)}, u32[]{:S(2)}) %collective-permute-start.14) | collective-permute-done | bytes 45088 | tf_op jit(solution)/shard_map/ppermute | solution.py:262
  40.5 4.0 %finish_upper.1 = (bf16[4,1280,128]{2,1,0:T(8,128)(2,1)S(1)}, bf16[4,16,128]{2,1,0:T(8,128)(2,1)S(1)}) custom-call(s32[4,4,4]{2,1,0:T(4,128)S(1)} %copy-done.5, f32[8,128]{1,0:T(8,128)S(1)} %fusion.7.refs_1_.refs_0_, f32[16,128]{1,0:T(8,128)S(1)} %pad_maximum_fusion.6.refs_2_.refs_1_, f32[88,128]{1,0:T(8,128)S(1)} %collective-permute-done.14.refs_3_, ...), custom_call_target="tpu_custom_call" | custom-call | flops 4 | bytes 1 | tf_op jit(solution)/shard_map/finish_upper/pallas_call | solution.py:645
  44.5 0.1 collective-permute-start.16
  44.6 1.2 %collective-permute-done.16.refs_8_ = bf16[4,16,128]{2,1,0:T(8,128)(2,1)S(1)} collective-permute-done((bf16[4,16,128]{2,1,0:T(8,128)(2,1)S(1)}, bf16[4,16,128]{2,1,0:T(8,128)(2,1)S(1)}, u32[]{:S(2)}, u32[]{:S(2)}) %collective-permute-start.16) | collective-permute-done | bytes 16416 | tf_op jit(solution)/shard_map/ppermute | solution.py:262
  45.8 8.7 %own_block.1 = (bf16[4,1024,128]{2,1,0:T(8,128)(2,1)S(1)}, f32[4,16,128]{2,1,0:T(8,128)S(1)}, f32[576,128]{1,0:T(8,128)S(1)}, f32[640,128]{1,0:T(8,128)S(1)}) custom-call(s32[4,4,4]{2,1,0:T(4,128)S(1)} %copy-done.5, f32[8,128]{1,0:T(8,128)S(1)} %fusion.7.refs_1_.refs_0_, f32[16,128]{1,0:T(8,128)S(1)} %pad_maximum_fusion.6.refs_2_.refs_1_, ...), custom_call_target="tpu_custom_call" | custom-call | flops 4 | bytes 1 | tf_op jit(solution)/shard_map/own_block/pallas_call | solution.py:645
  54.5 0.2 collective-permute-start.17
  54.7 1.5 %collective-permute-done.17 = f32[640,128]{1,0:T(8,128)S(1)} collective-permute-done((f32[640,128]{1,0:T(8,128)S(1)}, f32[640,128]{1,0:T(8,128)S(1)}, u32[]{:S(2)}, u32[]{:S(2)}) %collective-permute-start.17) | collective-permute-done | bytes 327712 | tf_op jit(solution)/shard_map/ppermute | solution.py:262
  56.2 1.9 %collective-permute-start.21 = (bf16[576,128]{1,0:T(8,128)(2,1)S(1)}, bf16[576,128]{1,0:T(8,128)(2,1)S(1)}, u32[]{:S(2)}, u32[]{:S(2)}) collective-permute-start(bf16[576,128]{1,0:T(8,128)(2,1)S(1)} %fusion), channel_id=1, source_target_pairs={{0,4},{4,0},{8,12},{12,8},{1,5},{5,1},{9,13},{13,9},{2,6},{6,2},{1... | collective-permute-start | bytes 442376 | tf_op jit(solution)/shard_map/ppermute | solution.py:272
  58.1 2.6 %collective-permute-start.18 = (f32[64,128]{1,0:T(8,128)S(1)}, f32[64,128]{1,0:T(8,128)S(1)}, u32[]{:S(2)}, u32[]{:S(2)}) collective-permute-start(f32[64,128]{1,0:T(8,128)S(1)} %slice_add_fusion.1), channel_id=1, source_target_pairs={{0,8},{4,12},{8,0},{12,4},{1,9},{5,13},{9,1},{13,5},{2,10},{6,14},... | collective-permute-start | bytes 98312 | tf_op jit(solution)/shard_map/ppermute | solution.py:267
  60.8 0.4 collective-permute-start.19
  61.2 3.4 %collective-permute-start.20 = (f32[64,128]{1,0:T(8,128)S(1)}, f32[64,128]{1,0:T(8,128)S(1)}, u32[]{:S(2)}, u32[]{:S(2)}) collective-permute-start(f32[64,128]{1,0:T(8,128)S(1)} %slice_add_fusion.1), channel_id=1, source_target_pairs={{0,12},{4,0},{8,4},{12,8},{1,13},{5,1},{9,5},{13,9},{2,14},{6,2},{... | collective-permute-start | bytes 98312 | tf_op jit(solution)/shard_map/ppermute | solution.py:267
  64.6 0.0 collective-permute-done.21
  64.6 0.9 %collective-permute-start.22 = (bf16[576,128]{1,0:T(8,128)(2,1)S(1)}, bf16[576,128]{1,0:T(8,128)(2,1)S(1)}, u32[]{:S(2)}, u32[]{:S(2)}) collective-permute-start(bf16[576,128]{1,0:T(8,128)(2,1)S(1)} %add_convert_fusion), channel_id=1, source_target_pairs={{0,8},{4,12},{8,0},{12,4},{1,9},{5,13},{9,1},{13,5},{2,10},{6,14},... | collective-permute-start | bytes 442376 | tf_op jit(solution)/shard_map/ppermute | solution.py:272
  65.6 0.0 collective-permute-done.18
  65.6 0.9 %collective-permute-done.19 = f32[64,128]{1,0:T(8,128)S(1)} collective-permute-done((f32[64,128]{1,0:T(8,128)S(1)}, f32[64,128]{1,0:T(8,128)S(1)}, u32[]{:S(2)}, u32[]{:S(2)}) %collective-permute-start.19) | collective-permute-done | bytes 32800 | tf_op jit(solution)/shard_map/ppermute | solution.py:267
  66.5 0.0 collective-permute-done.20
  66.5 2.8 %input_gradient.1 = (bf16[4,1024,128]{2,1,0:T(8,128)(2,1)}, f32[1,4,256]{2,1,0:T(4,128)}, f32[1,256]{1,0:T(1,128)}) custom-call(f32[8,128]{1,0:T(8,128)S(1)} %fusion.7.refs_1_.refs_0_, f32[16,128]{1,0:T(8,128)S(1)} %pad_maximum_fusion.6.refs_2_.refs_1_, f32[64,128]{1,0:T(8,128)S(1)} %add_add_fusion.refs_2_, f32[64,128]{1,0:T(8,128)S(1)} %add_add_fusion.1.refs_4_.refs_3_, ...), custom_call_target="tpu_custom_call" | custom-call | flops 33554432 | bytes 8388608 | tf_op jit(solution)/shard_map/input_gradient/pallas_call | solution.py:645
  69.2 4.1 %collective-permute-done.22 = bf16[576,128]{1,0:T(8,128)(2,1)S(1)} collective-permute-done((bf16[576,128]{1,0:T(8,128)(2,1)S(1)}, bf16[576,128]{1,0:T(8,128)(2,1)S(1)}, u32[]{:S(2)}, u32[]{:S(2)}) %collective-permute-start.22) | collective-permute-done | bytes 147488 | tf_op jit(solution)/shard_map/ppermute | solution.py:272
  73.4 0.1 collective-permute-start.23
  73.5 1.6 %collective-permute-done.23 = f32[576,128]{1,0:T(8,128)S(1)} collective-permute-done((f32[576,128]{1,0:T(8,128)S(1)}, f32[576,128]{1,0:T(8,128)S(1)}, u32[]{:S(2)}, u32[]{:S(2)}) %collective-permute-start.23) | collective-permute-done | bytes 294944 | tf_op jit(solution)/shard_map/ppermute | solution.py:262
  75.1 0.9 %maximum_select_fusion = f32[1,1152,128]{2,1,0:T(8,128)} fusion(f32[1,576,128]{2,1,0:T(8,128)S(1)} %bitcast.35, f32[1,576,128]{2,1,0:T(8,128)S(1)} %get-tuple-element.46, pred[]{:T(512)S(6)} %eq.3), kind=kLoop, calls=%fused_computation | loop fusion | flops 442368 | bytes 1179649 | tf_op jit(solution)/shard_map/jit(_where)/select_n | solution.py:802
  (36 shorter events, 0.4 us)
Async XLA Ops:
  0.6 5.8 %copy-start.9 = (bf16[1,128]{1,0:T(2,128)(2,1)S(1)}, bf16[1,128]{1,0:T(2,128)(2,1)}, u32[]{:S(2)}) copy-start(bf16[1,128]{1,0:T(2,128)(2,1)} %refs_4_.1) | copy-start | bytes 772
  0.6 5.8 %copy-start.8 = (bf16[1,128]{1,0:T(2,128)(2,1)S(1)}, bf16[1,128]{1,0:T(2,128)(2,1)}, u32[]{:S(2)}) copy-start(bf16[1,128]{1,0:T(2,128)(2,1)} %refs_5_.1) | copy-start | bytes 772
  0.7 9.0 %collective-permute-start.2 = (bf16[4,3,8,128]{3,2,1,0:T(8,128)(2,1)}, bf16[4,3,8,128]{3,2,1,0:T(8,128)(2,1)S(1)}, u32[]{:S(2)}, u32[]{:S(2)}) collective-permute-start(bf16[4,3,8,128]{3,2,1,0:T(8,128)(2,1)} %refs_11_.1), channel_id=1, source_target_pairs={{0,1},{1,0},{2,3},{3,2},{4,5},{5,4},{6,7},{7,6},{8,9},{9,8},{10,11... | collective-permute-start | bytes 73736 | tf_op jit(solution)/shard_map/ppermute | solution.py:262
  1.2 8.5 %collective-permute-start.3 = (bf16[4,3,8,128]{3,2,1,0:T(8,128)(2,1)}, bf16[4,3,8,128]{3,2,1,0:T(8,128)(2,1)S(1)}, u32[]{:S(2)}, u32[]{:S(2)}) collective-permute-start(bf16[4,3,8,128]{3,2,1,0:T(8,128)(2,1)} %refs_12_.3), channel_id=1, source_target_pairs={{0,1},{1,0},{2,3},{3,2},{4,5},{5,4},{6,7},{7,6},{8,9},{9,8},{10,11... | collective-permute-start | bytes 73736 | tf_op jit(solution)/shard_map/ppermute | solution.py:262
  1.2 1.2 %copy-start = (bf16[1,4,8,128,128]{4,3,2,1,0:T(8,128)(2,1)S(1)}, bf16[1,4,8,128,128]{4,3,2,1,0:T(8,128)(2,1)}, u32[]{:S(2)}) copy-start(bf16[1,4,8,128,128]{4,3,2,1,0:T(8,128)(2,1)} %param.10) | copy-start | bytes 3145732
  2.5 3.9 %copy-start.3 = (bf16[4,3,8,128]{3,2,1,0:T(8,128)(2,1)S(1)}, bf16[4,3,8,128]{3,2,1,0:T(8,128)(2,1)}, u32[]{:S(2)}) copy-start(bf16[4,3,8,128]{3,2,1,0:T(8,128)(2,1)} %refs_12_.3) | copy-start | bytes 73732
  2.5 3.9 %copy-start.4 = (bf16[4,3,8,128]{3,2,1,0:T(8,128)(2,1)S(1)}, bf16[4,3,8,128]{3,2,1,0:T(8,128)(2,1)}, u32[]{:S(2)}) copy-start(bf16[4,3,8,128]{3,2,1,0:T(8,128)(2,1)} %refs_11_.1) | copy-start | bytes 73732
  2.5 3.9 %copy-start.2 = (bf16[4,4,8,128]{3,2,1,0:T(8,128)(2,1)S(1)}, bf16[4,4,8,128]{3,2,1,0:T(8,128)(2,1)}, u32[]{:S(2)}) copy-start(bf16[4,4,8,128]{3,2,1,0:T(8,128)(2,1)} %refs_10_.3) | copy-start | bytes 98308
  2.5 4.0 %copy-start.7 = (bf16[1,4,256]{2,1,0:T(4,128)(2,1)S(1)}, bf16[1,4,256]{2,1,0:T(4,128)(2,1)}, u32[]{:S(2)}) copy-start(bf16[1,4,256]{2,1,0:T(4,128)(2,1)} %refs_3_.1) | copy-start | bytes 6148
  3.1 3.4 %collective-permute-start = (f32[8,128]{1,0:T(8,128)S(1)}, f32[8,128]{1,0:T(8,128)S(1)}, u32[]{:S(2)}, u32[]{:S(2)}) collective-permute-start(f32[8,128]{1,0:T(8,128)S(1)} %input_sums.1), channel_id=1, source_target_pairs={{0,1},{1,0},{2,3},{3,2},{4,5},{5,4},{6,7},{7,6},{8,9},{9,8},{10,11... | collective-permute-start | bytes 12296 | tf_op jit(solution)/shard_map/ppermute | solution.py:262
  3.6 13.6 %collective-permute-start.5 = (bf16[1152,128]{1,0:T(8,128)(2,1)}, bf16[1152,128]{1,0:T(8,128)(2,1)S(1)}, u32[]{:S(2)}, u32[]{:S(2)}) collective-permute-start(bf16[1152,128]{1,0:T(8,128)(2,1)} %bitcast.30), channel_id=1, source_target_pairs={{0,2},{2,0},{1,3},{3,1},{4,6},{6,4},{5,7},{7,5},{8,10},{10,8},{9,1... | collective-permute-start | bytes 884744 | tf_op jit(solution)/shard_map/ppermute | solution.py:262
  6.2 11.0 %copy-start.1 = (bf16[1,1152,128]{2,1,0:T(8,128)(2,1)S(1)}, bf16[1,1152,128]{2,1,0:T(8,128)(2,1)}, u32[]{:S(2)}) copy-start(bf16[1,1152,128]{2,1,0:T(8,128)(2,1)} %param.15) | copy-start | bytes 884740
  6.2 11.0 %copy-start.5 = (s32[4,4,4]{2,1,0:T(4,128)S(1)}, s32[4,4,4]{2,1,0:T(4,128)}, u32[]{:S(2)}) copy-start(s32[4,4,4]{2,1,0:T(4,128)} %refs_0_.5) | copy-start | bytes 772
  6.2 11.0 %copy-start.6 = (bf16[3,128]{1,0:T(4,128)(2,1)S(1)}, bf16[3,128]{1,0:T(4,128)(2,1)}, u32[]{:S(2)}) copy-start(bf16[3,128]{1,0:T(4,128)(2,1)} %refs_6_.1) | copy-start | bytes 2308
  6.3 16.7 %collective-permute-start.7 = (bf16[4,256,128]{2,1,0:T(8,128)(2,1)S(1)}, bf16[4,256,128]{2,1,0:T(8,128)(2,1)S(1)}, u32[]{:S(2)}, u32[]{:S(2)}) collective-permute-start(bf16[4,256,128]{2,1,0:T(8,128)(2,1)S(1)} %pad_maximum_fusion), channel_id=1, source_target_pairs={{0,2},{2,0},{1,3},{3,1},{4,6},{6,4},{5,7},{7,5},{8,10},{10,8},{9,1... | collective-permute-start | bytes 786440 | tf_op jit(solution)/shard_map/ppermute | solution.py:262
  6.5 10.7 %collective-permute-start.1 = (f32[8,128]{1,0:T(8,128)S(1)}, f32[8,128]{1,0:T(8,128)S(1)}, u32[]{:S(2)}, u32[]{:S(2)}) collective-permute-start(f32[8,128]{1,0:T(8,128)S(1)} %add.47.refs_1_), channel_id=1, source_target_pairs={{0,8},{4,12},{8,0},{12,4},{1,9},{5,13},{9,1},{13,5},{2,10},{6,14},... | collective-permute-start | bytes 12296 | tf_op jit(solution)/shard_map/ppermute | solution.py:267
  9.8 5.9 %collective-permute-start.4 = (f32[72,128]{1,0:T(8,128)S(1)}, f32[72,128]{1,0:T(8,128)S(1)}, u32[]{:S(2)}, u32[]{:S(2)}) collective-permute-start(f32[72,128]{1,0:T(8,128)S(1)} %get-tuple-element.58), channel_id=1, source_target_pairs={{0,4},{4,8},{8,12},{12,0},{1,5},{5,9},{9,13},{13,1},{2,6},{6,10},{... | collective-permute-start | bytes 110600 | tf_op jit(solution)/shard_map/ppermute | solution.py:267
  11.4 5.8 %collective-permute-start.6 = (f32[72,128]{1,0:T(8,128)S(1)}, f32[72,128]{1,0:T(8,128)S(1)}, u32[]{:S(2)}, u32[]{:S(2)}) collective-permute-start(f32[72,128]{1,0:T(8,128)S(1)} %get-tuple-element.59), channel_id=1, source_target_pairs={{0,12},{4,0},{8,4},{12,8},{1,13},{5,1},{9,5},{13,9},{2,14},{6,2},{... | collective-permute-start | bytes 110600 | tf_op jit(solution)/shard_map/ppermute | solution.py:267
  15.7 20.8 %collective-permute-start.12 = (bf16[4,768,128]{2,1,0:T(8,128)(2,1)S(1)}, bf16[4,768,128]{2,1,0:T(8,128)(2,1)S(1)}, u32[]{:S(2)}, u32[]{:S(2)}) collective-permute-start(bf16[4,768,128]{2,1,0:T(8,128)(2,1)S(1)} %slice.93), channel_id=1, source_target_pairs={{0,2},{2,0},{1,3},{3,1},{4,6},{6,4},{5,7},{7,5},{8,10},{10,8},{9,1... | collective-permute-start | bytes 2359304 | tf_op jit(solution)/shard_map/ppermute | solution.py:262
  23.0 1.3 %collective-permute-start.8 = (f32[64,128]{1,0:T(8,128)S(1)}, f32[64,128]{1,0:T(8,128)S(1)}, u32[]{:S(2)}, u32[]{:S(2)}) collective-permute-start(f32[64,128]{1,0:T(8,128)S(1)} %bitcast.33), channel_id=1, source_target_pairs={{0,1},{1,0},{2,3},{3,2},{4,5},{5,4},{6,7},{7,6},{8,9},{9,8},{10,11... | collective-permute-start | bytes 98312 | tf_op jit(solution)/shard_map/ppermute | solution.py:262
  23.1 10.7 %collective-permute-start.13 = (bf16[4,128,128]{2,1,0:T(8,128)(2,1)S(1)}, bf16[4,128,128]{2,1,0:T(8,128)(2,1)S(1)}, u32[]{:S(2)}, u32[]{:S(2)}) collective-permute-start(bf16[4,128,128]{2,1,0:T(8,128)(2,1)S(1)} %get-tuple-element.49), channel_id=1, source_target_pairs={{0,4},{4,8},{8,12},{12,0},{1,5},{5,9},{9,13},{13,1},{2,6},{6,10},{... | collective-permute-start | bytes 393224 | tf_op jit(solution)/shard_map/ppermute | solution.py:267
  24.2 7.7 %collective-permute-start.10 = (f32[64,128]{1,0:T(8,128)S(1)}, f32[64,128]{1,0:T(8,128)S(1)}, u32[]{:S(2)}, u32[]{:S(2)}) collective-permute-start(f32[64,128]{1,0:T(8,128)S(1)} %bitcast_add_fusion), channel_id=1, source_target_pairs={{0,4},{4,8},{8,12},{12,0},{1,5},{5,9},{9,13},{13,1},{2,6},{6,10},{... | collective-permute-start | bytes 98312 | tf_op jit(solution)/shard_map/ppermute | solution.py:267
  24.2 7.7 %collective-permute-start.11 = (f32[64,128]{1,0:T(8,128)S(1)}, f32[64,128]{1,0:T(8,128)S(1)}, u32[]{:S(2)}, u32[]{:S(2)}) collective-permute-start(f32[64,128]{1,0:T(8,128)S(1)} %bitcast_add_fusion), channel_id=1, source_target_pairs={{0,12},{4,0},{8,4},{12,8},{1,13},{5,1},{9,5},{13,9},{2,14},{6,2},{... | collective-permute-start | bytes 98312 | tf_op jit(solution)/shard_map/ppermute | solution.py:267
  28.1 5.6 %collective-permute-start.9 = (f32[64,128]{1,0:T(8,128)S(1)}, f32[64,128]{1,0:T(8,128)S(1)}, u32[]{:S(2)}, u32[]{:S(2)}) collective-permute-start(f32[64,128]{1,0:T(8,128)S(1)} %bitcast_add_fusion), channel_id=1, source_target_pairs={{0,8},{4,12},{8,0},{12,4},{1,9},{5,13},{9,1},{13,5},{2,10},{6,14},... | collective-permute-start | bytes 98312 | tf_op jit(solution)/shard_map/ppermute | solution.py:267
  32.0 6.3 %collective-permute-start.15 = (bf16[4,128,128]{2,1,0:T(8,128)(2,1)S(1)}, bf16[4,128,128]{2,1,0:T(8,128)(2,1)S(1)}, u32[]{:S(2)}, u32[]{:S(2)}) collective-permute-start(bf16[4,128,128]{2,1,0:T(8,128)(2,1)S(1)} %get-tuple-element.48), channel_id=1, source_target_pairs={{0,12},{4,0},{8,4},{12,8},{1,13},{5,1},{9,5},{13,9},{2,14},{6,2},{... | collective-permute-start | bytes 393224 | tf_op jit(solution)/shard_map/ppermute | solution.py:267
  36.5 4.0 %collective-permute-start.14 = (f32[88,128]{1,0:T(8,128)S(1)}, f32[88,128]{1,0:T(8,128)S(1)}, u32[]{:S(2)}, u32[]{:S(2)}) collective-permute-start(f32[88,128]{1,0:T(8,128)S(1)} %pad_maximum_fusion.3), channel_id=1, source_target_pairs={{0,2},{2,0},{1,3},{3,1},{4,6},{6,4},{5,7},{7,5},{8,10},{10,8},{9,1... | collective-permute-start | bytes 135176 | tf_op jit(solution)/shard_map/ppermute | solution.py:262
  44.5 1.2 %collective-permute-start.16 = (bf16[4,16,128]{2,1,0:T(8,128)(2,1)S(1)}, bf16[4,16,128]{2,1,0:T(8,128)(2,1)S(1)}, u32[]{:S(2)}, u32[]{:S(2)}) collective-permute-start(bf16[4,16,128]{2,1,0:T(8,128)(2,1)S(1)} %get-tuple-element.34), channel_id=1, source_target_pairs={{0,1},{1,0},{2,3},{3,2},{4,5},{5,4},{6,7},{7,6},{8,9},{9,8},{10,11... | collective-permute-start | bytes 49160 | tf_op jit(solution)/shard_map/ppermute | solution.py:262
  54.5 1.7 %collective-permute-start.17 = (f32[640,128]{1,0:T(8,128)S(1)}, f32[640,128]{1,0:T(8,128)S(1)}, u32[]{:S(2)}, u32[]{:S(2)}) collective-permute-start(f32[640,128]{1,0:T(8,128)S(1)} %get-tuple-element.36), channel_id=1, source_target_pairs={{0,1},{1,0},{2,3},{3,2},{4,5},{5,4},{6,7},{7,6},{8,9},{9,8},{10,11... | collective-permute-start | bytes 983048 | tf_op jit(solution)/shard_map/ppermute | solution.py:262
  56.2 8.3 %collective-permute-start.21 = (bf16[576,128]{1,0:T(8,128)(2,1)S(1)}, bf16[576,128]{1,0:T(8,128)(2,1)S(1)}, u32[]{:S(2)}, u32[]{:S(2)}) collective-permute-start(bf16[576,128]{1,0:T(8,128)(2,1)S(1)} %fusion), channel_id=1, source_target_pairs={{0,4},{4,0},{8,12},{12,8},{1,5},{5,1},{9,13},{13,9},{2,6},{6,2},{1... | collective-permute-start | bytes 442376 | tf_op jit(solution)/shard_map/ppermute | solution.py:272
  58.1 7.4 %collective-permute-start.18 = (f32[64,128]{1,0:T(8,128)S(1)}, f32[64,128]{1,0:T(8,128)S(1)}, u32[]{:S(2)}, u32[]{:S(2)}) collective-permute-start(f32[64,128]{1,0:T(8,128)S(1)} %slice_add_fusion.1), channel_id=1, source_target_pairs={{0,8},{4,12},{8,0},{12,4},{1,9},{5,13},{9,1},{13,5},{2,10},{6,14},... | collective-permute-start | bytes 98312 | tf_op jit(solution)/shard_map/ppermute | solution.py:267
  60.8 5.7 %collective-permute-start.19 = (f32[64,128]{1,0:T(8,128)S(1)}, f32[64,128]{1,0:T(8,128)S(1)}, u32[]{:S(2)}, u32[]{:S(2)}) collective-permute-start(f32[64,128]{1,0:T(8,128)S(1)} %slice_add_fusion.1), channel_id=1, source_target_pairs={{0,4},{4,8},{8,12},{12,0},{1,5},{5,9},{9,13},{13,1},{2,6},{6,10},{... | collective-permute-start | bytes 98312 | tf_op jit(solution)/shard_map/ppermute | solution.py:267
  61.2 5.3 %collective-permute-start.20 = (f32[64,128]{1,0:T(8,128)S(1)}, f32[64,128]{1,0:T(8,128)S(1)}, u32[]{:S(2)}, u32[]{:S(2)}) collective-permute-start(f32[64,128]{1,0:T(8,128)S(1)} %slice_add_fusion.1), channel_id=1, source_target_pairs={{0,12},{4,0},{8,4},{12,8},{1,13},{5,1},{9,5},{13,9},{2,14},{6,2},{... | collective-permute-start | bytes 98312 | tf_op jit(solution)/shard_map/ppermute | solution.py:267
  64.6 8.7 %collective-permute-start.22 = (bf16[576,128]{1,0:T(8,128)(2,1)S(1)}, bf16[576,128]{1,0:T(8,128)(2,1)S(1)}, u32[]{:S(2)}, u32[]{:S(2)}) collective-permute-start(bf16[576,128]{1,0:T(8,128)(2,1)S(1)} %add_convert_fusion), channel_id=1, source_target_pairs={{0,8},{4,12},{8,0},{12,4},{1,9},{5,13},{9,1},{13,5},{2,10},{6,14},... | collective-permute-start | bytes 442376 | tf_op jit(solution)/shard_map/ppermute | solution.py:272
  73.4 1.6 %collective-permute-start.23 = (f32[576,128]{1,0:T(8,128)S(1)}, f32[576,128]{1,0:T(8,128)S(1)}, u32[]{:S(2)}, u32[]{:S(2)}) collective-permute-start(f32[576,128]{1,0:T(8,128)S(1)} %get-tuple-element.47), channel_id=1, source_target_pairs={{0,1},{1,0},{2,3},{3,2},{4,5},{5,4},{6,7},{7,6},{8,9},{9,8},{10,11... | collective-permute-start | bytes 884744 | tf_op jit(solution)/shard_map/ppermute | solution.py:262
